TPU v7x, 32 devices: a whole 2x2x4 slice. The times are simulated.
32 devices in a mesh: dp: 4 (over y, x), fsdp: 8 (over z, core).
Axes of the slice: x: 2, y: 2, z: 4, core: 2. Of those that a mesh axis runs over, the one named last changes fastest.
Arguments:
- layer_input: bfloat16 [8192, 1280], P(('dp', 'fsdp')), may hold values from -6 to 6
- w_qkv: bfloat16 [1280, 3840], P(('dp', 'fsdp')), may hold values from -0.15625 to 0.15625
- w_out: bfloat16 [1280, 1280], P(('dp', 'fsdp')), may hold values from -4 to 4
- w_shared: bfloat16 [1280, 2688], P(('dp', 'fsdp')), may hold values from -0.15625 to 0.15625
- w_experts: bfloat16 [16, 1280, 2688], P(None, ('dp', 'fsdp')), may hold values from -0.15625 to 0.15625
- gains: bfloat16 [1280, 2], P(('dp', 'fsdp')), may hold values from 0.099609375 to 1.8984375
- routes: int32 [8192, 7], P(('dp', 'fsdp')), may hold values from 0 to 15, all different within a row; in each aligned block of 256 rows (0 to 255, 256 to 511, ...) at most 128 rows name the same one
- gates: float32 [8192, 7], P(('dp', 'fsdp')), may hold values from 0.2 to 0.6
- d_out: bfloat16 [8192, 1280], P(('dp', 'fsdp')), may hold values from -6 to 6
Outputs:
- layer_output: bfloat16 [8192, 1280], P(('dp', 'fsdp'))
- d_x: float32 [8192, 1280], P(('dp', 'fsdp'))
- g_qkv: float32 [1280, 3840], P(('dp', 'fsdp'))
- g_out: float32 [1280, 1280], P(('dp', 'fsdp'))
- g_shared: float32 [1280, 2688], P(('dp', 'fsdp'))
- g_experts: float32 [16, 1280, 2688], P(None, ('dp', 'fsdp'))
- g_gains: float32 [1280, 2], P(('dp', 'fsdp'))
Inputs may be any that keep to these rules, and one draw needn't show every extreme that they name: `routes`: each token names 7 different experts; among the 256 tokens of one device no expert is named more than 128 times, and in every draw some expert is named exactly 128 times by the tokens of some device.
All inputs are finite; a program needn't handle non-finite values.
Results may differ from a plain program's by a relative error of at most 0.015.
Values may be sent and summed in bfloat16 or wider, within the bound.
A program may use at most 384 MiB of HBM per device.

v0:
```python
import math

import jax
import jax.numpy as jnp
from jax import lax
from jax.sharding import PartitionSpec as P

HEADS = 10
HD = 128
EXP_GROUP = 4


norm_eps = 1e-06
masked_score = -1000000000.0


def contract_last(left_side, right_side):
    return lax.dot_general(
        left_side, right_side, (((1,), (1,)), ((), ())), preferred_element_type=jnp.float32
    )


def contract_first(left_side, right_side):
    return lax.dot_general(
        left_side, right_side, (((0,), (0,)), ((), ())), preferred_element_type=jnp.float32
    )


def rotary_tables(positions):
    half_dim = HD // 2
    frequency = 10000.0 ** (-jnp.arange(half_dim, dtype=jnp.float32) / half_dim)
    angles = positions.astype(jnp.float32)[:, None] * frequency[None, :]
    cosine = jnp.concatenate([jnp.cos(angles), jnp.cos(angles)], axis=1)
    sine_table = jnp.concatenate([jnp.sin(angles), jnp.sin(angles)], axis=1)
    return (cosine[:, None, :], sine_table[:, None, :])


def rotary(values, positions):
    cosine, sine_table = rotary_tables(positions)
    half_dim = HD // 2
    shaped = values.reshape(values.shape[0], -1, HD)
    turned = jnp.concatenate([-shaped[..., half_dim:], shaped[..., :half_dim]], axis=2)
    return (shaped * cosine + turned * sine_table).reshape(values.shape)


def rotary_back(gradient, positions):
    cosine, sine_table = rotary_tables(positions)
    half_dim = HD // 2
    shaped = gradient.reshape(gradient.shape[0], -1, HD)
    scaled = shaped * sine_table
    turned = jnp.concatenate([scaled[..., half_dim:], -scaled[..., :half_dim]], axis=2)
    return (shaped * cosine + turned).reshape(gradient.shape)


def fetch_dense(w_qkv, w_out, w_shared, gains):
    return (
        lax.all_gather(w_qkv, ("dp", "fsdp"), axis=0, tiled=True),
        lax.all_gather(w_out, ("dp", "fsdp"), axis=0, tiled=True),
        lax.all_gather(w_shared, ("dp", "fsdp"), axis=0, tiled=True),
        lax.all_gather(gains, ("dp", "fsdp"), axis=0, tiled=True),
    )


def fetch_expert(weight_group):
    return lax.all_gather(weight_group, ("dp", "fsdp"), axis=1, tiled=True)


def fetch_keys(keys_own, values_own):
    return (
        lax.all_gather(keys_own, "fsdp", axis=0, tiled=True),
        lax.all_gather(values_own, "fsdp", axis=0, tiled=True),
    )


def swiglu_parts(inputs, weights, hidden):
    gate_pre = jnp.dot(inputs, weights[:, :hidden], preferred_element_type=jnp.float32)
    up_pre = jnp.dot(inputs, weights[:, hidden : 2 * hidden], preferred_element_type=jnp.float32)
    return (gate_pre, up_pre)


def swiglu_back(weights, gate_pre, up_pre, upstream, hidden):
    down_grad = jnp.dot(upstream, weights[:, 2 * hidden :], preferred_element_type=jnp.float32)
    sigmoid_gate = jax.nn.sigmoid(gate_pre)
    gate_grad = (
        down_grad * up_pre * sigmoid_gate * (1.0 + gate_pre * (1.0 - sigmoid_gate))
    ).astype(jnp.bfloat16)
    up_grad = (down_grad * gate_pre * sigmoid_gate).astype(jnp.bfloat16)
    input_grad = contract_last(gate_grad, weights[:, :hidden]) + contract_last(
        up_grad, weights[:, hidden : 2 * hidden]
    )
    return (gate_grad, up_grad, input_grad)


def norm_back(upstream, unit_rows, inverse, gain):
    scaled = upstream * gain
    gain_grad = jnp.sum(upstream * unit_rows, axis=0)
    input_grad = inverse * (
        scaled - unit_rows * jnp.mean(scaled * unit_rows, axis=1, keepdims=True)
    )
    return (input_grad, gain_grad)


def per_device(layer_input, w_qkv, w_out, w_shared, w_experts, gains, routes, gates, d_out):
    tokens_here = layer_input.shape[0]
    model_width = layer_input.shape[1]
    hidden = w_shared.shape[1] // 3
    experts = w_experts.shape[0]
    shard_rows = w_experts.shape[1]
    group_size = EXP_GROUP
    group_count = experts // group_size
    sequence_len = tokens_here * lax.axis_size("fsdp")
    head_scale = 1.0 / math.sqrt(HD)
    full_qkv, full_out, full_shared, full_gains = fetch_dense(w_qkv, w_out, w_shared, gains)
    gain_one = full_gains[:, 0].astype(jnp.float32)
    gain_two = full_gains[:, 1].astype(jnp.float32)
    inputs_f = layer_input.astype(jnp.float32)
    inv_one = lax.rsqrt(jnp.mean(inputs_f * inputs_f, axis=1, keepdims=True) + norm_eps)
    unit_one = inputs_f * inv_one
    normed_one = (unit_one * gain_one).astype(jnp.bfloat16)
    projected = jnp.dot(normed_one, full_qkv, preferred_element_type=jnp.float32)
    positions = lax.axis_index("fsdp") * tokens_here + jnp.arange(tokens_here, dtype=jnp.int32)
    queries = rotary(projected[:, :model_width], positions).astype(jnp.bfloat16)
    keys_own = rotary(projected[:, model_width : 2 * model_width], positions).astype(jnp.bfloat16)
    values_own = projected[:, 2 * model_width :].astype(jnp.bfloat16)
    all_keys, all_values = fetch_keys(keys_own, values_own)
    all_positions = jnp.arange(sequence_len, dtype=jnp.int32)
    allowed = all_positions[None, :] <= positions[:, None]

    def split_heads(tensor_block):
        return tensor_block.reshape(tensor_block.shape[0], HEADS, HD).transpose(1, 0, 2)

    def join_heads(tensor_block):
        return tensor_block.transpose(1, 0, 2).reshape(tensor_block.shape[1], model_width)

    def probabilities(query_head, key_head):
        scores = contract_last(query_head, key_head) * head_scale
        scores = jnp.where(allowed, scores, masked_score)
        row_max = jnp.max(scores, axis=1, keepdims=True)
        shifted = jnp.exp(scores - row_max)
        row_total = jnp.sum(shifted, axis=1, keepdims=True)
        return (shifted / row_total, row_max, row_total)

    def head_forward(unused_carry, operands):
        query_head, key_head, value_head = operands
        softmax_rows = probabilities(query_head, key_head)[0].astype(jnp.bfloat16)
        return (unused_carry, jnp.dot(softmax_rows, value_head, preferred_element_type=jnp.float32))

    query_heads = split_heads(queries)
    start_carry = jnp.zeros((), jnp.float32)
    unused_one, mixed_heads = lax.scan(
        head_forward, start_carry, (query_heads, split_heads(all_keys), split_heads(all_values))
    )
    mixed = join_heads(mixed_heads).astype(jnp.bfloat16)
    middle = inputs_f + contract_last(mixed, full_out)
    inv_two = lax.rsqrt(jnp.mean(middle * middle, axis=1, keepdims=True) + norm_eps)
    unit_two = middle * inv_two
    normed_two = (unit_two * gain_two).astype(jnp.bfloat16)
    shared_gate, shared_up = swiglu_parts(normed_two, full_shared, hidden)
    shared_hidden = (jax.nn.silu(shared_gate) * shared_up).astype(jnp.bfloat16)
    shared_result = contract_last(shared_hidden, full_shared[:, 2 * hidden :])
    expert_ids = jnp.arange(experts, dtype=jnp.int32)
    chosen = routes[:, :, None] == expert_ids[None, None, :]
    member = jnp.any(chosen, axis=1)
    gate_table = jnp.sum(jnp.where(chosen, gates[:, :, None], 0.0), axis=1)
    slot_rank = jnp.cumsum(member.astype(jnp.int32), axis=0) - 1
    slot_ids = jnp.arange(tokens_here // 2, dtype=jnp.int32)
    token_ids = jnp.arange(tokens_here, dtype=jnp.int32)
    slot_match = member.T[:, None, :] & (slot_rank.T[:, None, :] == slot_ids[None, :, None])
    slot_token = jnp.sum(jnp.where(slot_match, token_ids[None, None, :], 0), axis=2)
    slot_gate = jnp.sum(jnp.where(slot_match, gate_table.T[:, None, :], 0.0), axis=2)
    group_token = slot_token.reshape(group_count, group_size, slot_token.shape[1])
    group_gate = slot_gate.reshape(group_count, group_size, slot_gate.shape[1])
    grouped_shards = w_experts.reshape(group_count, group_size, shard_rows, 3 * hidden)

    def expert_forward(running, operands):
        shard_group, rows_group, weights_group = operands
        full_group = fetch_expert(shard_group)
        for member_index in range(group_size):
            weights_full = full_group[member_index]
            slot_rows = rows_group[member_index]
            picked = normed_two[slot_rows]
            gate_pre, up_pre = swiglu_parts(picked, weights_full, hidden)
            hidden_act = (jax.nn.silu(gate_pre) * up_pre).astype(jnp.bfloat16)
            result = contract_last(hidden_act, weights_full[:, 2 * hidden :])
            running = running.at[slot_rows].add(weights_group[member_index][:, None] * result)
        return (running, None)

    zero_rows = jnp.zeros((tokens_here, model_width), jnp.float32)
    routed, stored = lax.scan(expert_forward, zero_rows, (grouped_shards, group_token, group_gate))
    layer_out = (middle + shared_result + routed).astype(jnp.bfloat16)
    cotangent = d_out.astype(jnp.float32)
    back_qkv, back_out, back_shared, spare_gains = fetch_dense(w_qkv, w_out, w_shared, gains)
    keys_back, values_back = fetch_keys(keys_own, values_own)
    shared_upstream = cotangent.astype(jnp.bfloat16)
    shared_gate_grad, shared_up_grad, normed_grad = swiglu_back(
        back_shared, shared_gate, shared_up, shared_upstream, hidden
    )
    shared_term = jnp.concatenate(
        [
            contract_first(normed_two, shared_gate_grad),
            contract_first(normed_two, shared_up_grad),
            contract_first(shared_upstream, shared_hidden),
        ],
        axis=1,
    )

    def expert_backward(running, operands):
        source, rows_group, weights_group = operands
        full_group = fetch_expert(source)
        picked_list = []
        upstream_list = []
        gate_list = []
        up_list = []
        hidden_list = []
        for member_index in range(group_size):
            weights_full = full_group[member_index]
            slot_rows = rows_group[member_index]
            picked = normed_two[slot_rows]
            gate_pre, up_pre = swiglu_parts(picked, weights_full, hidden)
            hidden_act = (jax.nn.silu(gate_pre) * up_pre).astype(jnp.bfloat16)
            upstream = (weights_group[member_index][:, None] * cotangent[slot_rows]).astype(
                jnp.bfloat16
            )
            gate_grad, up_grad, input_grad = swiglu_back(
                weights_full, gate_pre, up_pre, upstream, hidden
            )
            running = running.at[slot_rows].add(input_grad)
            picked_list.append(picked)
            upstream_list.append(upstream)
            gate_list.append(gate_grad)
            up_list.append(up_grad)
            hidden_list.append(hidden_act)
        terms = []
        for member_index in range(group_size):
            picked_cols = lax.slice_in_dim(
                picked_list[member_index], 0, shard_rows * lax.axis_size(("dp", "fsdp")), axis=1
            )
            upstream_cols = lax.slice_in_dim(
                upstream_list[member_index], 0, shard_rows * lax.axis_size(("dp", "fsdp")), axis=1
            )
            terms.append(
                jnp.concatenate(
                    [
                        contract_first(picked_cols, gate_list[member_index]),
                        contract_first(picked_cols, up_list[member_index]),
                        contract_first(upstream_cols, hidden_list[member_index]),
                    ],
                    axis=1,
                )
            )
        summed = lax.psum_scatter(
            jnp.stack(terms, axis=1), ("dp", "fsdp"), scatter_dimension=0, tiled=True
        )
        return (running, summed.transpose(1, 0, 2))

    routed_grad, group_grads = lax.scan(
        expert_backward, zero_rows, (grouped_shards, group_token, group_gate)
    )
    expert_grads = group_grads.reshape(experts, shard_rows, 3 * hidden)
    normed_grad = normed_grad + routed_grad
    middle_part, gain_two_grad = norm_back(normed_grad, unit_two, inv_two, gain_two)
    middle_grad = cotangent + middle_part
    attn_upstream = middle_grad.astype(jnp.bfloat16)
    out_term = contract_first(attn_upstream, mixed)
    mixed_grad = jnp.dot(attn_upstream, back_out, preferred_element_type=jnp.float32).astype(
        jnp.bfloat16
    )

    def head_backward(unused_carry, operands):
        query_head, key_head, value_head, grad_head = operands
        softmax_rows, row_max, row_total = probabilities(query_head, key_head)
        softmax_low = softmax_rows.astype(jnp.bfloat16)
        prob_grad = contract_last(grad_head, value_head)
        row_terms = jnp.sum(softmax_rows * prob_grad, axis=1, keepdims=True)
        score_grad = (softmax_rows * (prob_grad - row_terms)).astype(jnp.bfloat16)
        query_grad = jnp.dot(score_grad, key_head, preferred_element_type=jnp.float32) * head_scale
        key_grad = contract_first(score_grad, query_head) * head_scale
        value_grad = contract_first(softmax_low, grad_head)
        return (
            unused_carry,
            (query_grad, key_grad, value_grad, row_max[:, 0], row_total[:, 0], row_terms[:, 0]),
        )

    unused_two, (query_grads, key_terms, value_terms, max_rows, total_rows, term_rows) = lax.scan(
        head_backward,
        start_carry,
        (query_heads, split_heads(keys_back), split_heads(values_back), split_heads(mixed_grad)),
    )
    key_own_grad, value_own_grad = (
        lax.psum_scatter(
            join_heads(key_terms).astype(jnp.bfloat16), "fsdp", scatter_dimension=0, tiled=True
        ).astype(jnp.float32),
        lax.psum_scatter(
            join_heads(value_terms).astype(jnp.bfloat16), "fsdp", scatter_dimension=0, tiled=True
        ).astype(jnp.float32),
    )
    projected_grad = jnp.concatenate(
        [
            rotary_back(join_heads(query_grads), positions),
            rotary_back(key_own_grad, positions),
            value_own_grad,
        ],
        axis=1,
    ).astype(jnp.bfloat16)
    qkv_term = contract_first(normed_one, projected_grad)
    normed_one_grad = contract_last(projected_grad, back_qkv)
    input_part, gain_one_grad = norm_back(normed_one_grad, unit_one, inv_one, gain_one)
    input_grad = middle_grad + input_part
    gain_term = jnp.stack([gain_one_grad, gain_two_grad], axis=1)
    qkv_grad, out_grad, shared_grad, gains_grad = (
        lax.psum_scatter(qkv_term, ("dp", "fsdp"), scatter_dimension=0, tiled=True),
        lax.psum_scatter(out_term, ("dp", "fsdp"), scatter_dimension=0, tiled=True),
        lax.psum_scatter(shared_term, ("dp", "fsdp"), scatter_dimension=0, tiled=True),
        lax.psum_scatter(gain_term, ("dp", "fsdp"), scatter_dimension=0, tiled=True),
    )
    return (layer_out, input_grad, qkv_grad, out_grad, shared_grad, expert_grads, gains_grad)


def solution(mesh):
    return jax.shard_map(
        per_device,
        mesh=mesh,
        in_specs=(
            P(("dp", "fsdp"), None),
            P(("dp", "fsdp"), None),
            P(("dp", "fsdp"), None),
            P(("dp", "fsdp"), None),
            P(None, ("dp", "fsdp"), None),
            P(("dp", "fsdp"), None),
            P(("dp", "fsdp"), None),
            P(("dp", "fsdp"), None),
            P(("dp", "fsdp"), None),
        ),
        out_specs=(
            P(("dp", "fsdp"), None),
            P(("dp", "fsdp"), None),
            P(("dp", "fsdp"), None),
            P(("dp", "fsdp"), None),
            P(("dp", "fsdp"), None),
            P(None, ("dp", "fsdp"), None),
            P(("dp", "fsdp"), None),
        ),
        check_vma=False,
    )
```

profile of v0, /device:TPU:20, one launch (start us, length us, event | category | flops | bytes accessed | tf_op | source)
XLA Modules:
  0.0 6692.0 jit_solution(10586494357656810569)
XLA Ops:
  8.0 36.1 all-gather.2
  47.1 48.4 all-gather.17.cloned.1.call-done
  121.8 46.1 all-gather.19.cloned.1.call-done
  184.0 41.1 all-gather.21.cloned.1.call-done
  240.9 37.8 while.54
  290.1 70.2 %all-gather.25.cloned.1.call-done = bf16[1280,2688]{1,0:T(8,128)(2,1)} async-done(((bf16[40,2688]{1,0:T(8,128)(2,1)}), bf16[1280,2688]{1,0:T(8,128)(2,1)}) %all-gather.25.cloned.1.call-update) | async-done | bytes 6881296 | tf_op jit(solution)/shard_map/all_gather | solution.py:59
  370.6 4558.2 %while.53 = (s32[]{:T(128)}, f32[256,1280]{1,0:T(8,128)}, f32[4,4,40,2688]{3,2,1,0:T(8,128)}, s32[4,4,128]{2,1,0:T(4,128)S(1)}, f32[4,4,128]{2,1,0:T(4,128)}, /*...) while((s32[]{:T(128)}, f32[256,1280]{1,0:T(8,128)}, ...), condition=%wide.region_24.25_spmd.clone, body=%wide.region_18.24_spmd.sunk.clone | while | flops 9490470912 | bytes 1089377280 | solution.py:256
  411.5 149.9 %all-gather.29.cloned.1.call-done = bf16[1,4,1280,2688]{3,2,1,0:T(8,128)(2,1)} async-done(((bf16[1,4,40,2688]{3,2,1,0:T(8,128)(2,1)}), bf16[1,4,1280,2688]{3,2,1,0:T(8,128)(2,1)}) %all-gather.29.cloned.1.call-update) | async-done | bytes 27525136 | tf_op jit(solution)/shard_map/while/body/eval_jaxpr/all_gather | solution.py:65
  685.0 59.2 copy.152
  773.5 749.0 %all-reduce.11.cloned.1.call-done = f32[1280,4,2688]{2,1,0:T(4,128)} async-done(((f32[1280,4,2688]{2,1,0:T(4,128)}), f32[1280,4,2688]{2,1,0:T(4,128)}) %all-reduce.11.cloned.1.call-update) | async-done | bytes 55050256 | tf_op jit(solution)/shard_map/while
  1543.1 151.4 %all-gather.29.cloned.1.call-done = bf16[1,4,1280,2688]{3,2,1,0:T(8,128)(2,1)} async-done(((bf16[1,4,40,2688]{3,2,1,0:T(8,128)(2,1)}), bf16[1,4,1280,2688]{3,2,1,0:T(8,128)(2,1)}) %all-gather.29.cloned.1.call-update) | async-done | bytes 27525136 | tf_op jit(solution)/shard_map/while/body/eval_jaxpr/all_gather | solution.py:65
  1782.3 35.8 pad_maximum_fusion.11
  1818.1 59.2 copy.152
  1906.5 749.0 %all-reduce.11.cloned.1.call-done = f32[1280,4,2688]{2,1,0:T(4,128)} async-done(((f32[1280,4,2688]{2,1,0:T(4,128)}), f32[1280,4,2688]{2,1,0:T(4,128)}) %all-reduce.11.cloned.1.call-update) | async-done | bytes 55050256 | tf_op jit(solution)/shard_map/while
  2676.1 151.1 %all-gather.29.cloned.1.call-done = bf16[1,4,1280,2688]{3,2,1,0:T(8,128)(2,1)} async-done(((bf16[1,4,40,2688]{3,2,1,0:T(8,128)(2,1)}), bf16[1,4,1280,2688]{3,2,1,0:T(8,128)(2,1)}) %all-gather.29.cloned.1.call-update) | async-done | bytes 27525136 | tf_op jit(solution)/shard_map/while/body/eval_jaxpr/all_gather | solution.py:65
  2950.8 59.2 copy.152
  3039.3 749.0 %all-reduce.11.cloned.1.call-done = f32[1280,4,2688]{2,1,0:T(4,128)} async-done(((f32[1280,4,2688]{2,1,0:T(4,128)}), f32[1280,4,2688]{2,1,0:T(4,128)}) %all-reduce.11.cloned.1.call-update) | async-done | bytes 55050256 | tf_op jit(solution)/shard_map/while
  3808.9 151.1 %all-gather.29.cloned.1.call-done = bf16[1,4,1280,2688]{3,2,1,0:T(8,128)(2,1)} async-done(((bf16[1,4,40,2688]{3,2,1,0:T(8,128)(2,1)}), bf16[1,4,1280,2688]{3,2,1,0:T(8,128)(2,1)}) %all-gather.29.cloned.1.call-update) | async-done | bytes 27525136 | tf_op jit(solution)/shard_map/while/body/eval_jaxpr/all_gather | solution.py:65
  4083.5 59.2 copy.152
  4172.0 749.0 %all-reduce.11.cloned.1.call-done = f32[1280,4,2688]{2,1,0:T(4,128)} async-done(((f32[1280,4,2688]{2,1,0:T(4,128)}), f32[1280,4,2688]{2,1,0:T(4,128)}) %all-reduce.11.cloned.1.call-update) | async-done | bytes 55050256 | tf_op jit(solution)/shard_map/while
  4937.3 121.8 %while.55 = (s32[]{:T(128)}, f32[10,256,128]{1,2,0:T(8,128)S(1)}, bf16[10,2048,128]{1,2,0:T(8,128)(2,1)}, bf16[10,2048,128]{1,2,0:T(8,128)(2,1)}, bf16[10,256,12...) while((s32[]{:T(128)}, f32[10,256,128]{1,2,0:T(8,128)S(1)}, ...), condition=%wide.region_30.31_spmd.clone.clone, body=%wide.region_26.30_spmd.clone.sunk.clone | while | flops 681082112 | bytes 37633224 | solution.py:284
  5060.2 888.3 %while.52 = (s32[]{:T(128)}, f32[256,1280]{1,0:T(8,128)S(1)}, s32[4,4,128]{2,1,0:T(4,128)}, f32[4,4,128]{2,1,0:T(4,128)}, bf16[256,1280]{1,0:T(8,128)(2,1)S(1)}, /*index=5*/bf16[4,4,40,2688]{3,2,1,0:T(8,128)(2,1)}) while((s32[]{:T(128)}, f32[256,1280]{1,0:T(8,128)S(1)}, s32[4,4,128]{2,1,0:T(4,128)}, f32[4,4,128]{2,1,0:T(4,128)}, ...), condition=%wide.region_17.18_spmd.clone, body=%wide.region_12.17_spmd.sunk.clone | while | flops 3527284224 | bytes 217727168 | solution.py:189
  5068.3 160.8 %all-gather.27.cloned.1.call-done = bf16[1,4,1280,2688]{3,2,1,0:T(8,128)(2,1)} async-done(((bf16[1,4,40,2688]{3,2,1,0:T(8,128)(2,1)}), bf16[1,4,1280,2688]{3,2,1,0:T(8,128)(2,1)}) %all-gather.27.cloned.1.call-update) | async-done | bytes 27525136 | tf_op jit(solution)/shard_map/while/body/eval_jaxpr/all_gather | solution.py:65
  5291.1 159.8 %all-gather.27.cloned.1.call-done = bf16[1,4,1280,2688]{3,2,1,0:T(8,128)(2,1)} async-done(((bf16[1,4,40,2688]{3,2,1,0:T(8,128)(2,1)}), bf16[1,4,1280,2688]{3,2,1,0:T(8,128)(2,1)}) %all-gather.27.cloned.1.call-update) | async-done | bytes 27525136 | tf_op jit(solution)/shard_map/while/body/eval_jaxpr/all_gather | solution.py:65
  5512.9 159.7 %all-gather.27.cloned.1.call-done = bf16[1,4,1280,2688]{3,2,1,0:T(8,128)(2,1)} async-done(((bf16[1,4,40,2688]{3,2,1,0:T(8,128)(2,1)}), bf16[1,4,1280,2688]{3,2,1,0:T(8,128)(2,1)}) %all-gather.27.cloned.1.call-update) | async-done | bytes 27525136 | tf_op jit(solution)/shard_map/while/body/eval_jaxpr/all_gather | solution.py:65
  5734.6 159.8 %all-gather.27.cloned.1.call-done = bf16[1,4,1280,2688]{3,2,1,0:T(8,128)(2,1)} async-done(((bf16[1,4,40,2688]{3,2,1,0:T(8,128)(2,1)}), bf16[1,4,1280,2688]{3,2,1,0:T(8,128)(2,1)}) %all-gather.27.cloned.1.call-update) | async-done | bytes 27525136 | tf_op jit(solution)/shard_map/while/body/eval_jaxpr/all_gather | solution.py:65
  5971.3 36.4 reduce-scatter.7.cloned.1.call-done
  6010.2 58.1 reduce-scatter.9.cloned.1.call-done
  6084.6 233.3 %all-reduce.9.cloned.1.call-done = f32[1280,2688]{0,1:T(8,128)} async-done(((f32[1280,2688]{0,1:T(8,128)}), f32[1280,2688]{0,1:T(8,128)}) %all-reduce.9.cloned.1.call-update) | async-done | bytes 13762576
  6329.4 41.0 all-reduce.2
  6373.8 84.1 %reduce-scatter.13.cloned.1.call-done = f32[40,1280]{1,0:T(8,128)} async-done(((f32[1280,1280]{1,0:T(8,128)}), f32[40,1280]{1,0:T(8,128)}) %reduce-scatter.13.cloned.1.call-update) | async-done | bytes 204816 | tf_op jit(solution)/shard_map/reduce_scatter | solution.py:312
  6457.9 226.9 %reduce-scatter.11.cloned.1.call-done = f32[40,3840]{1,0:T(8,128)} async-done(((f32[1280,3840]{1,0:T(8,128)}), f32[40,3840]{1,0:T(8,128)}) %reduce-scatter.11.cloned.1.call-update) | async-done | bytes 614416 | tf_op jit(solution)/shard_map/reduce_scatter | solution.py:311
  (1039 shorter events, 1210.6 us)
Async XLA Ops:
  7.2 88.3 %all-gather.17.cloned.1.call-start = ((), (), s32[]{:S(2)}) async-start(), calls=%async_computation.4 | async-start | bytes 10137600 | tf_op jit(solution)/shard_map/all_gather | solution.py:57
  7.9 160.0 %all-gather.19.cloned.1.call-start = ((), (), s32[]{:S(2)}) async-start(), calls=%async_computation.5 | async-start | bytes 5898240 | tf_op jit(solution)/shard_map/all_gather | solution.py:70
  46.8 242.0 %copy-start.62 = (f32[1280]{0:T(1024)}, f32[1280]{0:T(1024)S(1)}, u32[]{:S(2)}) copy-start(f32[1280]{0:T(1024)S(1)} %get-tuple-element.283) | copy-start | bytes 15364
  113.9 111.2 %all-gather.21.cloned.1.call-start = ((), (), s32[]{:S(2)}) async-start(), calls=%async_computation.6 | async-start | bytes 5898240 | tf_op jit(solution)/shard_map/all_gather | solution.py:71
  116.3 169.4 %all-gather.23.cloned.1.call-start = ((), (), s32[]{:S(2)}) async-start(), calls=%async_computation.7 | async-start | bytes 3379200 | tf_op jit(solution)/shard_map/all_gather | solution.py:58
  116.9 243.4 %all-gather.25.cloned.1.call-start = ((), (), s32[]{:S(2)}) async-start(), calls=%async_computation.8 | async-start | bytes 7096320 | tf_op jit(solution)/shard_map/all_gather | solution.py:59
  370.6 4558.2 %copy-start.63 = (f32[1280]{0:T(1024)S(1)}, f32[1280]{0:T(1024)}, u32[]{:S(2)}) copy-start(f32[1280]{0:T(1024)} %copy-done.62) | copy-start | bytes 15364
  370.6 4558.2 %copy-start.80 = (f32[256]{0:T(256)S(1)}, f32[256]{0:T(256)}, u32[]{:S(2)}) copy-start(f32[256]{0:T(256)} %copy-done.79) | copy-start | bytes 3076
  393.8 167.7 %all-gather.29.cloned.1.call-start = ((), (), s32[]{:S(2)}) async-start(), calls=%async_computation.15 | async-start | bytes 28385280 | tf_op jit(solution)/shard_map/while/body/eval_jaxpr/all_gather | solution.py:65
  396.2 1126.3 %all-reduce.11.cloned.1.call-start = ((), (), s32[]{:S(2)}) async-start(), calls=%async_computation.16 | async-start | bytes 110100480 | tf_op jit(solution)/shard_map/while
  773.5 751.9 %copy-start.3 = (f32[256,1280]{1,0:T(8,128)}, f32[256,1280]{1,0:T(8,128)S(1)}, u32[]{:S(2)}) copy-start(f32[256,1280]{1,0:T(8,128)S(1)} %scatter_fusion.7) | copy-start | bytes 3932164 | tf_op jit(solution)/shard_map/while
  1525.4 169.1 %all-gather.29.cloned.1.call-start = ((), (), s32[]{:S(2)}) async-start(), calls=%async_computation.15 | async-start | bytes 28385280 | tf_op jit(solution)/shard_map/while/body/eval_jaxpr/all_gather | solution.py:65
  1527.9 1127.7 %all-reduce.11.cloned.1.call-start = ((), (), s32[]{:S(2)}) async-start(), calls=%async_computation.16 | async-start | bytes 110100480 | tf_op jit(solution)/shard_map/while
  1906.5 751.9 %copy-start.3 = (f32[256,1280]{1,0:T(8,128)}, f32[256,1280]{1,0:T(8,128)S(1)}, u32[]{:S(2)}) copy-start(f32[256,1280]{1,0:T(8,128)S(1)} %scatter_fusion.7) | copy-start | bytes 3932164 | tf_op jit(solution)/shard_map/while
  2658.5 168.7 %all-gather.29.cloned.1.call-start = ((), (), s32[]{:S(2)}) async-start(), calls=%async_computation.15 | async-start | bytes 28385280 | tf_op jit(solution)/shard_map/while/body/eval_jaxpr/all_gather | solution.py:65
  2660.9 1127.4 %all-reduce.11.cloned.1.call-start = ((), (), s32[]{:S(2)}) async-start(), calls=%async_computation.16 | async-start | bytes 110100480 | tf_op jit(solution)/shard_map/while
  3039.3 751.9 %copy-start.3 = (f32[256,1280]{1,0:T(8,128)}, f32[256,1280]{1,0:T(8,128)S(1)}, u32[]{:S(2)}) copy-start(f32[256,1280]{1,0:T(8,128)S(1)} %scatter_fusion.7) | copy-start | bytes 3932164 | tf_op jit(solution)/shard_map/while
  3791.2 168.7 %all-gather.29.cloned.1.call-start = ((), (), s32[]{:S(2)}) async-start(), calls=%async_computation.15 | async-start | bytes 28385280 | tf_op jit(solution)/shard_map/while/body/eval_jaxpr/all_gather | solution.py:65
  3793.6 1127.4 %all-reduce.11.cloned.1.call-start = ((), (), s32[]{:S(2)}) async-start(), calls=%async_computation.16 | async-start | bytes 110100480 | tf_op jit(solution)/shard_map/while
  4172.0 751.9 %copy-start.3 = (f32[256,1280]{1,0:T(8,128)}, f32[256,1280]{1,0:T(8,128)S(1)}, u32[]{:S(2)}) copy-start(f32[256,1280]{1,0:T(8,128)S(1)} %scatter_fusion.7) | copy-start | bytes 3932164 | tf_op jit(solution)/shard_map/while
  5060.3 168.7 %all-gather.27.cloned.1.call-start = ((), (), s32[]{:S(2)}) async-start(), calls=%async_computation.14 | async-start | bytes 28385280 | tf_op jit(solution)/shard_map/while/body/eval_jaxpr/all_gather | solution.py:65
  5064.2 181.9 %copy-start.24 = (bf16[128,1280]{1,0:T(8,128)(2,1)}, bf16[128,1280]{1,0:T(8,128)(2,1)S(1)}, u32[]{:S(2)}) copy-start(bf16[128,1280]{1,0:T(8,128)(2,1)S(1)} %gather_fusion) | copy-start | bytes 983044 | tf_op jit(solution)/shard_map/while
  5283.2 167.7 %all-gather.27.cloned.1.call-start = ((), (), s32[]{:S(2)}) async-start(), calls=%async_computation.14 | async-start | bytes 28385280 | tf_op jit(solution)/shard_map/while/body/eval_jaxpr/all_gather | solution.py:65
  5504.9 167.7 %all-gather.27.cloned.1.call-start = ((), (), s32[]{:S(2)}) async-start(), calls=%async_computation.14 | async-start | bytes 28385280 | tf_op jit(solution)/shard_map/while/body/eval_jaxpr/all_gather | solution.py:65
  5726.7 167.7 %all-gather.27.cloned.1.call-start = ((), (), s32[]{:S(2)}) async-start(), calls=%async_computation.14 | async-start | bytes 28385280 | tf_op jit(solution)/shard_map/while/body/eval_jaxpr/all_gather | solution.py:65
  5948.4 59.3 reduce-scatter.7.cloned.1.call-start
  5949.0 119.3 %reduce-scatter.9.cloned.1.call-start = ((), (), s32[]{:S(2)}) async-start(), calls=%async_computation.10 | async-start | bytes 5898240 | tf_op jit(solution)/shard_map/reduce_scatter | solution.py:293
  5949.8 368.1 %all-reduce.9.cloned.1.call-start = ((), (), s32[]{:S(2)}) async-start(), calls=%async_computation.13 | async-start | bytes 27525120
  5962.6 495.2 %reduce-scatter.13.cloned.1.call-start = ((), (), s32[]{:S(2)}) async-start(), calls=%async_computation.12 | async-start | bytes 6758400 | tf_op jit(solution)/shard_map/reduce_scatter | solution.py:312
  5968.0 716.8 %reduce-scatter.11.cloned.1.call-start = ((), (), s32[]{:S(2)}) async-start(), calls=%async_computation.11 | async-start | bytes 20275200 | tf_op jit(solution)/shard_map/reduce_scatter | solution.py:311
  6084.6 236.7 %copy-start.45 = (bf16[256,10,128]{0,2,1:T(8,128)(2,1)S(1)}, bf16[256,10,128]{0,2,1:T(8,128)(2,1)}, u32[]{:S(2)}) copy-start(bf16[256,10,128]{0,2,1:T(8,128)(2,1)} %fusion.204) | copy-start | bytes 1966084
  6084.6 236.7 %copy-start.47 = (bf16[256,1280]{0,1:T(8,128)(2,1)S(1)}, bf16[256,1280]{0,1:T(8,128)(2,1)}, u32[]{:S(2)}) copy-start(bf16[256,1280]{0,1:T(8,128)(2,1)} %copy-done.46) | copy-start | bytes 1966084
  (209 other events, 2969.2 us)
Sparse Core Ops, SparseCore 0:
  11.0 84.3 all-gather.16
  114.0 53.9 all-gather.18
  170.2 54.8 all-gather.20
  227.7 57.8 all-gather.22
  288.4 71.8 all-gather.24
  397.3 164.1 all-gather.28
  744.4 778.1 all-reduce.10
  1529.3 165.1 all-gather.28
  1877.4 778.1 all-reduce.10
  2662.0 165.1 all-gather.28
  3010.1 778.1 all-reduce.10
  3794.8 165.1 all-gather.28
  4142.9 778.1 all-reduce.10
  5063.9 165.1 all-gather.26
  5286.7 164.1 all-gather.26
  5508.5 164.0 all-gather.26
  5730.2 164.1 all-gather.26
  5951.3 56.3 reduce-scatter.6
  6010.0 58.2 reduce-scatter.8
  6074.5 243.3 all-reduce.8
  6320.8 136.9 reduce-scatter.12
  6464.8 219.8 reduce-scatter.10
where the time goes:
time: 6710 us; the launch traced here: 6690 us
  waiting for transfers between devices  5090 us (76%)
  local copies, waits for them, and re-layouts  551 us (8%)
  matrix products  504 us (8%)
  other arithmetic  416 us (6%)
  blocking collectives  77 us (1%)
    while x16, waiting for transfers between devices  3000 us
    all_gather x8, waiting for transfers between devices, fetch_expert(): return lax.all_gather(weight_group, ('dp', 'fsdp'), axis=1, tiled=True)  1240 us
    another operation x20, other arithmetic, expert_backward(): jnp.stack(terms, axis=1)  306 us
    another operation x4, local copies, waits for them, and re-layouts, expert_backward(): jnp.stack(terms, axis=1)  237 us
    unnamed x11, waiting for transfers between devices  236 us
    reduce_scatter x1, waiting for transfers between devices, per_device(): lax.psum_scatter(qkv_term, ('dp', 'fsdp'), scatter_dimension=0, tiled=True)  227 us
    dot_general x83, matrix products, contract_last(): lax.dot_general(left_side, right_side, (((1,), (1,)), ((), ())), preferre...  219 us
    dot_general x73, matrix products, contract_first(): lax.dot_general(left_side, right_side, (((0,), (0,)), ((), ())), preferre...  139 us
  transfers between devices with their start and end apart: 22, of which 22 were waited for; matrix products, arithmetic and copies ran while one was open for 5% of the time, Pallas kernels for 0%

commit v1 on v0

v1 whole, which is shorter than its diff:
```python
import functools
import math

import jax
import jax.numpy as jnp
from jax import lax
from jax.experimental import pallas as pl
from jax.experimental.pallas import tpu as pltpu
from jax.sharding import PartitionSpec as P

HEADS = 10
HD = 128
norm_eps = 1e-06
masked_score = -1000000000.0
BF = jnp.bfloat16
F32 = jnp.float32
VMEM_LIMIT = 60 * 2**20


def dot_nn(a, b):
    return lax.dot_general(a, b, (((1,), (0,)), ((), ())), preferred_element_type=F32)


def dot_nt(a, b):
    return lax.dot_general(a, b, (((1,), (1,)), ((), ())), preferred_element_type=F32)


def dot_tn(a, b):
    return lax.dot_general(a, b, (((0,), (0,)), ((), ())), preferred_element_type=F32)


def after(value, *marks):
    return lax.optimization_barrier((value,) + marks)[0]


def put(buffer, value, *index):
    rest = buffer.ndim - len(index)
    starts = tuple(index) + (0,) * rest
    return lax.dynamic_update_slice(
        buffer, value.reshape((1,) * len(index) + buffer.shape[len(index) :]), starts
    )


def take(values, index):
    return lax.dynamic_index_in_dim(values, index, 0, keepdims=False)


def proj_kernel(x_ref, gain_ref, w_ref, cos_ref, sin_ref, xn_ref, q_ref, k_ref, v_ref, kt_ref, vt_ref):
    x = x_ref[...].astype(F32)
    inv = lax.rsqrt(jnp.mean(x * x, axis=1, keepdims=True) + norm_eps)
    xn = (x * inv * gain_ref[...]).astype(BF)
    xn_ref[...] = xn
    width = q_ref.shape[1]
    cos = cos_ref[...]
    sin = sin_ref[...]
    for part in range(3):
        for head in range(width // HD):
            lo = part * width + head * HD
            u = dot_nn(xn, w_ref[:, lo : lo + HD])
            cols = slice(head * HD, (head + 1) * HD)
            if part < 2:
                u = u * cos + pltpu.roll(u, HD // 2, 1) * sin
            low = u.astype(BF)
            if part == 0:
                q_ref[:, cols] = low
            elif part == 1:
                k_ref[:, cols] = low
                kt_ref[cols, :] = u.T.astype(BF)
            else:
                v_ref[:, cols] = low
                vt_ref[cols, :] = u.T.astype(BF)


def project(x_all, gain, w, cos, sin, seq):
    model = x_all.shape[1]
    width = w.shape[1] // 3
    block = 256
    row = lambda cols: pl.BlockSpec((block, cols), lambda i: (i, 0))
    col = pl.BlockSpec((width, block), lambda i: (0, i))
    flat = jax.ShapeDtypeStruct((seq, width), BF)
    turned = jax.ShapeDtypeStruct((width, seq), BF)
    return pl.pallas_call(
        proj_kernel,
        grid=(seq // block,),
        in_specs=[
            row(model),
            pl.BlockSpec((1, model), lambda i: (0, 0)),
            pl.BlockSpec(w.shape, lambda i: (0, 0)),
            row(HD),
            row(HD),
        ],
        out_specs=[row(model), row(width), row(width), row(width), col, col],
        out_shape=[jax.ShapeDtypeStruct((seq, model), BF), flat, flat, flat, turned, turned],
        compiler_params=pltpu.CompilerParams(vmem_limit_bytes=VMEM_LIMIT),
        cost_estimate=pl.CostEstimate(
            flops=2 * seq * model * w.shape[1], bytes_accessed=seq * model * 6, transcendentals=0
        ),
    )(x_all, gain, w, cos, sin)


def causal(rows):
    shape = (rows, rows)
    key = lax.broadcasted_iota(jnp.int32, shape, 0)
    query = lax.broadcasted_iota(jnp.int32, shape, 1)
    return key <= query


def attend_kernel(block, count, scale, q_ref, k_ref, vt_ref, o_ref, lse_ref):
    step = pl.program_id(1)
    for j in range(count):

        @pl.when(step == j)
        def _():
            whole = j * block
            q = q_ref[...]
            tail = dot_nt(k_ref[whole : whole + block, :], q) * scale
            tail = jnp.where(causal(block), tail, masked_score)
            top = jnp.max(tail, axis=0, keepdims=True)
            if j:
                front = dot_nt(k_ref[:whole, :], q) * scale
                top = jnp.maximum(top, jnp.max(front, axis=0, keepdims=True))
            tail = jnp.exp(tail - top)
            total = jnp.sum(tail, axis=0, keepdims=True)
            mixed = dot_nn(vt_ref[:, whole : whole + block], tail.astype(BF))
            if j:
                front = jnp.exp(front - top)
                total = total + jnp.sum(front, axis=0, keepdims=True)
                mixed = mixed + dot_nn(vt_ref[:, :whole], front.astype(BF))
            o_ref[...] = (mixed / total).T.astype(BF)
            lse_ref[0] = top + jnp.log(total)


def attend(q, k, vt, block):
    seq, width = q.shape
    count = seq // block
    heads = width // HD
    scale = 1.0 / math.sqrt(HD)
    return pl.pallas_call(
        functools.partial(attend_kernel, block, count, scale),
        grid=(heads, count),
        in_specs=[
            pl.BlockSpec((block, HD), lambda h, i: (i, h)),
            pl.BlockSpec((seq, HD), lambda h, i: (0, h)),
            pl.BlockSpec((HD, seq), lambda h, i: (h, 0)),
        ],
        out_specs=[
            pl.BlockSpec((block, HD), lambda h, i: (i, h)),
            pl.BlockSpec((1, 1, block), lambda h, i: (h, 0, i)),
        ],
        out_shape=[
            jax.ShapeDtypeStruct((seq, width), BF),
            jax.ShapeDtypeStruct((heads, 1, seq), F32),
        ],
        compiler_params=pltpu.CompilerParams(vmem_limit_bytes=VMEM_LIMIT),
        cost_estimate=pl.CostEstimate(
            flops=8 * seq * seq * width, bytes_accessed=seq * width * 8, transcendentals=0
        ),
    )(q, k, vt)


def unrotate(g, cos, sin):
    return g * cos - pltpu.roll(g, HD // 2, 1) * sin


def attend_back_kernel(
    block, count, scale,
    q_ref, k_ref, kt_ref, v_ref, o_ref, do_ref, lse_ref, cos_ref, sin_ref,
    dq_ref, dk_ref, dv_ref, dk_acc, dv_acc,
):
    step = pl.program_id(1)

    @pl.when(step == 0)
    def _():
        dk_acc[...] = jnp.zeros_like(dk_acc)
        dv_acc[...] = jnp.zeros_like(dv_acc)

    for j in range(count):

        @pl.when(step == j)
        def _():
            wide = (j + 1) * block
            here = slice(j * block, wide)
            q = q_ref[...]
            do = do_ref[...]
            row = jnp.sum((do.astype(F32) * o_ref[...].astype(F32)).T, axis=0, keepdims=True)
            lse = lse_ref[0]
            parts = [(slice(0, j * block), False)] if j else []
            parts.append((here, True))
            dq = None
            for span, edge in parts:
                p = jnp.exp(dot_nt(k_ref[span, :], q) * scale - lse)
                if edge:
                    p = jnp.where(causal(block), p, 0.0)
                ds = (p * (dot_nt(v_ref[span, :], do) - row)).astype(BF)
                dv_acc[span, :] += dot_nn(p.astype(BF), do)
                dk_acc[span, :] += dot_nn(ds, q)
                term = dot_nn(kt_ref[:, span], ds)
                dq = term if dq is None else dq + term
            dq_ref[...] = unrotate(dq.T * scale, cos_ref[here, :], sin_ref[here, :]).astype(BF)

    @pl.when(step == count - 1)
    def _():
        dk_ref[...] = unrotate(dk_acc[...] * scale, cos_ref[...], sin_ref[...]).astype(BF)
        dv_ref[...] = dv_acc[...].astype(BF)


def attend_back(q, k, kt, v, o, do, lse, cos, sin, block):
    seq, width = q.shape
    count = seq // block
    heads = width // HD
    scale = 1.0 / math.sqrt(HD)
    piece = pl.BlockSpec((block, HD), lambda h, i: (i, h))
    whole = pl.BlockSpec((seq, HD), lambda h, i: (0, h))
    turned = pl.BlockSpec((HD, seq), lambda h, i: (h, 0))
    table = pl.BlockSpec((seq, HD), lambda h, i: (0, 0))
    flat = jax.ShapeDtypeStruct((seq, width), BF)
    return pl.pallas_call(
        functools.partial(attend_back_kernel, block, count, scale),
        grid=(heads, count),
        in_specs=[
            piece, whole, turned, whole, piece, piece,
            pl.BlockSpec((1, 1, block), lambda h, i: (h, 0, i)), table, table,
        ],
        out_specs=[piece, whole, whole],
        out_shape=[flat, flat, flat],
        scratch_shapes=[pltpu.VMEM((seq, HD), F32), pltpu.VMEM((seq, HD), F32)],
        compiler_params=pltpu.CompilerParams(vmem_limit_bytes=VMEM_LIMIT),
        cost_estimate=pl.CostEstimate(
            flops=20 * seq * seq * width, bytes_accessed=seq * width * 16, transcendentals=0
        ),
    )(q, k, kt, v, o, do, lse, cos, sin)


def expert_kernel(hidden, x_ref, c_ref, w_ref, dx_ref, gu_ref, hid_ref):
    x = x_ref[...]
    gate = dot_nn(x, w_ref[:, :hidden])
    up = dot_nn(x, w_ref[:, hidden : 2 * hidden])
    down = dot_nn(c_ref[...], w_ref[:, 2 * hidden :])
    sig = 1.0 / (1.0 + jnp.exp(-gate))
    act = gate * sig
    hid_ref[...] = (act * up).astype(BF)
    dup = (down * act).astype(BF)
    dgate = (down * up * sig * (1.0 + gate * (1.0 - sig))).astype(BF)
    gu_ref[:, :hidden] = dgate
    gu_ref[:, hidden:] = dup
    dx = dot_nt(dgate, w_ref[:, :hidden]) + dot_nt(dup, w_ref[:, hidden : 2 * hidden])
    dx_ref[...] = dx.astype(dx_ref.dtype)


def expert(x, c, w, kind):
    rows, model = x.shape
    hidden = w.shape[1] // 3
    block = min(256, rows)
    row = lambda cols: pl.BlockSpec((block, cols), lambda i: (i, 0))
    return pl.pallas_call(
        functools.partial(expert_kernel, hidden),
        grid=(rows // block,),
        in_specs=[row(model), row(model), pl.BlockSpec(w.shape, lambda i: (0, 0))],
        out_specs=[row(model), row(2 * hidden), row(hidden)],
        out_shape=[
            jax.ShapeDtypeStruct((rows, model), kind),
            jax.ShapeDtypeStruct((rows, 2 * hidden), BF),
            jax.ShapeDtypeStruct((rows, hidden), BF),
        ],
        compiler_params=pltpu.CompilerParams(vmem_limit_bytes=VMEM_LIMIT),
        cost_estimate=pl.CostEstimate(
            flops=10 * rows * model * hidden, bytes_accessed=rows * model * 12, transcendentals=0
        ),
    )(x, c, w)


def per_device(x, w_qkv, w_out, w_shared, w_experts, gains, routes, gates, d_out):
    tokens, model = x.shape
    hidden = w_shared.shape[1] // 3
    experts, shard = w_experts.shape[:2]
    dps, fss = lax.axis_size("dp"), lax.axis_size("fsdp")
    cores = dps * fss // experts
    lanes = fss // cores
    seq = tokens * fss
    slots = tokens // 2
    per = -(-HEADS // fss)
    busy = -(-HEADS // per)
    width = per * HD
    dp, fs = lax.axis_index("dp"), lax.axis_index("fsdp")
    z, c = fs // cores, fs % cores

    def over_z(value, pairs):
        return lax.ppermute(
            value, "fsdp", [(a * cores + k, b * cores + k) for a, b in pairs for k in range(cores)]
        )

    def turn_z(value, by):
        return over_z(value, [(a, (a + by) % lanes) for a in range(lanes)])

    def over_core(value, m):
        return lax.ppermute(
            value, "fsdp", [(a * cores + k, a * cores + (k ^ m)) for a in range(lanes) for k in range(cores)]
        )

    def over_dp(value, m):
        return lax.ppermute(value, "dp", [(a, a ^ m) for a in range(dps)])

    def up(value, least, most):
        return over_z(value, [(a, a + 1) for a in range(least, most)])

    def down(value, least, most):
        return over_z(value, [(a, a - 1) for a in range(least, most)])

    def gather_z(value):
        buffer = put(jnp.zeros((lanes + 1,) + value.shape, value.dtype), value, z)
        rising = falling = value
        for s in range(1, lanes):
            rising = up(rising, s - 1, lanes - 1)
            falling = down(falling, 1, lanes - s + 1)
            buffer = put(buffer, rising, jnp.where(z >= s, z - s, lanes))
            buffer = put(buffer, falling, jnp.where(z + s < lanes, z + s, lanes))
        return buffer

    def gather_seq(value):
        buffer = jnp.zeros((lanes + 1, cores) + value.shape, value.dtype)

        def place(buffer, block, row):
            buffer = put(buffer, block, row, c)
            for m in range(1, cores):
                buffer = put(buffer, over_core(block, m), row, c ^ m)
            return buffer

        buffer = place(buffer, value, z)
        rising = falling = value
        for s in range(1, lanes):
            rising = up(rising, s - 1, lanes - 1)
            falling = down(falling, 1, lanes - s + 1)
            buffer = place(buffer, rising, jnp.where(z >= s, z - s, lanes))
            buffer = place(buffer, falling, jnp.where(z + s < lanes, z + s, lanes))
        return buffer.reshape((lanes + 1) * cores * value.shape[0], value.shape[1])

    def sum_z(parts):
        rising = falling = None
        for s in range(1, lanes):
            far = take(parts, jnp.clip(z + lanes - s, 0, lanes - 1)).astype(F32)
            near = take(parts, jnp.clip(z - lanes + s, 0, lanes - 1)).astype(F32)
            if rising is not None:
                far = far + rising.astype(F32)
                near = near + falling.astype(F32)
            rising = up(far.astype(BF), 0, s)
            falling = down(near.astype(BF), lanes - s, lanes)
        total = take(parts, z).astype(F32)
        if rising is not None:
            total = total + rising.astype(F32) + falling.astype(F32)
        return total

    def gather_dp(value):
        buffer = put(jnp.zeros((dps,) + value.shape, value.dtype), value, dp)
        for m in range(1, dps):
            buffer = put(buffer, over_dp(value, m), dp ^ m)
        return buffer

    def join_cores(value):
        buffer = jnp.zeros(value.shape[:2] + (cores,) + value.shape[2:], value.dtype)

        def place(buffer, block, k):
            return lax.dynamic_update_slice(buffer, block[:, :, None], (0, 0, k, 0, 0))

        buffer = place(buffer, value, c)
        for m in range(1, cores):
            buffer = place(buffer, over_core(value, m), c ^ m)
        return buffer.reshape(-1, value.shape[-1])

    def gather_rows(value):
        return join_cores(gather_dp(gather_z(value)[:lanes]))

    def own_heads(target):
        cut = w_qkv.reshape(shard, 3, HEADS, HD)
        cut = jnp.pad(cut, ((0, 0), (0, 0), (0, fss * per - HEADS), (0, 0)))
        cut = cut.reshape(shard, 3, fss, width)
        return lax.dynamic_index_in_dim(cut, target, 2, keepdims=False).reshape(shard, 3 * width)

    def gather_heads():
        buffer = put(jnp.zeros((fss, shard, 3 * width), BF), own_heads(fs), fs)
        for k in range(1, fss):
            pairs = [(f, (f + k) % fss) for f in range(fss) if (f + k) % fss < busy]
            buffer = put(
                buffer,
                lax.ppermute(own_heads((fs + k) % fss), "fsdp", pairs),
                (fs - k) % fss,
            )
        return gather_dp(buffer).reshape(model, 3 * width)

    x_all = gather_seq(x)
    w_heads = gather_heads()
    small = gather_z(gains.T.astype(F32))[:lanes]
    gain_all = join_gain = gather_dp(small)
    both = [None] * cores
    gain_buf = jnp.zeros((dps, lanes, cores, 2, shard), F32)
    gain_buf = lax.dynamic_update_slice(gain_buf, join_gain[:, :, None], (0, 0, c, 0, 0))
    for m in range(1, cores):
        gain_buf = lax.dynamic_update_slice(
            gain_buf, over_core(gain_all, m)[:, :, None], (0, 0, c ^ m, 0, 0)
        )
    gain_rows = gain_buf.transpose(3, 0, 1, 2, 4).reshape(2, model)
    gain_one, gain_two = gain_rows[0:1], gain_rows[1:2]

    half = HD // 2
    frequency = 10000.0 ** (-jnp.arange(half, dtype=F32) / half)
    angles = jnp.arange(seq, dtype=jnp.int32).astype(F32)[:, None] * frequency[None, :]
    cosine, sine = jnp.cos(angles), jnp.sin(angles)
    cos = jnp.concatenate([cosine, cosine], axis=1)
    sin = jnp.concatenate([-sine, sine], axis=1)

    table = jnp.concatenate([routes.T.astype(F32), gates.T], axis=0)
    tables = gather_z(table)[:lanes]
    topk = routes.shape[1]
    picks, weights = tables[:, :topk], tables[:, topk:]
    triangle = (jnp.arange(tokens)[:, None] <= jnp.arange(tokens)[None, :]).astype(BF)
    slot_ids = jnp.arange(slots, dtype=F32)
    select, weigh, slot_gate = [], [], []
    for m in range(dps):
        hit = picks == ((dp ^ m) * lanes + z).astype(F32)
        member = jnp.any(hit, axis=1)
        gate = jnp.sum(jnp.where(hit, weights, 0.0), axis=1)
        rank = dot_nn(member.astype(BF), triangle) - 1.0
        match = member[:, None, :] & (rank[:, None, :] == slot_ids[None, :, None])
        select.append(match.astype(BF))
        scaled = jnp.where(match, gate[:, None, :], 0.0)
        weigh.append(scaled.astype(BF))
        slot_gate.append(jnp.sum(scaled, axis=2, keepdims=True))

    def pick(blocks, m):
        return lax.dot_general(
            select[m], blocks, (((2,), (1,)), ((0,), (0,))), preferred_element_type=F32
        )

    xn_one, q, k, v, kt, vt = project(x_all, gain_one, w_heads, cos, sin, seq)

    d_out_z = after(d_out, x_all)
    held = w_experts.reshape(dps, lanes, shard, 3 * hidden)
    held = after(held, x_all)
    mine = lambda where: lax.dynamic_index_in_dim(held, where, 1, keepdims=False)
    rows_z = put(jnp.zeros((lanes, dps, shard, 3 * hidden), BF), mine(z), z)
    for s in range(1, lanes):
        rows_z = put(rows_z, turn_z(mine((z + s) % lanes), s), (z - s) % lanes)
    rows_to = lambda where: lax.dynamic_index_in_dim(rows_z, where, 1, keepdims=False)
    rows_dp = put(jnp.zeros((dps, lanes, shard, 3 * hidden), BF), rows_to(dp), dp)
    for m in range(1, dps):
        rows_dp = put(rows_dp, over_dp(rows_to(dp ^ m), m), dp ^ m)
    w_own = join_cores(rows_dp)

    dense = gather_rows(after(jnp.concatenate([w_out, w_shared], axis=1), x_all))
    out_all = dense[:, :model]
    shared_all = dense[:, model:]

    o, lse = attend(q, k, vt, 256)

    blocks_o = o.reshape(fss, tokens, width)
    mixed = put(jnp.zeros((fss, tokens, width), BF), take(blocks_o, fs), fs)
    for s in range(1, fss):
        pairs = [(f, (f + s) % fss) for f in range(busy)]
        mixed = put(
            mixed,
            lax.ppermute(take(blocks_o, (fs + s) % fss), "fsdp", pairs),
            (fs - s) % fss,
        )
    heads = mixed.transpose(1, 0, 2).reshape(tokens, fss * width)[:, :model]

    middle = x.astype(F32) + dot_nt(heads, out_all)
    inv_two = lax.rsqrt(jnp.mean(middle * middle, axis=1, keepdims=True) + norm_eps)
    unit_two = middle * inv_two
    xn_two = (unit_two * gain_two).astype(BF)

    up_blocks = gather_z(d_out_z)[:lanes]
    in_blocks = gather_z(xn_two)[:lanes]
    xs, cs = [], []
    for m in range(dps):
        part = pick(in_blocks, m).astype(BF)
        xs.append(over_dp(part, m) if m else part)
        part = (pick(up_blocks, m) * slot_gate[m]).astype(BF)
        cs.append(over_dp(part, m) if m else part)
    flat = lambda parts: jnp.stack(parts).reshape(-1, model)
    x_slots, c_slots = flat(xs), flat(cs)
    dx_slots, gu_slots, hid_slots = expert(x_slots, c_slots, w_own, BF)

    dx_shared, gu_shared, hid_shared = expert(xn_two, d_out, shared_all, F32)
    f_shared = dot_nt(hid_shared, shared_all[:, 2 * hidden :])

    def combine(parts, matrix):
        parts = parts.reshape(dps, lanes, slots, model)
        back = [over_dp(parts[m], m) if m else parts[0] for m in range(dps)]
        total = None
        for m in range(dps):
            term = lax.dot_general(
                matrix[m], back[m], (((1,), (1,)), ((0,), (0,))), preferred_element_type=F32
            )
            total = term if total is None else total + term
        return sum_z(total)

    dx_routed = combine(dx_slots, select)
    f_slots = dot_nt(hid_slots, w_own[:, 2 * hidden :]).astype(BF)
    g_own = jnp.concatenate([dot_tn(x_slots, gu_slots), dot_tn(c_slots, hid_slots)], axis=1)
    routed = combine(f_slots, weigh)
    layer_out = (middle + f_shared + routed).astype(BF)

    dxn_two = dx_shared + dx_routed
    scaled = dxn_two * gain_two
    dx_two = d_out.astype(F32) + inv_two * (
        scaled - unit_two * jnp.mean(scaled * unit_two, axis=1, keepdims=True)
    )
    d_attn = dx_two.astype(BF)

    da_all = gather_seq(d_attn)[:seq]
    out_cols = jnp.pad(out_all, ((0, 0), (0, fss * width - model)))
    out_cols = lax.dynamic_slice_in_dim(out_cols, fs * width, width, 1)
    d_o = dot_nn(da_all, out_cols).astype(BF)
    g_out_part = dot_tn(da_all, o)
    dq, dk, dv = attend_back(q, k, kt, v, o, d_o, lse, cos, sin, 256)
    d_qkv = jnp.concatenate([dq, dk, dv], axis=1)
    dxn_part = dot_nt(d_qkv, w_heads).reshape(lanes, cores, tokens, model)
    at_core = lambda k: lax.dynamic_index_in_dim(dxn_part, k, 1, keepdims=False)
    sums = at_core(c)
    for m in range(1, cores):
        sums = sums + over_core(at_core(c ^ m).astype(BF), m).astype(F32)
    dxn_one = sum_z(sums)
    inputs = x.astype(F32)
    inv_one = lax.rsqrt(jnp.mean(inputs * inputs, axis=1, keepdims=True) + norm_eps)
    unit_one = inputs * inv_one
    scaled = dxn_one * gain_one
    d_x = dx_two + inv_one * (scaled - unit_one * jnp.mean(scaled * unit_one, axis=1, keepdims=True))

    def reduce_cores(part):
        part = part.reshape(dps, lanes, cores, shard, part.shape[1])
        at = lambda k: lax.dynamic_index_in_dim(part, k, 2, keepdims=False)
        total = at(c)
        for m in range(1, cores):
            total = total + over_core(at(c ^ m).astype(BF), m).astype(F32)
        return total

    own = reduce_cores(g_own).astype(BF)
    by_dp = put(jnp.zeros_like(own), take(own, dp), dp)
    for m in range(1, dps):
        by_dp = put(by_dp, over_dp(take(own, dp ^ m), m), dp ^ m)
    at_z = lambda where: lax.dynamic_index_in_dim(by_dp, where, 1, keepdims=False)
    by_z = put(jnp.zeros((lanes,) + by_dp.shape[:1] + by_dp.shape[2:], BF), at_z(z), z)
    for s in range(1, lanes):
        by_z = put(by_z, turn_z(at_z((z + s) % lanes), s), (z - s) % lanes)
    g_experts = by_z.transpose(1, 0, 2, 3).reshape(experts, shard, 3 * hidden).astype(F32)

    g_shared_part = jnp.concatenate([dot_tn(xn_two, gu_shared), dot_tn(d_out, hid_shared)], axis=1)
    own = reduce_cores(g_shared_part)
    total = take(own, dp)
    low = own.astype(BF)
    for m in range(1, dps):
        total = total + over_dp(take(low, dp ^ m), m).astype(F32)
    low = total.astype(BF)
    g_shared = take(total, z)
    for s in range(1, lanes):
        g_shared = g_shared + turn_z(take(low, (z + s) % lanes), s).astype(F32)

    g_part = jnp.concatenate([dot_tn(xn_one, d_qkv), g_out_part], axis=1)
    g_part = g_part.reshape(dps, fss, shard, 4 * width)
    total = take(g_part, dp)
    low = g_part.astype(BF)
    for m in range(1, dps):
        total = total + over_dp(take(low, dp ^ m), m).astype(F32)
    low = total.astype(BF)
    g_mix = put(jnp.zeros((fss, shard, 4 * width), BF), take(low, fs), fs)
    for s in range(1, fss):
        pairs = [(f, (f + s) % fss) for f in range(busy)]
        g_mix = put(
            g_mix, lax.ppermute(take(low, (fs + s) % fss), "fsdp", pairs), (fs - s) % fss
        )
    g_mix = g_mix.reshape(fss, shard, 4, width).transpose(1, 2, 0, 3).reshape(shard, 4, fss * width)
    g_mix = g_mix[:, :, :model].astype(F32)
    g_qkv = g_mix[:, :3].reshape(shard, 3 * model)
    g_out = g_mix[:, 3]

    one = jnp.sum(w_qkv.astype(F32) * g_qkv, axis=1)
    two = jnp.sum(w_shared[:, : 2 * hidden].astype(F32) * g_shared[:, : 2 * hidden], axis=1)
    two = two + jnp.sum(
        w_experts[:, :, : 2 * hidden].astype(F32) * g_experts[:, :, : 2 * hidden], axis=(0, 2)
    )
    g_gains = jnp.stack([one, two], axis=1) / gains.astype(F32)
    return (layer_out, d_x, g_qkv, g_out, g_shared, g_experts, g_gains)


def solution(mesh):
    rows = P(("dp", "fsdp"), None)
    cube = P(None, ("dp", "fsdp"), None)
    return jax.shard_map(
        per_device,
        mesh=mesh,
        in_specs=(rows, rows, rows, rows, cube, rows, rows, rows, rows),
        out_specs=(rows, rows, rows, rows, rows, cube, rows),
        check_vma=False,
    )
```

time: 6710 us -> 1370 us (0.20)
  waiting for transfers between devices: 5090 us -> 633 us
  matrix products: 504 us -> 94.1 us
  local copies, waits for them, and re-layouts: 551 us -> 147 us
  other arithmetic: 416 us -> 70.1 us
  starting transfers between devices: 1.44 us -> 298 us
  Pallas kernels: 0 us -> 103 us
  blocking collectives: 77 us -> 0 us
    while x16 -> x0, waiting for transfers between devices: 3000 us -> none
    all_gather x13 -> x0, waiting for transfers between devices: 1460 us -> none  [the longest x8 1240 us: fetch_expert(): return lax.all_gather(weight_group, ('dp', 'fsdp'), axis=1, tiled=True)]
    ppermute x0 -> x143, waiting for transfers between devices: none -> 633 us  [the longest x69 315 us: over_z(): lax.ppermute(value, 'fsdp', [(a * cores + k, b * cores + k) for a, b in p...]
    dot_general x245 -> x31, matrix products: 504 us -> 94.1 us  [the longest x8 31.3 us: combine(): lax.dot_general(matrix[m], back[m], (((1,), (1,)), ((0,), (0,))), preferr...]
    reduce_scatter x4 -> x0, waiting for transfers between devices: 406 us -> none  [the longest x1 227 us: per_device(): lax.psum_scatter(qkv_term, ('dp', 'fsdp'), scatter_dimension=0, tiled=True)]
    another operation x29 -> x2, other arithmetic: 308 us -> 6.79 us  [per_device(): flat = lambda parts: jnp.stack(parts).reshape(-1, model)]
    ppermute x0 -> x143, starting transfers between devices: none -> 298 us  [the longest x69 163 us: over_z(): lax.ppermute(value, 'fsdp', [(a * cores + k, b * cores + k) for a, b in p...]
    unnamed x11 -> x0, waiting for transfers between devices: 236 us -> none
  transfers between devices with their start and end apart: 22 -> 143, of which waited for: 22 -> 62; matrix products, arithmetic and copies ran while one was open for 5% -> 19% of each run, Pallas kernels for 0% -> 6%
where the time goes in v1:
time: 1370 us; the launch traced here: 1350 us
  waiting for transfers between devices  633 us (46%)
  starting transfers between devices  298 us (22%)
  local copies, waits for them, and re-layouts  147 us (11%)
  Pallas kernels  103 us (8%)
  matrix products  94.1 us (7%)
  other arithmetic  70.1 us (5%)
    ppermute x69, waiting for transfers between devices, over_z(): lax.ppermute(value, 'fsdp', [(a * cores + k, b * cores + k) for a, b in p...  315 us
    ppermute x33, waiting for transfers between devices, over_dp(): return lax.ppermute(value, 'dp', [(a, a ^ m) for a in range(dps)])  289 us
    ppermute x69, starting transfers between devices, over_z(): lax.ppermute(value, 'fsdp', [(a * cores + k, b * cores + k) for a, b in p...  163 us
    ppermute x7, starting transfers between devices, gather_heads(): lax.ppermute(own_heads((fs + k) % fss), 'fsdp', pairs)  50.6 us
    pallas_call x2, Pallas kernels, expert(): pl.pallas_call(functools.partial(expert_kernel, hidden), grid=(rows // bl...  45.1 us
    dynamic_update_slice x110, local copies, waits for them, and re-layouts, put(): lax.dynamic_update_slice(buffer, value.reshape((1,) * len(index) + buffer...  42 us
    ppermute x33, starting transfers between devices, over_dp(): return lax.ppermute(value, 'dp', [(a, a ^ m) for a in range(dps)])  41.9 us
    dot_general x8, matrix products, combine(): lax.dot_general(matrix[m], back[m], (((1,), (1,)), ((0,), (0,))), preferr...  31.3 us
  transfers between devices with their start and end apart: 143, of which 62 were waited for; matrix products, arithmetic and copies ran while one was open for 19% of the time, Pallas kernels for 6%

profile of v1, /device:TPU:20, one launch (start us, length us, event | category | flops | bytes accessed | tf_op | source)
XLA Modules:
  0.0 1350.7 jit_solution(10469459245162085072)
XLA Ops:
  143.5 11.3 collective-permute-done.31
  181.6 10.1 collective-permute-done.9
  215.5 14.3 %shard_map.144 = (bf16[2048,1280]{1,0:T(8,128)(2,1)}, bf16[2048,256]{1,0:T(8,128)(2,1)}, bf16[2048,256]{1,0:T(8,128)(2,1)}, bf16[2048,256]{1,0:T(8,128)(2,1)}, b...) custom-call(bf16[2560,1280]{1,0:T(8,128)(2,1)} %bitcast.14.x_ref, f32[1,1280]{1,0:T(1,128)} %slice.111.gain_ref, ...), custom_call_target="tpu_custom_call" | custom-call | flops 4026531840 | bytes 15728640 | tf_op jit(solution)/shard_map/pallas_call | solution.py:82
  229.8 18.3 %shard_map.145 = (bf16[2048,256]{1,0:T(8,128)(2,1)}, f32[2,1,2048]{2,1,0:T(1,128)}) custom-call(bf16[2048,256]{1,0:T(8,128)(2,1)} %get-tuple-element.27.q_ref, bf16[2048,256]{1,0:T(8,128)(2,1)} %get-tuple-element.28.k_ref, bf16[256,2048]{1,0:T(8,128)(2,1)} %get-tuple-element.29.vt_ref), custom_call_target="tpu_custom_call" | custom-call | flops 8589934592 | bytes 4194304 | tf_op jit(solution)/shard_map/pallas_call | solution.py:138
  327.5 55.2 %collective-permute-done.42 = bf16[40,3968]{1,0:T(8,128)(2,1)S(1)} collective-permute-done((bf16[40,3968]{1,0:T(8,128)(2,1)}, bf16[40,3968]{1,0:T(8,128)(2,1)S(1)}, u32[]{:S(2)}, u32[]{:S(2)}) %collective-permute-start.42) | collective-permute-done | bytes 317472 | tf_op jit(solution)/shard_map/ppermute | solution.py:288
  439.0 19.9 %collective-permute-done.78 = bf16[4,40,2688]{2,1,0:T(8,128)(2,1)S(1)} collective-permute-done((bf16[4,40,2688]{2,1,0:T(8,128)(2,1)S(1)}, bf16[4,40,2688]{2,1,0:T(8,128)(2,1)S(1)}, u32[]{:S(2)}, u32[]{:S(2)}) %collective-permute-start.78) | collective-permute-done | bytes 860192 | tf_op jit(solution)/shard_map/ppermute | solution.py:301
  464.2 19.0 %collective-permute-done.46 = bf16[4,40,3968]{2,1,0:T(8,128)(2,1)S(1)} collective-permute-done((bf16[4,40,3968]{2,1,0:T(8,128)(2,1)S(1)}, bf16[4,40,3968]{2,1,0:T(8,128)(2,1)S(1)}, u32[]{:S(2)}, u32[]{:S(2)}) %collective-permute-start.46) | collective-permute-done | bytes 1269792 | tf_op jit(solution)/shard_map/ppermute | solution.py:301
  484.3 27.9 %collective-permute-done.47 = bf16[4,40,3968]{2,1,0:T(8,128)(2,1)S(1)} collective-permute-done((bf16[4,40,3968]{2,1,0:T(8,128)(2,1)S(1)}, bf16[4,40,3968]{2,1,0:T(8,128)(2,1)S(1)}, u32[]{:S(2)}, u32[]{:S(2)}) %collective-permute-start.47) | collective-permute-done | bytes 1269792 | tf_op jit(solution)/shard_map/ppermute | solution.py:301
  532.2 18.9 %collective-permute-done.73 = bf16[4,128,1280]{2,1,0:T(8,128)(2,1)S(1)} collective-permute-done((bf16[4,128,1280]{2,1,0:T(8,128)(2,1)}, bf16[4,128,1280]{2,1,0:T(8,128)(2,1)S(1)}, u32[]{:S(2)}, u32[]{:S(2)}) %collective-permute-start.73) | collective-permute-done | bytes 1310752 | tf_op jit(solution)/shard_map/ppermute | solution.py:301
  551.1 27.8 %collective-permute-done.72 = bf16[4,128,1280]{2,1,0:T(8,128)(2,1)} collective-permute-done((bf16[4,128,1280]{2,1,0:T(8,128)(2,1)}, bf16[4,128,1280]{2,1,0:T(8,128)(2,1)}, u32[]{:S(2)}, u32[]{:S(2)}) %collective-permute-start.72) | collective-permute-done | bytes 1310752 | tf_op jit(solution)/shard_map/ppermute | solution.py:301
  628.2 10.3 collective-permute-done.58
  643.6 11.8 collective-permute-done.60
  676.9 15.2 %collective-permute-done.64 = bf16[4,128,1280]{2,1,0:T(8,128)(2,1)S(1)} collective-permute-done((bf16[4,128,1280]{2,1,0:T(8,128)(2,1)}, bf16[4,128,1280]{2,1,0:T(8,128)(2,1)S(1)}, u32[]{:S(2)}, u32[]{:S(2)}) %collective-permute-start.64) | collective-permute-done | bytes 1310752 | tf_op jit(solution)/shard_map/ppermute | solution.py:301
  692.1 24.6 %collective-permute-done.63 = bf16[4,128,1280]{2,1,0:T(8,128)(2,1)S(1)} collective-permute-done((bf16[4,128,1280]{2,1,0:T(8,128)(2,1)S(1)}, bf16[4,128,1280]{2,1,0:T(8,128)(2,1)S(1)}, u32[]{:S(2)}, u32[]{:S(2)}) %collective-permute-start.63) | collective-permute-done | bytes 1310752 | tf_op jit(solution)/shard_map/ppermute | solution.py:301
  719.4 36.6 %shard_map.147 = (bf16[2048,1280]{1,0:T(8,128)(2,1)}, bf16[2048,1792]{1,0:T(8,128)(2,1)}, bf16[2048,896]{1,0:T(8,128)(2,1)}) custom-call(bf16[2048,1280]{1,0:T(8,128)(2,1)} %bitcast.581, bf16[2048,1280]{1,0:T(8,128)(2,1)} %bitcast.577, bf16[1280,2688]{1,0:T(8,128)(2,1)} %bitcast.575), custom_call_target="tpu_custom_call" | custom-call | flops 23488102400 | bytes 31457280 | tf_op jit(solution)/shard_map/pallas_call | solution.py:255
  772.8 10.3 fusion.156
  834.7 18.9 %collective-permute-done.91 = bf16[4,128,1280]{2,1,0:T(8,128)(2,1)} collective-permute-done((bf16[4,128,1280]{2,1,0:T(8,128)(2,1)}, bf16[4,128,1280]{2,1,0:T(8,128)(2,1)}, u32[]{:S(2)}, u32[]{:S(2)}) %collective-permute-start.91) | collective-permute-done | bytes 1310752 | tf_op jit(solution)/shard_map/ppermute | solution.py:301
  864.9 19.3 %collective-permute-done.92 = bf16[4,128,1280]{2,1,0:T(8,128)(2,1)S(1)} collective-permute-done((bf16[4,128,1280]{2,1,0:T(8,128)(2,1)S(1)}, bf16[4,128,1280]{2,1,0:T(8,128)(2,1)S(1)}, u32[]{:S(2)}, u32[]{:S(2)}) %collective-permute-start.92) | collective-permute-done | bytes 1310752 | tf_op jit(solution)/shard_map/ppermute | solution.py:301
  891.1 11.6 collective-permute-done.132
  903.4 16.0 %collective-permute-done.131 = bf16[4,40,2688]{2,1,0:T(8,128)(2,1)} collective-permute-done((bf16[4,40,2688]{2,1,0:T(8,128)(2,1)}, bf16[4,40,2688]{2,1,0:T(8,128)(2,1)}, u32[]{:S(2)}, u32[]{:S(2)}) %collective-permute-start.131) | collective-permute-done | bytes 860192 | tf_op jit(solution)/shard_map/ppermute | solution.py:301
  928.7 12.8 collective-permute-done.87
  986.7 10.9 collective-permute-done.97
  1011.7 12.9 collective-permute-done.98
  1050.4 41.8 %collective-permute-done.102 = bf16[256,1280]{1,0:T(8,128)(2,1)S(1)} collective-permute-done((bf16[256,1280]{1,0:T(8,128)(2,1)S(1)}, bf16[256,1280]{1,0:T(8,128)(2,1)S(1)}, u32[]{:S(2)}, u32[]{:S(2)}) %collective-permute-start.102) | collective-permute-done | bytes 655392 | tf_op jit(solution)/shard_map/ppermute | solution.py:288
  1094.1 12.4 collective-permute-done.140
  1110.8 15.7 %collective-permute-start.106 = (bf16[256,1280]{1,0:T(8,128)(2,1)S(1)}, bf16[256,1280]{1,0:T(8,128)(2,1)S(1)}, u32[]{:S(2)}, u32[]{:S(2)}) collective-permute-start(bf16[256,1280]{1,0:T(8,128)(2,1)S(1)} %collective-permute-done.102), channel_id=1, source_target_pairs={{2,0},{3,1},{4,2},{5,3},{10,8},{11,9},{12,10},{13,11},{18,16},{19,... | collective-permute-start | bytes 1966088 | tf_op jit(solution)/shard_map/ppermute | solution.py:288
  1162.9 25.4 %shard_map.148 = (bf16[2048,256]{1,0:T(8,128)(2,1)}, bf16[2048,256]{1,0:T(8,128)(2,1)}, bf16[2048,256]{1,0:T(8,128)(2,1)}) custom-call(bf16[2048,256]{1,0:T(8,128)(2,1)} %get-tuple-element.27.q_ref, bf16[2048,256]{1,0:T(8,128)(2,1)} %get-tuple-element.28.k_ref, bf16[256,2048]{1,0:T(8,128)(2,1)} %get-tuple-element.38.kt_ref, ...), custom_call_target="tpu_custom_call" | custom-call | flops 21474836480 | bytes 8388608 | tf_op jit(solution)/shard_map/pallas_call | solution.py:217
  1226.5 10.7 collective-permute-done.121
  1237.2 13.4 collective-permute-done.120
  1293.7 18.6 %collective-permute-done.114 = bf16[256,1280]{1,0:T(8,128)(2,1)} collective-permute-done((bf16[256,1280]{1,0:T(8,128)(2,1)}, bf16[256,1280]{1,0:T(8,128)(2,1)}, u32[]{:S(2)}, u32[]{:S(2)}) %collective-permute-start.114) | collective-permute-done | bytes 655392 | tf_op jit(solution)/shard_map/ppermute | solution.py:288
  1321.1 10.0 collective-permute-done.117
  1335.9 10.9 collective-permute-done.118
  (708 shorter events, 753.7 us)
Async XLA Ops:
  0.7 161.8 %collective-permute-start = (bf16[256,1280]{1,0:T(8,128)(2,1)}, bf16[256,1280]{1,0:T(8,128)(2,1)}, u32[]{:S(2)}, u32[]{:S(2)}) collective-permute-start(bf16[256,1280]{1,0:T(8,128)(2,1)} %param.9), channel_id=1, source_target_pairs={{0,1},{1,0},{2,3},{3,2},{4,5},{5,4},{6,7},{7,6},{8,9},{9,8},{10,11... | collective-permute-start | bytes 1966088 | tf_op jit(solution)/shard_map/ppermute | solution.py:296
  0.8 154.1 %collective-permute-start.1 = (bf16[256,1280]{1,0:T(8,128)(2,1)}, bf16[256,1280]{1,0:T(8,128)(2,1)}, u32[]{:S(2)}, u32[]{:S(2)}) collective-permute-start(bf16[256,1280]{1,0:T(8,128)(2,1)} %param.9), channel_id=1, source_target_pairs={{0,2},{1,3},{2,4},{3,5},{4,6},{5,7},{8,10},{9,11},{10,12},{11,13},... | collective-permute-start | bytes 1966088 | tf_op jit(solution)/shard_map/ppermute | solution.py:288
  4.4 153.2 %collective-permute-start.3 = (bf16[256,1280]{1,0:T(8,128)(2,1)}, bf16[256,1280]{1,0:T(8,128)(2,1)S(1)}, u32[]{:S(2)}, u32[]{:S(2)}) collective-permute-start(bf16[256,1280]{1,0:T(8,128)(2,1)} %param.9), channel_id=1, source_target_pairs={{2,0},{3,1},{4,2},{5,3},{6,4},{7,5},{10,8},{11,9},{12,10},{13,11},... | collective-permute-start | bytes 1966088 | tf_op jit(solution)/shard_map/ppermute | solution.py:288
  198.4 119.8 %collective-permute-start.40 = (bf16[40,3968]{1,0:T(8,128)(2,1)}, bf16[40,3968]{1,0:T(8,128)(2,1)}, u32[]{:S(2)}, u32[]{:S(2)}) collective-permute-start(bf16[40,3968]{1,0:T(8,128)(2,1)} %pad_maximum_fusion.7), channel_id=1, source_target_pairs={{0,2},{1,3},{2,4},{3,5},{4,6},{5,7},{8,10},{9,11},{10,12},{11,13},... | collective-permute-start | bytes 952328 | tf_op jit(solution)/shard_map/ppermute | solution.py:288
  202.8 119.4 %collective-permute-start.41 = (bf16[40,3968]{1,0:T(8,128)(2,1)}, bf16[40,3968]{1,0:T(8,128)(2,1)}, u32[]{:S(2)}, u32[]{:S(2)}) collective-permute-start(bf16[40,3968]{1,0:T(8,128)(2,1)} %pad_maximum_fusion.7), channel_id=1, source_target_pairs={{2,0},{3,1},{4,2},{5,3},{6,4},{7,5},{10,8},{11,9},{12,10},{13,11},... | collective-permute-start | bytes 952328 | tf_op jit(solution)/shard_map/ppermute | solution.py:288
  205.9 188.8 %collective-permute-start.65 = (bf16[256,1280]{1,0:T(8,128)(2,1)}, bf16[256,1280]{1,0:T(8,128)(2,1)}, u32[]{:S(2)}, u32[]{:S(2)}) collective-permute-start(bf16[256,1280]{1,0:T(8,128)(2,1)} %c_ref.1), channel_id=1, source_target_pairs={{0,2},{1,3},{2,4},{3,5},{4,6},{5,7},{8,10},{9,11},{10,12},{11,13},... | collective-permute-start | bytes 1966088 | tf_op jit(solution)/shard_map/ppermute | solution.py:288
  209.3 188.1 %collective-permute-start.66 = (bf16[256,1280]{1,0:T(8,128)(2,1)}, bf16[256,1280]{1,0:T(8,128)(2,1)}, u32[]{:S(2)}, u32[]{:S(2)}) collective-permute-start(bf16[256,1280]{1,0:T(8,128)(2,1)} %c_ref.1), channel_id=1, source_target_pairs={{2,0},{3,1},{4,2},{5,3},{6,4},{7,5},{10,8},{11,9},{12,10},{13,11},... | collective-permute-start | bytes 1966088 | tf_op jit(solution)/shard_map/ppermute | solution.py:288
  316.0 83.2 %collective-permute-start.74 = (bf16[4,40,2688]{2,1,0:T(8,128)(2,1)}, bf16[4,40,2688]{2,1,0:T(8,128)(2,1)S(1)}, u32[]{:S(2)}, u32[]{:S(2)}) collective-permute-start(bf16[4,40,2688]{2,1,0:T(8,128)(2,1)} %get-tuple-element.108), channel_id=1, source_target_pairs={{0,2},{1,3},{2,4},{3,5},{4,6},{5,7},{6,0},{7,1},{8,10},{9,11},{10,... | collective-permute-start | bytes 2580488 | tf_op jit(solution)/shard_map/ppermute | solution.py:288
  318.2 83.2 %collective-permute-start.75 = (bf16[4,40,2688]{2,1,0:T(8,128)(2,1)}, bf16[4,40,2688]{2,1,0:T(8,128)(2,1)S(1)}, u32[]{:S(2)}, u32[]{:S(2)}) collective-permute-start(bf16[4,40,2688]{2,1,0:T(8,128)(2,1)} %get-tuple-element.107), channel_id=1, source_target_pairs={{0,4},{1,5},{2,6},{3,7},{4,0},{5,1},{6,2},{7,3},{8,12},{9,13},{10,... | collective-permute-start | bytes 2580488 | tf_op jit(solution)/shard_map/ppermute | solution.py:288
  322.2 60.6 %collective-permute-start.42 = (bf16[40,3968]{1,0:T(8,128)(2,1)}, bf16[40,3968]{1,0:T(8,128)(2,1)S(1)}, u32[]{:S(2)}, u32[]{:S(2)}) collective-permute-start(bf16[40,3968]{1,0:T(8,128)(2,1)} %collective-permute-done.40), channel_id=1, source_target_pairs={{2,4},{3,5},{4,6},{5,7},{10,12},{11,13},{12,14},{13,15},{18,20},{1... | collective-permute-start | bytes 952328 | tf_op jit(solution)/shard_map/ppermute | solution.py:288
  434.0 78.2 %collective-permute-start.47 = (bf16[4,40,3968]{2,1,0:T(8,128)(2,1)S(1)}, bf16[4,40,3968]{2,1,0:T(8,128)(2,1)S(1)}, u32[]{:S(2)}, u32[]{:S(2)}) collective-permute-start(bf16[4,40,3968]{2,1,0:T(8,128)(2,1)S(1)} %slice.144), channel_id=1, source_target_pairs={{0,16},{8,24},{16,0},{24,8},{1,17},{9,25},{17,1},{25,9},{2,18},{10... | collective-permute-start | bytes 3809288 | tf_op jit(solution)/shard_map/ppermute | solution.py:301
  437.5 75.9 %collective-permute-start.48 = (bf16[4,40,3968]{2,1,0:T(8,128)(2,1)S(1)}, bf16[4,40,3968]{2,1,0:T(8,128)(2,1)S(1)}, u32[]{:S(2)}, u32[]{:S(2)}) collective-permute-start(bf16[4,40,3968]{2,1,0:T(8,128)(2,1)S(1)} %slice.144), channel_id=1, source_target_pairs={{0,24},{8,16},{16,8},{24,0},{1,25},{9,17},{17,9},{25,1},{2,26},{10... | collective-permute-start | bytes 3809288 | tf_op jit(solution)/shard_map/ppermute | solution.py:301
  458.9 56.6 %collective-permute-start.69 = (bf16[256,1280]{1,0:T(8,128)(2,1)S(1)}, bf16[256,1280]{1,0:T(8,128)(2,1)S(1)}, u32[]{:S(2)}, u32[]{:S(2)}) collective-permute-start(bf16[256,1280]{1,0:T(8,128)(2,1)S(1)} %collective-permute-done.67), channel_id=1, source_target_pairs={{4,6},{5,7},{12,14},{13,15},{20,22},{21,23},{28,30},{29,31}} | collective-permute-start | bytes 1966088 | tf_op jit(solution)/shard_map/ppermute | solution.py:288
  483.2 99.8 %collective-permute-start.80 = (bf16[4,4,40,2688]{3,2,1,0:T(8,128)(2,1)S(1)}, bf16[4,4,40,2688]{3,2,1,0:T(8,128)(2,1)}, u32[]{:S(2)}, u32[]{:S(2)}) collective-permute-start(bf16[4,4,40,2688]{3,2,1,0:T(8,128)(2,1)S(1)} %bitcast_dynamic-update-slice_fusion.15), channel_id=1, source_target_pairs={{0,1},{1,0},{2,3},{3,2},{4,5},{5,4},{6,7},{7,6},{8,9},{9,8},{10,11... | collective-permute-start | bytes 10321928 | tf_op jit(solution)/shard_map/ppermute | solution.py:296
  514.5 73.7 %collective-permute-start.49 = (bf16[4,4,40,3968]{3,2,1,0:T(8,128)(2,1)}, bf16[4,4,40,3968]{3,2,1,0:T(8,128)(2,1)}, u32[]{:S(2)}, u32[]{:S(2)}) collective-permute-start(bf16[4,4,40,3968]{3,2,1,0:T(8,128)(2,1)} %bitcast_dynamic-update-slice_fusion.4), channel_id=1, source_target_pairs={{0,1},{1,0},{2,3},{3,2},{4,5},{5,4},{6,7},{7,6},{8,9},{9,8},{10,11... | collective-permute-start | bytes 15237128 | tf_op jit(solution)/shard_map/ppermute | solution.py:296
  521.9 57.0 %collective-permute-start.72 = (bf16[4,128,1280]{2,1,0:T(8,128)(2,1)}, bf16[4,128,1280]{2,1,0:T(8,128)(2,1)}, u32[]{:S(2)}, u32[]{:S(2)}) collective-permute-start(bf16[4,128,1280]{2,1,0:T(8,128)(2,1)} %fusion.8), channel_id=1, source_target_pairs={{0,16},{8,24},{16,0},{24,8},{1,17},{9,25},{17,1},{25,9},{2,18},{10... | collective-permute-start | bytes 3932168 | tf_op jit(solution)/shard_map/ppermute | solution.py:301
  660.6 56.1 %collective-permute-start.63 = (bf16[4,128,1280]{2,1,0:T(8,128)(2,1)S(1)}, bf16[4,128,1280]{2,1,0:T(8,128)(2,1)S(1)}, u32[]{:S(2)}, u32[]{:S(2)}) collective-permute-start(bf16[4,128,1280]{2,1,0:T(8,128)(2,1)S(1)} %convolution_convert_fusion.2), channel_id=1, source_target_pairs={{0,16},{8,24},{16,0},{24,8},{1,17},{9,25},{17,1},{25,9},{2,18},{10... | collective-permute-start | bytes 3932168 | tf_op jit(solution)/shard_map/ppermute | solution.py:301
  676.1 122.5 %collective-permute-start.129 = (bf16[4,4,40,2688]{3,2,1,0:T(8,128)(2,1)}, bf16[4,4,40,2688]{3,2,1,0:T(8,128)(2,1)}, u32[]{:S(2)}, u32[]{:S(2)}) collective-permute-start(bf16[4,4,40,2688]{3,2,1,0:T(8,128)(2,1)} %fusion.2), channel_id=1, source_target_pairs={{0,1},{1,0},{2,3},{3,2},{4,5},{5,4},{6,7},{7,6},{8,9},{9,8},{10,11... | collective-permute-start | bytes 10321928 | tf_op jit(solution)/shard_map/ppermute | solution.py:296
  768.6 59.4 %collective-permute-start.83 = (bf16[4,128,1280]{2,1,0:T(8,128)(2,1)}, bf16[4,128,1280]{2,1,0:T(8,128)(2,1)}, u32[]{:S(2)}, u32[]{:S(2)}) collective-permute-start(bf16[4,128,1280]{2,1,0:T(8,128)(2,1)} %bitcast.140), channel_id=1, source_target_pairs={{0,24},{8,16},{16,8},{24,0},{1,25},{9,17},{17,9},{25,1},{2,26},{10... | collective-permute-start | bytes 3932168 | tf_op jit(solution)/shard_map/ppermute | solution.py:301
  772.0 81.6 %collective-permute-start.91 = (bf16[4,128,1280]{2,1,0:T(8,128)(2,1)}, bf16[4,128,1280]{2,1,0:T(8,128)(2,1)}, u32[]{:S(2)}, u32[]{:S(2)}) collective-permute-start(bf16[4,128,1280]{2,1,0:T(8,128)(2,1)} %bitcast.150), channel_id=1, source_target_pairs={{0,16},{8,24},{16,0},{24,8},{1,17},{9,25},{17,1},{25,9},{2,18},{10... | collective-permute-start | bytes 3932168 | tf_op jit(solution)/shard_map/ppermute | solution.py:301
  798.5 60.4 %collective-permute-start.90 = (bf16[4,128,1280]{2,1,0:T(8,128)(2,1)}, bf16[4,128,1280]{2,1,0:T(8,128)(2,1)}, u32[]{:S(2)}, u32[]{:S(2)}) collective-permute-start(bf16[4,128,1280]{2,1,0:T(8,128)(2,1)} %bitcast.149), channel_id=1, source_target_pairs={{0,8},{8,0},{16,24},{24,16},{1,9},{9,1},{17,25},{25,17},{2,10},{10... | collective-permute-start | bytes 3932168 | tf_op jit(solution)/shard_map/ppermute | solution.py:301
  812.0 72.2 %collective-permute-start.92 = (bf16[4,128,1280]{2,1,0:T(8,128)(2,1)S(1)}, bf16[4,128,1280]{2,1,0:T(8,128)(2,1)S(1)}, u32[]{:S(2)}, u32[]{:S(2)}) collective-permute-start(bf16[4,128,1280]{2,1,0:T(8,128)(2,1)S(1)} %bitcast.596), channel_id=1, source_target_pairs={{0,24},{8,16},{16,8},{24,0},{1,25},{9,17},{17,9},{25,1},{2,26},{10... | collective-permute-start | bytes 3932168 | tf_op jit(solution)/shard_map/ppermute | solution.py:301
  815.9 184.8 %collective-permute-start.136 = (bf16[4,4,40,2688]{3,2,1,0:T(8,128)(2,1)}, bf16[4,4,40,2688]{3,2,1,0:T(8,128)(2,1)}, u32[]{:S(2)}, u32[]{:S(2)}) collective-permute-start(bf16[4,4,40,2688]{3,2,1,0:T(8,128)(2,1)} %fusion.3), channel_id=1, source_target_pairs={{0,1},{1,0},{2,3},{3,2},{4,5},{5,4},{6,7},{7,6},{8,9},{9,8},{10,11... | collective-permute-start | bytes 10321928 | tf_op jit(solution)/shard_map/ppermute | solution.py:296
  828.0 74.7 %collective-permute-start.132 = (bf16[4,40,2688]{2,1,0:T(8,128)(2,1)}, bf16[4,40,2688]{2,1,0:T(8,128)(2,1)}, u32[]{:S(2)}, u32[]{:S(2)}) collective-permute-start(bf16[4,40,2688]{2,1,0:T(8,128)(2,1)} %get-tuple-element.101), channel_id=1, source_target_pairs={{0,24},{8,16},{16,8},{24,0},{1,25},{9,17},{17,9},{25,1},{2,26},{10... | collective-permute-start | bytes 2580488 | tf_op jit(solution)/shard_map/ppermute | solution.py:301
  853.7 65.7 %collective-permute-start.131 = (bf16[4,40,2688]{2,1,0:T(8,128)(2,1)}, bf16[4,40,2688]{2,1,0:T(8,128)(2,1)}, u32[]{:S(2)}, u32[]{:S(2)}) collective-permute-start(bf16[4,40,2688]{2,1,0:T(8,128)(2,1)} %get-tuple-element.102), channel_id=1, source_target_pairs={{0,16},{8,24},{16,0},{24,8},{1,17},{9,25},{17,1},{25,9},{2,18},{10... | collective-permute-start | bytes 2580488 | tf_op jit(solution)/shard_map/ppermute | solution.py:301
  858.9 60.5 %collective-permute-start.130 = (bf16[4,40,2688]{2,1,0:T(8,128)(2,1)S(1)}, bf16[4,40,2688]{2,1,0:T(8,128)(2,1)}, u32[]{:S(2)}, u32[]{:S(2)}) collective-permute-start(bf16[4,40,2688]{2,1,0:T(8,128)(2,1)S(1)} %get-tuple-element.100), channel_id=1, source_target_pairs={{0,8},{8,0},{16,24},{24,16},{1,9},{9,1},{17,25},{25,17},{2,10},{10... | collective-permute-start | bytes 2580488 | tf_op jit(solution)/shard_map/ppermute | solution.py:301
  1036.5 55.7 %collective-permute-start.102 = (bf16[256,1280]{1,0:T(8,128)(2,1)S(1)}, bf16[256,1280]{1,0:T(8,128)(2,1)S(1)}, u32[]{:S(2)}, u32[]{:S(2)}) collective-permute-start(bf16[256,1280]{1,0:T(8,128)(2,1)S(1)} %get-tuple-element.64), channel_id=1, source_target_pairs={{2,0},{3,1},{4,2},{5,3},{6,4},{7,5},{10,8},{11,9},{12,10},{13,11},... | collective-permute-start | bytes 1966088 | tf_op jit(solution)/shard_map/ppermute | solution.py:288
  1047.5 59.0 %collective-permute-start.140 = (bf16[4,40,2688]{2,1,0:T(8,128)(2,1)S(1)}, bf16[4,40,2688]{2,1,0:T(8,128)(2,1)S(1)}, u32[]{:S(2)}, u32[]{:S(2)}) collective-permute-start(bf16[4,40,2688]{2,1,0:T(8,128)(2,1)S(1)} %get-tuple-element.95), channel_id=1, source_target_pairs={{0,2},{1,3},{2,4},{3,5},{4,6},{5,7},{6,0},{7,1},{8,10},{9,11},{10,... | collective-permute-start | bytes 2580488 | tf_op jit(solution)/shard_map/ppermute | solution.py:288
  1047.8 63.0 %collective-permute-start.141 = (bf16[4,40,2688]{2,1,0:T(8,128)(2,1)S(1)}, bf16[4,40,2688]{2,1,0:T(8,128)(2,1)S(1)}, u32[]{:S(2)}, u32[]{:S(2)}) collective-permute-start(bf16[4,40,2688]{2,1,0:T(8,128)(2,1)S(1)} %get-tuple-element.94), channel_id=1, source_target_pairs={{0,4},{1,5},{2,6},{3,7},{4,0},{5,1},{6,2},{7,3},{8,12},{9,13},{10,... | collective-permute-start | bytes 2580488 | tf_op jit(solution)/shard_map/ppermute | solution.py:288
  1050.1 79.1 %collective-permute-start.142 = (bf16[4,40,2688]{2,1,0:T(8,128)(2,1)S(1)}, bf16[4,40,2688]{2,1,0:T(8,128)(2,1)S(1)}, u32[]{:S(2)}, u32[]{:S(2)}) collective-permute-start(bf16[4,40,2688]{2,1,0:T(8,128)(2,1)S(1)} %get-tuple-element.93), channel_id=1, source_target_pairs={{0,6},{1,7},{2,0},{3,1},{4,2},{5,3},{6,4},{7,5},{8,14},{9,15},{10,... | collective-permute-start | bytes 2580488 | tf_op jit(solution)/shard_map/ppermute | solution.py:288
  1050.2 92.3 %collective-permute-start.101 = (bf16[256,1280]{1,0:T(8,128)(2,1)S(1)}, bf16[256,1280]{1,0:T(8,128)(2,1)S(1)}, u32[]{:S(2)}, u32[]{:S(2)}) collective-permute-start(bf16[256,1280]{1,0:T(8,128)(2,1)S(1)} %collective-permute-done.100), channel_id=1, source_target_pairs={{0,1},{1,0},{2,3},{3,2},{4,5},{5,4},{6,7},{7,6},{8,9},{9,8},{10,11... | collective-permute-start | bytes 1966088 | tf_op jit(solution)/shard_map/ppermute | solution.py:296
  1201.9 67.6 %collective-permute-start.112 = (bf16[4,256,1280]{2,1,0:T(8,128)(2,1)}, bf16[4,256,1280]{2,1,0:T(8,128)(2,1)}, u32[]{:S(2)}, u32[]{:S(2)}) collective-permute-start(bf16[4,256,1280]{2,1,0:T(8,128)(2,1)} %fusion.16), channel_id=1, source_target_pairs={{0,1},{1,0},{2,3},{3,2},{4,5},{5,4},{6,7},{7,6},{8,9},{9,8},{10,11... | collective-permute-start | bytes 7864328 | tf_op jit(solution)/shard_map/ppermute | solution.py:296
  (190 other events, 3974.5 us)

commit v2 on v1

--- a/solution.py
+++ b/solution.py
@@ -269,6 +269,696 @@
     )(x, c, w)
 
 
+MESH = pl.DeviceIdType.MESH
+ANY = pl.BlockSpec(memory_space=pl.ANY)
+
+
+def place(cores):
+    dp, fs = lax.axis_index("dp"), lax.axis_index("fsdp")
+    return dp, fs, fs // cores, fs % cores
+
+
+def greet(peers):
+    barrier = pltpu.get_barrier_semaphore()
+    for peer in peers:
+        pl.semaphore_signal(barrier, inc=1, device_id=peer, device_id_type=MESH)
+    pl.semaphore_wait(barrier, len(peers))
+
+
+def sequence_peers(dp, fs, fss):
+    return [(dp, lax.rem(fs + k, fss)) for k in range(1, fss)]
+
+
+def send(source, target, out, came, peer):
+    return pltpu.make_async_remote_copy(
+        src_ref=source, dst_ref=target, send_sem=out, recv_sem=came, device_id=peer, device_id_type=MESH
+    )
+
+
+class Chain:
+    def __init__(self, own, full, lanes, cores, sems):
+        self.own, self.full, self.lanes, self.cores = own, full, lanes, cores
+        self.z_out, self.z_in, self.c_out, self.c_in, self.local = sems
+        self.dp, self.fs, self.z, self.c = place(cores)
+
+    def hop(self, side, step, block):
+        by = self.cores if side == 0 else -self.cores
+        source = self.own if step == 0 else self.full.at[block, self.c]
+        return send(
+            source, self.full.at[block, self.c], self.z_out.at[side, step], self.z_in.at[side, step],
+            (self.dp, self.fs + by),
+        )
+
+    def across(self, m, block, source, core):
+        return send(
+            source, self.full.at[block, core], self.c_out.at[m - 1, block], self.c_in.at[m - 1, block],
+            (self.dp, self.z * self.cores + lax.rem(self.c + m, self.cores)),
+        )
+
+    def keep(self):
+        return pltpu.make_async_copy(self.own, self.full.at[self.z, self.c], self.local)
+
+    def has_next(self, side):
+        return self.z < self.lanes - 1 if side == 0 else self.z > 0
+
+    def begin(self):
+        for side in (0, 1):
+
+            @pl.when(self.has_next(side))
+            def _():
+                self.hop(side, 0, self.z).start()
+
+        for m in range(1, self.cores):
+            self.across(m, self.z, self.own, self.c).start()
+        self.keep().start()
+
+    def came(self, side, step):
+        block = self.z - step if side == 0 else self.z + step
+        return block, (block >= 0) & (block < self.lanes)
+
+    def advance(self, step):
+        for side in (0, 1):
+            block, there = self.came(side, step)
+
+            @pl.when(there)
+            def _():
+                self.hop(side, step - 1, block).wait_recv()
+
+            @pl.when(there & self.has_next(side))
+            def _():
+                self.hop(side, step, block).start()
+
+            @pl.when(there)
+            def _():
+                for m in range(1, self.cores):
+                    self.across(m, block, self.full.at[block, self.c], self.c).start()
+
+    def finish(self):
+        self.keep().wait()
+        for m in range(1, self.cores):
+            for block in range(self.lanes):
+                self.across(m, block, self.own, lax.rem(self.c + self.cores - m, self.cores)).wait_recv()
+        for side in (0, 1):
+            for step in range(self.lanes - 1):
+                block, there = self.came(side, step)
+
+                @pl.when(there & self.has_next(side))
+                def _():
+                    self.hop(side, step, block).wait_send()
+
+        for m in range(1, self.cores):
+            for block in range(self.lanes):
+                self.across(m, block, self.own, self.c).wait_send()
+
+
+def chain_sems(lanes, cores):
+    dma = pltpu.SemaphoreType.DMA
+    hops = (2, max(lanes - 1, 1))
+    ways = (max(cores - 1, 1), lanes)
+    return [dma(hops), dma(hops), dma(ways), dma(ways), dma]
+
+
+def gather_kernel(lanes, cores, x_ref, full_ref, *sems):
+    chain = Chain(x_ref, full_ref, lanes, cores, sems)
+    greet(sequence_peers(chain.dp, chain.fs, lanes * cores))
+    chain.begin()
+    for step in range(1, lanes):
+        chain.advance(step)
+    chain.finish()
+
+
+def gather_sequence(x, lanes, cores):
+    return pl.pallas_call(
+        functools.partial(gather_kernel, lanes, cores),
+        in_specs=[ANY],
+        out_specs=ANY,
+        out_shape=jax.ShapeDtypeStruct((lanes, cores) + x.shape, x.dtype),
+        scratch_shapes=chain_sems(lanes, cores),
+        compiler_params=pltpu.CompilerParams(collective_id=1, has_side_effects=True),
+    )(x)
+
+
+def start_kernel(
+    dps, lanes, cores, x_ref, wh_ref, tab_ref, wo_ref, full_ref, heads_ref, tabs_ref, out_ref,
+    h_out, h_in, hd_out, hd_in, t_out, t_in, o_out, o_in, od_out, od_in, oc_out, oc_in, locals_, *sems,
+):
+    chain = Chain(x_ref, full_ref, lanes, cores, sems)
+    dp, fs, z, c = chain.dp, chain.fs, chain.z, chain.c
+    fss = lanes * cores
+    greet(sequence_peers(dp, fs, fss) + [(lax.rem(dp + m, dps), fs) for m in range(1, dps)])
+    chain.begin()
+    kept = [
+        pltpu.make_async_copy(wh_ref.at[fs], heads_ref.at[dp, fs], locals_.at[0]),
+        pltpu.make_async_copy(tab_ref, tabs_ref.at[z], locals_.at[1]),
+        pltpu.make_async_copy(wo_ref, out_ref.at[dp, z, c], locals_.at[2]),
+    ]
+    for copy in kept:
+        copy.start()
+
+    def heads_to(k):
+        t = lax.rem(fs + k, fss)
+        return send(wh_ref.at[t], heads_ref.at[dp, fs], h_out.at[k - 1], h_in.at[k - 1], (dp, t))
+
+    def table_to(k):
+        t = lax.rem(z + k, lanes) * cores + c
+        return send(tab_ref, tabs_ref.at[z], t_out.at[k - 1], t_in.at[k - 1], (dp, t))
+
+    def out_to(k):
+        t = lax.rem(z + k, lanes) * cores + c
+        return send(wo_ref, out_ref.at[dp, z, c], o_out.at[k - 1], o_in.at[k - 1], (dp, t))
+
+    def heads_over(m, block):
+        return send(
+            heads_ref.at[block], heads_ref.at[block], hd_out.at[m - 1], hd_in.at[m - 1],
+            (lax.rem(dp + m, dps), fs),
+        )
+
+    def out_over(m, block):
+        piece = out_ref.at[block, :, c]
+        return send(piece, piece, od_out.at[m - 1], od_in.at[m - 1], (lax.rem(dp + m, dps), fs))
+
+    def out_across(m, core):
+        piece = out_ref.at[:, :, core]
+        return send(piece, piece, oc_out.at[m - 1], oc_in.at[m - 1], (dp, z * cores + lax.rem(c + m, cores)))
+
+    for k in range(1, fss):
+        heads_to(k).start()
+    for k in range(1, lanes):
+        out_to(k).start()
+        table_to(k).start()
+    if lanes > 1:
+        chain.advance(1)
+    for copy in kept:
+        copy.wait()
+    for k in range(1, fss):
+        heads_to(k).wait_recv()
+    for m in range(1, dps):
+        heads_over(m, dp).start()
+    for k in range(1, lanes):
+        out_to(k).wait_recv()
+    for m in range(1, dps):
+        out_over(m, dp).start()
+    for step in range(2, lanes):
+        chain.advance(step)
+    for k in range(1, lanes):
+        table_to(k).wait_recv()
+    for m in range(1, dps):
+        out_over(m, lax.rem(dp + dps - m, dps)).wait_recv()
+    for m in range(1, cores):
+        out_across(m, c).start()
+    for m in range(1, dps):
+        heads_over(m, lax.rem(dp + dps - m, dps)).wait_recv()
+    chain.finish()
+    for m in range(1, cores):
+        out_across(m, lax.rem(c + cores - m, cores)).wait_recv()
+    for k in range(1, fss):
+        heads_to(k).wait_send()
+    for k in range(1, lanes):
+        out_to(k).wait_send()
+        table_to(k).wait_send()
+    for m in range(1, dps):
+        heads_over(m, dp).wait_send()
+        out_over(m, dp).wait_send()
+    for m in range(1, cores):
+        out_across(m, c).wait_send()
+
+
+def start(x, wh, table, w_out, dps, lanes, cores):
+    fss = lanes * cores
+    dma = pltpu.SemaphoreType.DMA
+    pair = lambda n: [dma((max(n - 1, 1),)), dma((max(n - 1, 1),))]
+    shapes = [
+        jax.ShapeDtypeStruct((lanes, cores) + x.shape, x.dtype),
+        jax.ShapeDtypeStruct((dps,) + wh.shape, wh.dtype),
+        jax.ShapeDtypeStruct((lanes,) + table.shape, table.dtype),
+        jax.ShapeDtypeStruct((dps, lanes, cores) + w_out.shape, w_out.dtype),
+    ]
+    return pl.pallas_call(
+        functools.partial(start_kernel, dps, lanes, cores),
+        in_specs=[ANY] * 4,
+        out_specs=[ANY] * 4,
+        out_shape=shapes,
+        scratch_shapes=pair(fss) + pair(dps) + pair(lanes) + pair(lanes) + pair(dps) + pair(cores)
+        + [dma((3,))] + chain_sems(lanes, cores),
+        compiler_params=pltpu.CompilerParams(collective_id=0, has_side_effects=True),
+    )(x, wh, table, w_out)
+
+
+def heads_kernel(lanes, cores, busy, o_ref, mix_ref, out, came, local):
+    dp, fs, z, c = place(cores)
+    fss = lanes * cores
+    tokens, width = mix_ref.shape[0], o_ref.shape[1]
+    greet(sequence_peers(dp, fs, fss))
+
+    def columns(f):
+        return mix_ref.at[:, pl.ds(pl.multiple_of(f * width, HD), width)]
+
+    def rows(f):
+        return o_ref.at[pl.ds(pl.multiple_of(f * tokens, tokens), tokens), :]
+
+    def to(k, owner):
+        t = lax.rem(fs + k, fss)
+        return send(rows(t), columns(owner), out.at[k - 1], came.at[k - 1], (dp, t))
+
+    keep = pltpu.make_async_copy(rows(fs), columns(fs), local)
+
+    @pl.when(fs < busy)
+    def _():
+        for k in range(1, fss):
+            to(k, fs).start()
+        keep.start()
+
+    for k in range(1, fss):
+        owner = lax.rem(fs + fss - k, fss)
+
+        @pl.when(owner < busy)
+        def _():
+            to(k, owner).wait_recv()
+
+    @pl.when(fs < busy)
+    def _():
+        keep.wait()
+        for k in range(1, fss):
+            to(k, fs).wait_send()
+
+
+def heads_home(o, tokens, lanes, cores, busy):
+    fss = lanes * cores
+    dma = pltpu.SemaphoreType.DMA
+    return pl.pallas_call(
+        functools.partial(heads_kernel, lanes, cores, busy),
+        in_specs=[ANY],
+        out_specs=ANY,
+        out_shape=jax.ShapeDtypeStruct((tokens, busy * o.shape[1]), o.dtype),
+        scratch_shapes=[dma((fss - 1,)), dma((fss - 1,)), dma],
+        compiler_params=pltpu.CompilerParams(collective_id=2, has_side_effects=True),
+    )(o)
+
+
+def dispatch_kernel(
+    dps, lanes, cores, x_ref, pick_ref, out_ref, line, stage,
+    z_out, z_in, d_out_, d_in, local,
+):
+    dp, fs, z, c = place(cores)
+    peers = [(lax.rem(dp + m, dps), fs) for m in range(1, dps)]
+    barrier = pltpu.get_barrier_semaphore()
+    for peer in peers:
+        pl.semaphore_signal(barrier, inc=1, device_id=peer, device_id_type=MESH)
+    for side in (0, 1):
+        near = fs + (cores if side == 0 else -cores)
+
+        @pl.when(z < lanes - 1 if side == 0 else z > 0)
+        def _():
+            pl.semaphore_signal(barrier, inc=1, device_id=(dp, near), device_id_type=MESH)
+
+    ends = (z > 0).astype(jnp.int32) + (z < lanes - 1).astype(jnp.int32)
+    pl.semaphore_wait(barrier, len(peers) + ends)
+
+    def hop(side, step, block):
+        near = fs + (cores if side == 0 else -cores)
+        source = x_ref if step == 0 else line.at[block]
+        return send(source, line.at[block], z_out.at[side, step], z_in.at[side, step], (dp, near))
+
+    def over(m, block):
+        return send(
+            stage.at[m, block], out_ref.at[m, block], d_out_.at[m - 1, block], d_in.at[m - 1, block],
+            (lax.rem(dp + m, dps), fs),
+        )
+
+    def keep(block):
+        return pltpu.make_async_copy(stage.at[0, block], out_ref.at[0, block], local.at[block])
+
+    def has_next(side):
+        return z < lanes - 1 if side == 0 else z > 0
+
+    def pick(block, source):
+        for m in list(range(1, dps)) + [0]:
+            stage[m, block] = dot_nn(pick_ref[m, block], source[...]).astype(BF)
+            if m:
+                over(m, block).start()
+            else:
+                keep(block).start()
+
+    for side in (0, 1):
+
+        @pl.when(has_next(side))
+        def _():
+            hop(side, 0, z).start()
+
+    pick(z, x_ref)
+    for step in range(1, lanes):
+        for side in (0, 1):
+            block = z - step if side == 0 else z + step
+            there = (block >= 0) & (block < lanes)
+
+            @pl.when(there)
+            def _():
+                hop(side, step - 1, block).wait_recv()
+
+            @pl.when(there & has_next(side))
+            def _():
+                hop(side, step, block).start()
+
+            @pl.when(there)
+            def _():
+                pick(block, line.at[block])
+
+    for block in range(lanes):
+        keep(block).wait()
+        for m in range(1, dps):
+            over(m, block).wait_recv()
+    for step in range(lanes - 1):
+        for side in (0, 1):
+            block = z - step if side == 0 else z + step
+            there = (block >= 0) & (block < lanes)
+
+            @pl.when(there & has_next(side))
+            def _():
+                hop(side, step, block).wait_send()
+
+    for block in range(lanes):
+        for m in range(1, dps):
+            over(m, block).wait_send()
+
+
+def dispatch(x, picks, lanes, cores, number):
+    dps, _, slots, tokens = picks.shape
+    model = x.shape[1]
+    dma = pltpu.SemaphoreType.DMA
+    hops = (2, max(lanes - 1, 1))
+    ways = (dps - 1, lanes)
+    whole = pl.BlockSpec(memory_space=pltpu.VMEM)
+    return pl.pallas_call(
+        functools.partial(dispatch_kernel, dps, lanes, cores),
+        in_specs=[whole, whole],
+        out_specs=ANY,
+        out_shape=jax.ShapeDtypeStruct((dps, lanes, slots, model), BF),
+        scratch_shapes=[
+            pltpu.VMEM((lanes, tokens, model), BF),
+            pltpu.VMEM((dps, lanes, slots, model), BF),
+            dma(hops), dma(hops), dma(ways), dma(ways), dma((lanes,)),
+        ],
+        compiler_params=pltpu.CompilerParams(
+            collective_id=number, has_side_effects=True, vmem_limit_bytes=VMEM_LIMIT
+        ),
+    )(x, picks)
+
+
+def combine_kernel(
+    dps, lanes, cores, part_ref, mat_ref, out_ref, back, stage, inbox,
+    z_out, z_in, d_out_, d_in, local,
+):
+    dp, fs, z, c = place(cores)
+    slots = part_ref.shape[2]
+    peers = [(lax.rem(dp + m, dps), fs) for m in range(1, dps)]
+    barrier = pltpu.get_barrier_semaphore()
+    for peer in peers:
+        pl.semaphore_signal(barrier, inc=1, device_id=peer, device_id_type=MESH)
+
+    def has_next(side):
+        return z < lanes - 1 if side == 0 else z > 0
+
+    def near(side):
+        return (dp, fs + (cores if side == 0 else -cores))
+
+    for side in (0, 1):
+
+        @pl.when(has_next(side))
+        def _():
+            pl.semaphore_signal(barrier, inc=1, device_id=near(side), device_id_type=MESH)
+
+    ends = (z > 0).astype(jnp.int32) + (z < lanes - 1).astype(jnp.int32)
+    pl.semaphore_wait(barrier, len(peers) + ends)
+
+    def over(m, block):
+        return send(
+            part_ref.at[m, block], back.at[block, m], d_out_.at[m - 1, block], d_in.at[m - 1, block],
+            (lax.rem(dp + dps - m, dps), fs),
+        )
+
+    def keep(block):
+        return pltpu.make_async_copy(part_ref.at[0, block], back.at[block, 0], local.at[block])
+
+    def hop(side, step):
+        return send(
+            stage.at[side, step - 1], inbox.at[side, step - 1], z_out.at[side, step - 1],
+            z_in.at[side, step - 1], near(side),
+        )
+
+    def goal(side, step):
+        block = z + lanes - step if side == 0 else z - lanes + step
+        return block, (block >= 0) & (block < lanes)
+
+    def begin(block):
+        for m in range(1, dps):
+            over(m, block).start()
+        keep(block).start()
+
+    def partial_sum(block):
+        keep(block).wait()
+        for m in range(1, dps):
+            over(m, block).wait_recv()
+        total = None
+        for m in range(dps):
+            term = dot_nn(mat_ref[block, :, m * slots : (m + 1) * slots], back[block, m])
+            total = term if total is None else total + term
+        return total
+
+    for step in range(1, lanes):
+        for side in (0, 1):
+            block, there = goal(side, step)
+
+            @pl.when(there)
+            def _():
+                begin(block)
+
+    begin(z)
+    for step in range(1, lanes):
+        for side in (0, 1):
+            block, there = goal(side, step)
+            fed = z > 0 if side == 0 else z < lanes - 1
+
+            @pl.when(there)
+            def _():
+                total = partial_sum(block)
+                stage[side, step - 1] = total.astype(BF)
+                if step > 1:
+
+                    @pl.when(fed)
+                    def _():
+                        hop(side, step - 1).wait_recv()
+                        stage[side, step - 1] = (total + inbox[side, step - 2].astype(F32)).astype(BF)
+
+                hop(side, step).start()
+
+    out_ref[...] = partial_sum(z)
+    for side in (0, 1):
+        fed = z > 0 if side == 0 else z < lanes - 1
+
+        @pl.when(fed)
+        def _():
+            hop(side, lanes - 1).wait_recv()
+            out_ref[...] += inbox[side, lanes - 2].astype(F32)
+
+    for step in range(1, lanes):
+        for side in (0, 1):
+            block, there = goal(side, step)
+
+            @pl.when(there)
+            def _():
+                hop(side, step).wait_send()
+
+    for block in range(lanes):
+        for m in range(1, dps):
+            over(m, block).wait_send()
+
+
+def combine(parts, matrix, lanes, cores, number):
+    dps, _, slots, model = parts.shape
+    tokens = matrix.shape[1]
+    dma = pltpu.SemaphoreType.DMA
+    hops = (2, max(lanes - 1, 1))
+    ways = (dps - 1, lanes)
+    whole = pl.BlockSpec(memory_space=pltpu.VMEM)
+    return pl.pallas_call(
+        functools.partial(combine_kernel, dps, lanes, cores),
+        in_specs=[ANY, whole],
+        out_specs=whole,
+        out_shape=jax.ShapeDtypeStruct((tokens, model), F32),
+        scratch_shapes=[
+            pltpu.VMEM((lanes, dps, slots, model), BF),
+            pltpu.VMEM(hops + (tokens, model), BF),
+            pltpu.VMEM(hops + (tokens, model), BF),
+            dma(hops), dma(hops), dma(ways), dma(ways), dma((lanes,)),
+        ],
+        compiler_params=pltpu.CompilerParams(
+            collective_id=number, has_side_effects=True, vmem_limit_bytes=VMEM_LIMIT
+        ),
+    )(parts, matrix)
+
+
+def finish_kernel(
+    dps, lanes, cores, busy, part_ref, g_ref, out_ref, mix_ref, from_core, stage, inbox, from_dp, total_g,
+    z_out, z_in, c_out, c_in, g_out, g_in, m_out, m_in, local,
+):
+    dp, fs, z, c = place(cores)
+    fss = lanes * cores
+    greet(sequence_peers(dp, fs, fss) + [(lax.rem(dp + m, dps), fs) for m in range(1, dps)])
+
+    def has_next(side):
+        return z < lanes - 1 if side == 0 else z > 0
+
+    def over(m):
+        t = lax.rem(dp + m, dps)
+        return send(g_ref.at[t], from_dp.at[m - 1], g_out.at[m - 1], g_in.at[m - 1], (t, fs))
+
+    def across(m, block):
+        t = lax.rem(c + m, cores)
+        return send(
+            part_ref.at[block, t], from_core.at[m - 1, block], c_out.at[m - 1, block], c_in.at[m - 1, block],
+            (dp, z * cores + t),
+        )
+
+    def hop(side, step):
+        return send(
+            stage.at[side, step - 1], inbox.at[side, step - 1], z_out.at[side, step - 1],
+            z_in.at[side, step - 1], (dp, fs + (cores if side == 0 else -cores)),
+        )
+
+    def home(k, owner):
+        t = lax.rem(fs + k, fss)
+        return send(total_g.at[t], mix_ref.at[owner], m_out.at[k - 1], m_in.at[k - 1], (dp, t))
+
+    def goal(side, step):
+        block = z + lanes - step if side == 0 else z - lanes + step
+        return block, (block >= 0) & (block < lanes)
+
+    def begin(block):
+        for m in range(1, cores):
+            across(m, block).start()
+
+    def partial_sum(block):
+        total = part_ref[block, c].astype(F32)
+        for m in range(1, cores):
+            across(m, block).wait_recv()
+            total = total + from_core[m - 1, block].astype(F32)
+        return total
+
+    def advance(step):
+        for side in (0, 1):
+            block, there = goal(side, step)
+            fed = z > 0 if side == 0 else z < lanes - 1
+
+            @pl.when(there)
+            def _():
+                total = partial_sum(block)
+                stage[side, step - 1] = total.astype(BF)
+                if step > 1:
+
+                    @pl.when(fed)
+                    def _():
+                        hop(side, step - 1).wait_recv()
+                        stage[side, step - 1] = (total + inbox[side, step - 2].astype(F32)).astype(BF)
+
+                hop(side, step).start()
+
+    for step in range(1, lanes):
+        for side in (0, 1):
+            block, there = goal(side, step)
+
+            @pl.when(there)
+            def _():
+                begin(block)
+
+    begin(z)
+    for m in range(1, dps):
+        over(m).start()
+    for step in range(1, max(lanes - 1, 1)):
+        advance(step)
+    for m in range(1, dps):
+        over(m).wait_recv()
+    for f in range(fss):
+        total = g_ref[dp, f].astype(F32)
+        for m in range(1, dps):
+            total = total + from_dp[m - 1, f].astype(F32)
+        total_g[f] = total.astype(BF)
+    keep = pltpu.make_async_copy(total_g.at[fs], mix_ref.at[fs], local)
+
+    @pl.when(fs < busy)
+    def _():
+        for k in range(1, fss):
+            home(k, fs).start()
+        keep.start()
+
+    if lanes > 1:
+        advance(lanes - 1)
+    out_ref[...] = partial_sum(z)
+    for side in (0, 1):
+        fed = z > 0 if side == 0 else z < lanes - 1
+
+        @pl.when(fed)
+        def _():
+            hop(side, lanes - 1).wait_recv()
+            out_ref[...] += inbox[side, lanes - 2].astype(F32)
+
+    for k in range(1, fss):
+        owner = lax.rem(fs + fss - k, fss)
+
+        @pl.when(owner < busy)
+        def _():
+            home(k, owner).wait_recv()
+
+    @pl.when(fs < busy)
+    def _():
+        keep.wait()
+        for k in range(1, fss):
+            home(k, fs).wait_send()
+
+    for step in range(1, lanes):
+        for side in (0, 1):
+            block, there = goal(side, step)
+
+            @pl.when(there)
+            def _():
+                hop(side, step).wait_send()
+
+    for m in range(1, cores):
+        for block in range(lanes):
+            across(m, block).wait_send()
+    for m in range(1, dps):
+        over(m).wait_send()
+
+
+def finish(part, g, lanes, cores, busy):
+    dps, fss = g.shape[:2]
+    tokens, model = part.shape[2:]
+    dma = pltpu.SemaphoreType.DMA
+    hops = (2, max(lanes - 1, 1))
+    ways = (max(cores - 1, 1), lanes)
+    whole = pl.BlockSpec(memory_space=pltpu.VMEM)
+    return pl.pallas_call(
+        functools.partial(finish_kernel, dps, lanes, cores, busy),
+        in_specs=[whole, whole],
+        out_specs=[whole, ANY],
+        out_shape=[
+            jax.ShapeDtypeStruct((tokens, model), F32),
+            jax.ShapeDtypeStruct((busy,) + g.shape[2:], BF),
+        ],
+        scratch_shapes=[
+            pltpu.VMEM(ways + (tokens, model), BF),
+            pltpu.VMEM(hops + (tokens, model), BF),
+            pltpu.VMEM(hops + (tokens, model), BF),
+            pltpu.VMEM((dps - 1,) + g.shape[1:], BF),
+            pltpu.VMEM(g.shape[1:], BF),
+            dma(hops), dma(hops), dma(ways), dma(ways), dma((dps - 1,)), dma((dps - 1,)),
+            dma((fss - 1,)), dma((fss - 1,)), dma,
+        ],
+        compiler_params=pltpu.CompilerParams(
+            collective_id=6, has_side_effects=True, vmem_limit_bytes=VMEM_LIMIT
+        ),
+    )(part, g)
+
+
 def per_device(x, w_qkv, w_out, w_shared, w_experts, gains, routes, gates, d_out):
     tokens, model = x.shape
     hidden = w_shared.shape[1] // 3
@@ -298,7 +988,7 @@
         )
 
     def over_dp(value, m):
-        return lax.ppermute(value, "dp", [(a, a ^ m) for a in range(dps)])
+        return lax.ppermute(value, "dp", [(a, (a + m) % dps) for a in range(dps)])
 
     def up(value, least, most):
         return over_z(value, [(a, a + 1) for a in range(least, most)])
@@ -316,43 +1006,10 @@
             buffer = put(buffer, falling, jnp.where(z + s < lanes, z + s, lanes))
         return buffer
 
-    def gather_seq(value):
-        buffer = jnp.zeros((lanes + 1, cores) + value.shape, value.dtype)
-
-        def place(buffer, block, row):
-            buffer = put(buffer, block, row, c)
-            for m in range(1, cores):
-                buffer = put(buffer, over_core(block, m), row, c ^ m)
-            return buffer
-
-        buffer = place(buffer, value, z)
-        rising = falling = value
-        for s in range(1, lanes):
-            rising = up(rising, s - 1, lanes - 1)
-            falling = down(falling, 1, lanes - s + 1)
-            buffer = place(buffer, rising, jnp.where(z >= s, z - s, lanes))
-            buffer = place(buffer, falling, jnp.where(z + s < lanes, z + s, lanes))
-        return buffer.reshape((lanes + 1) * cores * value.shape[0], value.shape[1])
-
-    def sum_z(parts):
-        rising = falling = None
-        for s in range(1, lanes):
-            far = take(parts, jnp.clip(z + lanes - s, 0, lanes - 1)).astype(F32)
-            near = take(parts, jnp.clip(z - lanes + s, 0, lanes - 1)).astype(F32)
-            if rising is not None:
-                far = far + rising.astype(F32)
-                near = near + falling.astype(F32)
-            rising = up(far.astype(BF), 0, s)
-            falling = down(near.astype(BF), lanes - s, lanes)
-        total = take(parts, z).astype(F32)
-        if rising is not None:
-            total = total + rising.astype(F32) + falling.astype(F32)
-        return total
-
     def gather_dp(value):
         buffer = put(jnp.zeros((dps,) + value.shape, value.dtype), value, dp)
         for m in range(1, dps):
-            buffer = put(buffer, over_dp(value, m), dp ^ m)
+            buffer = put(buffer, over_dp(value, m), (dp - m) % dps)
         return buffer
 
     def join_cores(value):
@@ -369,35 +1026,20 @@
     def gather_rows(value):
         return join_cores(gather_dp(gather_z(value)[:lanes]))
 
-    def own_heads(target):
-        cut = w_qkv.reshape(shard, 3, HEADS, HD)
-        cut = jnp.pad(cut, ((0, 0), (0, 0), (0, fss * per - HEADS), (0, 0)))
-        cut = cut.reshape(shard, 3, fss, width)
-        return lax.dynamic_index_in_dim(cut, target, 2, keepdims=False).reshape(shard, 3 * width)
-
-    def gather_heads():
-        buffer = put(jnp.zeros((fss, shard, 3 * width), BF), own_heads(fs), fs)
-        for k in range(1, fss):
-            pairs = [(f, (f + k) % fss) for f in range(fss) if (f + k) % fss < busy]
-            buffer = put(
-                buffer,
-                lax.ppermute(own_heads((fs + k) % fss), "fsdp", pairs),
-                (fs - k) % fss,
-            )
-        return gather_dp(buffer).reshape(model, 3 * width)
-
-    x_all = gather_seq(x)
-    w_heads = gather_heads()
-    small = gather_z(gains.T.astype(F32))[:lanes]
-    gain_all = join_gain = gather_dp(small)
-    both = [None] * cores
-    gain_buf = jnp.zeros((dps, lanes, cores, 2, shard), F32)
-    gain_buf = lax.dynamic_update_slice(gain_buf, join_gain[:, :, None], (0, 0, c, 0, 0))
-    for m in range(1, cores):
-        gain_buf = lax.dynamic_update_slice(
-            gain_buf, over_core(gain_all, m)[:, :, None], (0, 0, c ^ m, 0, 0)
-        )
-    gain_rows = gain_buf.transpose(3, 0, 1, 2, 4).reshape(2, model)
+    cut = w_qkv.reshape(shard, 3, HEADS, HD)
+    cut = jnp.pad(cut, ((0, 0), (0, 0), (0, fss * per - HEADS), (0, 0)))
+    cut = cut.reshape(shard, 3, fss, width).transpose(2, 0, 1, 3).reshape(fss, shard, 3 * width)
+    extra = jnp.broadcast_to(jnp.pad(gains, ((0, 0), (0, HD - 2))), (fss, shard, HD))
+    slabs = jnp.concatenate([cut, extra], axis=2)
+    topk = routes.shape[1]
+    table = jnp.concatenate([routes.T.astype(F32), gates.T], axis=0)
+    table = jnp.pad(table, ((0, -2 * topk % 8), (0, 0)))
+    x_all, slabs, tables, out_all = start(x, slabs, table, w_out, dps, lanes, cores)
+    x_all = x_all.reshape(seq, model)
+    slabs = slabs.reshape(model, 3 * width + HD)
+    out_all = out_all.reshape(model, model)
+    w_heads = jnp.where(fs < busy, slabs[:, : 3 * width], 0)
+    gain_rows = slabs[:, 3 * width : 3 * width + 2].astype(F32).T
     gain_one, gain_two = gain_rows[0:1], gain_rows[1:2]
 
     half = HD // 2
@@ -407,23 +1049,25 @@
     cos = jnp.concatenate([cosine, cosine], axis=1)
     sin = jnp.concatenate([-sine, sine], axis=1)
 
-    table = jnp.concatenate([routes.T.astype(F32), gates.T], axis=0)
-    tables = gather_z(table)[:lanes]
-    topk = routes.shape[1]
-    picks, weights = tables[:, :topk], tables[:, topk:]
+    picks, weights = tables[:, :topk], tables[:, topk : 2 * topk]
     triangle = (jnp.arange(tokens)[:, None] <= jnp.arange(tokens)[None, :]).astype(BF)
     slot_ids = jnp.arange(slots, dtype=F32)
-    select, weigh, slot_gate = [], [], []
+    select, slot_gate, gather_back, weigh_back = [], [], [], []
     for m in range(dps):
-        hit = picks == ((dp ^ m) * lanes + z).astype(F32)
+        hit = picks == ((dp + m) % dps * lanes + z).astype(F32)
         member = jnp.any(hit, axis=1)
         gate = jnp.sum(jnp.where(hit, weights, 0.0), axis=1)
         rank = dot_nn(member.astype(BF), triangle) - 1.0
         match = member[:, None, :] & (rank[:, None, :] == slot_ids[None, :, None])
         select.append(match.astype(BF))
         scaled = jnp.where(match, gate[:, None, :], 0.0)
-        weigh.append(scaled.astype(BF))
         slot_gate.append(jnp.sum(scaled, axis=2, keepdims=True))
+        turned = member[:, :, None] & (rank[:, :, None] == slot_ids[None, None, :])
+        gather_back.append(turned.astype(BF))
+        weigh_back.append(jnp.where(turned, gate[:, :, None], 0.0).astype(BF))
+    select = jnp.stack(select)
+    gather_back = jnp.concatenate(gather_back, axis=2)
+    weigh_back = jnp.concatenate(weigh_back, axis=2)
 
     def pick(blocks, m):
         return lax.dot_general(
@@ -433,70 +1077,42 @@
     xn_one, q, k, v, kt, vt = project(x_all, gain_one, w_heads, cos, sin, seq)
 
     d_out_z = after(d_out, x_all)
-    held = w_experts.reshape(dps, lanes, shard, 3 * hidden)
-    held = after(held, x_all)
-    mine = lambda where: lax.dynamic_index_in_dim(held, where, 1, keepdims=False)
-    rows_z = put(jnp.zeros((lanes, dps, shard, 3 * hidden), BF), mine(z), z)
-    for s in range(1, lanes):
-        rows_z = put(rows_z, turn_z(mine((z + s) % lanes), s), (z - s) % lanes)
-    rows_to = lambda where: lax.dynamic_index_in_dim(rows_z, where, 1, keepdims=False)
-    rows_dp = put(jnp.zeros((dps, lanes, shard, 3 * hidden), BF), rows_to(dp), dp)
-    for m in range(1, dps):
-        rows_dp = put(rows_dp, over_dp(rows_to(dp ^ m), m), dp ^ m)
-    w_own = join_cores(rows_dp)
-
-    dense = gather_rows(after(jnp.concatenate([w_out, w_shared], axis=1), x_all))
-    out_all = dense[:, :model]
-    shared_all = dense[:, model:]
+    groups = [[e * cores + k for e in range(experts)] for k in range(cores)]
+
+    def swap(value):
+        return lax.all_to_all(
+            value, ("dp", "fsdp"), split_axis=0, concat_axis=0, tiled=True, axis_index_groups=groups
+        )
+
+    rows_here = swap(after(w_experts, x_all))
+    w_own = join_cores(rows_here.reshape(dps, lanes, shard, 3 * hidden))
 
     o, lse = attend(q, k, vt, 256)
 
-    blocks_o = o.reshape(fss, tokens, width)
-    mixed = put(jnp.zeros((fss, tokens, width), BF), take(blocks_o, fs), fs)
-    for s in range(1, fss):
-        pairs = [(f, (f + s) % fss) for f in range(busy)]
-        mixed = put(
-            mixed,
-            lax.ppermute(take(blocks_o, (fs + s) % fss), "fsdp", pairs),
-            (fs - s) % fss,
-        )
-    heads = mixed.transpose(1, 0, 2).reshape(tokens, fss * width)[:, :model]
-
+    heads = heads_home(o, tokens, lanes, cores, busy)[:, :model]
     middle = x.astype(F32) + dot_nt(heads, out_all)
     inv_two = lax.rsqrt(jnp.mean(middle * middle, axis=1, keepdims=True) + norm_eps)
     unit_two = middle * inv_two
     xn_two = (unit_two * gain_two).astype(BF)
 
-    up_blocks = gather_z(d_out_z)[:lanes]
-    in_blocks = gather_z(xn_two)[:lanes]
-    xs, cs = [], []
+    up_blocks = gather_z(after(d_out, x_all))[:lanes]
+    cs = []
     for m in range(dps):
-        part = pick(in_blocks, m).astype(BF)
-        xs.append(over_dp(part, m) if m else part)
         part = (pick(up_blocks, m) * slot_gate[m]).astype(BF)
         cs.append(over_dp(part, m) if m else part)
-    flat = lambda parts: jnp.stack(parts).reshape(-1, model)
-    x_slots, c_slots = flat(xs), flat(cs)
+    c_slots = jnp.stack(cs).reshape(-1, model)
+    x_slots = dispatch(xn_two, select, lanes, cores, 3).reshape(-1, model)
     dx_slots, gu_slots, hid_slots = expert(x_slots, c_slots, w_own, BF)
 
+    shared_all = gather_rows(after(w_shared, heads))
     dx_shared, gu_shared, hid_shared = expert(xn_two, d_out, shared_all, F32)
     f_shared = dot_nt(hid_shared, shared_all[:, 2 * hidden :])
 
-    def combine(parts, matrix):
-        parts = parts.reshape(dps, lanes, slots, model)
-        back = [over_dp(parts[m], m) if m else parts[0] for m in range(dps)]
-        total = None
-        for m in range(dps):
-            term = lax.dot_general(
-                matrix[m], back[m], (((1,), (1,)), ((0,), (0,))), preferred_element_type=F32
-            )
-            total = term if total is None else total + term
-        return sum_z(total)
-
-    dx_routed = combine(dx_slots, select)
+    shape = (dps, lanes, slots, model)
+    dx_routed = combine(dx_slots.reshape(shape), gather_back, lanes, cores, 4)
     f_slots = dot_nt(hid_slots, w_own[:, 2 * hidden :]).astype(BF)
     g_own = jnp.concatenate([dot_tn(x_slots, gu_slots), dot_tn(c_slots, hid_slots)], axis=1)
-    routed = combine(f_slots, weigh)
+    routed = combine(f_slots.reshape(shape), weigh_back, lanes, cores, 5)
     layer_out = (middle + f_shared + routed).astype(BF)
 
     dxn_two = dx_shared + dx_routed
@@ -506,19 +1122,16 @@
     )
     d_attn = dx_two.astype(BF)
 
-    da_all = gather_seq(d_attn)[:seq]
+    da_all = gather_sequence(d_attn, lanes, cores).reshape(seq, model)
     out_cols = jnp.pad(out_all, ((0, 0), (0, fss * width - model)))
     out_cols = lax.dynamic_slice_in_dim(out_cols, fs * width, width, 1)
     d_o = dot_nn(da_all, out_cols).astype(BF)
     g_out_part = dot_tn(da_all, o)
     dq, dk, dv = attend_back(q, k, kt, v, o, d_o, lse, cos, sin, 256)
     d_qkv = jnp.concatenate([dq, dk, dv], axis=1)
-    dxn_part = dot_nt(d_qkv, w_heads).reshape(lanes, cores, tokens, model)
-    at_core = lambda k: lax.dynamic_index_in_dim(dxn_part, k, 1, keepdims=False)
-    sums = at_core(c)
-    for m in range(1, cores):
-        sums = sums + over_core(at_core(c ^ m).astype(BF), m).astype(F32)
-    dxn_one = sum_z(sums)
+    dxn_part = dot_nt(d_qkv, w_heads).astype(BF).reshape(lanes, cores, tokens, model)
+    g_part = jnp.concatenate([dot_tn(xn_one, d_qkv), g_out_part], axis=1).astype(BF)
+    dxn_one, g_mix = finish(dxn_part, g_part.reshape(dps, fss, shard, 4 * width), lanes, cores, busy)
     inputs = x.astype(F32)
     inv_one = lax.rsqrt(jnp.mean(inputs * inputs, axis=1, keepdims=True) + norm_eps)
     unit_one = inputs * inv_one
@@ -534,40 +1147,20 @@
         return total
 
     own = reduce_cores(g_own).astype(BF)
-    by_dp = put(jnp.zeros_like(own), take(own, dp), dp)
-    for m in range(1, dps):
-        by_dp = put(by_dp, over_dp(take(own, dp ^ m), m), dp ^ m)
-    at_z = lambda where: lax.dynamic_index_in_dim(by_dp, where, 1, keepdims=False)
-    by_z = put(jnp.zeros((lanes,) + by_dp.shape[:1] + by_dp.shape[2:], BF), at_z(z), z)
-    for s in range(1, lanes):
-        by_z = put(by_z, turn_z(at_z((z + s) % lanes), s), (z - s) % lanes)
-    g_experts = by_z.transpose(1, 0, 2, 3).reshape(experts, shard, 3 * hidden).astype(F32)
+    g_experts = swap(own.reshape(experts, shard, 3 * hidden)).astype(F32)
 
     g_shared_part = jnp.concatenate([dot_tn(xn_two, gu_shared), dot_tn(d_out, hid_shared)], axis=1)
     own = reduce_cores(g_shared_part)
     total = take(own, dp)
     low = own.astype(BF)
     for m in range(1, dps):
-        total = total + over_dp(take(low, dp ^ m), m).astype(F32)
+        total = total + over_dp(take(low, (dp + m) % dps), m).astype(F32)
     low = total.astype(BF)
     g_shared = take(total, z)
     for s in range(1, lanes):
         g_shared = g_shared + turn_z(take(low, (z + s) % lanes), s).astype(F32)
 
-    g_part = jnp.concatenate([dot_tn(xn_one, d_qkv), g_out_part], axis=1)
-    g_part = g_part.reshape(dps, fss, shard, 4 * width)
-    total = take(g_part, dp)
-    low = g_part.astype(BF)
-    for m in range(1, dps):
-        total = total + over_dp(take(low, dp ^ m), m).astype(F32)
-    low = total.astype(BF)
-    g_mix = put(jnp.zeros((fss, shard, 4 * width), BF), take(low, fs), fs)
-    for s in range(1, fss):
-        pairs = [(f, (f + s) % fss) for f in range(busy)]
-        g_mix = put(
-            g_mix, lax.ppermute(take(low, (fs + s) % fss), "fsdp", pairs), (fs - s) % fss
-        )
-    g_mix = g_mix.reshape(fss, shard, 4, width).transpose(1, 2, 0, 3).reshape(shard, 4, fss * width)
+    g_mix = g_mix.reshape(busy, shard, 4, width).transpose(1, 2, 0, 3).reshape(shard, 4, busy * width)
     g_mix = g_mix[:, :, :model].astype(F32)
     g_qkv = g_mix[:, :3].reshape(shard, 3 * model)
     g_out = g_mix[:, 3]

time: 1370 us -> 1030 us (0.75)
  waiting for transfers between devices: 633 us -> 192 us
  Pallas kernels: 103 us -> 536 us
  starting transfers between devices: 298 us -> 78.4 us
  local copies, waits for them, and re-layouts: 147 us -> 77.8 us
  matrix products: 94.1 us -> 75.2 us
    pallas_call x0 -> x7, Pallas kernels: none -> 433 us  [the longest x2 130 us: combine(): pl.pallas_call(functools.partial(combine_kernel, dps, lanes, cores), in_s...]
    ppermute x69 -> x15, waiting for transfers between devices: 315 us -> 85.4 us  [over_z(): lax.ppermute(value, 'fsdp', [(a * cores + k, b * cores + k) for a, b in p...]
    ppermute x54 -> x9, waiting for transfers between devices: 316 us -> 107 us  [over_dp(): return lax.ppermute(value, 'dp', [(a, (a + m) % dps) for a in range(dps)])]
    ppermute x54 -> x9, starting transfers between devices: 133 us -> 9.45 us  [over_dp(): return lax.ppermute(value, 'dp', [(a, (a + m) % dps) for a in range(dps)])]
    ppermute x69 -> x15, starting transfers between devices: 163 us -> 50.4 us  [over_z(): lax.ppermute(value, 'fsdp', [(a * cores + k, b * cores + k) for a, b in p...]
    dot_general x8 -> x0, matrix products: 31.3 us -> none  [combine(): lax.dot_general(matrix[m], back[m], (((1,), (1,)), ((0,), (0,))), preferr...]
    dynamic_update_slice x110 -> x18, local copies, waits for them, and re-layouts: 42 us -> 16.7 us  [put(): lax.dynamic_update_slice(buffer, value.reshape((1,) * len(index) + buffer...]
    all_to_all x0 -> x2, starting transfers between devices: none -> 18.6 us  [swap(): lax.all_to_all(value, ('dp', 'fsdp'), split_axis=0, concat_axis=0, tiled=...]
  transfers between devices with their start and end apart: 143 -> 30, of which waited for: 62 -> 12; matrix products, arithmetic and copies ran while one was open for 19% -> 16% of each run, Pallas kernels for 6% -> 35%
where the time goes in v2:
time: 1030 us; the launch traced here: 1020 us
  Pallas kernels  536 us (52%)
  waiting for transfers between devices  192 us (19%)
  starting transfers between devices  78.4 us (8%)
  local copies, waits for them, and re-layouts  77.8 us (8%)
  matrix products  75.2 us (7%)
  other arithmetic  60.9 us (6%)
    pallas_call x2, Pallas kernels, combine(): pl.pallas_call(functools.partial(combine_kernel, dps, lanes, cores), in_s...  130 us
    ppermute x9, waiting for transfers between devices, over_dp(): return lax.ppermute(value, 'dp', [(a, (a + m) % dps) for a in range(dps)])  107 us
    pallas_call x1, Pallas kernels, finish(): pl.pallas_call(functools.partial(finish_kernel, dps, lanes, cores, busy),...  96.7 us
    ppermute x15, waiting for transfers between devices, over_z(): lax.ppermute(value, 'fsdp', [(a * cores + k, b * cores + k) for a, b in p...  85.4 us
    pallas_call x1, Pallas kernels, start(): pl.pallas_call(functools.partial(start_kernel, dps, lanes, cores), in_spe...  77.4 us
    pallas_call x1, Pallas kernels, dispatch(): pl.pallas_call(functools.partial(dispatch_kernel, dps, lanes, cores), in_...  66.2 us
    ppermute x15, starting transfers between devices, over_z(): lax.ppermute(value, 'fsdp', [(a * cores + k, b * cores + k) for a, b in p...  50.4 us
    pallas_call x1, Pallas kernels, gather_sequence(): pl.pallas_call(functools.partial(gather_kernel, lanes, cores), in_specs=[...  48.2 us
  transfers between devices with their start and end apart: 30, of which 12 were waited for; matrix products, arithmetic and copies ran while one was open for 16% of the time, Pallas kernels for 35%

profile of v2, /device:TPU:20, one launch (start us, length us, event | category | flops | bytes accessed | tf_op | source)
XLA Modules:
  0.0 1022.9 jit_solution(6545430779383623600)
XLA Ops:
  5.2 77.4 %shard_map.144 = (bf16[4,2,256,1280]{3,2,1,0:T(8,128)(2,1)}, bf16[4,8,40,896]{3,2,1,0:T(8,128)(2,1)}, f32[4,16,256]{2,1,0:T(8,128)}, bf16[4,4,2,40,1280]{4,3,2,1,0:T(8,128)(2,1)}) custom-call(bf16[256,1280]{1,0:T(8,128)(2,1)} %x_ref.1, bf16[8,40,896]{2,1,0:T(8,128)(2,1)} %pad_maximum_fusion.7.wh_ref, f32[16,256]{1,0:T(8,128)} %select_maximum_fusion.tab_ref, ...), custom_call_target="tpu_custom_call" | custom-call | tf_op jit(solution)/shard_map/pallas_call | solution.py:496
  87.7 6.7 collective-permute-start.11
  105.8 14.3 %shard_map.145 = (bf16[2048,1280]{1,0:T(8,128)(2,1)}, bf16[2048,256]{1,0:T(8,128)(2,1)}, bf16[2048,256]{1,0:T(8,128)(2,1)}, bf16[2048,256]{1,0:T(8,128)(2,1)}, b...) custom-call(bf16[2048,1280]{1,0:T(8,128)(2,1)} %bitcast.184, f32[1,1280]{1,0:T(1,128)} %copy.26.gain_ref, ...), custom_call_target="tpu_custom_call" | custom-call | flops 4026531840 | bytes 15728640 | tf_op jit(solution)/shard_map/pallas_call | solution.py:82
  120.1 18.3 %shard_map.146 = (bf16[2048,256]{1,0:T(8,128)(2,1)}, f32[2,1,2048]{2,1,0:T(1,128)}) custom-call(bf16[2048,256]{1,0:T(8,128)(2,1)} %get-tuple-element.35.q_ref, bf16[2048,256]{1,0:T(8,128)(2,1)} %get-tuple-element.36.k_ref, bf16[256,2048]{1,0:T(8,128)(2,1)} %get-tuple-element.37.vt_ref), custom_call_target="tpu_custom_call" | custom-call | flops 8589934592 | bytes 4194304 | tf_op jit(solution)/shard_map/pallas_call | solution.py:138
  138.5 14.8 %shard_map.147 = bf16[256,1280]{1,0:T(8,128)(2,1)} custom-call(bf16[2048,256]{1,0:T(8,128)(2,1)} %get-tuple-element.38.o_ref), custom_call_target="tpu_custom_call" | custom-call | tf_op jit(solution)/shard_map/pallas_call | solution.py:548
  153.3 13.3 %collective-permute-start = (bf16[40,2688]{1,0:T(8,128)(2,1)S(1)}, bf16[40,2688]{1,0:T(8,128)(2,1)}, u32[]{:S(2)}, u32[]{:S(2)}) collective-permute-start(bf16[40,2688]{1,0:T(8,128)(2,1)S(1)} %copy-done.24), channel_id=1, source_target_pairs={{0,2},{1,3},{2,4},{3,5},{4,6},{5,7},{8,10},{9,11},{10,12},{11,13},... | collective-permute-start | bytes 645128 | tf_op jit(solution)/shard_map/ppermute | solution.py:978
  169.2 7.3 all-to-all-start
  199.5 62.4 %collective-permute-done.2 = bf16[40,2688]{1,0:T(8,128)(2,1)S(1)} collective-permute-done((bf16[40,2688]{1,0:T(8,128)(2,1)}, bf16[40,2688]{1,0:T(8,128)(2,1)S(1)}, u32[]{:S(2)}, u32[]{:S(2)}) %collective-permute-start.2) | collective-permute-done | bytes 215072 | tf_op jit(solution)/shard_map/ppermute | solution.py:978
  275.6 15.8 %collective-permute-done.6 = bf16[4,40,2688]{2,1,0:T(8,128)(2,1)S(1)} collective-permute-done((bf16[4,40,2688]{2,1,0:T(8,128)(2,1)S(1)}, bf16[4,40,2688]{2,1,0:T(8,128)(2,1)S(1)}, u32[]{:S(2)}, u32[]{:S(2)}) %collective-permute-start.6) | collective-permute-done | bytes 860192 | tf_op jit(solution)/shard_map/ppermute | solution.py:991
  292.4 16.0 %collective-permute-done.7 = bf16[4,40,2688]{2,1,0:T(8,128)(2,1)S(1)} collective-permute-done((bf16[4,40,2688]{2,1,0:T(8,128)(2,1)S(1)}, bf16[4,40,2688]{2,1,0:T(8,128)(2,1)S(1)}, u32[]{:S(2)}, u32[]{:S(2)}) %collective-permute-start.7) | collective-permute-done | bytes 860192 | tf_op jit(solution)/shard_map/ppermute | solution.py:991
  314.4 66.2 %shard_map.149 = bf16[4,4,128,1280]{3,2,1,0:T(8,128)(2,1)} custom-call(bf16[256,1280]{1,0:T(8,128)(2,1)} %multiply_convert_fusion.x_ref, bf16[4,4,128,256]{3,2,1,0:T(8,128)(2,1)} %add_convert_fusion.pick_ref), custom_call_target="tpu_custom_call" | custom-call | tf_op jit(solution)/shard_map/pallas_call | solution.py:651
  404.5 8.5 shard_map.148
  428.1 11.1 %collective-permute-done.14 = bf16[256,1280]{1,0:T(8,128)(2,1)S(1)} collective-permute-done((bf16[256,1280]{1,0:T(8,128)(2,1)}, bf16[256,1280]{1,0:T(8,128)(2,1)S(1)}, u32[]{:S(2)}, u32[]{:S(2)}) %collective-permute-start.14) | collective-permute-done | bytes 655392 | tf_op jit(solution)/shard_map/ppermute | solution.py:978
  461.7 14.5 %collective-permute-done.18 = bf16[4,128,1280]{2,1,0:T(8,128)(2,1)S(1)} collective-permute-done((bf16[4,128,1280]{2,1,0:T(8,128)(2,1)}, bf16[4,128,1280]{2,1,0:T(8,128)(2,1)S(1)}, u32[]{:S(2)}, u32[]{:S(2)}) %collective-permute-start.18) | collective-permute-done | bytes 1310752 | tf_op jit(solution)/shard_map/ppermute | solution.py:991
  476.9 32.3 %collective-permute-done.17 = bf16[4,128,1280]{2,1,0:T(8,128)(2,1)} collective-permute-done((bf16[4,128,1280]{2,1,0:T(8,128)(2,1)}, bf16[4,128,1280]{2,1,0:T(8,128)(2,1)}, u32[]{:S(2)}, u32[]{:S(2)}) %collective-permute-start.17) | collective-permute-done | bytes 1310752 | tf_op jit(solution)/shard_map/ppermute | solution.py:991
  515.4 7.4 collective-permute-done.23
  522.8 21.0 %collective-permute-done.22 = bf16[4,40,2688]{2,1,0:T(8,128)(2,1)S(1)} collective-permute-done((bf16[4,40,2688]{2,1,0:T(8,128)(2,1)S(1)}, bf16[4,40,2688]{2,1,0:T(8,128)(2,1)S(1)}, u32[]{:S(2)}, u32[]{:S(2)}) %collective-permute-start.22) | collective-permute-done | bytes 860192 | tf_op jit(solution)/shard_map/ppermute | solution.py:991
  569.8 36.6 %shard_map.150 = (bf16[2048,1280]{1,0:T(8,128)(2,1)}, bf16[2048,1792]{1,0:T(8,128)(2,1)}, bf16[2048,896]{1,0:T(8,128)(2,1)}) custom-call(bf16[2048,1280]{1,0:T(8,128)(2,1)} %bitcast.164, bf16[2048,1280]{1,0:T(8,128)(2,1)} %bitcast.168, bf16[1280,2688]{1,0:T(8,128)(2,1)} %bitcast.39.w_ref), custom_call_target="tpu_custom_call" | custom-call | flops 23488102400 | bytes 31457280 | tf_op jit(solution)/shard_map/pallas_call | solution.py:255
  606.4 64.3 %shard_map.152 = f32[256,1280]{1,0:T(8,128)} custom-call(bf16[4,4,128,1280]{3,2,1,0:T(8,128)(2,1)} %bitcast.172, bf16[4,256,512]{2,1,0:T(8,128)(2,1)} %add_convert_fusion.1.mat_ref), custom_call_target="tpu_custom_call" | custom-call | tf_op jit(solution)/shard_map/pallas_call | solution.py:783
  673.1 9.3 fusion.63
  682.5 10.5 %fusion.62 = f32[1280,1792]{1,0:T(8,128)S(1)} fusion(bf16[2048,1280]{1,0:T(8,128)(2,1)S(1)} %bitcast.167, bf16[2048,1792]{1,0:T(8,128)(2,1)S(1)} %copy-done.51), kind=kOutput, calls=%fused_computation.180 | convolution fusion | flops 9395240960 | bytes 21757952 | tf_op jit(solution)/shard_map/dot_general | solution.py:29
  705.4 48.2 %shard_map.153 = bf16[4,2,256,1280]{3,2,1,0:T(8,128)(2,1)} custom-call(bf16[256,1280]{1,0:T(8,128)(2,1)} %get-tuple-element.69.x_ref), custom_call_target="tpu_custom_call" | custom-call | tf_op jit(solution)/shard_map/pallas_call | solution.py:391
  753.6 5.2 convolution_convert_fusion.3.do_ref
  758.8 25.2 %shard_map.154 = (bf16[2048,256]{1,0:T(8,128)(2,1)}, bf16[2048,256]{1,0:T(8,128)(2,1)}, bf16[2048,256]{1,0:T(8,128)(2,1)}) custom-call(bf16[2048,256]{1,0:T(8,128)(2,1)} %get-tuple-element.35.q_ref, bf16[2048,256]{1,0:T(8,128)(2,1)} %get-tuple-element.36.k_ref, bf16[256,2048]{1,0:T(8,128)(2,1)} %get-tuple-element.48.kt_ref, ...), custom_call_target="tpu_custom_call" | custom-call | flops 21474836480 | bytes 8388608 | tf_op jit(solution)/shard_map/pallas_call | solution.py:217
  786.3 6.3 fusion
  792.7 11.3 %all-to-all-start.1 = ((bf16[16,40,2688]{2,1,0:T(8,128)(2,1)}), bf16[16,40,2688]{2,1,0:T(8,128)(2,1)}, u32[]{:S(2)}, u32[]{:S(2)}) async-start(bf16[16,40,2688]{2,1,0:T(8,128)(2,1)} %bitcast.163), calls=%async_computation.1 | async-start | bytes 6881280 | tf_op jit(solution)/shard_map/all_to_all | solution.py:1083
  805.2 8.1 copy.29
  818.6 6.8 convolution_convert_fusion.2
  827.5 6.0 convolution_convert_fusion.1
  833.5 96.7 %shard_map.155 = (f32[256,1280]{1,0:T(8,128)}, bf16[5,40,1024]{2,1,0:T(8,128)(2,1)}) custom-call(bf16[4,2,256,1280]{3,2,1,0:T(8,128)(2,1)} %bitcast.171, bf16[4,8,40,1024]{3,2,1,0:T(8,128)(2,1)} %pad_maximum_fusion.3.g_ref), custom_call_target="tpu_custom_call" | custom-call | tf_op jit(solution)/shard_map/pallas_call | solution.py:939
  933.3 9.6 convolution_convert_fusion
  942.8 65.8 %shard_map.151 = f32[256,1280]{1,0:T(8,128)} custom-call(bf16[4,4,128,1280]{3,2,1,0:T(8,128)(2,1)} %bitcast.173, bf16[4,256,512]{2,1,0:T(8,128)(2,1)} %pad_maximum_fusion.6.mat_ref), custom_call_target="tpu_custom_call" | custom-call | tf_op jit(solution)/shard_map/pallas_call | solution.py:783
  (271 shorter events, 204.0 us)
Async XLA Ops:
  82.6 302.2 %collective-permute-start.10 = (bf16[256,1280]{1,0:T(8,128)(2,1)S(1)}, bf16[256,1280]{1,0:T(8,128)(2,1)}, u32[]{:S(2)}, u32[]{:S(2)}) collective-permute-start(bf16[256,1280]{1,0:T(8,128)(2,1)S(1)} %copy-done.8), channel_id=1, source_target_pairs={{0,2},{1,3},{2,4},{3,5},{4,6},{5,7},{8,10},{9,11},{10,12},{11,13},... | collective-permute-start | bytes 1966088 | tf_op jit(solution)/shard_map/ppermute | solution.py:978
  87.7 302.3 %collective-permute-start.11 = (bf16[256,1280]{1,0:T(8,128)(2,1)S(1)}, bf16[256,1280]{1,0:T(8,128)(2,1)}, u32[]{:S(2)}, u32[]{:S(2)}) collective-permute-start(bf16[256,1280]{1,0:T(8,128)(2,1)S(1)} %copy-done.8), channel_id=1, source_target_pairs={{2,0},{3,1},{4,2},{5,3},{6,4},{7,5},{10,8},{11,9},{12,10},{13,11},... | collective-permute-start | bytes 1966088 | tf_op jit(solution)/shard_map/ppermute | solution.py:978
  153.3 38.4 %collective-permute-start = (bf16[40,2688]{1,0:T(8,128)(2,1)S(1)}, bf16[40,2688]{1,0:T(8,128)(2,1)}, u32[]{:S(2)}, u32[]{:S(2)}) collective-permute-start(bf16[40,2688]{1,0:T(8,128)(2,1)S(1)} %copy-done.24), channel_id=1, source_target_pairs={{0,2},{1,3},{2,4},{3,5},{4,6},{5,7},{8,10},{9,11},{10,12},{11,13},... | collective-permute-start | bytes 645128 | tf_op jit(solution)/shard_map/ppermute | solution.py:978
  166.5 28.5 %collective-permute-start.1 = (bf16[40,2688]{1,0:T(8,128)(2,1)S(1)}, bf16[40,2688]{1,0:T(8,128)(2,1)}, u32[]{:S(2)}, u32[]{:S(2)}) collective-permute-start(bf16[40,2688]{1,0:T(8,128)(2,1)S(1)} %copy-done.24), channel_id=1, source_target_pairs={{2,0},{3,1},{4,2},{5,3},{6,4},{7,5},{10,8},{11,9},{12,10},{13,11},... | collective-permute-start | bytes 645128 | tf_op jit(solution)/shard_map/ppermute | solution.py:978
  169.2 285.0 %all-to-all-start = ((bf16[16,40,2688]{2,1,0:T(8,128)(2,1)}), bf16[16,40,2688]{2,1,0:T(8,128)(2,1)}, u32[]{:S(2)}, u32[]{:S(2)}) async-start(bf16[16,40,2688]{2,1,0:T(8,128)(2,1)} %param.13), calls=%async_computation | async-start | bytes 6881280 | tf_op jit(solution)/shard_map/all_to_all | solution.py:1083
  188.6 81.4 %copy-start.20 = (bf16[4,256,128]{2,1,0:T(8,128)(2,1)S(1)}, bf16[4,256,128]{2,1,0:T(8,128)(2,1)}, u32[]{:S(2)}) copy-start(bf16[4,256,128]{2,1,0:T(8,128)(2,1)} %get-tuple-element.90) | copy-start | bytes 786436
  191.7 121.5 %copy-start.40 = (f32[256]{0:T(256)}, f32[256]{0:T(256)S(1)}, u32[]{:S(2)}) copy-start(f32[256]{0:T(256)S(1)} %add_rsqrt_fusion.1) | copy-start | bytes 3076
  191.7 70.2 %collective-permute-start.2 = (bf16[40,2688]{1,0:T(8,128)(2,1)}, bf16[40,2688]{1,0:T(8,128)(2,1)S(1)}, u32[]{:S(2)}, u32[]{:S(2)}) collective-permute-start(bf16[40,2688]{1,0:T(8,128)(2,1)} %collective-permute-done), channel_id=1, source_target_pairs={{2,4},{3,5},{4,6},{5,7},{10,12},{11,13},{12,14},{13,15},{18,20},{1... | collective-permute-start | bytes 645128 | tf_op jit(solution)/shard_map/ppermute | solution.py:978
  195.1 68.1 %collective-permute-start.3 = (bf16[40,2688]{1,0:T(8,128)(2,1)}, bf16[40,2688]{1,0:T(8,128)(2,1)S(1)}, u32[]{:S(2)}, u32[]{:S(2)}) collective-permute-start(bf16[40,2688]{1,0:T(8,128)(2,1)} %collective-permute-done.1), channel_id=1, source_target_pairs={{2,0},{3,1},{4,2},{5,3},{10,8},{11,9},{12,10},{13,11},{18,16},{19,... | collective-permute-start | bytes 645128 | tf_op jit(solution)/shard_map/ppermute | solution.py:978
  261.8 6.4 collective-permute-start.4
  263.1 5.1 collective-permute-start.5
  268.4 23.0 %collective-permute-start.6 = (bf16[4,40,2688]{2,1,0:T(8,128)(2,1)S(1)}, bf16[4,40,2688]{2,1,0:T(8,128)(2,1)S(1)}, u32[]{:S(2)}, u32[]{:S(2)}) collective-permute-start(bf16[4,40,2688]{2,1,0:T(8,128)(2,1)S(1)} %slice.68), channel_id=1, source_target_pairs={{0,8},{8,16},{16,24},{24,0},{1,9},{9,17},{17,25},{25,1},{2,10},{10... | collective-permute-start | bytes 2580488 | tf_op jit(solution)/shard_map/ppermute | solution.py:991
  271.1 37.3 %collective-permute-start.7 = (bf16[4,40,2688]{2,1,0:T(8,128)(2,1)S(1)}, bf16[4,40,2688]{2,1,0:T(8,128)(2,1)S(1)}, u32[]{:S(2)}, u32[]{:S(2)}) collective-permute-start(bf16[4,40,2688]{2,1,0:T(8,128)(2,1)S(1)} %slice.68), channel_id=1, source_target_pairs={{0,16},{8,24},{16,0},{24,8},{1,17},{9,25},{17,1},{25,9},{2,18},{10... | collective-permute-start | bytes 2580488 | tf_op jit(solution)/shard_map/ppermute | solution.py:991
  271.1 38.2 %collective-permute-start.8 = (bf16[4,40,2688]{2,1,0:T(8,128)(2,1)S(1)}, bf16[4,40,2688]{2,1,0:T(8,128)(2,1)S(1)}, u32[]{:S(2)}, u32[]{:S(2)}) collective-permute-start(bf16[4,40,2688]{2,1,0:T(8,128)(2,1)S(1)} %slice.68), channel_id=1, source_target_pairs={{0,24},{8,0},{16,8},{24,16},{1,25},{9,1},{17,9},{25,17},{2,26},{10... | collective-permute-start | bytes 2580488 | tf_op jit(solution)/shard_map/ppermute | solution.py:991
  310.3 90.3 %collective-permute-start.9 = (bf16[4,4,40,2688]{3,2,1,0:T(8,128)(2,1)}, bf16[4,4,40,2688]{3,2,1,0:T(8,128)(2,1)}, u32[]{:S(2)}, u32[]{:S(2)}) collective-permute-start(bf16[4,4,40,2688]{3,2,1,0:T(8,128)(2,1)} %bitcast_dynamic-update-slice_fusion.3), channel_id=1, source_target_pairs={{0,1},{1,0},{2,3},{3,2},{4,5},{5,4},{6,7},{7,6},{8,9},{9,8},{10,11... | collective-permute-start | bytes 10321928 | tf_op jit(solution)/shard_map/ppermute | solution.py:986
  384.8 38.4 %collective-permute-start.12 = (bf16[256,1280]{1,0:T(8,128)(2,1)}, bf16[256,1280]{1,0:T(8,128)(2,1)}, u32[]{:S(2)}, u32[]{:S(2)}) collective-permute-start(bf16[256,1280]{1,0:T(8,128)(2,1)} %collective-permute-done.10), channel_id=1, source_target_pairs={{2,4},{3,5},{4,6},{5,7},{10,12},{11,13},{12,14},{13,15},{18,20},{1... | collective-permute-start | bytes 1966088 | tf_op jit(solution)/shard_map/ppermute | solution.py:978
  389.9 36.6 %collective-permute-start.13 = (bf16[256,1280]{1,0:T(8,128)(2,1)}, bf16[256,1280]{1,0:T(8,128)(2,1)S(1)}, u32[]{:S(2)}, u32[]{:S(2)}) collective-permute-start(bf16[256,1280]{1,0:T(8,128)(2,1)} %collective-permute-done.11), channel_id=1, source_target_pairs={{2,0},{3,1},{4,2},{5,3},{10,8},{11,9},{12,10},{13,11},{18,16},{19,... | collective-permute-start | bytes 1966088 | tf_op jit(solution)/shard_map/ppermute | solution.py:978
  419.9 34.2 %collective-permute-start.20 = (bf16[4,4,40,2688]{3,2,1,0:T(8,128)(2,1)}, bf16[4,4,40,2688]{3,2,1,0:T(8,128)(2,1)}, u32[]{:S(2)}, u32[]{:S(2)}) collective-permute-start(bf16[4,4,40,2688]{3,2,1,0:T(8,128)(2,1)} %fusion.2), channel_id=1, source_target_pairs={{0,1},{1,0},{2,3},{3,2},{4,5},{5,4},{6,7},{7,6},{8,9},{9,8},{10,11... | collective-permute-start | bytes 10321928 | tf_op jit(solution)/shard_map/ppermute | solution.py:986
  423.2 16.0 %collective-permute-start.14 = (bf16[256,1280]{1,0:T(8,128)(2,1)}, bf16[256,1280]{1,0:T(8,128)(2,1)S(1)}, u32[]{:S(2)}, u32[]{:S(2)}) collective-permute-start(bf16[256,1280]{1,0:T(8,128)(2,1)} %collective-permute-done.12), channel_id=1, source_target_pairs={{4,6},{5,7},{12,14},{13,15},{20,22},{21,23},{28,30},{29,31}} | collective-permute-start | bytes 1966088 | tf_op jit(solution)/shard_map/ppermute | solution.py:978
  426.5 13.6 %collective-permute-start.15 = (bf16[256,1280]{1,0:T(8,128)(2,1)S(1)}, bf16[256,1280]{1,0:T(8,128)(2,1)S(1)}, u32[]{:S(2)}, u32[]{:S(2)}) collective-permute-start(bf16[256,1280]{1,0:T(8,128)(2,1)S(1)} %collective-permute-done.13), channel_id=1, source_target_pairs={{2,0},{3,1},{10,8},{11,9},{18,16},{19,17},{26,24},{27,25}} | collective-permute-start | bytes 1966088 | tf_op jit(solution)/shard_map/ppermute | solution.py:978
  444.3 31.9 %collective-permute-start.18 = (bf16[4,128,1280]{2,1,0:T(8,128)(2,1)}, bf16[4,128,1280]{2,1,0:T(8,128)(2,1)S(1)}, u32[]{:S(2)}, u32[]{:S(2)}) collective-permute-start(bf16[4,128,1280]{2,1,0:T(8,128)(2,1)} %fusion.7), channel_id=1, source_target_pairs={{0,24},{8,0},{16,8},{24,16},{1,25},{9,1},{17,9},{25,17},{2,26},{10... | collective-permute-start | bytes 3932168 | tf_op jit(solution)/shard_map/ppermute | solution.py:991
  449.0 60.1 %collective-permute-start.17 = (bf16[4,128,1280]{2,1,0:T(8,128)(2,1)}, bf16[4,128,1280]{2,1,0:T(8,128)(2,1)}, u32[]{:S(2)}, u32[]{:S(2)}) collective-permute-start(bf16[4,128,1280]{2,1,0:T(8,128)(2,1)} %fusion.6), channel_id=1, source_target_pairs={{0,16},{8,24},{16,0},{24,8},{1,17},{9,25},{17,1},{25,9},{2,18},{10... | collective-permute-start | bytes 3932168 | tf_op jit(solution)/shard_map/ppermute | solution.py:991
  453.2 58.2 %collective-permute-start.16 = (bf16[4,128,1280]{2,1,0:T(8,128)(2,1)}, bf16[4,128,1280]{2,1,0:T(8,128)(2,1)}, u32[]{:S(2)}, u32[]{:S(2)}) collective-permute-start(bf16[4,128,1280]{2,1,0:T(8,128)(2,1)} %fusion.5), channel_id=1, source_target_pairs={{0,8},{8,16},{16,24},{24,0},{1,9},{9,17},{17,25},{25,1},{2,10},{10... | collective-permute-start | bytes 3932168 | tf_op jit(solution)/shard_map/ppermute | solution.py:991
  454.1 111.7 %collective-permute-start.19 = (bf16[4,4,40,2688]{3,2,1,0:T(8,128)(2,1)}, bf16[4,4,40,2688]{3,2,1,0:T(8,128)(2,1)}, u32[]{:S(2)}, u32[]{:S(2)}) collective-permute-start(bf16[4,4,40,2688]{3,2,1,0:T(8,128)(2,1)} %bitcast.37), channel_id=1, source_target_pairs={{0,1},{1,0},{2,3},{3,2},{4,5},{5,4},{6,7},{7,6},{8,9},{9,8},{10,11... | collective-permute-start | bytes 10321928 | tf_op jit(solution)/shard_map/ppermute | solution.py:986
  459.2 63.6 %collective-permute-start.23 = (bf16[4,40,2688]{2,1,0:T(8,128)(2,1)S(1)}, bf16[4,40,2688]{2,1,0:T(8,128)(2,1)S(1)}, u32[]{:S(2)}, u32[]{:S(2)}) collective-permute-start(bf16[4,40,2688]{2,1,0:T(8,128)(2,1)S(1)} %get-tuple-element.76), channel_id=1, source_target_pairs={{0,24},{8,0},{16,8},{24,16},{1,25},{9,1},{17,9},{25,17},{2,26},{10... | collective-permute-start | bytes 2580488 | tf_op jit(solution)/shard_map/ppermute | solution.py:991
  476.2 67.6 %collective-permute-start.22 = (bf16[4,40,2688]{2,1,0:T(8,128)(2,1)S(1)}, bf16[4,40,2688]{2,1,0:T(8,128)(2,1)S(1)}, u32[]{:S(2)}, u32[]{:S(2)}) collective-permute-start(bf16[4,40,2688]{2,1,0:T(8,128)(2,1)S(1)} %get-tuple-element.77), channel_id=1, source_target_pairs={{0,16},{8,24},{16,0},{24,8},{1,17},{9,25},{17,1},{25,9},{2,18},{10... | collective-permute-start | bytes 2580488 | tf_op jit(solution)/shard_map/ppermute | solution.py:991
  509.1 34.7 %collective-permute-start.21 = (bf16[4,40,2688]{2,1,0:T(8,128)(2,1)S(1)}, bf16[4,40,2688]{2,1,0:T(8,128)(2,1)S(1)}, u32[]{:S(2)}, u32[]{:S(2)}) collective-permute-start(bf16[4,40,2688]{2,1,0:T(8,128)(2,1)S(1)} %get-tuple-element.75), channel_id=1, source_target_pairs={{0,8},{8,16},{16,24},{24,0},{1,9},{9,17},{17,25},{25,1},{2,10},{10... | collective-permute-start | bytes 2580488 | tf_op jit(solution)/shard_map/ppermute | solution.py:991
  544.3 16.4 %collective-permute-start.26 = (bf16[40,2688]{1,0:T(8,128)(2,1)S(1)}, bf16[40,2688]{1,0:T(8,128)(2,1)S(1)}, u32[]{:S(2)}, u32[]{:S(2)}) collective-permute-start(bf16[40,2688]{1,0:T(8,128)(2,1)S(1)} %get-tuple-element.79), channel_id=1, source_target_pairs={{0,6},{1,7},{2,0},{3,1},{4,2},{5,3},{6,4},{7,5},{8,14},{9,15},{10,... | collective-permute-start | bytes 645128 | tf_op jit(solution)/shard_map/ppermute | solution.py:978
  546.6 16.4 %collective-permute-start.25 = (bf16[40,2688]{1,0:T(8,128)(2,1)S(1)}, bf16[40,2688]{1,0:T(8,128)(2,1)S(1)}, u32[]{:S(2)}, u32[]{:S(2)}) collective-permute-start(bf16[40,2688]{1,0:T(8,128)(2,1)S(1)} %get-tuple-element.80), channel_id=1, source_target_pairs={{0,4},{1,5},{2,6},{3,7},{4,0},{5,1},{6,2},{7,3},{8,12},{9,13},{10,... | collective-permute-start | bytes 645128 | tf_op jit(solution)/shard_map/ppermute | solution.py:978
  549.1 16.5 %collective-permute-start.24 = (bf16[40,2688]{1,0:T(8,128)(2,1)S(1)}, bf16[40,2688]{1,0:T(8,128)(2,1)S(1)}, u32[]{:S(2)}, u32[]{:S(2)}) collective-permute-start(bf16[40,2688]{1,0:T(8,128)(2,1)S(1)} %get-tuple-element.78), channel_id=1, source_target_pairs={{0,2},{1,3},{2,4},{3,5},{4,6},{5,7},{6,0},{7,1},{8,10},{9,11},{10,... | collective-permute-start | bytes 645128 | tf_op jit(solution)/shard_map/ppermute | solution.py:978
  703.6 82.7 %collective-permute-start.27 = (bf16[4,4,40,2688]{3,2,1,0:T(8,128)(2,1)}, bf16[4,4,40,2688]{3,2,1,0:T(8,128)(2,1)}, u32[]{:S(2)}, u32[]{:S(2)}) collective-permute-start(bf16[4,4,40,2688]{3,2,1,0:T(8,128)(2,1)} %fusion.3), channel_id=1, source_target_pairs={{0,1},{1,0},{2,3},{3,2},{4,5},{5,4},{6,7},{7,6},{8,9},{9,8},{10,11... | collective-permute-start | bytes 10321928 | tf_op jit(solution)/shard_map/ppermute | solution.py:986
  792.7 223.5 %all-to-all-start.1 = ((bf16[16,40,2688]{2,1,0:T(8,128)(2,1)}), bf16[16,40,2688]{2,1,0:T(8,128)(2,1)}, u32[]{:S(2)}, u32[]{:S(2)}) async-start(bf16[16,40,2688]{2,1,0:T(8,128)(2,1)} %bitcast.163), calls=%async_computation.1 | async-start | bytes 6881280 | tf_op jit(solution)/shard_map/all_to_all | solution.py:1083
  (52 other events, 1188.4 us)

commit v3 on v2

--- a/solution.py
+++ b/solution.py
@@ -27,6 +27,10 @@
 
 def dot_tn(a, b):
     return lax.dot_general(a, b, (((0,), (0,)), ((), ())), preferred_element_type=F32)
+
+
+def lasts(us):
+    return pl.CostEstimate(flops=0, bytes_accessed=int(us * 3.6e6), transcendentals=0)
 
 
 def after(value, *marks):
@@ -92,9 +96,7 @@
         out_specs=[row(model), row(width), row(width), row(width), col, col],
         out_shape=[jax.ShapeDtypeStruct((seq, model), BF), flat, flat, flat, turned, turned],
         compiler_params=pltpu.CompilerParams(vmem_limit_bytes=VMEM_LIMIT),
-        cost_estimate=pl.CostEstimate(
-            flops=2 * seq * model * w.shape[1], bytes_accessed=seq * model * 6, transcendentals=0
-        ),
+        cost_estimate=lasts(14),
     )(x_all, gain, w, cos, sin)
 
 
@@ -152,9 +154,7 @@
             jax.ShapeDtypeStruct((heads, 1, seq), F32),
         ],
         compiler_params=pltpu.CompilerParams(vmem_limit_bytes=VMEM_LIMIT),
-        cost_estimate=pl.CostEstimate(
-            flops=8 * seq * seq * width, bytes_accessed=seq * width * 8, transcendentals=0
-        ),
+        cost_estimate=lasts(18),
     )(q, k, vt)
 
 
@@ -225,9 +225,7 @@
         out_shape=[flat, flat, flat],
         scratch_shapes=[pltpu.VMEM((seq, HD), F32), pltpu.VMEM((seq, HD), F32)],
         compiler_params=pltpu.CompilerParams(vmem_limit_bytes=VMEM_LIMIT),
-        cost_estimate=pl.CostEstimate(
-            flops=20 * seq * seq * width, bytes_accessed=seq * width * 16, transcendentals=0
-        ),
+        cost_estimate=lasts(25),
     )(q, k, kt, v, o, do, lse, cos, sin)
 
 
@@ -263,9 +261,7 @@
             jax.ShapeDtypeStruct((rows, hidden), BF),
         ],
         compiler_params=pltpu.CompilerParams(vmem_limit_bytes=VMEM_LIMIT),
-        cost_estimate=pl.CostEstimate(
-            flops=10 * rows * model * hidden, bytes_accessed=rows * model * 12, transcendentals=0
-        ),
+        cost_estimate=lasts(0.018 * rows),
     )(x, c, w)
 
 
@@ -378,33 +374,109 @@
     return [dma(hops), dma(hops), dma(ways), dma(ways), dma]
 
 
-def gather_kernel(lanes, cores, x_ref, full_ref, *sems):
-    chain = Chain(x_ref, full_ref, lanes, cores, sems)
-    greet(sequence_peers(chain.dp, chain.fs, lanes * cores))
-    chain.begin()
-    for step in range(1, lanes):
-        chain.advance(step)
-    chain.finish()
-
-
-def gather_sequence(x, lanes, cores):
-    return pl.pallas_call(
-        functools.partial(gather_kernel, lanes, cores),
-        in_specs=[ANY],
-        out_specs=ANY,
-        out_shape=jax.ShapeDtypeStruct((lanes, cores) + x.shape, x.dtype),
-        scratch_shapes=chain_sems(lanes, cores),
-        compiler_params=pltpu.CompilerParams(collective_id=1, has_side_effects=True),
-    )(x)
+class Line:
+    def __init__(self, own, buffer, lanes, cores, out, came):
+        self.own, self.buffer, self.lanes, self.cores = own, buffer, lanes, cores
+        self.out, self.into = out, came
+        self.dp, self.fs, self.z, self.c = place(cores)
+
+    def has_next(self, side):
+        return self.z < self.lanes - 1 if side == 0 else self.z > 0
+
+    def near(self, side):
+        return (self.dp, self.fs + (self.cores if side == 0 else -self.cores))
+
+    def hop(self, side, step, block):
+        source = self.own if step == 0 else self.buffer.at[block]
+        return send(
+            source, self.buffer.at[block], self.out.at[side, step], self.into.at[side, step], self.near(side)
+        )
+
+    def begin(self):
+        for side in (0, 1):
+
+            @pl.when(self.has_next(side))
+            def _():
+                self.hop(side, 0, self.z).start()
+
+    def came(self, side, step):
+        block = self.z - step if side == 0 else self.z + step
+        return block, (block >= 0) & (block < self.lanes)
+
+    def advance(self, step, then):
+        for side in (0, 1):
+            block, there = self.came(side, step)
+
+            @pl.when(there)
+            def _():
+                self.hop(side, step - 1, block).wait_recv()
+
+            @pl.when(there & self.has_next(side))
+            def _():
+                self.hop(side, step, block).start()
+
+            @pl.when(there)
+            def _():
+                then(block, self.buffer.at[block])
+
+    def finish(self):
+        for step in range(self.lanes - 1):
+            for side in (0, 1):
+                block, there = self.came(side, step)
+
+                @pl.when(there & self.has_next(side))
+                def _():
+                    self.hop(side, step, block).wait_send()
+
+
+class Spread:
+    def __init__(self, stage, target, dps, lanes, cores, out, came, local):
+        self.stage, self.target, self.dps, self.lanes = stage, target, dps, lanes
+        self.out, self.into, self.local = out, came, local
+        self.dp, self.fs, self.z, self.c = place(cores)
+
+    def over(self, m, block):
+        return send(
+            self.stage.at[m, block], self.target.at[m, block], self.out.at[m - 1, block],
+            self.into.at[m - 1, block], (lax.rem(self.dp + m, self.dps), self.fs),
+        )
+
+    def keep(self, block):
+        return pltpu.make_async_copy(
+            self.stage.at[0, block], self.target.at[0, block], self.local.at[block]
+        )
+
+    def go(self, m, block):
+        if m:
+            self.over(m, block).start()
+        else:
+            self.keep(block).start()
+
+    def order(self):
+        return list(range(1, self.dps)) + [0]
+
+    def finish(self):
+        for block in range(self.lanes):
+            self.keep(block).wait()
+            for m in range(1, self.dps):
+                self.over(m, block).wait_recv()
+        for block in range(self.lanes):
+            for m in range(1, self.dps):
+                self.over(m, block).wait_send()
 
 
 def start_kernel(
-    dps, lanes, cores, x_ref, wh_ref, tab_ref, wo_ref, full_ref, heads_ref, tabs_ref, out_ref,
-    h_out, h_in, hd_out, hd_in, t_out, t_in, o_out, o_in, od_out, od_in, oc_out, oc_in, locals_, *sems,
+    dps, lanes, cores, topk, x_ref, wh_ref, tab_ref, wo_ref, up_ref,
+    full_ref, heads_ref, tabs_ref, out_ref, pick_ref, weigh_ref, c_ref, line_buf, stage,
+    h_out, h_in, hd_out, hd_in, t_out, t_in, o_out, o_in, od_out, od_in, oc_out, oc_in, locals_,
+    l_out, l_in, s_out, s_in, s_local, *sems,
 ):
     chain = Chain(x_ref, full_ref, lanes, cores, sems)
     dp, fs, z, c = chain.dp, chain.fs, chain.z, chain.c
     fss = lanes * cores
+    line = Line(up_ref, line_buf, lanes, cores, l_out, l_in)
+    spread = Spread(stage, c_ref, dps, lanes, cores, s_out, s_in, s_local)
+    slots, tokens = pick_ref.shape[2:]
     greet(sequence_peers(dp, fs, fss) + [(lax.rem(dp + m, dps), fs) for m in range(1, dps)])
     chain.begin()
     kept = [
@@ -439,17 +511,51 @@
 
     def out_across(m, core):
         piece = out_ref.at[:, :, core]
-        return send(piece, piece, oc_out.at[m - 1], oc_in.at[m - 1], (dp, z * cores + lax.rem(c + m, cores)))
-
+        return send(
+            piece, piece, oc_out.at[m - 1], oc_in.at[m - 1], (dp, z * cores + lax.rem(c + m, cores))
+        )
+
+    for k in range(1, lanes):
+        table_to(k).start()
+    line.begin()
     for k in range(1, fss):
         heads_to(k).start()
     for k in range(1, lanes):
         out_to(k).start()
-        table_to(k).start()
+    for copy in kept:
+        copy.wait()
+    for k in range(1, lanes):
+        table_to(k).wait_recv()
+
+    triangle = (
+        lax.broadcasted_iota(jnp.int32, (tokens, tokens), 0)
+        <= lax.broadcasted_iota(jnp.int32, (tokens, tokens), 1)
+    ).astype(BF)
+    slot = lax.broadcasted_iota(jnp.int32, (slots, tokens), 0).astype(F32)
+    for m in range(dps):
+        name = (lax.rem(dp + m, dps) * lanes + z).astype(F32)
+        for block in range(lanes):
+            hit = tabs_ref[block, :topk, :] == name
+            member = jnp.max(jnp.where(hit, 1.0, 0.0), axis=0, keepdims=True)
+            gate = jnp.sum(jnp.where(hit, tabs_ref[block, topk : 2 * topk, :], 0.0), axis=0, keepdims=True)
+            rank = dot_nn(jnp.broadcast_to(member, (8, tokens)).astype(BF), triangle)[:1] - 1.0
+            match = (rank == slot) & (member > 0.5)
+            pick_ref[m, block] = jnp.where(match, 1.0, 0.0).astype(BF)
+            weigh_ref[m, block] = jnp.where(match, gate, 0.0).astype(BF)
+
+    def pick(block, source):
+        for m in spread.order():
+            name = (lax.rem(dp + m, dps) * lanes + z).astype(F32)
+            hit = tabs_ref[block, :topk, :] == name
+            gate = jnp.sum(jnp.where(hit, tabs_ref[block, topk : 2 * topk, :], 0.0), axis=0, keepdims=True)
+            one = pick_ref[m, block]
+            scale = jnp.sum(one.astype(F32) * gate, axis=1, keepdims=True)
+            stage[m, block] = (dot_nn(one, source[...]) * scale).astype(BF)
+            spread.go(m, block)
+
     if lanes > 1:
         chain.advance(1)
-    for copy in kept:
-        copy.wait()
+    pick(z, up_ref)
     for k in range(1, fss):
         heads_to(k).wait_recv()
     for m in range(1, dps):
@@ -458,10 +564,11 @@
         out_to(k).wait_recv()
     for m in range(1, dps):
         out_over(m, dp).start()
+    if lanes > 1:
+        line.advance(1, pick)
     for step in range(2, lanes):
         chain.advance(step)
-    for k in range(1, lanes):
-        table_to(k).wait_recv()
+        line.advance(step, pick)
     for m in range(1, dps):
         out_over(m, lax.rem(dp + dps - m, dps)).wait_recv()
     for m in range(1, cores):
@@ -469,6 +576,8 @@
     for m in range(1, dps):
         heads_over(m, lax.rem(dp + dps - m, dps)).wait_recv()
     chain.finish()
+    line.finish()
+    spread.finish()
     for m in range(1, cores):
         out_across(m, lax.rem(c + cores - m, cores)).wait_recv()
     for k in range(1, fss):
@@ -483,25 +592,42 @@
         out_across(m, c).wait_send()
 
 
-def start(x, wh, table, w_out, dps, lanes, cores):
+def start(x, wh, table, w_out, upstream, topk, dps, lanes, cores):
     fss = lanes * cores
+    tokens, model = x.shape
+    slots = tokens // 2
     dma = pltpu.SemaphoreType.DMA
     pair = lambda n: [dma((max(n - 1, 1),)), dma((max(n - 1, 1),))]
+    hops = (2, max(lanes - 1, 1))
+    ways = (dps - 1, lanes)
+    whole = pl.BlockSpec(memory_space=pltpu.VMEM)
+    picks = jax.ShapeDtypeStruct((dps, lanes, slots, tokens), BF)
     shapes = [
         jax.ShapeDtypeStruct((lanes, cores) + x.shape, x.dtype),
         jax.ShapeDtypeStruct((dps,) + wh.shape, wh.dtype),
         jax.ShapeDtypeStruct((lanes,) + table.shape, table.dtype),
         jax.ShapeDtypeStruct((dps, lanes, cores) + w_out.shape, w_out.dtype),
+        picks,
+        picks,
+        jax.ShapeDtypeStruct((dps, lanes, slots, model), BF),
     ]
     return pl.pallas_call(
-        functools.partial(start_kernel, dps, lanes, cores),
-        in_specs=[ANY] * 4,
-        out_specs=[ANY] * 4,
+        functools.partial(start_kernel, dps, lanes, cores, topk),
+        in_specs=[ANY] * 4 + [whole],
+        out_specs=[ANY, ANY, whole, ANY, whole, whole, ANY],
         out_shape=shapes,
-        scratch_shapes=pair(fss) + pair(dps) + pair(lanes) + pair(lanes) + pair(dps) + pair(cores)
-        + [dma((3,))] + chain_sems(lanes, cores),
-        compiler_params=pltpu.CompilerParams(collective_id=0, has_side_effects=True),
-    )(x, wh, table, w_out)
+        scratch_shapes=[
+            pltpu.VMEM((lanes, tokens, model), BF),
+            pltpu.VMEM((dps, lanes, slots, model), BF),
+        ]
+        + pair(fss) + pair(dps) + pair(lanes) + pair(lanes) + pair(dps) + pair(cores) + [dma((3,))]
+        + [dma(hops), dma(hops), dma(ways), dma(ways), dma((lanes,))]
+        + chain_sems(lanes, cores),
+        cost_estimate=lasts(130),
+        compiler_params=pltpu.CompilerParams(
+            collective_id=0, has_side_effects=True, vmem_limit_bytes=VMEM_LIMIT
+        ),
+    )(x, wh, table, w_out, upstream)
 
 
 def heads_kernel(lanes, cores, busy, o_ref, mix_ref, out, came, local):
@@ -551,97 +677,64 @@
         out_specs=ANY,
         out_shape=jax.ShapeDtypeStruct((tokens, busy * o.shape[1]), o.dtype),
         scratch_shapes=[dma((fss - 1,)), dma((fss - 1,)), dma],
+        cost_estimate=lasts(25),
         compiler_params=pltpu.CompilerParams(collective_id=2, has_side_effects=True),
     )(o)
 
 
-def dispatch_kernel(
-    dps, lanes, cores, x_ref, pick_ref, out_ref, line, stage,
-    z_out, z_in, d_out_, d_in, local,
-):
-    dp, fs, z, c = place(cores)
-    peers = [(lax.rem(dp + m, dps), fs) for m in range(1, dps)]
+def greet_cross(line, dps, cores=1):
     barrier = pltpu.get_barrier_semaphore()
-    for peer in peers:
+    for m in range(1, dps):
+        peer = (lax.rem(line.dp + m, dps), line.fs)
         pl.semaphore_signal(barrier, inc=1, device_id=peer, device_id_type=MESH)
     for side in (0, 1):
-        near = fs + (cores if side == 0 else -cores)
-
-        @pl.when(z < lanes - 1 if side == 0 else z > 0)
+
+        @pl.when(line.has_next(side))
         def _():
-            pl.semaphore_signal(barrier, inc=1, device_id=(dp, near), device_id_type=MESH)
-
-    ends = (z > 0).astype(jnp.int32) + (z < lanes - 1).astype(jnp.int32)
-    pl.semaphore_wait(barrier, len(peers) + ends)
-
-    def hop(side, step, block):
-        near = fs + (cores if side == 0 else -cores)
-        source = x_ref if step == 0 else line.at[block]
-        return send(source, line.at[block], z_out.at[side, step], z_in.at[side, step], (dp, near))
-
-    def over(m, block):
-        return send(
-            stage.at[m, block], out_ref.at[m, block], d_out_.at[m - 1, block], d_in.at[m - 1, block],
-            (lax.rem(dp + m, dps), fs),
-        )
-
-    def keep(block):
-        return pltpu.make_async_copy(stage.at[0, block], out_ref.at[0, block], local.at[block])
-
-    def has_next(side):
-        return z < lanes - 1 if side == 0 else z > 0
+            pl.semaphore_signal(barrier, inc=1, device_id=line.near(side), device_id_type=MESH)
+
+    for m in range(1, cores):
+        peer = (line.dp, line.z * cores + lax.rem(line.c + m, cores))
+        pl.semaphore_signal(barrier, inc=1, device_id=peer, device_id_type=MESH)
+    ends = line.has_next(0).astype(jnp.int32) + line.has_next(1).astype(jnp.int32)
+    pl.semaphore_wait(barrier, dps - 1 + cores - 1 + ends)
+
+
+def dispatch_kernel(
+    dps, lanes, cores, x_ref, pick_ref, rows_ref, out_ref, w_ref, buffer, stage,
+    l_out, l_in, s_out, s_in, s_local, w_out, w_in, w_local,
+):
+    line = Line(x_ref, buffer, lanes, cores, l_out, l_in)
+    spread = Spread(stage, out_ref, dps, lanes, cores, s_out, s_in, s_local)
+    greet_cross(line, dps, cores)
+
+    def across(m, core):
+        peer = (line.dp, line.z * cores + lax.rem(line.c + m, cores))
+        return send(rows_ref, w_ref.at[:, :, core], w_out.at[m - 1], w_in.at[m - 1], peer)
+
+    keep = pltpu.make_async_copy(rows_ref, w_ref.at[:, :, line.c], w_local)
 
     def pick(block, source):
-        for m in list(range(1, dps)) + [0]:
+        for m in spread.order():
             stage[m, block] = dot_nn(pick_ref[m, block], source[...]).astype(BF)
-            if m:
-                over(m, block).start()
-            else:
-                keep(block).start()
-
-    for side in (0, 1):
-
-        @pl.when(has_next(side))
-        def _():
-            hop(side, 0, z).start()
-
-    pick(z, x_ref)
+            spread.go(m, block)
+
+    line.begin()
+    keep.start()
+    for m in range(1, cores):
+        across(m, line.c).start()
+    pick(line.z, x_ref)
     for step in range(1, lanes):
-        for side in (0, 1):
-            block = z - step if side == 0 else z + step
-            there = (block >= 0) & (block < lanes)
-
-            @pl.when(there)
-            def _():
-                hop(side, step - 1, block).wait_recv()
-
-            @pl.when(there & has_next(side))
-            def _():
-                hop(side, step, block).start()
-
-            @pl.when(there)
-            def _():
-                pick(block, line.at[block])
-
-    for block in range(lanes):
-        keep(block).wait()
-        for m in range(1, dps):
-            over(m, block).wait_recv()
-    for step in range(lanes - 1):
-        for side in (0, 1):
-            block = z - step if side == 0 else z + step
-            there = (block >= 0) & (block < lanes)
-
-            @pl.when(there & has_next(side))
-            def _():
-                hop(side, step, block).wait_send()
-
-    for block in range(lanes):
-        for m in range(1, dps):
-            over(m, block).wait_send()
-
-
-def dispatch(x, picks, lanes, cores, number):
+        line.advance(step, pick)
+    spread.finish()
+    line.finish()
+    keep.wait()
+    for m in range(1, cores):
+        across(m, lax.rem(line.c + cores - m, cores)).wait_recv()
+        across(m, line.c).wait_send()
+
+
+def dispatch(x, picks, rows, lanes, cores, number):
     dps, _, slots, tokens = picks.shape
     model = x.shape[1]
     dma = pltpu.SemaphoreType.DMA
@@ -650,156 +743,258 @@
     whole = pl.BlockSpec(memory_space=pltpu.VMEM)
     return pl.pallas_call(
         functools.partial(dispatch_kernel, dps, lanes, cores),
-        in_specs=[whole, whole],
-        out_specs=ANY,
-        out_shape=jax.ShapeDtypeStruct((dps, lanes, slots, model), BF),
+        in_specs=[whole, whole, ANY],
+        out_specs=[ANY, ANY],
+        out_shape=[
+            jax.ShapeDtypeStruct((dps, lanes, slots, model), BF),
+            jax.ShapeDtypeStruct((dps, lanes, cores) + rows.shape[2:], BF),
+        ],
         scratch_shapes=[
             pltpu.VMEM((lanes, tokens, model), BF),
             pltpu.VMEM((dps, lanes, slots, model), BF),
             dma(hops), dma(hops), dma(ways), dma(ways), dma((lanes,)),
+            dma((max(cores - 1, 1),)), dma((max(cores - 1, 1),)), dma,
         ],
+        cost_estimate=lasts(70),
         compiler_params=pltpu.CompilerParams(
             collective_id=number, has_side_effects=True, vmem_limit_bytes=VMEM_LIMIT
         ),
-    )(x, picks)
-
-
-def combine_kernel(
-    dps, lanes, cores, part_ref, mat_ref, out_ref, back, stage, inbox,
-    z_out, z_in, d_out_, d_in, local,
-):
-    dp, fs, z, c = place(cores)
-    slots = part_ref.shape[2]
-    peers = [(lax.rem(dp + m, dps), fs) for m in range(1, dps)]
-    barrier = pltpu.get_barrier_semaphore()
-    for peer in peers:
-        pl.semaphore_signal(barrier, inc=1, device_id=peer, device_id_type=MESH)
-
-    def has_next(side):
-        return z < lanes - 1 if side == 0 else z > 0
-
-    def near(side):
-        return (dp, fs + (cores if side == 0 else -cores))
-
-    for side in (0, 1):
-
-        @pl.when(has_next(side))
-        def _():
-            pl.semaphore_signal(barrier, inc=1, device_id=near(side), device_id_type=MESH)
-
-    ends = (z > 0).astype(jnp.int32) + (z < lanes - 1).astype(jnp.int32)
-    pl.semaphore_wait(barrier, len(peers) + ends)
-
-    def over(m, block):
+    )(x, picks, rows)
+
+
+class Combine:
+    def __init__(self, parts, picks, result, scratch, dps, lanes, cores):
+        self.parts, self.picks, self.result = parts, picks, result
+        self.back, self.stage, self.inbox = scratch[:3]
+        self.z_out, self.z_in, self.d_out, self.d_in, self.local = scratch[3:]
+        self.dps, self.lanes, self.cores = dps, lanes, cores
+        self.dp, self.fs, self.z, self.c = place(cores)
+
+    def over(self, m, block):
         return send(
-            part_ref.at[m, block], back.at[block, m], d_out_.at[m - 1, block], d_in.at[m - 1, block],
-            (lax.rem(dp + dps - m, dps), fs),
-        )
-
-    def keep(block):
-        return pltpu.make_async_copy(part_ref.at[0, block], back.at[block, 0], local.at[block])
-
-    def hop(side, step):
+            self.parts.at[m, block], self.back.at[block, m], self.d_out.at[m - 1, block],
+            self.d_in.at[m - 1, block], (lax.rem(self.dp + self.dps - m, self.dps), self.fs),
+        )
+
+    def keep(self, block):
+        return pltpu.make_async_copy(
+            self.parts.at[0, block], self.back.at[block, 0], self.local.at[block]
+        )
+
+    def hop(self, side, step):
         return send(
-            stage.at[side, step - 1], inbox.at[side, step - 1], z_out.at[side, step - 1],
-            z_in.at[side, step - 1], near(side),
-        )
-
-    def goal(side, step):
-        block = z + lanes - step if side == 0 else z - lanes + step
-        return block, (block >= 0) & (block < lanes)
-
-    def begin(block):
-        for m in range(1, dps):
-            over(m, block).start()
-        keep(block).start()
-
-    def partial_sum(block):
-        keep(block).wait()
-        for m in range(1, dps):
-            over(m, block).wait_recv()
-        total = None
-        for m in range(dps):
-            term = dot_nn(mat_ref[block, :, m * slots : (m + 1) * slots], back[block, m])
-            total = term if total is None else total + term
+            self.stage.at[side, step - 1], self.inbox.at[side, step - 1], self.z_out.at[side, step - 1],
+            self.z_in.at[side, step - 1],
+            (self.dp, self.fs + (self.cores if side == 0 else -self.cores)),
+        )
+
+    def goal(self, side, step):
+        block = self.z + self.lanes - step if side == 0 else self.z - self.lanes + step
+        return block, (block >= 0) & (block < self.lanes)
+
+    def fed(self, side):
+        return self.z > 0 if side == 0 else self.z < self.lanes - 1
+
+    def send_block(self, block):
+        for m in range(1, self.dps):
+            self.over(m, block).start()
+        self.keep(block).start()
+
+    def begin(self):
+        for step in range(1, self.lanes):
+            for side in (0, 1):
+                block, there = self.goal(side, step)
+
+                @pl.when(there)
+                def _():
+                    self.send_block(block)
+
+        self.send_block(self.z)
+
+    def partial_sum(self, block):
+        self.keep(block).wait()
+        total = dot_tn(self.picks[0, block], self.back[block, 0])
+        for m in range(1, self.dps):
+            self.over(m, block).wait_recv()
+            total = total + dot_tn(self.picks[m, block], self.back[block, m])
         return total
 
-    for step in range(1, lanes):
+    def advance(self, step):
         for side in (0, 1):
-            block, there = goal(side, step)
+            block, there = self.goal(side, step)
 
             @pl.when(there)
             def _():
-                begin(block)
-
-    begin(z)
-    for step in range(1, lanes):
+                total = self.partial_sum(block)
+                self.stage[side, step - 1] = total.astype(BF)
+                if step > 1:
+
+                    @pl.when(self.fed(side))
+                    def _():
+                        self.hop(side, step - 1).wait_recv()
+                        more = self.inbox[side, step - 2].astype(F32)
+                        self.stage[side, step - 1] = (total + more).astype(BF)
+
+                self.hop(side, step).start()
+
+    def finish(self):
+        self.result[...] = self.partial_sum(self.z)
         for side in (0, 1):
-            block, there = goal(side, step)
-            fed = z > 0 if side == 0 else z < lanes - 1
-
-            @pl.when(there)
+
+            @pl.when(self.fed(side))
             def _():
-                total = partial_sum(block)
-                stage[side, step - 1] = total.astype(BF)
-                if step > 1:
-
-                    @pl.when(fed)
-                    def _():
-                        hop(side, step - 1).wait_recv()
-                        stage[side, step - 1] = (total + inbox[side, step - 2].astype(F32)).astype(BF)
-
-                hop(side, step).start()
-
-    out_ref[...] = partial_sum(z)
-    for side in (0, 1):
-        fed = z > 0 if side == 0 else z < lanes - 1
-
-        @pl.when(fed)
-        def _():
-            hop(side, lanes - 1).wait_recv()
-            out_ref[...] += inbox[side, lanes - 2].astype(F32)
-
-    for step in range(1, lanes):
-        for side in (0, 1):
-            block, there = goal(side, step)
-
-            @pl.when(there)
-            def _():
-                hop(side, step).wait_send()
-
-    for block in range(lanes):
-        for m in range(1, dps):
-            over(m, block).wait_send()
-
-
-def combine(parts, matrix, lanes, cores, number):
-    dps, _, slots, model = parts.shape
-    tokens = matrix.shape[1]
+                self.hop(side, self.lanes - 1).wait_recv()
+                self.result[...] += self.inbox[side, self.lanes - 2].astype(F32)
+
+        for step in range(1, self.lanes):
+            for side in (0, 1):
+                block, there = self.goal(side, step)
+
+                @pl.when(there)
+                def _():
+                    self.hop(side, step).wait_send()
+
+        for block in range(self.lanes):
+            for m in range(1, self.dps):
+                self.over(m, block).wait_send()
+
+
+def combine_scratch(dps, lanes, slots, tokens, model):
     dma = pltpu.SemaphoreType.DMA
     hops = (2, max(lanes - 1, 1))
     ways = (dps - 1, lanes)
+    return [
+        pltpu.VMEM((lanes, dps, slots, model), BF),
+        pltpu.VMEM(hops + (tokens, model), BF),
+        pltpu.VMEM(hops + (tokens, model), BF),
+        dma(hops), dma(hops), dma(ways), dma(ways), dma((lanes,)),
+    ]
+
+
+def combine_kernel(dps, lanes, cores, part_ref, pick_ref, out_ref, *scratch):
+    work = Combine(part_ref, pick_ref, out_ref, scratch, dps, lanes, cores)
+    greet_cross(Line(None, None, lanes, cores, None, None), dps)
+    work.begin()
+    for step in range(1, lanes):
+        work.advance(step)
+    work.finish()
+
+
+def combine(parts, picks, lanes, cores, number):
+    dps, _, slots, model = parts.shape
+    tokens = picks.shape[3]
     whole = pl.BlockSpec(memory_space=pltpu.VMEM)
     return pl.pallas_call(
         functools.partial(combine_kernel, dps, lanes, cores),
         in_specs=[ANY, whole],
         out_specs=whole,
         out_shape=jax.ShapeDtypeStruct((tokens, model), F32),
-        scratch_shapes=[
-            pltpu.VMEM((lanes, dps, slots, model), BF),
-            pltpu.VMEM(hops + (tokens, model), BF),
-            pltpu.VMEM(hops + (tokens, model), BF),
-            dma(hops), dma(hops), dma(ways), dma(ways), dma((lanes,)),
-        ],
+        scratch_shapes=combine_scratch(dps, lanes, slots, tokens, model),
+        cost_estimate=lasts(70),
         compiler_params=pltpu.CompilerParams(
             collective_id=number, has_side_effects=True, vmem_limit_bytes=VMEM_LIMIT
         ),
-    )(parts, matrix)
+    )(parts, picks)
+
+
+def turn_kernel(
+    dps, lanes, cores, x_ref, part_ref, pick_ref, g_ref, full_ref, out_ref, total_ref,
+    own, from_core, from_dp, gc_out, gc_in, gd_out, gd_in, g_local, *scratch,
+):
+    work = Combine(part_ref, pick_ref, out_ref, scratch[:8], dps, lanes, cores)
+    chain = Chain(x_ref, full_ref, lanes, cores, scratch[8:])
+    dp, fs, z, c = chain.dp, chain.fs, chain.z, chain.c
+    fss = lanes * cores
+
+    def across(m):
+        t = lax.rem(c + m, cores)
+        return send(
+            g_ref.at[:, :, t], from_core.at[m - 1], gc_out.at[m - 1], gc_in.at[m - 1], (dp, z * cores + t)
+        )
+
+    def over(m):
+        t = lax.rem(dp + m, dps)
+        return send(own.at[t], from_dp.at[m - 1], gd_out.at[m - 1], gd_in.at[m - 1], (t, fs))
+
+    keep = pltpu.make_async_copy(g_ref.at[:, :, c], own, g_local)
+
+    def cores_added():
+        keep.wait()
+        for m in range(1, cores):
+            across(m).wait_recv()
+
+        def add(i, carry):
+            p, q = i // lanes, lax.rem(i, lanes)
+            total = own[p, q].astype(F32)
+            for m in range(1, cores):
+                total = total + from_core[m - 1, p, q].astype(F32)
+            own[p, q] = total.astype(BF)
+            return carry
+
+        lax.fori_loop(0, dps * lanes, add, 0)
+        for m in range(1, dps):
+            over(m).start()
+
+    def dp_added():
+        for m in range(1, dps):
+            over(m).wait_recv()
+        for q in range(lanes):
+            total = own[dp, q].astype(F32)
+            for m in range(1, dps):
+                total = total + from_dp[m - 1, q].astype(F32)
+            total_ref[q] = total.astype(BF)
+        for m in range(1, cores):
+            across(m).wait_send()
+        for m in range(1, dps):
+            over(m).wait_send()
+
+    greet(sequence_peers(dp, fs, fss) + [(lax.rem(dp + m, dps), fs) for m in range(1, dps)])
+    chain.begin()
+    work.begin()
+    keep.start()
+    for m in range(1, cores):
+        across(m).start()
+    cores_added()
+    for step in range(1, lanes):
+        chain.advance(step)
+        work.advance(step)
+    chain.finish()
+    work.finish()
+    dp_added()
+
+
+def turn(x, parts, picks, g, lanes, cores):
+    dps, _, slots, model = parts.shape
+    tokens = picks.shape[3]
+    dma = pltpu.SemaphoreType.DMA
+    whole = pl.BlockSpec(memory_space=pltpu.VMEM)
+    return pl.pallas_call(
+        functools.partial(turn_kernel, dps, lanes, cores),
+        in_specs=[ANY, ANY, whole, ANY],
+        out_specs=[ANY, whole, whole],
+        out_shape=[
+            jax.ShapeDtypeStruct((lanes, cores) + x.shape, x.dtype),
+            jax.ShapeDtypeStruct((tokens, model), F32),
+            jax.ShapeDtypeStruct((lanes,) + g.shape[3:], BF),
+        ],
+        scratch_shapes=[
+            pltpu.VMEM((dps, lanes) + g.shape[3:], BF),
+            pltpu.VMEM((max(cores - 1, 1), dps, lanes) + g.shape[3:], BF),
+            pltpu.VMEM((dps - 1, lanes) + g.shape[3:], BF),
+            dma((max(cores - 1, 1),)), dma((max(cores - 1, 1),)), dma((dps - 1,)), dma((dps - 1,)), dma,
+        ]
+        + combine_scratch(dps, lanes, slots, tokens, model) + chain_sems(lanes, cores),
+        cost_estimate=lasts(100),
+        compiler_params=pltpu.CompilerParams(
+            collective_id=1, has_side_effects=True, vmem_limit_bytes=VMEM_LIMIT
+        ),
+    )(x, parts, picks, g)
 
 
 def finish_kernel(
-    dps, lanes, cores, busy, part_ref, g_ref, out_ref, mix_ref, from_core, stage, inbox, from_dp, total_g,
-    z_out, z_in, c_out, c_in, g_out, g_in, m_out, m_in, local,
+    dps, lanes, cores, busy, part_ref, g_ref, s_ref, out_ref, mix_ref, sum_ref,
+    from_core, stage, inbox, from_dp, total_g, from_z,
+    z_out, z_in, c_out, c_in, g_out, g_in, m_out, m_in, local, s_out, s_in,
 ):
     dp, fs, z, c = place(cores)
     fss = lanes * cores
@@ -828,6 +1023,12 @@
     def home(k, owner):
         t = lax.rem(fs + k, fss)
         return send(total_g.at[t], mix_ref.at[owner], m_out.at[k - 1], m_in.at[k - 1], (dp, t))
+
+    def along(k):
+        t = lax.rem(z + k, lanes)
+        return send(
+            s_ref.at[t], from_z.at[k - 1], s_out.at[k - 1], s_in.at[k - 1], (dp, t * cores + c)
+        )
 
     def goal(side, step):
         block = z + lanes - step if side == 0 else z - lanes + step
@@ -875,6 +1076,8 @@
         over(m).start()
     for step in range(1, max(lanes - 1, 1)):
         advance(step)
+    for k in range(1, lanes):
+        along(k).start()
     for m in range(1, dps):
         over(m).wait_recv()
     for f in range(fss):
@@ -901,6 +1104,13 @@
             hop(side, lanes - 1).wait_recv()
             out_ref[...] += inbox[side, lanes - 2].astype(F32)
 
+    total = s_ref[z].astype(F32)
+    for k in range(1, lanes):
+        along(k).wait_recv()
+        total = total + from_z[k - 1].astype(F32)
+    sum_ref[...] = total
+    for k in range(1, lanes):
+        along(k).wait_send()
     for k in range(1, fss):
         owner = lax.rem(fs + fss - k, fss)
 
@@ -929,7 +1139,7 @@
         over(m).wait_send()
 
 
-def finish(part, g, lanes, cores, busy):
+def finish(part, g, g_line, lanes, cores, busy):
     dps, fss = g.shape[:2]
     tokens, model = part.shape[2:]
     dma = pltpu.SemaphoreType.DMA
@@ -938,11 +1148,12 @@
     whole = pl.BlockSpec(memory_space=pltpu.VMEM)
     return pl.pallas_call(
         functools.partial(finish_kernel, dps, lanes, cores, busy),
-        in_specs=[whole, whole],
-        out_specs=[whole, ANY],
+        in_specs=[whole, whole, whole],
+        out_specs=[whole, ANY, whole],
         out_shape=[
             jax.ShapeDtypeStruct((tokens, model), F32),
             jax.ShapeDtypeStruct((busy,) + g.shape[2:], BF),
+            jax.ShapeDtypeStruct(g_line.shape[1:], F32),
         ],
         scratch_shapes=[
             pltpu.VMEM(ways + (tokens, model), BF),
@@ -950,13 +1161,15 @@
             pltpu.VMEM(hops + (tokens, model), BF),
             pltpu.VMEM((dps - 1,) + g.shape[1:], BF),
             pltpu.VMEM(g.shape[1:], BF),
+            pltpu.VMEM((max(lanes - 1, 1),) + g_line.shape[1:], BF),
             dma(hops), dma(hops), dma(ways), dma(ways), dma((dps - 1,)), dma((dps - 1,)),
-            dma((fss - 1,)), dma((fss - 1,)), dma,
+            dma((fss - 1,)), dma((fss - 1,)), dma, dma((max(lanes - 1, 1),)), dma((max(lanes - 1, 1),)),
         ],
+        cost_estimate=lasts(66),
         compiler_params=pltpu.CompilerParams(
             collective_id=6, has_side_effects=True, vmem_limit_bytes=VMEM_LIMIT
         ),
-    )(part, g)
+    )(part, g, g_line)
 
 
 def per_device(x, w_qkv, w_out, w_shared, w_experts, gains, routes, gates, d_out):
@@ -979,9 +1192,6 @@
             value, "fsdp", [(a * cores + k, b * cores + k) for a, b in pairs for k in range(cores)]
         )
 
-    def turn_z(value, by):
-        return over_z(value, [(a, (a + by) % lanes) for a in range(lanes)])
-
     def over_core(value, m):
         return lax.ppermute(
             value, "fsdp", [(a * cores + k, a * cores + (k ^ m)) for a in range(lanes) for k in range(cores)]
@@ -989,42 +1199,6 @@
 
     def over_dp(value, m):
         return lax.ppermute(value, "dp", [(a, (a + m) % dps) for a in range(dps)])
-
-    def up(value, least, most):
-        return over_z(value, [(a, a + 1) for a in range(least, most)])
-
-    def down(value, least, most):
-        return over_z(value, [(a, a - 1) for a in range(least, most)])
-
-    def gather_z(value):
-        buffer = put(jnp.zeros((lanes + 1,) + value.shape, value.dtype), value, z)
-        rising = falling = value
-        for s in range(1, lanes):
-            rising = up(rising, s - 1, lanes - 1)
-            falling = down(falling, 1, lanes - s + 1)
-            buffer = put(buffer, rising, jnp.where(z >= s, z - s, lanes))
-            buffer = put(buffer, falling, jnp.where(z + s < lanes, z + s, lanes))
-        return buffer
-
-    def gather_dp(value):
-        buffer = put(jnp.zeros((dps,) + value.shape, value.dtype), value, dp)
-        for m in range(1, dps):
-            buffer = put(buffer, over_dp(value, m), (dp - m) % dps)
-        return buffer
-
-    def join_cores(value):
-        buffer = jnp.zeros(value.shape[:2] + (cores,) + value.shape[2:], value.dtype)
-
-        def place(buffer, block, k):
-            return lax.dynamic_update_slice(buffer, block[:, :, None], (0, 0, k, 0, 0))
-
-        buffer = place(buffer, value, c)
-        for m in range(1, cores):
-            buffer = place(buffer, over_core(value, m), c ^ m)
-        return buffer.reshape(-1, value.shape[-1])
-
-    def gather_rows(value):
-        return join_cores(gather_dp(gather_z(value)[:lanes]))
 
     cut = w_qkv.reshape(shard, 3, HEADS, HD)
     cut = jnp.pad(cut, ((0, 0), (0, 0), (0, fss * per - HEADS), (0, 0)))
@@ -1034,7 +1208,10 @@
     topk = routes.shape[1]
     table = jnp.concatenate([routes.T.astype(F32), gates.T], axis=0)
     table = jnp.pad(table, ((0, -2 * topk % 8), (0, 0)))
-    x_all, slabs, tables, out_all = start(x, slabs, table, w_out, dps, lanes, cores)
+    x_all, slabs, tables, out_all, picks, weigh, c_slots = start(
+        x, slabs, table, w_out, d_out, topk, dps, lanes, cores
+    )
+    c_slots = c_slots.reshape(-1, model)
     x_all = x_all.reshape(seq, model)
     slabs = slabs.reshape(model, 3 * width + HD)
     out_all = out_all.reshape(model, model)
@@ -1049,34 +1226,8 @@
     cos = jnp.concatenate([cosine, cosine], axis=1)
     sin = jnp.concatenate([-sine, sine], axis=1)
 
-    picks, weights = tables[:, :topk], tables[:, topk : 2 * topk]
-    triangle = (jnp.arange(tokens)[:, None] <= jnp.arange(tokens)[None, :]).astype(BF)
-    slot_ids = jnp.arange(slots, dtype=F32)
-    select, slot_gate, gather_back, weigh_back = [], [], [], []
-    for m in range(dps):
-        hit = picks == ((dp + m) % dps * lanes + z).astype(F32)
-        member = jnp.any(hit, axis=1)
-        gate = jnp.sum(jnp.where(hit, weights, 0.0), axis=1)
-        rank = dot_nn(member.astype(BF), triangle) - 1.0
-        match = member[:, None, :] & (rank[:, None, :] == slot_ids[None, :, None])
-        select.append(match.astype(BF))
-        scaled = jnp.where(match, gate[:, None, :], 0.0)
-        slot_gate.append(jnp.sum(scaled, axis=2, keepdims=True))
-        turned = member[:, :, None] & (rank[:, :, None] == slot_ids[None, None, :])
-        gather_back.append(turned.astype(BF))
-        weigh_back.append(jnp.where(turned, gate[:, :, None], 0.0).astype(BF))
-    select = jnp.stack(select)
-    gather_back = jnp.concatenate(gather_back, axis=2)
-    weigh_back = jnp.concatenate(weigh_back, axis=2)
-
-    def pick(blocks, m):
-        return lax.dot_general(
-            select[m], blocks, (((2,), (1,)), ((0,), (0,))), preferred_element_type=F32
-        )
-
     xn_one, q, k, v, kt, vt = project(x_all, gain_one, w_heads, cos, sin, seq)
 
-    d_out_z = after(d_out, x_all)
     groups = [[e * cores + k for e in range(experts)] for k in range(cores)]
 
     def swap(value):
@@ -1084,8 +1235,7 @@
             value, ("dp", "fsdp"), split_axis=0, concat_axis=0, tiled=True, axis_index_groups=groups
         )
 
-    rows_here = swap(after(w_experts, x_all))
-    w_own = join_cores(rows_here.reshape(dps, lanes, shard, 3 * hidden))
+    rows_here = swap(after(w_experts, x_all)).reshape(dps, lanes, shard, 3 * hidden)
 
     o, lse = attend(q, k, vt, 256)
 
@@ -1095,26 +1245,28 @@
     unit_two = middle * inv_two
     xn_two = (unit_two * gain_two).astype(BF)
 
-    up_blocks = gather_z(after(d_out, x_all))[:lanes]
-    cs = []
-    for m in range(dps):
-        part = (pick(up_blocks, m) * slot_gate[m]).astype(BF)
-        cs.append(over_dp(part, m) if m else part)
-    c_slots = jnp.stack(cs).reshape(-1, model)
-    x_slots = dispatch(xn_two, select, lanes, cores, 3).reshape(-1, model)
+    def reduce_cores(part):
+        part = part.reshape(dps, lanes, cores, shard, part.shape[1])
+        at = lambda k: lax.dynamic_index_in_dim(part, k, 2, keepdims=False)
+        total = at(c)
+        for m in range(1, cores):
+            total = total + over_core(at(c ^ m).astype(BF), m).astype(F32)
+        return total
+
+    x_slots, w_own = dispatch(xn_two, picks, rows_here, lanes, cores, 3)
+    x_slots = x_slots.reshape(-1, model)
+    w_own = w_own.reshape(model, 3 * hidden)
     dx_slots, gu_slots, hid_slots = expert(x_slots, c_slots, w_own, BF)
 
-    shared_all = gather_rows(after(w_shared, heads))
+    shared_all = lax.all_gather(after(w_shared, heads), ("dp", "fsdp"), axis=0, tiled=True)
     dx_shared, gu_shared, hid_shared = expert(xn_two, d_out, shared_all, F32)
     f_shared = dot_nt(hid_shared, shared_all[:, 2 * hidden :])
 
     shape = (dps, lanes, slots, model)
-    dx_routed = combine(dx_slots.reshape(shape), gather_back, lanes, cores, 4)
+    g_own = jnp.concatenate([dot_tn(x_slots, gu_slots), dot_tn(c_slots, hid_slots)], axis=1)
+    own = reduce_cores(g_own).astype(BF)
+    dx_routed = combine(after(dx_slots, own).reshape(shape), picks, lanes, cores, 4)
     f_slots = dot_nt(hid_slots, w_own[:, 2 * hidden :]).astype(BF)
-    g_own = jnp.concatenate([dot_tn(x_slots, gu_slots), dot_tn(c_slots, hid_slots)], axis=1)
-    routed = combine(f_slots.reshape(shape), weigh_back, lanes, cores, 5)
-    layer_out = (middle + f_shared + routed).astype(BF)
-
     dxn_two = dx_shared + dx_routed
     scaled = dxn_two * gain_two
     dx_two = d_out.astype(F32) + inv_two * (
@@ -1122,7 +1274,11 @@
     )
     d_attn = dx_two.astype(BF)
 
-    da_all = gather_sequence(d_attn, lanes, cores).reshape(seq, model)
+    g_shared_part = jnp.concatenate([dot_tn(xn_two, gu_shared), dot_tn(d_out, hid_shared)], axis=1)
+    g_shared_part = g_shared_part.astype(BF).reshape(dps, lanes, cores, shard, 3 * hidden)
+    da_all, routed, g_line = turn(d_attn, f_slots.reshape(shape), weigh, g_shared_part, lanes, cores)
+    da_all = da_all.reshape(seq, model)
+    layer_out = (middle + f_shared + routed).astype(BF)
     out_cols = jnp.pad(out_all, ((0, 0), (0, fss * width - model)))
     out_cols = lax.dynamic_slice_in_dim(out_cols, fs * width, width, 1)
     d_o = dot_nn(da_all, out_cols).astype(BF)
@@ -1131,34 +1287,15 @@
     d_qkv = jnp.concatenate([dq, dk, dv], axis=1)
     dxn_part = dot_nt(d_qkv, w_heads).astype(BF).reshape(lanes, cores, tokens, model)
     g_part = jnp.concatenate([dot_tn(xn_one, d_qkv), g_out_part], axis=1).astype(BF)
-    dxn_one, g_mix = finish(dxn_part, g_part.reshape(dps, fss, shard, 4 * width), lanes, cores, busy)
+    g_part = g_part.reshape(dps, fss, shard, 4 * width)
+    dxn_one, g_mix, g_shared = finish(dxn_part, g_part, g_line, lanes, cores, busy)
     inputs = x.astype(F32)
     inv_one = lax.rsqrt(jnp.mean(inputs * inputs, axis=1, keepdims=True) + norm_eps)
     unit_one = inputs * inv_one
     scaled = dxn_one * gain_one
     d_x = dx_two + inv_one * (scaled - unit_one * jnp.mean(scaled * unit_one, axis=1, keepdims=True))
 
-    def reduce_cores(part):
-        part = part.reshape(dps, lanes, cores, shard, part.shape[1])
-        at = lambda k: lax.dynamic_index_in_dim(part, k, 2, keepdims=False)
-        total = at(c)
-        for m in range(1, cores):
-            total = total + over_core(at(c ^ m).astype(BF), m).astype(F32)
-        return total
-
-    own = reduce_cores(g_own).astype(BF)
     g_experts = swap(own.reshape(experts, shard, 3 * hidden)).astype(F32)
-
-    g_shared_part = jnp.concatenate([dot_tn(xn_two, gu_shared), dot_tn(d_out, hid_shared)], axis=1)
-    own = reduce_cores(g_shared_part)
-    total = take(own, dp)
-    low = own.astype(BF)
-    for m in range(1, dps):
-        total = total + over_dp(take(low, (dp + m) % dps), m).astype(F32)
-    low = total.astype(BF)
-    g_shared = take(total, z)
-    for s in range(1, lanes):
-        g_shared = g_shared + turn_z(take(low, (z + s) % lanes), s).astype(F32)
 
     g_mix = g_mix.reshape(busy, shard, 4, width).transpose(1, 2, 0, 3).reshape(shard, 4, busy * width)
     g_mix = g_mix[:, :, :model].astype(F32)

time: 1030 us -> 860 us (0.83)
  waiting for transfers between devices: 192 us -> 0.05 us
  Pallas kernels: 536 us -> 677 us
  starting transfers between devices: 78.4 us -> 22.2 us
  local copies, waits for them, and re-layouts: 77.8 us -> 35.2 us
  other arithmetic: 60.9 us -> 41.8 us
  matrix products: 75.2 us -> 60.1 us
  between operations: 1.87 us -> 14.9 us
    ppermute x24 -> x0, waiting for transfers between devices: 192 us -> none  [the longest x9 107 us: over_dp(): return lax.ppermute(value, 'dp', [(a, (a + m) % dps) for a in range(dps)])]
    pallas_call x2, Pallas kernels: 126 us -> 252 us  [the longest x1 133 us: start(): pl.pallas_call(functools.partial(start_kernel, dps, lanes, cores, topk),...]
    pallas_call x2 -> x1, Pallas kernels: 130 us -> 64.7 us  [combine(): pl.pallas_call(functools.partial(combine_kernel, dps, lanes, cores), in_s...]
    ppermute x24 -> x0, starting transfers between devices: 59.8 us -> none  [the longest x15 50.4 us: over_z(): lax.ppermute(value, 'fsdp', [(a * cores + k, b * cores + k) for a, b in p...]
    pallas_call x1, Pallas kernels: 66.2 us -> 115 us  [dispatch(): pl.pallas_call(functools.partial(dispatch_kernel, dps, lanes, cores), in_...]
    pallas_call x1, Pallas kernels: 14.8 us -> 50.8 us  [heads_home(): pl.pallas_call(functools.partial(heads_kernel, lanes, cores, busy), in_sp...]
    dynamic_update_slice x22 -> x0, local copies, waits for them, and re-layouts: 32.5 us -> none  [the longest x18 16.7 us: put(): lax.dynamic_update_slice(buffer, value.reshape((1,) * len(index) + buffer...]
    dot_general x4 -> x0, matrix products: 12.3 us -> none  [pick(): lax.dot_general(select[m], blocks, (((2,), (1,)), ((0,), (0,))), preferre...]
  transfers between devices with their start and end apart: 30 -> 4, of which waited for: 12 -> 0; matrix products, arithmetic and copies ran while one was open for 16% -> 14% of each run, Pallas kernels for 35% -> 64%
where the time goes in v3:
time: 860 us; the launch traced here: 851 us
  Pallas kernels  677 us (79%)
  matrix products  60.1 us (7%)
  other arithmetic  41.8 us (5%)
  local copies, waits for them, and re-layouts  35.2 us (4%)
  starting transfers between devices  22.2 us (3%)
  between operations  14.9 us (2%)
    pallas_call x1, Pallas kernels, start(): pl.pallas_call(functools.partial(start_kernel, dps, lanes, cores, topk),...  133 us
    pallas_call x1, Pallas kernels, turn(): pl.pallas_call(functools.partial(turn_kernel, dps, lanes, cores), in_spec...  119 us
    pallas_call x1, Pallas kernels, dispatch(): pl.pallas_call(functools.partial(dispatch_kernel, dps, lanes, cores), in_...  115 us
    pallas_call x1, Pallas kernels, finish(): pl.pallas_call(functools.partial(finish_kernel, dps, lanes, cores, busy),...  91 us
    pallas_call x1, Pallas kernels, combine(): pl.pallas_call(functools.partial(combine_kernel, dps, lanes, cores), in_s...  64.7 us
    pallas_call x1, Pallas kernels, heads_home(): pl.pallas_call(functools.partial(heads_kernel, lanes, cores, busy), in_sp...  50.8 us
    pallas_call x2, Pallas kernels, expert(): pl.pallas_call(functools.partial(expert_kernel, hidden), grid=(rows // bl...  45.1 us
    dot_general x6, matrix products, dot_tn(): lax.dot_general(a, b, (((0,), (0,)), ((), ())), preferred_element_type=F32)  31.8 us
  transfers between devices with their start and end apart: 4, of which 0 were waited for; matrix products, arithmetic and copies ran while one was open for 14% of the time, Pallas kernels for 64%

profile of v3, /device:TPU:20, one launch (start us, length us, event | category | flops | bytes accessed | tf_op | source)
XLA Modules:
  0.0 851.3 jit_solution(7602765237552539946)
XLA Ops:
  11.7 133.4 %shard_map.144 = (bf16[4,2,256,1280]{3,2,1,0:T(8,128)(2,1)}, bf16[4,8,40,896]{3,2,1,0:T(8,128)(2,1)}, f32[4,16,256]{2,1,0:T(8,128)}, bf16[4,4,2,40,1280]{4,3,2,1...) custom-call(bf16[256,1280]{1,0:T(8,128)(2,1)} %x_ref.1, ...), custom_call_target="tpu_custom_call" | custom-call | bytes 468000000 | tf_op jit(solution)/shard_map/pallas_call | solution.py:614
  145.1 11.9 %all-to-all-start = ((bf16[16,40,2688]{2,1,0:T(8,128)(2,1)}), bf16[16,40,2688]{2,1,0:T(8,128)(2,1)}, u32[]{:S(2)}, u32[]{:S(2)}) async-start(bf16[16,40,2688]{2,1,0:T(8,128)(2,1)} %param.13), calls=%async_computation | async-start | bytes 6881280 | tf_op jit(solution)/shard_map/all_to_all | solution.py:1234
  158.8 3.7 fusion.16
  165.9 14.3 %shard_map.145 = (bf16[2048,1280]{1,0:T(8,128)(2,1)}, bf16[2048,256]{1,0:T(8,128)(2,1)}, bf16[2048,256]{1,0:T(8,128)(2,1)}, bf16[2048,256]{1,0:T(8,128)(2,1)}, b...) custom-call(bf16[2048,1280]{1,0:T(8,128)(2,1)} %bitcast.83, f32[1,1280]{1,0:T(1,128)} %copy.24.gain_ref, ...), custom_call_target="tpu_custom_call" | custom-call | bytes 50400000 | tf_op jit(solution)/shard_map/pallas_call | solution.py:86
  180.2 18.4 %shard_map.146 = (bf16[2048,256]{1,0:T(8,128)(2,1)}, f32[2,1,2048]{2,1,0:T(1,128)}) custom-call(bf16[2048,256]{1,0:T(8,128)(2,1)} %get-tuple-element.43.q_ref, bf16[2048,256]{1,0:T(8,128)(2,1)} %get-tuple-element.44.k_ref, bf16[256,2048]{1,0:T(8,128)(2,1)} %get-tuple-element.45.vt_ref), custom_call_target="tpu_custom_call" | custom-call | bytes 64800000 | tf_op jit(solution)/shard_map/pallas_call | solution.py:140
  198.6 50.8 %shard_map.147 = bf16[256,1280]{1,0:T(8,128)(2,1)} custom-call(bf16[2048,256]{1,0:T(8,128)(2,1)} %get-tuple-element.46.o_ref), custom_call_target="tpu_custom_call" | custom-call | bytes 90000000 | tf_op jit(solution)/shard_map/pallas_call | solution.py:674
  249.5 3.3 multiply_reduce_fusion.1
  253.8 115.0 %shard_map.149 = (bf16[4,4,128,1280]{3,2,1,0:T(8,128)(2,1)}, bf16[4,4,2,40,2688]{4,3,2,1,0:T(8,128)(2,1)}) custom-call(bf16[256,1280]{1,0:T(8,128)(2,1)} %multiply_convert_fusion.x_ref, bf16[4,4,128,256]{3,2,1,0:T(8,128)(2,1)} %get-tuple-element.51.pick_ref, bf16[4,4,40,2688]{3,2,1,0:T(8,128)(2,1)} %bitcast.7.rows_ref), custom_call_target="tpu_custom_call" | custom-call | bytes 252000000 | tf_op jit(solution)/shard_map/pallas_call | solution.py:744
  368.8 36.6 %shard_map.150 = (bf16[2048,1280]{1,0:T(8,128)(2,1)}, bf16[2048,1792]{1,0:T(8,128)(2,1)}, bf16[2048,896]{1,0:T(8,128)(2,1)}) custom-call(bf16[2048,1280]{1,0:T(8,128)(2,1)} %bitcast.88, bf16[2048,1280]{1,0:T(8,128)(2,1)} %bitcast.81, bf16[1280,2688]{1,0:T(8,128)(2,1)} %bitcast.78), custom_call_target="tpu_custom_call" | custom-call | bytes 132710400 | tf_op jit(solution)/shard_map/pallas_call | solution.py:253
  405.4 10.6 %fusion.21 = f32[1280,896]{1,0:T(8,128)} fusion(bf16[2048,1280]{1,0:T(8,128)(2,1)} %bitcast.82, bf16[2048,896]{1,0:T(8,128)(2,1)} %get-tuple-element.58), kind=kOutput, calls=%fused_computation.72 | convolution fusion | flops 4697620480 | bytes 13500416 | tf_op jit(solution)/shard_map/dot_general | solution.py:29
  416.0 10.5 %fusion.20 = f32[1280,1792]{1,0:T(8,128)S(1)} fusion(bf16[2048,1280]{1,0:T(8,128)(2,1)S(1)} %bitcast.89, bf16[2048,1792]{1,0:T(8,128)(2,1)S(1)} %copy-done.24), kind=kOutput, calls=%fused_computation.71 | convolution fusion | flops 9395240960 | bytes 21757952 | tf_op jit(solution)/shard_map/dot_general | solution.py:29
  426.5 3.5 pad_maximum_fusion
  430.0 4.9 copy-done
  439.3 10.2 %convolution_convert_fusion = bf16[2048,1280]{1,0:T(8,128)(2,1)} fusion(bf16[2048,896]{1,0:T(8,128)(2,1)} %get-tuple-element.58, bf16[1280,2688]{1,0:T(8,128)(2,1)} %bitcast.79), kind=kOutput, calls=%fused_computation.1 | convolution fusion | flops 4700241920 | bytes 11206656 | tf_op jit(solution)/shard_map/dot_general | solution.py:25
  449.5 4.5 fusion
  454.0 64.7 %shard_map.151 = f32[256,1280]{1,0:T(8,128)} custom-call(bf16[4,4,128,1280]{3,2,1,0:T(8,128)(2,1)} %bitcast.90, bf16[4,4,128,256]{3,2,1,0:T(8,128)(2,1)} %get-tuple-element.51.pick_ref), custom_call_target="tpu_custom_call" | custom-call | bytes 252000000 | tf_op jit(solution)/shard_map/pallas_call | solution.py:887
  518.8 8.6 %all-to-all-start.1 = ((bf16[16,40,2688]{2,1,0:T(8,128)(2,1)}), bf16[16,40,2688]{2,1,0:T(8,128)(2,1)}, u32[]{:S(2)}, u32[]{:S(2)}) async-start(bf16[16,40,2688]{2,1,0:T(8,128)(2,1)} %bitcast.76), calls=%async_computation.1 | async-start | bytes 6881280 | tf_op jit(solution)/shard_map/all_to_all | solution.py:1234
  527.5 8.5 %shard_map.148 = (f32[256,1280]{1,0:T(8,128)}, bf16[256,1792]{1,0:T(8,128)(2,1)}, bf16[256,896]{1,0:T(8,128)(2,1)}) custom-call(bf16[256,1280]{1,0:T(8,128)(2,1)} %multiply_convert_fusion.x_ref, bf16[256,1280]{1,0:T(8,128)(2,1)} %c_ref.1, bf16[1280,2688]{1,0:T(8,128)(2,1)} %all-gather.2.cloned.1.call-done.w_ref), custom_call_target="tpu_custom_call" | custom-call | bytes 16588799 | tf_op jit(solution)/shard_map/pallas_call | solution.py:253
  539.7 2.2 fusion.3
  541.9 4.4 copy.26
  546.3 2.6 convolution_convert_fusion.2
  548.9 5.0 pad_maximum_fusion.1.g_ref
  553.9 118.8 %shard_map.152 = (bf16[4,2,256,1280]{3,2,1,0:T(8,128)(2,1)}, f32[256,1280]{1,0:T(8,128)}, bf16[4,40,2688]{2,1,0:T(8,128)(2,1)}) custom-call(bf16[256,1280]{1,0:T(8,128)(2,1)} %get-tuple-element.77.x_ref, bf16[4,4,128,1280]{3,2,1,0:T(8,128)(2,1)} %bitcast.84, bf16[4,4,128,256]{3,2,1,0:T(8,128)(2,1)} %get-tuple-element.60.pick_ref, ...), custom_call_target="tpu_custom_call" | custom-call | bytes 360000000 | tf_op jit(solution)/shard_map/pallas_call | solution.py:971
  672.8 7.9 copy.27
  680.7 5.2 convolution_convert_fusion.5.do_ref
  685.9 25.4 %shard_map.153 = (bf16[2048,256]{1,0:T(8,128)(2,1)}, bf16[2048,256]{1,0:T(8,128)(2,1)}, bf16[2048,256]{1,0:T(8,128)(2,1)}) custom-call(bf16[2048,256]{1,0:T(8,128)(2,1)} %get-tuple-element.43.q_ref, bf16[2048,256]{1,0:T(8,128)(2,1)} %get-tuple-element.44.k_ref, bf16[256,2048]{1,0:T(8,128)(2,1)} %get-tuple-element.63.kt_ref, ...), custom_call_target="tpu_custom_call" | custom-call | bytes 90000000 | tf_op jit(solution)/shard_map/pallas_call | solution.py:217
  718.1 4.3 convolution_convert_fusion.4
  724.5 6.0 convolution_convert_fusion.1
  730.5 91.0 %shard_map.154 = (f32[256,1280]{1,0:T(8,128)}, bf16[5,40,1024]{2,1,0:T(8,128)(2,1)}, f32[40,2688]{1,0:T(8,128)}) custom-call(bf16[4,2,256,1280]{3,2,1,0:T(8,128)(2,1)} %bitcast.80, bf16[4,8,40,1024]{3,2,1,0:T(8,128)(2,1)} %pad_maximum_fusion.2.g_ref, bf16[4,40,2688]{2,1,0:T(8,128)(2,1)} %get-tuple-element.71.s_ref), custom_call_target="tpu_custom_call" | custom-call | bytes 237600000 | tf_op jit(solution)/shard_map/pallas_call | solution.py:1149
  830.5 3.6 fusion.5
  836.3 2.5 convert_element_type.117
  838.8 4.1 fusion.1
  (115 shorter events, 39.8 us)
Async XLA Ops:
  7.2 3.1 copy-start.21
  7.9 3.2 copy-start.22
  145.1 12.2 %copy-start.15 = (bf16[4,8,40,896]{3,2,1,0:T(8,128)(2,1)S(1)}, bf16[4,8,40,896]{3,2,1,0:T(8,128)(2,1)}, u32[]{:S(2)}) copy-start(bf16[4,8,40,896]{3,2,1,0:T(8,128)(2,1)} %get-tuple-element.42) | copy-start | bytes 6881284
  145.1 108.7 %all-to-all-start = ((bf16[16,40,2688]{2,1,0:T(8,128)(2,1)}), bf16[16,40,2688]{2,1,0:T(8,128)(2,1)}, u32[]{:S(2)}, u32[]{:S(2)}) async-start(bf16[16,40,2688]{2,1,0:T(8,128)(2,1)} %param.13), calls=%async_computation | async-start | bytes 6881280 | tf_op jit(solution)/shard_map/all_to_all | solution.py:1234
  157.1 370.4 %all-gather.2.cloned.1.call-start = ((), (), s32[]{:S(2)}) async-start(), calls=%async_computation.2 | async-start | bytes 7096320 | tf_op jit(solution)/shard_map/all_gather | solution.py:1261
  180.2 69.3 %copy-start.5 = (bf16[256,1280]{1,0:T(8,128)(2,1)S(1)}, bf16[256,1280]{1,0:T(8,128)(2,1)}, u32[]{:S(2)}) copy-start(bf16[256,1280]{1,0:T(8,128)(2,1)} %x_ref.1) | copy-start | bytes 1966084
  405.4 10.6 %copy-start.9 = (bf16[4,4,128,1280]{3,2,1,0:T(8,128)(2,1)S(1)}, bf16[4,4,128,1280]{3,2,1,0:T(8,128)(2,1)}, u32[]{:S(2)}) copy-start(bf16[4,4,128,1280]{3,2,1,0:T(8,128)(2,1)} %get-tuple-element.53) | copy-start | bytes 15728644
  405.4 10.6 %copy-start.24 = (bf16[2048,1792]{1,0:T(8,128)(2,1)S(1)}, bf16[2048,1792]{1,0:T(8,128)(2,1)}, u32[]{:S(2)}) copy-start(bf16[2048,1792]{1,0:T(8,128)(2,1)} %get-tuple-element.57) | copy-start | bytes 22020100
  430.0 4.9 copy-start
  437.0 12.5 %collective-permute-start = (bf16[4,4,40,2688]{3,2,1,0:T(8,128)(2,1)}, bf16[4,4,40,2688]{3,2,1,0:T(8,128)(2,1)}, u32[]{:S(2)}, u32[]{:S(2)}) collective-permute-start(bf16[4,4,40,2688]{3,2,1,0:T(8,128)(2,1)} %fusion.2), channel_id=1, source_target_pairs={{0,1},{1,0},{2,3},{3,2},{4,5},{5,4},{6,7},{7,6},{8,9},{9,8},{10,11... | collective-permute-start | bytes 10321928 | tf_op jit(solution)/shard_map/ppermute | solution.py:1196
  438.5 11.0 %slice-start = ((s8[13762560]{0:T(1024)(128)(4,1)}), s8[4194304]{0:T(1024)(128)(4,1)S(1)}, s32[]{:S(2)}) async-start(s8[13762560]{0:T(1024)(128)(4,1)} %bitcast.72), calls=%async_computation.3 | async-start | bytes 8388608
  439.2 10.2 %slice-start.1 = ((s8[13762560]{0:T(1024)(128)(4,1)}), s8[4194304]{0:T(1024)(128)(4,1)S(1)}, s32[]{:S(2)}) async-start(s8[13762560]{0:T(1024)(128)(4,1)} %bitcast.72), calls=%async_computation.4 | async-start | bytes 8388608
  439.2 10.2 %slice-start.2 = ((s8[13762560]{0:T(1024)(128)(4,1)}), s8[4194304]{0:T(1024)(128)(4,1)S(1)}, s32[]{:S(2)}) async-start(s8[13762560]{0:T(1024)(128)(4,1)} %bitcast.72), calls=%async_computation.5 | async-start | bytes 8388608
  439.2 10.2 %slice-start.3 = ((s8[13762560]{0:T(1024)(128)(4,1)}), s8[1179648]{0:T(1024)(128)(4,1)S(1)}, s32[]{:S(2)}) async-start(s8[13762560]{0:T(1024)(128)(4,1)} %bitcast.72), calls=%async_computation.6 | async-start | bytes 2359296
  518.8 317.5 %all-to-all-start.1 = ((bf16[16,40,2688]{2,1,0:T(8,128)(2,1)}), bf16[16,40,2688]{2,1,0:T(8,128)(2,1)}, u32[]{:S(2)}, u32[]{:S(2)}) async-start(bf16[16,40,2688]{2,1,0:T(8,128)(2,1)} %bitcast.76), calls=%async_computation.1 | async-start | bytes 6881280 | tf_op jit(solution)/shard_map/all_to_all | solution.py:1234
  527.4 8.6 %copy-start.3 = (f32[256,1280]{1,0:T(8,128)S(1)}, f32[256,1280]{1,0:T(8,128)}, u32[]{:S(2)}) copy-start(f32[256,1280]{1,0:T(8,128)} %shard_map.151) | copy-start | bytes 3932164
  541.9 4.4 copy-start.2
  685.9 32.1 %slice-start.4 = ((s8[5242880]{0:T(1024)(128)(4,1)}), s8[1048576]{0:T(1024)(128)(4,1)S(1)}, s32[]{:S(2)}) async-start(s8[5242880]{0:T(1024)(128)(4,1)} %bitcast.100), calls=%async_computation.7 | async-start | bytes 2097152
  711.3 5.0 copy-start.8
  711.3 5.0 copy-start.13
  712.8 5.3 slice-start.5
  722.4 2.0 copy-start.7
  824.4 4.4 copy-start.6
  824.4 4.4 copy-start.20
  826.1 4.4 copy-start.17
  826.1 4.4 copy-start.18
  826.2 7.9 copy-start.14
  830.5 4.3 copy-start.11
  830.5 4.3 copy-start.12
  838.7 4.1 copy-start.1
  838.7 4.1 copy-start.23
  838.8 4.7 copy-start.19
  (3 other events, 5.5 us)
Sparse Core Ops, SparseCore 0:
  249.6 102.1 all-gather.1

commit v4 on v3

--- a/solution.py
+++ b/solution.py
@@ -229,20 +229,24 @@
     )(q, k, kt, v, o, do, lse, cos, sin)
 
 
-def expert_kernel(hidden, x_ref, c_ref, w_ref, dx_ref, gu_ref, hid_ref):
-    x = x_ref[...]
+def feed(x, c, w_ref, hidden):
     gate = dot_nn(x, w_ref[:, :hidden])
     up = dot_nn(x, w_ref[:, hidden : 2 * hidden])
-    down = dot_nn(c_ref[...], w_ref[:, 2 * hidden :])
+    down = dot_nn(c, w_ref[:, 2 * hidden :])
     sig = 1.0 / (1.0 + jnp.exp(-gate))
     act = gate * sig
-    hid_ref[...] = (act * up).astype(BF)
     dup = (down * act).astype(BF)
     dgate = (down * up * sig * (1.0 + gate * (1.0 - sig))).astype(BF)
+    dx = dot_nt(dgate, w_ref[:, :hidden]) + dot_nt(dup, w_ref[:, hidden : 2 * hidden])
+    return dx, dgate, dup, (act * up).astype(BF)
+
+
+def expert_kernel(hidden, x_ref, c_ref, w_ref, dx_ref, gu_ref, hid_ref):
+    dx, dgate, dup, hid = feed(x_ref[...], c_ref[...], w_ref, hidden)
+    dx_ref[...] = dx.astype(dx_ref.dtype)
     gu_ref[:, :hidden] = dgate
     gu_ref[:, hidden:] = dup
-    dx = dot_nt(dgate, w_ref[:, :hidden]) + dot_nt(dup, w_ref[:, hidden : 2 * hidden])
-    dx_ref[...] = dx.astype(dx_ref.dtype)
+    hid_ref[...] = hid
 
 
 def expert(x, c, w, kind):
@@ -281,6 +285,10 @@
     pl.semaphore_wait(barrier, len(peers))
 
 
+def head_slot(f, lanes, cores):
+    return lax.rem(f, cores) * lanes + f // cores
+
+
 def sequence_peers(dp, fs, fss):
     return [(dp, lax.rem(fs + k, fss)) for k in range(1, fss)]
 
@@ -465,24 +473,85 @@
                 self.over(m, block).wait_send()
 
 
+class Rows:
+    def __init__(self, own, full, dps, lanes, cores, sems):
+        self.own, self.full, self.dps, self.lanes, self.cores = own, full, dps, lanes, cores
+        self.z_out, self.z_in, self.d_out, self.d_in, self.c_out, self.c_in, self.local = sems
+        self.dp, self.fs, self.z, self.c = place(cores)
+
+    def along(self, k):
+        t = lax.rem(self.z + k, self.lanes) * self.cores + self.c
+        return send(
+            self.own, self.full.at[self.dp, self.z, self.c], self.z_out.at[k - 1], self.z_in.at[k - 1],
+            (self.dp, t),
+        )
+
+    def over(self, m, block):
+        piece = self.full.at[block, :, self.c]
+        return send(
+            piece, piece, self.d_out.at[m - 1], self.d_in.at[m - 1], (lax.rem(self.dp + m, self.dps), self.fs)
+        )
+
+    def across(self, m, core):
+        piece = self.full.at[:, :, core]
+        peer = (self.dp, self.z * self.cores + lax.rem(self.c + m, self.cores))
+        return send(piece, piece, self.c_out.at[m - 1], self.c_in.at[m - 1], peer)
+
+    def keep(self):
+        return pltpu.make_async_copy(self.own, self.full.at[self.dp, self.z, self.c], self.local)
+
+    def begin(self):
+        for k in range(1, self.lanes):
+            self.along(k).start()
+        self.keep().start()
+
+    def to_dp(self):
+        self.keep().wait()
+        for k in range(1, self.lanes):
+            self.along(k).wait_recv()
+        for m in range(1, self.dps):
+            self.over(m, self.dp).start()
+
+    def to_cores(self):
+        for m in range(1, self.dps):
+            self.over(m, lax.rem(self.dp + self.dps - m, self.dps)).wait_recv()
+        for m in range(1, self.cores):
+            self.across(m, self.c).start()
+
+    def finish(self):
+        for m in range(1, self.cores):
+            self.across(m, lax.rem(self.c + self.cores - m, self.cores)).wait_recv()
+        for k in range(1, self.lanes):
+            self.along(k).wait_send()
+        for m in range(1, self.dps):
+            self.over(m, self.dp).wait_send()
+        for m in range(1, self.cores):
+            self.across(m, self.c).wait_send()
+
+
+def pair(n):
+    return [pltpu.SemaphoreType.DMA((max(n - 1, 1),)) for _ in range(2)]
+
+
+def rows_sems(dps, lanes, cores):
+    return pair(lanes) + pair(dps) + pair(cores) + [pltpu.SemaphoreType.DMA]
+
+
 def start_kernel(
-    dps, lanes, cores, topk, x_ref, wh_ref, tab_ref, wo_ref, up_ref,
-    full_ref, heads_ref, tabs_ref, out_ref, pick_ref, weigh_ref, c_ref, line_buf, stage,
-    h_out, h_in, hd_out, hd_in, t_out, t_in, o_out, o_in, od_out, od_in, oc_out, oc_in, locals_,
-    l_out, l_in, s_out, s_in, s_local, *sems,
+    dps, lanes, cores, topk, busy, x_ref, wh_ref, tab_ref, wo_ref,
+    full_ref, heads_ref, tabs_ref, out_ref, pick_ref, weigh_ref,
+    h_out, h_in, hd_out, hd_in, t_out, t_in, locals_, *sems,
 ):
-    chain = Chain(x_ref, full_ref, lanes, cores, sems)
+    rows = Rows(wo_ref, out_ref, dps, lanes, cores, sems[:7])
+    chain = Chain(x_ref, full_ref, lanes, cores, sems[7:])
     dp, fs, z, c = chain.dp, chain.fs, chain.z, chain.c
     fss = lanes * cores
-    line = Line(up_ref, line_buf, lanes, cores, l_out, l_in)
-    spread = Spread(stage, c_ref, dps, lanes, cores, s_out, s_in, s_local)
     slots, tokens = pick_ref.shape[2:]
     greet(sequence_peers(dp, fs, fss) + [(lax.rem(dp + m, dps), fs) for m in range(1, dps)])
     chain.begin()
     kept = [
         pltpu.make_async_copy(wh_ref.at[fs], heads_ref.at[dp, fs], locals_.at[0]),
         pltpu.make_async_copy(tab_ref, tabs_ref.at[z], locals_.at[1]),
-        pltpu.make_async_copy(wo_ref, out_ref.at[dp, z, c], locals_.at[2]),
     ]
     for copy in kept:
         copy.start()
@@ -494,10 +563,6 @@
     def table_to(k):
         t = lax.rem(z + k, lanes) * cores + c
         return send(tab_ref, tabs_ref.at[z], t_out.at[k - 1], t_in.at[k - 1], (dp, t))
-
-    def out_to(k):
-        t = lax.rem(z + k, lanes) * cores + c
-        return send(wo_ref, out_ref.at[dp, z, c], o_out.at[k - 1], o_in.at[k - 1], (dp, t))
 
     def heads_over(m, block):
         return send(
@@ -505,25 +570,30 @@
             (lax.rem(dp + m, dps), fs),
         )
 
-    def out_over(m, block):
-        piece = out_ref.at[block, :, c]
-        return send(piece, piece, od_out.at[m - 1], od_in.at[m - 1], (lax.rem(dp + m, dps), fs))
-
-    def out_across(m, core):
-        piece = out_ref.at[:, :, core]
-        return send(
-            piece, piece, oc_out.at[m - 1], oc_in.at[m - 1], (dp, z * cores + lax.rem(c + m, cores))
-        )
+    mine = head_slot(fs, lanes, cores) < busy
+    for k in range(1, fss):
+
+        @pl.when(head_slot(lax.rem(fs + k, fss), lanes, cores) < busy)
+        def _():
+            heads_to(k).start()
 
     for k in range(1, lanes):
         table_to(k).start()
-    line.begin()
-    for k in range(1, fss):
-        heads_to(k).start()
-    for k in range(1, lanes):
-        out_to(k).start()
+    rows.begin()
     for copy in kept:
         copy.wait()
+    if lanes > 1:
+        chain.advance(1)
+    @pl.when(mine)
+    def _():
+        for k in range(1, fss):
+            heads_to(k).wait_recv()
+        for m in range(1, dps):
+            heads_over(m, dp).start()
+
+    rows.to_dp()
+    for step in range(2, lanes):
+        chain.advance(step)
     for k in range(1, lanes):
         table_to(k).wait_recv()
 
@@ -543,65 +613,31 @@
             pick_ref[m, block] = jnp.where(match, 1.0, 0.0).astype(BF)
             weigh_ref[m, block] = jnp.where(match, gate, 0.0).astype(BF)
 
-    def pick(block, source):
-        for m in spread.order():
-            name = (lax.rem(dp + m, dps) * lanes + z).astype(F32)
-            hit = tabs_ref[block, :topk, :] == name
-            gate = jnp.sum(jnp.where(hit, tabs_ref[block, topk : 2 * topk, :], 0.0), axis=0, keepdims=True)
-            one = pick_ref[m, block]
-            scale = jnp.sum(one.astype(F32) * gate, axis=1, keepdims=True)
-            stage[m, block] = (dot_nn(one, source[...]) * scale).astype(BF)
-            spread.go(m, block)
-
-    if lanes > 1:
-        chain.advance(1)
-    pick(z, up_ref)
+    rows.to_cores()
+    chain.finish()
+    rows.finish()
     for k in range(1, fss):
-        heads_to(k).wait_recv()
-    for m in range(1, dps):
-        heads_over(m, dp).start()
+
+        @pl.when(head_slot(lax.rem(fs + k, fss), lanes, cores) < busy)
+        def _():
+            heads_to(k).wait_send()
+
     for k in range(1, lanes):
-        out_to(k).wait_recv()
-    for m in range(1, dps):
-        out_over(m, dp).start()
-    if lanes > 1:
-        line.advance(1, pick)
-    for step in range(2, lanes):
-        chain.advance(step)
-        line.advance(step, pick)
-    for m in range(1, dps):
-        out_over(m, lax.rem(dp + dps - m, dps)).wait_recv()
-    for m in range(1, cores):
-        out_across(m, c).start()
-    for m in range(1, dps):
-        heads_over(m, lax.rem(dp + dps - m, dps)).wait_recv()
-    chain.finish()
-    line.finish()
-    spread.finish()
-    for m in range(1, cores):
-        out_across(m, lax.rem(c + cores - m, cores)).wait_recv()
-    for k in range(1, fss):
-        heads_to(k).wait_send()
-    for k in range(1, lanes):
-        out_to(k).wait_send()
         table_to(k).wait_send()
-    for m in range(1, dps):
-        heads_over(m, dp).wait_send()
-        out_over(m, dp).wait_send()
-    for m in range(1, cores):
-        out_across(m, c).wait_send()
-
-
-def start(x, wh, table, w_out, upstream, topk, dps, lanes, cores):
+
+    @pl.when(mine)
+    def _():
+        for m in range(1, dps):
+            heads_over(m, lax.rem(dp + dps - m, dps)).wait_recv()
+            heads_over(m, dp).wait_send()
+
+
+def start(x, wh, table, w_out, topk, busy, dps, lanes, cores):
     fss = lanes * cores
-    tokens, model = x.shape
-    slots = tokens // 2
+    tokens = x.shape[0]
     dma = pltpu.SemaphoreType.DMA
-    pair = lambda n: [dma((max(n - 1, 1),)), dma((max(n - 1, 1),))]
-    hops = (2, max(lanes - 1, 1))
-    ways = (dps - 1, lanes)
     whole = pl.BlockSpec(memory_space=pltpu.VMEM)
-    picks = jax.ShapeDtypeStruct((dps, lanes, slots, tokens), BF)
+    picks = jax.ShapeDtypeStruct((dps, lanes, tokens // 2, tokens), BF)
     shapes = [
         jax.ShapeDtypeStruct((lanes, cores) + x.shape, x.dtype),
         jax.ShapeDtypeStruct((dps,) + wh.shape, wh.dtype),
@@ -609,35 +645,31 @@
         jax.ShapeDtypeStruct((dps, lanes, cores) + w_out.shape, w_out.dtype),
         picks,
         picks,
-        jax.ShapeDtypeStruct((dps, lanes, slots, model), BF),
     ]
     return pl.pallas_call(
-        functools.partial(start_kernel, dps, lanes, cores, topk),
-        in_specs=[ANY] * 4 + [whole],
-        out_specs=[ANY, ANY, whole, ANY, whole, whole, ANY],
+        functools.partial(start_kernel, dps, lanes, cores, topk, busy),
+        in_specs=[ANY] * 4,
+        out_specs=[ANY, ANY, whole, ANY, whole, whole],
         out_shape=shapes,
-        scratch_shapes=[
-            pltpu.VMEM((lanes, tokens, model), BF),
-            pltpu.VMEM((dps, lanes, slots, model), BF),
-        ]
-        + pair(fss) + pair(dps) + pair(lanes) + pair(lanes) + pair(dps) + pair(cores) + [dma((3,))]
-        + [dma(hops), dma(hops), dma(ways), dma(ways), dma((lanes,))]
-        + chain_sems(lanes, cores),
-        cost_estimate=lasts(130),
+        scratch_shapes=pair(fss) + pair(dps) + pair(lanes) + [dma((2,))]
+        + rows_sems(dps, lanes, cores) + chain_sems(lanes, cores),
+        cost_estimate=lasts(70),
         compiler_params=pltpu.CompilerParams(
             collective_id=0, has_side_effects=True, vmem_limit_bytes=VMEM_LIMIT
         ),
-    )(x, wh, table, w_out, upstream)
-
-
-def heads_kernel(lanes, cores, busy, o_ref, mix_ref, out, came, local):
+    )(x, wh, table, w_out)
+
+
+def heads_kernel(dps, lanes, cores, busy, o_ref, sh_ref, mix_ref, all_ref, out, came, local, *sems):
     dp, fs, z, c = place(cores)
     fss = lanes * cores
     tokens, width = mix_ref.shape[0], o_ref.shape[1]
-    greet(sequence_peers(dp, fs, fss))
+    shared = Rows(sh_ref, all_ref, dps, lanes, cores, sems)
+    greet(sequence_peers(dp, fs, fss) + [(lax.rem(dp + m, dps), fs) for m in range(1, dps)])
 
     def columns(f):
-        return mix_ref.at[:, pl.ds(pl.multiple_of(f * width, HD), width)]
+        slot = head_slot(f, lanes, cores)
+        return mix_ref.at[:, pl.ds(pl.multiple_of(slot * width, HD), width)]
 
     def rows(f):
         return o_ref.at[pl.ds(pl.multiple_of(f * tokens, tokens), tokens), :]
@@ -647,39 +679,48 @@
         return send(rows(t), columns(owner), out.at[k - 1], came.at[k - 1], (dp, t))
 
     keep = pltpu.make_async_copy(rows(fs), columns(fs), local)
-
-    @pl.when(fs < busy)
+    shared.begin()
+
+    @pl.when(head_slot(fs, lanes, cores) < busy)
     def _():
         for k in range(1, fss):
             to(k, fs).start()
         keep.start()
 
+    shared.to_dp()
     for k in range(1, fss):
         owner = lax.rem(fs + fss - k, fss)
 
-        @pl.when(owner < busy)
+        @pl.when(head_slot(owner, lanes, cores) < busy)
         def _():
             to(k, owner).wait_recv()
 
-    @pl.when(fs < busy)
+    shared.to_cores()
+
+    @pl.when(head_slot(fs, lanes, cores) < busy)
     def _():
         keep.wait()
         for k in range(1, fss):
             to(k, fs).wait_send()
 
-
-def heads_home(o, tokens, lanes, cores, busy):
+    shared.finish()
+
+
+def heads_home(o, w_shared, tokens, dps, lanes, cores, busy):
     fss = lanes * cores
     dma = pltpu.SemaphoreType.DMA
     return pl.pallas_call(
-        functools.partial(heads_kernel, lanes, cores, busy),
-        in_specs=[ANY],
-        out_specs=ANY,
-        out_shape=jax.ShapeDtypeStruct((tokens, busy * o.shape[1]), o.dtype),
-        scratch_shapes=[dma((fss - 1,)), dma((fss - 1,)), dma],
-        cost_estimate=lasts(25),
+        functools.partial(heads_kernel, dps, lanes, cores, busy),
+        in_specs=[ANY, ANY],
+        out_specs=[ANY, ANY],
+        out_shape=[
+            jax.ShapeDtypeStruct((tokens, busy * o.shape[1]), o.dtype),
+            jax.ShapeDtypeStruct((dps, lanes, cores) + w_shared.shape, w_shared.dtype),
+        ],
+        scratch_shapes=[dma((fss - 1,)), dma((fss - 1,)), dma] + rows_sems(dps, lanes, cores),
+        cost_estimate=lasts(45),
         compiler_params=pltpu.CompilerParams(collective_id=2, has_side_effects=True),
-    )(o)
+    )(o, w_shared)
 
 
 def greet_cross(line, dps, cores=1):
@@ -701,11 +742,14 @@
 
 
 def dispatch_kernel(
-    dps, lanes, cores, x_ref, pick_ref, rows_ref, out_ref, w_ref, buffer, stage,
-    l_out, l_in, s_out, s_in, s_local, w_out, w_in, w_local,
+    dps, lanes, cores, topk, x_ref, up_ref, tabs_ref, pick_ref, rows_ref, shared_ref,
+    out_ref, c_ref, w_ref, dx_ref, f_ref, g_ref, acts, acc, buffer, stage, up_buffer, up_stage, l_out, l_in, s_out, s_in, s_local,
+    ul_out, ul_in, us_out, us_in, us_local, w_out, w_in, w_local,
 ):
     line = Line(x_ref, buffer, lanes, cores, l_out, l_in)
     spread = Spread(stage, out_ref, dps, lanes, cores, s_out, s_in, s_local)
+    up_line = Line(up_ref, up_buffer, lanes, cores, ul_out, ul_in)
+    up_spread = Spread(up_stage, c_ref, dps, lanes, cores, us_out, us_in, us_local)
     greet_cross(line, dps, cores)
 
     def across(m, core):
@@ -719,47 +763,90 @@
             stage[m, block] = dot_nn(pick_ref[m, block], source[...]).astype(BF)
             spread.go(m, block)
 
+    def up_pick(block, source):
+        for m in up_spread.order():
+            name = (lax.rem(line.dp + m, dps) * lanes + line.z).astype(F32)
+            hit = tabs_ref[block, :topk, :] == name
+            gate = jnp.sum(jnp.where(hit, tabs_ref[block, topk : 2 * topk, :], 0.0), axis=0, keepdims=True)
+            one = pick_ref[m, block]
+            scale = jnp.sum(one.astype(F32) * gate, axis=1, keepdims=True)
+            up_stage[m, block] = (dot_nn(one, source[...]) * scale).astype(BF)
+            up_spread.go(m, block)
+
     line.begin()
+    pick(line.z, x_ref)
+    up_line.begin()
+    up_pick(line.z, up_ref)
     keep.start()
     for m in range(1, cores):
         across(m, line.c).start()
-    pick(line.z, x_ref)
+    hidden = shared_ref.shape[1] // 3
+    experts, shard = dps * lanes, g_ref.shape[3]
+
+    def shared_forward():
+        dx, gate, up, hid = feed(x_ref[...], up_ref[...], shared_ref, hidden)
+        dx_ref[...] = dx
+        acts[0] = gate
+        acts[1] = up
+        acts[2] = hid
+        f_ref[...] = dot_nt(hid, shared_ref[:, 2 * hidden :])
+
+    def shared_gradient(third):
+        acc[...] = dot_tn((x_ref if third < 2 else up_ref)[...], acts[third])
+        for e in range(experts):
+            for k in range(cores):
+                row = (e * cores + k) * shard
+                piece = acc[row : row + shard, :].astype(BF)
+                g_ref[e // lanes, e % lanes, k, :, third * hidden : (third + 1) * hidden] = piece
+
+    work = [shared_forward] + [functools.partial(shared_gradient, third) for third in range(3)]
     for step in range(1, lanes):
         line.advance(step, pick)
+        up_line.advance(step, up_pick)
+        work.pop(0)()
+    for left in work:
+        left()
     spread.finish()
     line.finish()
+    up_spread.finish()
+    up_line.finish()
     keep.wait()
     for m in range(1, cores):
         across(m, lax.rem(line.c + cores - m, cores)).wait_recv()
         across(m, line.c).wait_send()
 
 
-def dispatch(x, picks, rows, lanes, cores, number):
+def dispatch(x, upstream, tables, picks, rows, shared, topk, lanes, cores):
     dps, _, slots, tokens = picks.shape
     model = x.shape[1]
     dma = pltpu.SemaphoreType.DMA
     hops = (2, max(lanes - 1, 1))
     ways = (dps - 1, lanes)
     whole = pl.BlockSpec(memory_space=pltpu.VMEM)
+    buffers = [pltpu.VMEM((lanes, tokens, model), BF), pltpu.VMEM((dps, lanes, slots, model), BF)]
+    moves = [dma(hops), dma(hops), dma(ways), dma(ways), dma((lanes,))]
     return pl.pallas_call(
-        functools.partial(dispatch_kernel, dps, lanes, cores),
-        in_specs=[whole, whole, ANY],
-        out_specs=[ANY, ANY],
+        functools.partial(dispatch_kernel, dps, lanes, cores, topk),
+        in_specs=[whole] * 4 + [ANY, whole],
+        out_specs=[ANY, ANY, ANY, whole, whole, whole],
         out_shape=[
             jax.ShapeDtypeStruct((dps, lanes, slots, model), BF),
+            jax.ShapeDtypeStruct((dps, lanes, slots, model), BF),
+            jax.ShapeDtypeStruct((dps, lanes, cores) + rows.shape[2:], BF),
+            jax.ShapeDtypeStruct((tokens, model), F32),
+            jax.ShapeDtypeStruct((tokens, model), F32),
             jax.ShapeDtypeStruct((dps, lanes, cores) + rows.shape[2:], BF),
         ],
         scratch_shapes=[
-            pltpu.VMEM((lanes, tokens, model), BF),
-            pltpu.VMEM((dps, lanes, slots, model), BF),
-            dma(hops), dma(hops), dma(ways), dma(ways), dma((lanes,)),
-            dma((max(cores - 1, 1),)), dma((max(cores - 1, 1),)), dma,
-        ],
-        cost_estimate=lasts(70),
+            pltpu.VMEM((3, tokens, shared.shape[1] // 3), BF),
+            pltpu.VMEM((model, shared.shape[1] // 3), F32),
+        ]
+        + buffers * 2 + moves * 2 + pair(cores) + [dma],
+        cost_estimate=lasts(125),
         compiler_params=pltpu.CompilerParams(
-            collective_id=number, has_side_effects=True, vmem_limit_bytes=VMEM_LIMIT
+            collective_id=3, has_side_effects=True, vmem_limit_bytes=VMEM_LIMIT
         ),
-    )(x, picks, rows)
+    )(x, upstream, tables, picks, rows, shared)
 
 
 class Combine:
@@ -871,133 +958,262 @@
     ]
 
 
-def combine_kernel(dps, lanes, cores, part_ref, pick_ref, out_ref, *scratch):
+class SharedSum:
+    def __init__(self, source, total, scratch, dps, lanes, cores):
+        self.source, self.total = source, total
+        self.own, self.from_core, self.from_dp = scratch[:3]
+        self.c_out, self.c_in, self.d_out, self.d_in, self.local = scratch[3:]
+        self.dps, self.lanes, self.cores = dps, lanes, cores
+        self.dp, self.fs, self.z, self.c = place(cores)
+
+    def across(self, m):
+        t = lax.rem(self.c + m, self.cores)
+        return send(
+            self.source.at[:, :, t], self.from_core.at[m - 1], self.c_out.at[m - 1], self.c_in.at[m - 1],
+            (self.dp, self.z * self.cores + t),
+        )
+
+    def over(self, m):
+        t = lax.rem(self.dp + m, self.dps)
+        return send(
+            self.own.at[t], self.from_dp.at[m - 1], self.d_out.at[m - 1], self.d_in.at[m - 1], (t, self.fs)
+        )
+
+    def keep(self):
+        return pltpu.make_async_copy(self.source.at[:, :, self.c], self.own, self.local)
+
+    def begin(self):
+        self.keep().start()
+        for m in range(1, self.cores):
+            self.across(m).start()
+
+    def add_cores(self):
+        self.keep().wait()
+        for m in range(1, self.cores):
+            self.across(m).wait_recv()
+
+        def add(i, carry):
+            p, q = i // self.lanes, lax.rem(i, self.lanes)
+            total = self.own[p, q].astype(F32)
+            for m in range(1, self.cores):
+                total = total + self.from_core[m - 1, p, q].astype(F32)
+            self.own[p, q] = total.astype(BF)
+            return carry
+
+        lax.fori_loop(0, self.dps * self.lanes, add, 0)
+        for m in range(1, self.dps):
+            self.over(m).start()
+
+    def add_dp(self):
+        for m in range(1, self.dps):
+            self.over(m).wait_recv()
+        for q in range(self.lanes):
+            total = self.own[self.dp, q].astype(F32)
+            for m in range(1, self.dps):
+                total = total + self.from_dp[m - 1, q].astype(F32)
+            self.total[q] = total.astype(BF)
+        for m in range(1, self.cores):
+            self.across(m).wait_send()
+        for m in range(1, self.dps):
+            self.over(m).wait_send()
+
+
+def shared_scratch(g, dps, lanes, cores):
+    return [
+        pltpu.VMEM((dps, lanes) + g.shape[3:], BF),
+        pltpu.VMEM((max(cores - 1, 1), dps, lanes) + g.shape[3:], BF),
+        pltpu.VMEM((dps - 1, lanes) + g.shape[3:], BF),
+    ] + pair(cores) + pair(dps) + [pltpu.SemaphoreType.DMA]
+
+
+def combine_kernel(
+    dps, lanes, cores, part_ref, pick_ref, hid_ref, w_ref, out_ref, f_ref, hid, down, load, *scratch
+):
     work = Combine(part_ref, pick_ref, out_ref, scratch, dps, lanes, cores)
+    hidden = hid.shape[1]
+    slots = f_ref.shape[2]
+    loads = [
+        pltpu.make_async_copy(hid_ref, hid, load.at[0]),
+        pltpu.make_async_copy(w_ref.at[:, 2 * hidden :], down, load.at[1]),
+    ]
+    for copy in loads:
+        copy.start()
     greet_cross(Line(None, None, lanes, cores, None, None), dps)
     work.begin()
-    for step in range(1, lanes):
-        work.advance(step)
+    for copy in loads:
+        copy.wait()
+
+    def forward(m):
+        for block in range(lanes):
+            row = (m * lanes + block) * slots
+            f_ref[m, block] = dot_nt(hid[row : row + slots, :], down[...]).astype(BF)
+
+    per = -(-dps // max(lanes - 1, 1))
+    for step in range(1, max(lanes, 2)):
+        for m in range((step - 1) * per, min(step * per, dps)):
+            forward(m)
+        if step < lanes:
+            work.advance(step)
     work.finish()
 
 
-def combine(parts, picks, lanes, cores, number):
+def combine(parts, picks, hid, w, lanes, cores):
     dps, _, slots, model = parts.shape
     tokens = picks.shape[3]
+    hidden = hid.shape[1]
+    dma = pltpu.SemaphoreType.DMA
     whole = pl.BlockSpec(memory_space=pltpu.VMEM)
     return pl.pallas_call(
         functools.partial(combine_kernel, dps, lanes, cores),
-        in_specs=[ANY, whole],
-        out_specs=whole,
-        out_shape=jax.ShapeDtypeStruct((tokens, model), F32),
-        scratch_shapes=combine_scratch(dps, lanes, slots, tokens, model),
+        in_specs=[ANY, whole, ANY, ANY],
+        out_specs=[whole, whole],
+        out_shape=[
+            jax.ShapeDtypeStruct((tokens, model), F32),
+            jax.ShapeDtypeStruct(parts.shape, BF),
+        ],
+        scratch_shapes=[pltpu.VMEM(hid.shape, BF), pltpu.VMEM((model, hidden), BF), dma((2,))]
+        + combine_scratch(dps, lanes, slots, tokens, model),
         cost_estimate=lasts(70),
         compiler_params=pltpu.CompilerParams(
-            collective_id=number, has_side_effects=True, vmem_limit_bytes=VMEM_LIMIT
+            collective_id=4, has_side_effects=True, vmem_limit_bytes=VMEM_LIMIT
         ),
-    )(parts, picks)
+    )(parts, picks, hid, w)
+
+
+class Gradient:
+    def __init__(self, refs, total, scratch, experts, shard, cores):
+        self.x, self.c_rows, self.gu, self.hid = refs
+        self.total = total
+        self.left, self.right, self.acc, self.stage, self.inbox, self.load, self.out, self.came = scratch
+        self.experts, self.shard, self.cores = experts, shard, cores
+        self.hidden = self.hid.shape[1]
+        self.dp, self.fs, self.z, self.c = place(cores)
+
+    def rows_in(self, third):
+        source = self.x if third < 2 else self.c_rows
+        return pltpu.make_async_copy(source, self.left, self.load.at[0])
+
+    def columns_in(self, third):
+        source = self.hid if third == 2 else self.gu.at[:, third * self.hidden : (third + 1) * self.hidden]
+        return pltpu.make_async_copy(source, self.right, self.load.at[1])
+
+    def across(self, third, m):
+        t = lax.rem(self.c + m, self.cores)
+        return send(
+            self.stage.at[third, t], self.inbox.at[third, m - 1], self.out.at[third, m - 1],
+            self.came.at[third, m - 1], (self.dp, self.z * self.cores + t),
+        )
+
+    def begin(self):
+        self.rows_in(0).start()
+        self.columns_in(0).start()
+
+    def multiply(self, third):
+        if third != 1:
+            self.rows_in(third).wait()
+        self.columns_in(third).wait()
+        self.acc[...] = dot_tn(self.left[...], self.right[...])
+        if third < 2:
+            self.columns_in(third + 1).start()
+        if third == 1:
+            self.rows_in(2).start()
+        for e in range(self.experts):
+            for k in range(self.cores):
+                row = (e * self.cores + k) * self.shard
+                self.stage[third, k, e] = self.acc[row : row + self.shard, :].astype(BF)
+        for m in range(1, self.cores):
+            self.across(third, m).start()
+
+    def collect(self, third):
+        for m in range(1, self.cores):
+            self.across(third, m).wait_recv()
+        for e in range(self.experts):
+            total = self.stage[third, self.c, e].astype(F32)
+            for m in range(1, self.cores):
+                total = total + self.inbox[third, m - 1, e].astype(F32)
+            self.total[e, :, third * self.hidden : (third + 1) * self.hidden] = total.astype(BF)
+
+    def finish(self):
+        for third in range(3):
+            for m in range(1, self.cores):
+                self.across(third, m).wait_send()
 
 
 def turn_kernel(
-    dps, lanes, cores, x_ref, part_ref, pick_ref, g_ref, full_ref, out_ref, total_ref,
-    own, from_core, from_dp, gc_out, gc_in, gd_out, gd_in, g_local, *scratch,
+    dps, lanes, cores, x_ref, part_ref, pick_ref, xs_ref, cs_ref, gu_ref, hid_ref,
+    full_ref, out_ref, g_ref, *scratch,
 ):
     work = Combine(part_ref, pick_ref, out_ref, scratch[:8], dps, lanes, cores)
-    chain = Chain(x_ref, full_ref, lanes, cores, scratch[8:])
-    dp, fs, z, c = chain.dp, chain.fs, chain.z, chain.c
+    gradient = Gradient(
+        (xs_ref, cs_ref, gu_ref, hid_ref), g_ref, scratch[8:16], g_ref.shape[0], g_ref.shape[1], cores
+    )
+    chain = Chain(x_ref, full_ref, lanes, cores, scratch[16:])
+    dp, fs = chain.dp, chain.fs
     fss = lanes * cores
-
-    def across(m):
-        t = lax.rem(c + m, cores)
-        return send(
-            g_ref.at[:, :, t], from_core.at[m - 1], gc_out.at[m - 1], gc_in.at[m - 1], (dp, z * cores + t)
-        )
-
-    def over(m):
-        t = lax.rem(dp + m, dps)
-        return send(own.at[t], from_dp.at[m - 1], gd_out.at[m - 1], gd_in.at[m - 1], (t, fs))
-
-    keep = pltpu.make_async_copy(g_ref.at[:, :, c], own, g_local)
-
-    def cores_added():
-        keep.wait()
-        for m in range(1, cores):
-            across(m).wait_recv()
-
-        def add(i, carry):
-            p, q = i // lanes, lax.rem(i, lanes)
-            total = own[p, q].astype(F32)
-            for m in range(1, cores):
-                total = total + from_core[m - 1, p, q].astype(F32)
-            own[p, q] = total.astype(BF)
-            return carry
-
-        lax.fori_loop(0, dps * lanes, add, 0)
-        for m in range(1, dps):
-            over(m).start()
-
-    def dp_added():
-        for m in range(1, dps):
-            over(m).wait_recv()
-        for q in range(lanes):
-            total = own[dp, q].astype(F32)
-            for m in range(1, dps):
-                total = total + from_dp[m - 1, q].astype(F32)
-            total_ref[q] = total.astype(BF)
-        for m in range(1, cores):
-            across(m).wait_send()
-        for m in range(1, dps):
-            over(m).wait_send()
-
+    gradient.begin()
     greet(sequence_peers(dp, fs, fss) + [(lax.rem(dp + m, dps), fs) for m in range(1, dps)])
     chain.begin()
     work.begin()
-    keep.start()
-    for m in range(1, cores):
-        across(m).start()
-    cores_added()
+    gradient.multiply(0)
     for step in range(1, lanes):
         chain.advance(step)
         work.advance(step)
+        if step == 1:
+            gradient.multiply(1)
+    if lanes == 1:
+        gradient.multiply(1)
+    gradient.multiply(2)
     chain.finish()
     work.finish()
-    dp_added()
-
-
-def turn(x, parts, picks, g, lanes, cores):
+    for third in range(3):
+        gradient.collect(third)
+    gradient.finish()
+
+
+def turn(x, parts, picks, slots_in, grads, shard, lanes, cores):
     dps, _, slots, model = parts.shape
     tokens = picks.shape[3]
+    xs, cs = slots_in
+    gu, hid = grads
+    experts = dps * lanes
+    hidden = hid.shape[1]
     dma = pltpu.SemaphoreType.DMA
+    others = max(cores - 1, 1)
     whole = pl.BlockSpec(memory_space=pltpu.VMEM)
     return pl.pallas_call(
         functools.partial(turn_kernel, dps, lanes, cores),
-        in_specs=[ANY, ANY, whole, ANY],
+        in_specs=[ANY, ANY, whole] + [ANY] * 4,
         out_specs=[ANY, whole, whole],
         out_shape=[
             jax.ShapeDtypeStruct((lanes, cores) + x.shape, x.dtype),
             jax.ShapeDtypeStruct((tokens, model), F32),
-            jax.ShapeDtypeStruct((lanes,) + g.shape[3:], BF),
+            jax.ShapeDtypeStruct((experts, shard, 3 * hidden), BF),
         ],
-        scratch_shapes=[
-            pltpu.VMEM((dps, lanes) + g.shape[3:], BF),
-            pltpu.VMEM((max(cores - 1, 1), dps, lanes) + g.shape[3:], BF),
-            pltpu.VMEM((dps - 1, lanes) + g.shape[3:], BF),
-            dma((max(cores - 1, 1),)), dma((max(cores - 1, 1),)), dma((dps - 1,)), dma((dps - 1,)), dma,
+        scratch_shapes=combine_scratch(dps, lanes, slots, tokens, model)
+        + [
+            pltpu.VMEM(xs.shape, BF),
+            pltpu.VMEM(hid.shape, BF),
+            pltpu.VMEM((model, hidden), F32),
+            pltpu.VMEM((3, cores, experts, shard, hidden), BF),
+            pltpu.VMEM((3, others, experts, shard, hidden), BF),
+            dma((2,)), dma((3, others)), dma((3, others)),
         ]
-        + combine_scratch(dps, lanes, slots, tokens, model) + chain_sems(lanes, cores),
-        cost_estimate=lasts(100),
+        + chain_sems(lanes, cores),
+        cost_estimate=lasts(90),
         compiler_params=pltpu.CompilerParams(
             collective_id=1, has_side_effects=True, vmem_limit_bytes=VMEM_LIMIT
         ),
-    )(x, parts, picks, g)
+    )(x, parts, picks, xs, cs, gu, hid)
 
 
 def finish_kernel(
     dps, lanes, cores, busy, part_ref, g_ref, s_ref, out_ref, mix_ref, sum_ref,
-    from_core, stage, inbox, from_dp, total_g, from_z,
-    z_out, z_in, c_out, c_in, g_out, g_in, m_out, m_in, local, s_out, s_in,
+    from_core, stage, inbox, from_dp, total_g, from_z, line_sum,
+    z_out, z_in, c_out, c_in, g_out, g_in, m_out, m_in, local, s_out, s_in, *scratch,
 ):
     dp, fs, z, c = place(cores)
     fss = lanes * cores
+    shared = SharedSum(s_ref, line_sum, scratch, dps, lanes, cores)
     greet(sequence_peers(dp, fs, fss) + [(lax.rem(dp + m, dps), fs) for m in range(1, dps)])
 
     def has_next(side):
@@ -1022,12 +1238,12 @@
 
     def home(k, owner):
         t = lax.rem(fs + k, fss)
-        return send(total_g.at[t], mix_ref.at[owner], m_out.at[k - 1], m_in.at[k - 1], (dp, t))
+        return send(total_g.at[t], mix_ref.at[head_slot(owner, lanes, cores)], m_out.at[k - 1], m_in.at[k - 1], (dp, t))
 
     def along(k):
         t = lax.rem(z + k, lanes)
         return send(
-            s_ref.at[t], from_z.at[k - 1], s_out.at[k - 1], s_in.at[k - 1], (dp, t * cores + c)
+            line_sum.at[t], from_z.at[k - 1], s_out.at[k - 1], s_in.at[k - 1], (dp, t * cores + c)
         )
 
     def goal(side, step):
@@ -1072,12 +1288,13 @@
                 begin(block)
 
     begin(z)
+    shared.begin()
     for m in range(1, dps):
         over(m).start()
     for step in range(1, max(lanes - 1, 1)):
         advance(step)
-    for k in range(1, lanes):
-        along(k).start()
+        if step == 1:
+            shared.add_cores()
     for m in range(1, dps):
         over(m).wait_recv()
     for f in range(fss):
@@ -1085,9 +1302,9 @@
         for m in range(1, dps):
             total = total + from_dp[m - 1, f].astype(F32)
         total_g[f] = total.astype(BF)
-    keep = pltpu.make_async_copy(total_g.at[fs], mix_ref.at[fs], local)
-
-    @pl.when(fs < busy)
+    keep = pltpu.make_async_copy(total_g.at[fs], mix_ref.at[head_slot(fs, lanes, cores)], local)
+
+    @pl.when(head_slot(fs, lanes, cores) < busy)
     def _():
         for k in range(1, fss):
             home(k, fs).start()
@@ -1095,6 +1312,9 @@
 
     if lanes > 1:
         advance(lanes - 1)
+    shared.add_dp()
+    for k in range(1, lanes):
+        along(k).start()
     out_ref[...] = partial_sum(z)
     for side in (0, 1):
         fed = z > 0 if side == 0 else z < lanes - 1
@@ -1104,7 +1324,7 @@
             hop(side, lanes - 1).wait_recv()
             out_ref[...] += inbox[side, lanes - 2].astype(F32)
 
-    total = s_ref[z].astype(F32)
+    total = line_sum[z].astype(F32)
     for k in range(1, lanes):
         along(k).wait_recv()
         total = total + from_z[k - 1].astype(F32)
@@ -1114,11 +1334,11 @@
     for k in range(1, fss):
         owner = lax.rem(fs + fss - k, fss)
 
-        @pl.when(owner < busy)
+        @pl.when(head_slot(owner, lanes, cores) < busy)
         def _():
             home(k, owner).wait_recv()
 
-    @pl.when(fs < busy)
+    @pl.when(head_slot(fs, lanes, cores) < busy)
     def _():
         keep.wait()
         for k in range(1, fss):
@@ -1139,7 +1359,7 @@
         over(m).wait_send()
 
 
-def finish(part, g, g_line, lanes, cores, busy):
+def finish(part, g, g_shared, lanes, cores, busy):
     dps, fss = g.shape[:2]
     tokens, model = part.shape[2:]
     dma = pltpu.SemaphoreType.DMA
@@ -1148,12 +1368,12 @@
     whole = pl.BlockSpec(memory_space=pltpu.VMEM)
     return pl.pallas_call(
         functools.partial(finish_kernel, dps, lanes, cores, busy),
-        in_specs=[whole, whole, whole],
+        in_specs=[whole, whole, ANY],
         out_specs=[whole, ANY, whole],
         out_shape=[
             jax.ShapeDtypeStruct((tokens, model), F32),
             jax.ShapeDtypeStruct((busy,) + g.shape[2:], BF),
-            jax.ShapeDtypeStruct(g_line.shape[1:], F32),
+            jax.ShapeDtypeStruct(g_shared.shape[3:], F32),
         ],
         scratch_shapes=[
             pltpu.VMEM(ways + (tokens, model), BF),
@@ -1161,15 +1381,17 @@
             pltpu.VMEM(hops + (tokens, model), BF),
             pltpu.VMEM((dps - 1,) + g.shape[1:], BF),
             pltpu.VMEM(g.shape[1:], BF),
-            pltpu.VMEM((max(lanes - 1, 1),) + g_line.shape[1:], BF),
+            pltpu.VMEM((max(lanes - 1, 1),) + g_shared.shape[3:], BF),
+            pltpu.VMEM((lanes,) + g_shared.shape[3:], BF),
             dma(hops), dma(hops), dma(ways), dma(ways), dma((dps - 1,)), dma((dps - 1,)),
             dma((fss - 1,)), dma((fss - 1,)), dma, dma((max(lanes - 1, 1),)), dma((max(lanes - 1, 1),)),
-        ],
+        ]
+        + shared_scratch(g_shared, dps, lanes, cores),
         cost_estimate=lasts(66),
         compiler_params=pltpu.CompilerParams(
             collective_id=6, has_side_effects=True, vmem_limit_bytes=VMEM_LIMIT
         ),
-    )(part, g, g_line)
+    )(part, g, g_shared)
 
 
 def per_device(x, w_qkv, w_out, w_shared, w_experts, gains, routes, gates, d_out):
@@ -1192,31 +1414,23 @@
             value, "fsdp", [(a * cores + k, b * cores + k) for a, b in pairs for k in range(cores)]
         )
 
-    def over_core(value, m):
-        return lax.ppermute(
-            value, "fsdp", [(a * cores + k, a * cores + (k ^ m)) for a in range(lanes) for k in range(cores)]
-        )
-
-    def over_dp(value, m):
-        return lax.ppermute(value, "dp", [(a, (a + m) % dps) for a in range(dps)])
-
     cut = w_qkv.reshape(shard, 3, HEADS, HD)
     cut = jnp.pad(cut, ((0, 0), (0, 0), (0, fss * per - HEADS), (0, 0)))
-    cut = cut.reshape(shard, 3, fss, width).transpose(2, 0, 1, 3).reshape(fss, shard, 3 * width)
-    extra = jnp.broadcast_to(jnp.pad(gains, ((0, 0), (0, HD - 2))), (fss, shard, HD))
-    slabs = jnp.concatenate([cut, extra], axis=2)
+    cut = cut.reshape(shard, 3, cores, lanes, width).transpose(3, 2, 0, 1, 4).reshape(fss, shard, 3 * width)
+    w_out_gains = jnp.concatenate([w_out, jnp.pad(gains, ((0, 0), (0, HD - 2)))], axis=1)
     topk = routes.shape[1]
     table = jnp.concatenate([routes.T.astype(F32), gates.T], axis=0)
     table = jnp.pad(table, ((0, -2 * topk % 8), (0, 0)))
-    x_all, slabs, tables, out_all, picks, weigh, c_slots = start(
-        x, slabs, table, w_out, d_out, topk, dps, lanes, cores
+    x_all, slabs, tables, out_all, picks, weigh = start(
+        x, cut, table, w_out_gains, topk, busy, dps, lanes, cores
     )
-    c_slots = c_slots.reshape(-1, model)
     x_all = x_all.reshape(seq, model)
-    slabs = slabs.reshape(model, 3 * width + HD)
-    out_all = out_all.reshape(model, model)
-    w_heads = jnp.where(fs < busy, slabs[:, : 3 * width], 0)
-    gain_rows = slabs[:, 3 * width : 3 * width + 2].astype(F32).T
+    slabs = slabs.reshape(model, 3 * width)
+    out_all = out_all.reshape(model, model + HD)
+    gain_rows = out_all[:, model : model + 2].astype(F32).T
+    out_all = out_all[:, :model]
+    slot = c * lanes + z
+    w_heads = jnp.where(slot < busy, slabs, 0)
     gain_one, gain_two = gain_rows[0:1], gain_rows[1:2]
 
     half = HD // 2
@@ -1239,34 +1453,24 @@
 
     o, lse = attend(q, k, vt, 256)
 
-    heads = heads_home(o, tokens, lanes, cores, busy)[:, :model]
+    heads, shared_all = heads_home(o, w_shared, tokens, dps, lanes, cores, busy)
+    heads = heads[:, :model]
+    shared_all = shared_all.reshape(model, 3 * hidden)
     middle = x.astype(F32) + dot_nt(heads, out_all)
     inv_two = lax.rsqrt(jnp.mean(middle * middle, axis=1, keepdims=True) + norm_eps)
     unit_two = middle * inv_two
     xn_two = (unit_two * gain_two).astype(BF)
 
-    def reduce_cores(part):
-        part = part.reshape(dps, lanes, cores, shard, part.shape[1])
-        at = lambda k: lax.dynamic_index_in_dim(part, k, 2, keepdims=False)
-        total = at(c)
-        for m in range(1, cores):
-            total = total + over_core(at(c ^ m).astype(BF), m).astype(F32)
-        return total
-
-    x_slots, w_own = dispatch(xn_two, picks, rows_here, lanes, cores, 3)
+    x_slots, c_slots, w_own, dx_shared, f_shared, g_shared_part = dispatch(
+        xn_two, d_out, tables, picks, rows_here, shared_all, topk, lanes, cores
+    )
     x_slots = x_slots.reshape(-1, model)
+    c_slots = c_slots.reshape(-1, model)
     w_own = w_own.reshape(model, 3 * hidden)
     dx_slots, gu_slots, hid_slots = expert(x_slots, c_slots, w_own, BF)
 
-    shared_all = lax.all_gather(after(w_shared, heads), ("dp", "fsdp"), axis=0, tiled=True)
-    dx_shared, gu_shared, hid_shared = expert(xn_two, d_out, shared_all, F32)
-    f_shared = dot_nt(hid_shared, shared_all[:, 2 * hidden :])
-
     shape = (dps, lanes, slots, model)
-    g_own = jnp.concatenate([dot_tn(x_slots, gu_slots), dot_tn(c_slots, hid_slots)], axis=1)
-    own = reduce_cores(g_own).astype(BF)
-    dx_routed = combine(after(dx_slots, own).reshape(shape), picks, lanes, cores, 4)
-    f_slots = dot_nt(hid_slots, w_own[:, 2 * hidden :]).astype(BF)
+    dx_routed, f_slots = combine(dx_slots.reshape(shape), picks, hid_slots, w_own, lanes, cores)
     dxn_two = dx_shared + dx_routed
     scaled = dxn_two * gain_two
     dx_two = d_out.astype(F32) + inv_two * (
@@ -1274,13 +1478,13 @@
     )
     d_attn = dx_two.astype(BF)
 
-    g_shared_part = jnp.concatenate([dot_tn(xn_two, gu_shared), dot_tn(d_out, hid_shared)], axis=1)
-    g_shared_part = g_shared_part.astype(BF).reshape(dps, lanes, cores, shard, 3 * hidden)
-    da_all, routed, g_line = turn(d_attn, f_slots.reshape(shape), weigh, g_shared_part, lanes, cores)
+    da_all, routed, g_own = turn(
+        d_attn, f_slots, weigh, (x_slots, c_slots), (gu_slots, hid_slots), shard, lanes, cores
+    )
     da_all = da_all.reshape(seq, model)
     layer_out = (middle + f_shared + routed).astype(BF)
     out_cols = jnp.pad(out_all, ((0, 0), (0, fss * width - model)))
-    out_cols = lax.dynamic_slice_in_dim(out_cols, fs * width, width, 1)
+    out_cols = lax.dynamic_slice_in_dim(out_cols, slot * width, width, 1)
     d_o = dot_nn(da_all, out_cols).astype(BF)
     g_out_part = dot_tn(da_all, o)
     dq, dk, dv = attend_back(q, k, kt, v, o, d_o, lse, cos, sin, 256)
@@ -1288,14 +1492,14 @@
     dxn_part = dot_nt(d_qkv, w_heads).astype(BF).reshape(lanes, cores, tokens, model)
     g_part = jnp.concatenate([dot_tn(xn_one, d_qkv), g_out_part], axis=1).astype(BF)
     g_part = g_part.reshape(dps, fss, shard, 4 * width)
-    dxn_one, g_mix, g_shared = finish(dxn_part, g_part, g_line, lanes, cores, busy)
+    dxn_one, g_mix, g_shared = finish(dxn_part, g_part, g_shared_part, lanes, cores, busy)
     inputs = x.astype(F32)
     inv_one = lax.rsqrt(jnp.mean(inputs * inputs, axis=1, keepdims=True) + norm_eps)
     unit_one = inputs * inv_one
     scaled = dxn_one * gain_one
     d_x = dx_two + inv_one * (scaled - unit_one * jnp.mean(scaled * unit_one, axis=1, keepdims=True))
 
-    g_experts = swap(own.reshape(experts, shard, 3 * hidden)).astype(F32)
+    g_experts = swap(g_own).astype(F32)
 
     g_mix = g_mix.reshape(busy, shard, 4, width).transpose(1, 2, 0, 3).reshape(shard, 4, busy * width)
     g_mix = g_mix[:, :, :model].astype(F32)

time: 860 us -> 737 us (0.86)
  Pallas kernels: 677 us -> 620 us
  matrix products: 60.1 us -> 22.9 us
  other arithmetic: 41.8 us -> 27 us
  between operations: 14.9 us -> 1.33 us
    pallas_call x1, Pallas kernels: 119 us -> 69.6 us  [turn(): pl.pallas_call(functools.partial(turn_kernel, dps, lanes, cores), in_spec...]
    dot_general x6 -> x2, matrix products: 31.8 us -> 8.49 us  [dot_tn(): lax.dot_general(a, b, (((0,), (0,)), ((), ())), preferred_element_type=F32)]
    dot_general x4 -> x2, matrix products: 23 us -> 9.26 us  [dot_nt(): lax.dot_general(a, b, (((1,), (1,)), ((), ())), preferred_element_type=F32)]
    concatenate x3 -> x1, other arithmetic: 9.38 us -> 0.65 us  [per_device(): jnp.concatenate([w_out, jnp.pad(gains, ((0, 0), (0, HD - 2)))], axis=1)]
    pallas_call x2 -> x1, Pallas kernels: 45.1 us -> 36.6 us  [expert(): pl.pallas_call(functools.partial(expert_kernel, hidden), grid=(rows // bl...]
  transfers between devices with their start and end apart: 4 -> 2, of which waited for: 0 -> 0; matrix products, arithmetic and copies ran while one was open for 14% -> 9% of each run, Pallas kernels for 64% -> 35%
where the time goes in v4:
time: 737 us; the launch traced here: 729 us
  Pallas kernels  620 us (84%)
  local copies, waits for them, and re-layouts  30.8 us (4%)
  starting transfers between devices  27.1 us (4%)
  other arithmetic  27 us (4%)
  matrix products  22.9 us (3%)
    pallas_call x1, Pallas kernels, dispatch(): pl.pallas_call(functools.partial(dispatch_kernel, dps, lanes, cores, topk...  128 us
    pallas_call x1, Pallas kernels, heads_home(): pl.pallas_call(functools.partial(heads_kernel, dps, lanes, cores, busy),...  103 us
    pallas_call x1, Pallas kernels, finish(): pl.pallas_call(functools.partial(finish_kernel, dps, lanes, cores, busy),...  93 us
    pallas_call x1, Pallas kernels, turn(): pl.pallas_call(functools.partial(turn_kernel, dps, lanes, cores), in_spec...  69.6 us
    pallas_call x1, Pallas kernels, combine(): pl.pallas_call(functools.partial(combine_kernel, dps, lanes, cores), in_s...  66.5 us
    pallas_call x1, Pallas kernels, start(): pl.pallas_call(functools.partial(start_kernel, dps, lanes, cores, topk, b...  65.2 us
    pallas_call x1, Pallas kernels, expert(): pl.pallas_call(functools.partial(expert_kernel, hidden), grid=(rows // bl...  36.6 us
    all_to_all x2, starting transfers between devices, swap(): lax.all_to_all(value, ('dp', 'fsdp'), split_axis=0, concat_axis=0, tiled=...  27.1 us
  transfers between devices with their start and end apart: 2, of which 0 were waited for; matrix products, arithmetic and copies ran while one was open for 9% of the time, Pallas kernels for 35%

profile of v4, /device:TPU:20, one launch (start us, length us, event | category | flops | bytes accessed | tf_op | source)
XLA Modules:
  0.0 729.0 jit_solution(17104046388147160449)
XLA Ops:
  6.6 65.2 %shard_map.144 = (bf16[4,2,256,1280]{3,2,1,0:T(8,128)(2,1)}, bf16[4,8,40,768]{3,2,1,0:T(8,128)(2,1)}, f32[4,16,256]{2,1,0:T(8,128)}, bf16[4,4,2,40,1408]{4,3,2,1...) custom-call(bf16[256,1280]{1,0:T(8,128)(2,1)} %x_ref.1, ...), custom_call_target="tpu_custom_call" | custom-call | bytes 252000000 | tf_op jit(solution)/shard_map/pallas_call | solution.py:649
  71.7 17.9 %all-to-all-start = ((bf16[16,40,2688]{2,1,0:T(8,128)(2,1)}), bf16[16,40,2688]{2,1,0:T(8,128)(2,1)}, u32[]{:S(2)}, u32[]{:S(2)}) async-start(bf16[16,40,2688]{2,1,0:T(8,128)(2,1)} %param.13), calls=%async_computation | async-start | bytes 6881280 | tf_op jit(solution)/shard_map/all_to_all | solution.py:1448
  89.7 3.8 slice.42
  95.4 3.7 fusion.9
  99.1 1.9 pad_maximum_fusion.1
  102.5 14.3 %shard_map.145 = (bf16[2048,1280]{1,0:T(8,128)(2,1)}, bf16[2048,256]{1,0:T(8,128)(2,1)}, bf16[2048,256]{1,0:T(8,128)(2,1)}, bf16[2048,256]{1,0:T(8,128)(2,1)}, b...) custom-call(bf16[2048,1280]{1,0:T(8,128)(2,1)} %bitcast.57, f32[1,1280]{1,0:T(1,128)} %get-tuple-element.85.gain_ref, ...), custom_call_target="tpu_custom_call" | custom-call | bytes 50400000 | tf_op jit(solution)/shard_map/pallas_call | solution.py:86
  116.8 18.4 %shard_map.146 = (bf16[2048,256]{1,0:T(8,128)(2,1)}, f32[2,1,2048]{2,1,0:T(1,128)}) custom-call(bf16[2048,256]{1,0:T(8,128)(2,1)} %get-tuple-element.47.q_ref, bf16[2048,256]{1,0:T(8,128)(2,1)} %get-tuple-element.48.k_ref, bf16[256,2048]{1,0:T(8,128)(2,1)} %get-tuple-element.49.vt_ref), custom_call_target="tpu_custom_call" | custom-call | bytes 64800000 | tf_op jit(solution)/shard_map/pallas_call | solution.py:140
  135.2 102.5 %shard_map.147 = (bf16[256,1280]{1,0:T(8,128)(2,1)}, bf16[4,4,2,40,2688]{4,3,2,1,0:T(8,128)(2,1)}) custom-call(bf16[2048,256]{1,0:T(8,128)(2,1)} %get-tuple-element.50.o_ref, bf16[40,2688]{1,0:T(8,128)(2,1)} %sh_ref.1), custom_call_target="tpu_custom_call" | custom-call | bytes 162000000 | tf_op jit(solution)/shard_map/pallas_call | solution.py:712
  238.0 3.3 multiply_reduce_fusion.1
  242.3 128.2 %shard_map.148 = (bf16[4,4,128,1280]{3,2,1,0:T(8,128)(2,1)}, bf16[4,4,128,1280]{3,2,1,0:T(8,128)(2,1)}, bf16[4,4,2,40,2688]{4,3,2,1,0:T(8,128)(2,1)}, f32[256,12...) custom-call(bf16[256,1280]{1,0:T(8,128)(2,1)} %multiply_convert_fusion.x_ref, ...), custom_call_target="tpu_custom_call" | custom-call | bytes 450000000 | tf_op jit(solution)/shard_map/pallas_call | solution.py:828
  370.5 36.6 %shard_map.149 = (bf16[2048,1280]{1,0:T(8,128)(2,1)}, bf16[2048,1792]{1,0:T(8,128)(2,1)}, bf16[2048,896]{1,0:T(8,128)(2,1)}) custom-call(bf16[2048,1280]{1,0:T(8,128)(2,1)} %bitcast.49, bf16[2048,1280]{1,0:T(8,128)(2,1)} %bitcast.51, bf16[1280,2688]{1,0:T(8,128)(2,1)} %bitcast.47), custom_call_target="tpu_custom_call" | custom-call | bytes 132710400 | tf_op jit(solution)/shard_map/pallas_call | solution.py:257
  407.1 66.5 %shard_map.150 = (f32[256,1280]{1,0:T(8,128)}, bf16[4,4,128,1280]{3,2,1,0:T(8,128)(2,1)}) custom-call(bf16[4,4,128,1280]{3,2,1,0:T(8,128)(2,1)} %bitcast.61, bf16[4,4,128,256]{3,2,1,0:T(8,128)(2,1)} %get-tuple-element.53.pick_ref, bf16[2048,896]{1,0:T(8,128)(2,1)} %get-tuple-element.62.hid_ref, bf16[1280,2688]{1,0:T(8,128)(2,1)} %bitcast.48), custom_call_target="tpu_custom_call" | custom-call | bytes 252000000 | tf_op jit(solution)/shard_map/pallas_call | solution.py:1066
  473.7 1.8 multiply_reduce_fusion
  475.5 1.7 fusion.15
  477.3 69.6 %shard_map.151 = (bf16[4,2,256,1280]{3,2,1,0:T(8,128)(2,1)}, f32[256,1280]{1,0:T(8,128)}, bf16[16,40,2688]{2,1,0:T(8,128)(2,1)}) custom-call(bf16[256,1280]{1,0:T(8,128)(2,1)} %get-tuple-element.83.x_ref, bf16[4,4,128,1280]{3,2,1,0:T(8,128)(2,1)} %get-tuple-element.64.part_ref, bf16[4,4,128,256]{3,2,1,0:T(8,128)(2,1)} %get-tuple-element.65.pick_ref, ...), custom_call_target="tpu_custom_call" | custom-call | bytes 324000000 | tf_op jit(solution)/shard_map/pallas_call | solution.py:1183
  546.9 9.2 %all-to-all-start.1 = ((bf16[16,40,2688]{2,1,0:T(8,128)(2,1)}), bf16[16,40,2688]{2,1,0:T(8,128)(2,1)}, u32[]{:S(2)}, u32[]{:S(2)}) async-start(bf16[16,40,2688]{2,1,0:T(8,128)(2,1)} %get-tuple-element.80), calls=%async_computation.1 | async-start | bytes 6881280 | tf_op jit(solution)/shard_map/all_to_all | solution.py:1448
  556.0 5.2 convolution_convert_fusion.2.do_ref
  561.2 8.0 %copy.23 = bf16[1280,2048]{1,0:T(8,128)(2,1)} copy(bf16[1280,2048]{0,1:T(8,128)(2,1)} %bitcast.60) | data formatting | bytes 10485760 | tf_op jit(solution)/shard_map/dot_general | solution.py:29
  569.2 25.5 %shard_map.152 = (bf16[2048,256]{1,0:T(8,128)(2,1)}, bf16[2048,256]{1,0:T(8,128)(2,1)}, bf16[2048,256]{1,0:T(8,128)(2,1)}) custom-call(bf16[2048,256]{1,0:T(8,128)(2,1)} %get-tuple-element.47.q_ref, bf16[2048,256]{1,0:T(8,128)(2,1)} %get-tuple-element.48.k_ref, bf16[256,2048]{1,0:T(8,128)(2,1)} %get-tuple-element.68.kt_ref, ...), custom_call_target="tpu_custom_call" | custom-call | bytes 90000000 | tf_op jit(solution)/shard_map/pallas_call | solution.py:217
  594.6 1.4 constant_dynamic-update-slice_fusion.2
  596.1 1.7 constant_dynamic-update-slice_fusion.1
  599.1 1.7 convolution_convert_fusion.3
  600.8 6.8 convolution_convert_fusion.1
  607.6 1.8 pad_maximum_fusion.g_ref
  609.7 6.0 convolution_convert_fusion
  615.7 93.0 %shard_map.153 = (f32[256,1280]{1,0:T(8,128)}, bf16[5,40,1024]{2,1,0:T(8,128)(2,1)}, f32[40,2688]{1,0:T(8,128)}) custom-call(bf16[4,2,256,1280]{3,2,1,0:T(8,128)(2,1)} %bitcast.56, bf16[4,8,40,1024]{3,2,1,0:T(8,128)(2,1)} %pad_maximum_fusion.g_ref, bf16[4,4,2,40,2688]{4,3,2,1,0:T(8,128)(2,1)} %get-tuple-element.76.s_ref), custom_call_target="tpu_custom_call" | custom-call | bytes 237600000 | tf_op jit(solution)/shard_map/pallas_call | solution.py:1369
  708.7 2.3 reshape.132
  710.9 1.7 copy.31
  715.9 1.9 slice_bitcast_fusion.1
  719.3 1.4 fusion.6
  720.8 2.5 convert_element_type.95
  723.3 4.0 fusion
  (74 shorter events, 18.2 us)
Async XLA Ops:
  3.2 2.1 copy-start.18
  3.3 2.7 copy-start.17
  71.7 170.6 %all-to-all-start = ((bf16[16,40,2688]{2,1,0:T(8,128)(2,1)}), bf16[16,40,2688]{2,1,0:T(8,128)(2,1)}, u32[]{:S(2)}, u32[]{:S(2)}) async-start(bf16[16,40,2688]{2,1,0:T(8,128)(2,1)} %param.13), calls=%async_computation | async-start | bytes 6881280 | tf_op jit(solution)/shard_map/all_to_all | solution.py:1448
  99.1 1.9 copy-start.11
  116.8 121.0 %copy-start.1 = (bf16[256,1280]{1,0:T(8,128)(2,1)S(1)}, bf16[256,1280]{1,0:T(8,128)(2,1)}, u32[]{:S(2)}) copy-start(bf16[256,1280]{1,0:T(8,128)(2,1)} %x_ref.1) | copy-start | bytes 1966084
  407.1 66.5 %copy-start.4 = (f32[256,1280]{1,0:T(8,128)S(1)}, f32[256,1280]{1,0:T(8,128)}, u32[]{:S(2)}) copy-start(f32[256,1280]{1,0:T(8,128)} %get-tuple-element.57) | copy-start | bytes 3932164
  473.6 1.8 copy-start.5
  473.6 1.9 copy-start.9
  546.9 173.9 %all-to-all-start.1 = ((bf16[16,40,2688]{2,1,0:T(8,128)(2,1)}), bf16[16,40,2688]{2,1,0:T(8,128)(2,1)}, u32[]{:S(2)}, u32[]{:S(2)}) async-start(bf16[16,40,2688]{2,1,0:T(8,128)(2,1)} %get-tuple-element.80), calls=%async_computation.1 | async-start | bytes 6881280 | tf_op jit(solution)/shard_map/all_to_all | solution.py:1448
  594.6 4.5 copy-start.3
  596.1 3.0 copy-start.8
  607.6 2.0 copy-start.2
  712.6 2.5 copy-start.16
  713.8 1.3 copy-start.15
  713.8 1.5 copy-start.14
  713.8 1.7 copy-start.6
  715.1 3.7 copy-start.10
  715.2 2.6 copy-start.12
  715.2 2.6 copy-start.13
  717.8 1.6 copy-start.7
  723.3 4.1 copy-start
  723.3 4.1 copy-start.19

commit v5 on v4

--- a/solution.py
+++ b/solution.py
@@ -3,6 +3,7 @@
 
 import jax
 import jax.numpy as jnp
+import numpy as np
 from jax import lax
 from jax.experimental import pallas as pl
 from jax.experimental.pallas import tpu as pltpu
@@ -33,73 +34,6 @@
     return pl.CostEstimate(flops=0, bytes_accessed=int(us * 3.6e6), transcendentals=0)
 
 
-def after(value, *marks):
-    return lax.optimization_barrier((value,) + marks)[0]
-
-
-def put(buffer, value, *index):
-    rest = buffer.ndim - len(index)
-    starts = tuple(index) + (0,) * rest
-    return lax.dynamic_update_slice(
-        buffer, value.reshape((1,) * len(index) + buffer.shape[len(index) :]), starts
-    )
-
-
-def take(values, index):
-    return lax.dynamic_index_in_dim(values, index, 0, keepdims=False)
-
-
-def proj_kernel(x_ref, gain_ref, w_ref, cos_ref, sin_ref, xn_ref, q_ref, k_ref, v_ref, kt_ref, vt_ref):
-    x = x_ref[...].astype(F32)
-    inv = lax.rsqrt(jnp.mean(x * x, axis=1, keepdims=True) + norm_eps)
-    xn = (x * inv * gain_ref[...]).astype(BF)
-    xn_ref[...] = xn
-    width = q_ref.shape[1]
-    cos = cos_ref[...]
-    sin = sin_ref[...]
-    for part in range(3):
-        for head in range(width // HD):
-            lo = part * width + head * HD
-            u = dot_nn(xn, w_ref[:, lo : lo + HD])
-            cols = slice(head * HD, (head + 1) * HD)
-            if part < 2:
-                u = u * cos + pltpu.roll(u, HD // 2, 1) * sin
-            low = u.astype(BF)
-            if part == 0:
-                q_ref[:, cols] = low
-            elif part == 1:
-                k_ref[:, cols] = low
-                kt_ref[cols, :] = u.T.astype(BF)
-            else:
-                v_ref[:, cols] = low
-                vt_ref[cols, :] = u.T.astype(BF)
-
-
-def project(x_all, gain, w, cos, sin, seq):
-    model = x_all.shape[1]
-    width = w.shape[1] // 3
-    block = 256
-    row = lambda cols: pl.BlockSpec((block, cols), lambda i: (i, 0))
-    col = pl.BlockSpec((width, block), lambda i: (0, i))
-    flat = jax.ShapeDtypeStruct((seq, width), BF)
-    turned = jax.ShapeDtypeStruct((width, seq), BF)
-    return pl.pallas_call(
-        proj_kernel,
-        grid=(seq // block,),
-        in_specs=[
-            row(model),
-            pl.BlockSpec((1, model), lambda i: (0, 0)),
-            pl.BlockSpec(w.shape, lambda i: (0, 0)),
-            row(HD),
-            row(HD),
-        ],
-        out_specs=[row(model), row(width), row(width), row(width), col, col],
-        out_shape=[jax.ShapeDtypeStruct((seq, model), BF), flat, flat, flat, turned, turned],
-        compiler_params=pltpu.CompilerParams(vmem_limit_bytes=VMEM_LIMIT),
-        cost_estimate=lasts(14),
-    )(x_all, gain, w, cos, sin)
-
-
 def causal(rows):
     shape = (rows, rows)
     key = lax.broadcasted_iota(jnp.int32, shape, 0)
@@ -107,132 +41,14 @@
     return key <= query
 
 
-def attend_kernel(block, count, scale, q_ref, k_ref, vt_ref, o_ref, lse_ref):
-    step = pl.program_id(1)
-    for j in range(count):
-
-        @pl.when(step == j)
-        def _():
-            whole = j * block
-            q = q_ref[...]
-            tail = dot_nt(k_ref[whole : whole + block, :], q) * scale
-            tail = jnp.where(causal(block), tail, masked_score)
-            top = jnp.max(tail, axis=0, keepdims=True)
-            if j:
-                front = dot_nt(k_ref[:whole, :], q) * scale
-                top = jnp.maximum(top, jnp.max(front, axis=0, keepdims=True))
-            tail = jnp.exp(tail - top)
-            total = jnp.sum(tail, axis=0, keepdims=True)
-            mixed = dot_nn(vt_ref[:, whole : whole + block], tail.astype(BF))
-            if j:
-                front = jnp.exp(front - top)
-                total = total + jnp.sum(front, axis=0, keepdims=True)
-                mixed = mixed + dot_nn(vt_ref[:, :whole], front.astype(BF))
-            o_ref[...] = (mixed / total).T.astype(BF)
-            lse_ref[0] = top + jnp.log(total)
-
-
-def attend(q, k, vt, block):
-    seq, width = q.shape
-    count = seq // block
-    heads = width // HD
-    scale = 1.0 / math.sqrt(HD)
-    return pl.pallas_call(
-        functools.partial(attend_kernel, block, count, scale),
-        grid=(heads, count),
-        in_specs=[
-            pl.BlockSpec((block, HD), lambda h, i: (i, h)),
-            pl.BlockSpec((seq, HD), lambda h, i: (0, h)),
-            pl.BlockSpec((HD, seq), lambda h, i: (h, 0)),
-        ],
-        out_specs=[
-            pl.BlockSpec((block, HD), lambda h, i: (i, h)),
-            pl.BlockSpec((1, 1, block), lambda h, i: (h, 0, i)),
-        ],
-        out_shape=[
-            jax.ShapeDtypeStruct((seq, width), BF),
-            jax.ShapeDtypeStruct((heads, 1, seq), F32),
-        ],
-        compiler_params=pltpu.CompilerParams(vmem_limit_bytes=VMEM_LIMIT),
-        cost_estimate=lasts(18),
-    )(q, k, vt)
-
-
 def unrotate(g, cos, sin):
     return g * cos - pltpu.roll(g, HD // 2, 1) * sin
 
 
-def attend_back_kernel(
-    block, count, scale,
-    q_ref, k_ref, kt_ref, v_ref, o_ref, do_ref, lse_ref, cos_ref, sin_ref,
-    dq_ref, dk_ref, dv_ref, dk_acc, dv_acc,
-):
-    step = pl.program_id(1)
-
-    @pl.when(step == 0)
-    def _():
-        dk_acc[...] = jnp.zeros_like(dk_acc)
-        dv_acc[...] = jnp.zeros_like(dv_acc)
-
-    for j in range(count):
-
-        @pl.when(step == j)
-        def _():
-            wide = (j + 1) * block
-            here = slice(j * block, wide)
-            q = q_ref[...]
-            do = do_ref[...]
-            row = jnp.sum((do.astype(F32) * o_ref[...].astype(F32)).T, axis=0, keepdims=True)
-            lse = lse_ref[0]
-            parts = [(slice(0, j * block), False)] if j else []
-            parts.append((here, True))
-            dq = None
-            for span, edge in parts:
-                p = jnp.exp(dot_nt(k_ref[span, :], q) * scale - lse)
-                if edge:
-                    p = jnp.where(causal(block), p, 0.0)
-                ds = (p * (dot_nt(v_ref[span, :], do) - row)).astype(BF)
-                dv_acc[span, :] += dot_nn(p.astype(BF), do)
-                dk_acc[span, :] += dot_nn(ds, q)
-                term = dot_nn(kt_ref[:, span], ds)
-                dq = term if dq is None else dq + term
-            dq_ref[...] = unrotate(dq.T * scale, cos_ref[here, :], sin_ref[here, :]).astype(BF)
-
-    @pl.when(step == count - 1)
-    def _():
-        dk_ref[...] = unrotate(dk_acc[...] * scale, cos_ref[...], sin_ref[...]).astype(BF)
-        dv_ref[...] = dv_acc[...].astype(BF)
-
-
-def attend_back(q, k, kt, v, o, do, lse, cos, sin, block):
-    seq, width = q.shape
-    count = seq // block
-    heads = width // HD
-    scale = 1.0 / math.sqrt(HD)
-    piece = pl.BlockSpec((block, HD), lambda h, i: (i, h))
-    whole = pl.BlockSpec((seq, HD), lambda h, i: (0, h))
-    turned = pl.BlockSpec((HD, seq), lambda h, i: (h, 0))
-    table = pl.BlockSpec((seq, HD), lambda h, i: (0, 0))
-    flat = jax.ShapeDtypeStruct((seq, width), BF)
-    return pl.pallas_call(
-        functools.partial(attend_back_kernel, block, count, scale),
-        grid=(heads, count),
-        in_specs=[
-            piece, whole, turned, whole, piece, piece,
-            pl.BlockSpec((1, 1, block), lambda h, i: (h, 0, i)), table, table,
-        ],
-        out_specs=[piece, whole, whole],
-        out_shape=[flat, flat, flat],
-        scratch_shapes=[pltpu.VMEM((seq, HD), F32), pltpu.VMEM((seq, HD), F32)],
-        compiler_params=pltpu.CompilerParams(vmem_limit_bytes=VMEM_LIMIT),
-        cost_estimate=lasts(25),
-    )(q, k, kt, v, o, do, lse, cos, sin)
-
-
-def feed(x, c, w_ref, hidden):
+def feed(x, c, w_ref, down_ref, hidden):
     gate = dot_nn(x, w_ref[:, :hidden])
     up = dot_nn(x, w_ref[:, hidden : 2 * hidden])
-    down = dot_nn(c, w_ref[:, 2 * hidden :])
+    down = dot_nn(c, down_ref[...])
     sig = 1.0 / (1.0 + jnp.exp(-gate))
     act = gate * sig
     dup = (down * act).astype(BF)
@@ -241,23 +57,28 @@
     return dx, dgate, dup, (act * up).astype(BF)
 
 
-def expert_kernel(hidden, x_ref, c_ref, w_ref, dx_ref, gu_ref, hid_ref):
-    dx, dgate, dup, hid = feed(x_ref[...], c_ref[...], w_ref, hidden)
+def expert_kernel(hidden, x_ref, c_ref, w_ref, down_ref, dx_ref, gu_ref, hid_ref):
+    dx, dgate, dup, hid = feed(x_ref[...], c_ref[...], w_ref, down_ref, hidden)
     dx_ref[...] = dx.astype(dx_ref.dtype)
     gu_ref[:, :hidden] = dgate
     gu_ref[:, hidden:] = dup
     hid_ref[...] = hid
 
 
-def expert(x, c, w, kind):
+def expert(x, c, w, down, kind):
     rows, model = x.shape
-    hidden = w.shape[1] // 3
-    block = min(256, rows)
+    hidden = down.shape[1]
+    block = min(512, rows)
     row = lambda cols: pl.BlockSpec((block, cols), lambda i: (i, 0))
     return pl.pallas_call(
         functools.partial(expert_kernel, hidden),
         grid=(rows // block,),
-        in_specs=[row(model), row(model), pl.BlockSpec(w.shape, lambda i: (0, 0))],
+        in_specs=[
+            row(model),
+            row(model),
+            pl.BlockSpec(w.shape, lambda i: (0, 0)),
+            pl.BlockSpec(down.shape, lambda i: (0, 0)),
+        ],
         out_specs=[row(model), row(2 * hidden), row(hidden)],
         out_shape=[
             jax.ShapeDtypeStruct((rows, model), kind),
@@ -266,7 +87,7 @@
         ],
         compiler_params=pltpu.CompilerParams(vmem_limit_bytes=VMEM_LIMIT),
         cost_estimate=lasts(0.018 * rows),
-    )(x, c, w)
+    )(x, c, w, down)
 
 
 MESH = pl.DeviceIdType.MESH
@@ -538,12 +359,13 @@
 
 
 def start_kernel(
-    dps, lanes, cores, topk, busy, x_ref, wh_ref, tab_ref, wo_ref,
-    full_ref, heads_ref, tabs_ref, out_ref, pick_ref, weigh_ref,
+    dps, lanes, cores, topk, busy, x_ref, wh_ref, tab_ref, wo_ref, gn_ref,
+    full_ref, heads_ref, tabs_ref, out_ref, gains_ref, pick_ref, weigh_ref,
     h_out, h_in, hd_out, hd_in, t_out, t_in, locals_, *sems,
 ):
     rows = Rows(wo_ref, out_ref, dps, lanes, cores, sems[:7])
-    chain = Chain(x_ref, full_ref, lanes, cores, sems[7:])
+    gains = Rows(gn_ref, gains_ref, dps, lanes, cores, sems[7:14])
+    chain = Chain(x_ref, full_ref, lanes, cores, sems[14:])
     dp, fs, z, c = chain.dp, chain.fs, chain.z, chain.c
     fss = lanes * cores
     slots, tokens = pick_ref.shape[2:]
@@ -579,6 +401,7 @@
 
     for k in range(1, lanes):
         table_to(k).start()
+    gains.begin()
     rows.begin()
     for copy in kept:
         copy.wait()
@@ -591,6 +414,7 @@
         for m in range(1, dps):
             heads_over(m, dp).start()
 
+    gains.to_dp()
     rows.to_dp()
     for step in range(2, lanes):
         chain.advance(step)
@@ -613,8 +437,10 @@
             pick_ref[m, block] = jnp.where(match, 1.0, 0.0).astype(BF)
             weigh_ref[m, block] = jnp.where(match, gate, 0.0).astype(BF)
 
+    gains.to_cores()
     rows.to_cores()
     chain.finish()
+    gains.finish()
     rows.finish()
     for k in range(1, fss):
 
@@ -632,7 +458,7 @@
             heads_over(m, dp).wait_send()
 
 
-def start(x, wh, table, w_out, topk, busy, dps, lanes, cores):
+def start(x, wh, table, w_out, gains, topk, busy, dps, lanes, cores):
     fss = lanes * cores
     tokens = x.shape[0]
     dma = pltpu.SemaphoreType.DMA
@@ -643,29 +469,153 @@
         jax.ShapeDtypeStruct((dps,) + wh.shape, wh.dtype),
         jax.ShapeDtypeStruct((lanes,) + table.shape, table.dtype),
         jax.ShapeDtypeStruct((dps, lanes, cores) + w_out.shape, w_out.dtype),
+        jax.ShapeDtypeStruct((dps, lanes, cores) + gains.shape, gains.dtype),
         picks,
         picks,
     ]
     return pl.pallas_call(
         functools.partial(start_kernel, dps, lanes, cores, topk, busy),
-        in_specs=[ANY] * 4,
-        out_specs=[ANY, ANY, whole, ANY, whole, whole],
+        in_specs=[ANY] * 5,
+        out_specs=[ANY, ANY, whole, ANY, ANY, whole, whole],
         out_shape=shapes,
         scratch_shapes=pair(fss) + pair(dps) + pair(lanes) + [dma((2,))]
-        + rows_sems(dps, lanes, cores) + chain_sems(lanes, cores),
+        + rows_sems(dps, lanes, cores) * 2 + chain_sems(lanes, cores),
         cost_estimate=lasts(70),
         compiler_params=pltpu.CompilerParams(
             collective_id=0, has_side_effects=True, vmem_limit_bytes=VMEM_LIMIT
         ),
-    )(x, wh, table, w_out)
-
-
-def heads_kernel(dps, lanes, cores, busy, o_ref, sh_ref, mix_ref, all_ref, out, came, local, *sems):
+    )(x, wh, table, w_out, gains)
+
+
+class Slabs:
+    def __init__(self, source, columns, target, dps, lanes, cores, sems):
+        self.source, self.columns, self.target = source, columns, target
+        self.lanes, self.cores, self.experts = lanes, cores, dps * lanes
+        self.out, self.came, self.local = sems
+        self.dp, self.fs, self.z, self.c = place(cores)
+        self.me = self.dp * lanes + self.z
+
+    def peer(self, k):
+        e = lax.rem(self.me + k, self.experts)
+        return (e // self.lanes, lax.rem(e, self.lanes) * self.cores + self.c)
+
+    def to(self, k):
+        e = lax.rem(self.me + k, self.experts)
+        return send(
+            self.source.at[e, :, self.columns], self.target.at[self.dp, self.z], self.out.at[k - 1],
+            self.came.at[k - 1], self.peer(k),
+        )
+
+    def keep(self):
+        return pltpu.make_async_copy(
+            self.source.at[self.me, :, self.columns], self.target.at[self.dp, self.z], self.local
+        )
+
+    def begin(self):
+        for k in range(1, self.experts):
+            self.to(k).start()
+        self.keep().start()
+
+    def arrive(self):
+        self.keep().wait()
+        for k in range(1, self.experts):
+            self.to(k).wait_recv()
+
+    def finish(self):
+        for k in range(1, self.experts):
+            self.to(k).wait_send()
+
+
+def slab_sems(experts):
+    return pair(experts) + [pltpu.SemaphoreType.DMA]
+
+
+def layer_peers(slabs):
+    others = [
+        (slabs.dp, lax.rem(slabs.z + a, slabs.lanes) * slabs.cores + lax.rem(slabs.c + m, slabs.cores))
+        for a in range(slabs.lanes)
+        for m in range(1, slabs.cores)
+    ]
+    return [slabs.peer(k) for k in range(1, slabs.experts)] + others
+
+
+def attend_kernel(
+    dps, lanes, cores, busy, block, scale,
+    x_ref, gain_ref, w_ref, cos_ref, sin_ref, we_ref, sh_ref,
+    xn_ref, q_ref, k_ref, v_ref, kt_ref, vt_ref, o_ref, lse_ref, mix_ref, all_ref, rows_ref, low_ref,
+    out, came, local, *sems,
+):
     dp, fs, z, c = place(cores)
     fss = lanes * cores
     tokens, width = mix_ref.shape[0], o_ref.shape[1]
-    shared = Rows(sh_ref, all_ref, dps, lanes, cores, sems)
-    greet(sequence_peers(dp, fs, fss) + [(lax.rem(dp + m, dps), fs) for m in range(1, dps)])
+    seq = x_ref.shape[0]
+    up_width, low_width = rows_ref.shape[3], low_ref.shape[3]
+    slabs = Slabs(we_ref, pl.ds(0, up_width), rows_ref, dps, lanes, cores, sems[:3])
+    low_slabs = Slabs(we_ref, pl.ds(up_width, low_width), low_ref, dps, lanes, cores, sems[3:6])
+    shared = Rows(sh_ref, all_ref, dps, lanes, cores, sems[6:])
+    greet(layer_peers(slabs))
+    shared.begin()
+    slabs.begin()
+
+    def project(i, carry):
+        rows = pl.ds(pl.multiple_of(i * block, block), block)
+        x = x_ref[rows, :].astype(F32)
+        inv = lax.rsqrt(jnp.mean(x * x, axis=1, keepdims=True) + norm_eps)
+        xn = (x * inv * gain_ref[...]).astype(BF)
+        xn_ref[rows, :] = xn
+        cos, sin = cos_ref[rows, :], sin_ref[rows, :]
+        for part in range(3):
+            wide = dot_nn(xn, w_ref[:, part * width : (part + 1) * width])
+            for head in range(width // HD):
+                cols = slice(head * HD, (head + 1) * HD)
+                u = wide[:, cols]
+                if part < 2:
+                    u = u * cos + pltpu.roll(u, HD // 2, 1) * sin
+                low = u.astype(BF)
+                if part == 0:
+                    q_ref[rows, cols] = low
+                elif part == 1:
+                    k_ref[rows, cols] = low
+                    kt_ref[cols, rows] = u.T.astype(BF)
+                else:
+                    v_ref[rows, cols] = low
+                    vt_ref[cols, rows] = u.T.astype(BF)
+        return carry
+
+    mine = head_slot(fs, lanes, cores) < busy
+
+    @pl.when(mine)
+    def _():
+        lax.fori_loop(0, seq // block, project, 0)
+
+    shared.to_dp()
+
+    def head_rows(h, carry):
+        cols = pl.ds(pl.multiple_of(h * HD, HD), HD)
+        for j in range(seq // block):
+            whole = j * block
+            here = slice(whole, whole + block)
+            q = q_ref[here, cols]
+            tail = dot_nt(k_ref[here, cols], q) * scale
+            tail = jnp.where(causal(block), tail, masked_score)
+            top = jnp.max(tail, axis=0, keepdims=True)
+            if j:
+                front = dot_nt(k_ref[:whole, cols], q) * scale
+                top = jnp.maximum(top, jnp.max(front, axis=0, keepdims=True))
+            tail = jnp.exp(tail - top)
+            total = jnp.sum(tail, axis=0, keepdims=True)
+            mixed = dot_nn(vt_ref[cols, here], tail.astype(BF))
+            if j:
+                front = jnp.exp(front - top)
+                total = total + jnp.sum(front, axis=0, keepdims=True)
+                mixed = mixed + dot_nn(vt_ref[cols, :whole], front.astype(BF))
+            o_ref[here, cols] = (mixed / total).T.astype(BF)
+            lse_ref[h, :, here] = top + jnp.log(total)
+        return carry
+
+    @pl.when(mine)
+    def _():
+        lax.fori_loop(0, width // HD, head_rows, 0)
 
     def columns(f):
         slot = head_slot(f, lanes, cores)
@@ -679,7 +629,6 @@
         return send(rows(t), columns(owner), out.at[k - 1], came.at[k - 1], (dp, t))
 
     keep = pltpu.make_async_copy(rows(fs), columns(fs), local)
-    shared.begin()
 
     @pl.when(head_slot(fs, lanes, cores) < busy)
     def _():
@@ -687,15 +636,14 @@
             to(k, fs).start()
         keep.start()
 
-    shared.to_dp()
+    low_slabs.begin()
+    shared.to_cores()
     for k in range(1, fss):
         owner = lax.rem(fs + fss - k, fss)
 
         @pl.when(head_slot(owner, lanes, cores) < busy)
         def _():
             to(k, owner).wait_recv()
-
-    shared.to_cores()
 
     @pl.when(head_slot(fs, lanes, cores) < busy)
     def _():
@@ -704,23 +652,42 @@
             to(k, fs).wait_send()
 
     shared.finish()
-
-
-def heads_home(o, w_shared, tokens, dps, lanes, cores, busy):
+    slabs.arrive()
+    slabs.finish()
+    low_slabs.arrive()
+    low_slabs.finish()
+
+
+def attend(x_all, gain, w, cos, sin, w_experts, w_shared, tokens, busy, dps, lanes, cores):
+    seq, model = x_all.shape
+    width = w.shape[1] // 3
+    experts, shard, thrice = w_experts.shape
+    block = seq // 8
     fss = lanes * cores
     dma = pltpu.SemaphoreType.DMA
+    whole = pl.BlockSpec(memory_space=pltpu.VMEM)
+    flat = jax.ShapeDtypeStruct((seq, width), BF)
+    turned = jax.ShapeDtypeStruct((width, seq), BF)
     return pl.pallas_call(
-        functools.partial(heads_kernel, dps, lanes, cores, busy),
-        in_specs=[ANY, ANY],
-        out_specs=[ANY, ANY],
+        functools.partial(attend_kernel, dps, lanes, cores, busy, block, 1.0 / math.sqrt(HD)),
+        in_specs=[whole] * 5 + [ANY, ANY],
+        out_specs=[whole] * 8 + [ANY] * 4,
         out_shape=[
-            jax.ShapeDtypeStruct((tokens, busy * o.shape[1]), o.dtype),
-            jax.ShapeDtypeStruct((dps, lanes, cores) + w_shared.shape, w_shared.dtype),
+            jax.ShapeDtypeStruct((seq, model), BF),
+            flat, flat, flat, turned, turned, flat,
+            jax.ShapeDtypeStruct((width // HD, 1, seq), F32),
+            jax.ShapeDtypeStruct((tokens, busy * width), BF),
+            jax.ShapeDtypeStruct((dps, lanes, cores) + w_shared.shape, BF),
+            jax.ShapeDtypeStruct((dps, lanes, shard, thrice // 3 * 2), BF),
+            jax.ShapeDtypeStruct((dps, lanes, shard, thrice // 3), BF),
         ],
-        scratch_shapes=[dma((fss - 1,)), dma((fss - 1,)), dma] + rows_sems(dps, lanes, cores),
-        cost_estimate=lasts(45),
-        compiler_params=pltpu.CompilerParams(collective_id=2, has_side_effects=True),
-    )(o, w_shared)
+        scratch_shapes=[dma((fss - 1,)), dma((fss - 1,)), dma]
+        + slab_sems(experts) * 2 + rows_sems(dps, lanes, cores),
+        cost_estimate=lasts(100),
+        compiler_params=pltpu.CompilerParams(
+            collective_id=2, has_side_effects=True, vmem_limit_bytes=VMEM_LIMIT
+        ),
+    )(x_all, gain, w, cos, sin, w_experts, w_shared)
 
 
 def greet_cross(line, dps, cores=1):
@@ -742,21 +709,27 @@
 
 
 def dispatch_kernel(
-    dps, lanes, cores, topk, x_ref, up_ref, tabs_ref, pick_ref, rows_ref, shared_ref,
-    out_ref, c_ref, w_ref, dx_ref, f_ref, g_ref, acts, acc, buffer, stage, up_buffer, up_stage, l_out, l_in, s_out, s_in, s_local,
-    ul_out, ul_in, us_out, us_in, us_local, w_out, w_in, w_local,
+    dps, lanes, cores, topk, x_ref, up_ref, tabs_ref, pick_ref, rows_ref, low_ref, shared_ref,
+    out_ref, c_ref, w_ref, wd_ref, dx_ref, f_ref, g_ref, acts, acc, buffer, stage, up_buffer, up_stage, l_out, l_in, s_out, s_in, s_local,
+    ul_out, ul_in, us_out, us_in, us_local, w_out, w_in, w_local, wd_out, wd_in, wd_local,
 ):
     line = Line(x_ref, buffer, lanes, cores, l_out, l_in)
     spread = Spread(stage, out_ref, dps, lanes, cores, s_out, s_in, s_local)
     up_line = Line(up_ref, up_buffer, lanes, cores, ul_out, ul_in)
     up_spread = Spread(up_stage, c_ref, dps, lanes, cores, us_out, us_in, us_local)
+    hidden = shared_ref.shape[1] // 3
     greet_cross(line, dps, cores)
 
     def across(m, core):
         peer = (line.dp, line.z * cores + lax.rem(line.c + m, cores))
         return send(rows_ref, w_ref.at[:, :, core], w_out.at[m - 1], w_in.at[m - 1], peer)
 
+    def across_down(m, core):
+        peer = (line.dp, line.z * cores + lax.rem(line.c + m, cores))
+        return send(low_ref, wd_ref.at[:, :, core], wd_out.at[m - 1], wd_in.at[m - 1], peer)
+
     keep = pltpu.make_async_copy(rows_ref, w_ref.at[:, :, line.c], w_local)
+    keep_down = pltpu.make_async_copy(low_ref, wd_ref.at[:, :, line.c], wd_local)
 
     def pick(block, source):
         for m in spread.order():
@@ -778,18 +751,20 @@
     up_line.begin()
     up_pick(line.z, up_ref)
     keep.start()
+    keep_down.start()
     for m in range(1, cores):
         across(m, line.c).start()
-    hidden = shared_ref.shape[1] // 3
+        across_down(m, line.c).start()
     experts, shard = dps * lanes, g_ref.shape[3]
 
     def shared_forward():
-        dx, gate, up, hid = feed(x_ref[...], up_ref[...], shared_ref, hidden)
+        down_ref = shared_ref.at[:, 2 * hidden :]
+        dx, gate, up, hid = feed(x_ref[...], up_ref[...], shared_ref, down_ref, hidden)
         dx_ref[...] = dx
         acts[0] = gate
         acts[1] = up
         acts[2] = hid
-        f_ref[...] = dot_nt(hid, shared_ref[:, 2 * hidden :])
+        f_ref[...] = dot_nt(hid, down_ref[...])
 
     def shared_gradient(third):
         acc[...] = dot_tn((x_ref if third < 2 else up_ref)[...], acts[third])
@@ -811,14 +786,18 @@
     up_spread.finish()
     up_line.finish()
     keep.wait()
+    keep_down.wait()
     for m in range(1, cores):
         across(m, lax.rem(line.c + cores - m, cores)).wait_recv()
         across(m, line.c).wait_send()
-
-
-def dispatch(x, upstream, tables, picks, rows, shared, topk, lanes, cores):
+        across_down(m, lax.rem(line.c + cores - m, cores)).wait_recv()
+        across_down(m, line.c).wait_send()
+
+
+def dispatch(x, upstream, tables, picks, rows, low, shared, topk, lanes, cores):
     dps, _, slots, tokens = picks.shape
     model = x.shape[1]
+    shard, hidden = low.shape[2:]
     dma = pltpu.SemaphoreType.DMA
     hops = (2, max(lanes - 1, 1))
     ways = (dps - 1, lanes)
@@ -827,26 +806,27 @@
     moves = [dma(hops), dma(hops), dma(ways), dma(ways), dma((lanes,))]
     return pl.pallas_call(
         functools.partial(dispatch_kernel, dps, lanes, cores, topk),
-        in_specs=[whole] * 4 + [ANY, whole],
-        out_specs=[ANY, ANY, ANY, whole, whole, whole],
+        in_specs=[whole] * 4 + [ANY, ANY, whole],
+        out_specs=[ANY] * 4 + [whole] * 3,
         out_shape=[
             jax.ShapeDtypeStruct((dps, lanes, slots, model), BF),
             jax.ShapeDtypeStruct((dps, lanes, slots, model), BF),
             jax.ShapeDtypeStruct((dps, lanes, cores) + rows.shape[2:], BF),
+            jax.ShapeDtypeStruct((dps, lanes, cores, shard, hidden), BF),
             jax.ShapeDtypeStruct((tokens, model), F32),
             jax.ShapeDtypeStruct((tokens, model), F32),
-            jax.ShapeDtypeStruct((dps, lanes, cores) + rows.shape[2:], BF),
+            jax.ShapeDtypeStruct((dps, lanes, cores, shard, 3 * hidden), BF),
         ],
         scratch_shapes=[
             pltpu.VMEM((3, tokens, shared.shape[1] // 3), BF),
             pltpu.VMEM((model, shared.shape[1] // 3), F32),
         ]
-        + buffers * 2 + moves * 2 + pair(cores) + [dma],
+        + buffers * 2 + moves * 2 + (pair(cores) + [dma]) * 2,
         cost_estimate=lasts(125),
         compiler_params=pltpu.CompilerParams(
             collective_id=3, has_side_effects=True, vmem_limit_bytes=VMEM_LIMIT
         ),
-    )(x, upstream, tables, picks, rows, shared)
+    )(x, upstream, tables, picks, rows, low, shared)
 
 
 class Combine:
@@ -958,74 +938,6 @@
     ]
 
 
-class SharedSum:
-    def __init__(self, source, total, scratch, dps, lanes, cores):
-        self.source, self.total = source, total
-        self.own, self.from_core, self.from_dp = scratch[:3]
-        self.c_out, self.c_in, self.d_out, self.d_in, self.local = scratch[3:]
-        self.dps, self.lanes, self.cores = dps, lanes, cores
-        self.dp, self.fs, self.z, self.c = place(cores)
-
-    def across(self, m):
-        t = lax.rem(self.c + m, self.cores)
-        return send(
-            self.source.at[:, :, t], self.from_core.at[m - 1], self.c_out.at[m - 1], self.c_in.at[m - 1],
-            (self.dp, self.z * self.cores + t),
-        )
-
-    def over(self, m):
-        t = lax.rem(self.dp + m, self.dps)
-        return send(
-            self.own.at[t], self.from_dp.at[m - 1], self.d_out.at[m - 1], self.d_in.at[m - 1], (t, self.fs)
-        )
-
-    def keep(self):
-        return pltpu.make_async_copy(self.source.at[:, :, self.c], self.own, self.local)
-
-    def begin(self):
-        self.keep().start()
-        for m in range(1, self.cores):
-            self.across(m).start()
-
-    def add_cores(self):
-        self.keep().wait()
-        for m in range(1, self.cores):
-            self.across(m).wait_recv()
-
-        def add(i, carry):
-            p, q = i // self.lanes, lax.rem(i, self.lanes)
-            total = self.own[p, q].astype(F32)
-            for m in range(1, self.cores):
-                total = total + self.from_core[m - 1, p, q].astype(F32)
-            self.own[p, q] = total.astype(BF)
-            return carry
-
-        lax.fori_loop(0, self.dps * self.lanes, add, 0)
-        for m in range(1, self.dps):
-            self.over(m).start()
-
-    def add_dp(self):
-        for m in range(1, self.dps):
-            self.over(m).wait_recv()
-        for q in range(self.lanes):
-            total = self.own[self.dp, q].astype(F32)
-            for m in range(1, self.dps):
-                total = total + self.from_dp[m - 1, q].astype(F32)
-            self.total[q] = total.astype(BF)
-        for m in range(1, self.cores):
-            self.across(m).wait_send()
-        for m in range(1, self.dps):
-            self.over(m).wait_send()
-
-
-def shared_scratch(g, dps, lanes, cores):
-    return [
-        pltpu.VMEM((dps, lanes) + g.shape[3:], BF),
-        pltpu.VMEM((max(cores - 1, 1), dps, lanes) + g.shape[3:], BF),
-        pltpu.VMEM((dps - 1, lanes) + g.shape[3:], BF),
-    ] + pair(cores) + pair(dps) + [pltpu.SemaphoreType.DMA]
-
-
 def combine_kernel(
     dps, lanes, cores, part_ref, pick_ref, hid_ref, w_ref, out_ref, f_ref, hid, down, load, *scratch
 ):
@@ -1034,7 +946,7 @@
     slots = f_ref.shape[2]
     loads = [
         pltpu.make_async_copy(hid_ref, hid, load.at[0]),
-        pltpu.make_async_copy(w_ref.at[:, 2 * hidden :], down, load.at[1]),
+        pltpu.make_async_copy(w_ref, down, load.at[1]),
     ]
     for copy in loads:
         copy.start()
@@ -1149,9 +1061,8 @@
     )
     chain = Chain(x_ref, full_ref, lanes, cores, scratch[16:])
     dp, fs = chain.dp, chain.fs
-    fss = lanes * cores
     gradient.begin()
-    greet(sequence_peers(dp, fs, fss) + [(lax.rem(dp + m, dps), fs) for m in range(1, dps)])
+    greet(sequence_peers(dp, fs, lanes * cores) + [(lax.rem(dp + m, dps), fs) for m in range(1, dps)])
     chain.begin()
     work.begin()
     gradient.multiply(0)
@@ -1206,14 +1117,228 @@
     )(x, parts, picks, xs, cs, gu, hid)
 
 
+class LineSum:
+    def __init__(self, source, total, scratch, dps, lanes, cores):
+        self.source, self.total = source, total
+        self.own, self.from_core, self.from_dp = scratch[:3]
+        self.c_out, self.c_in, self.d_out, self.d_in, self.local = scratch[3:]
+        self.dps, self.lanes, self.cores = dps, lanes, cores
+        self.dp, self.fs, self.z, self.c = place(cores)
+
+    def across(self, m):
+        t = lax.rem(self.c + m, self.cores)
+        return send(
+            self.source.at[:, :, t], self.from_core.at[m - 1], self.c_out.at[m - 1], self.c_in.at[m - 1],
+            (self.dp, self.z * self.cores + t),
+        )
+
+    def over(self, m):
+        t = lax.rem(self.dp + m, self.dps)
+        return send(
+            self.own.at[t], self.from_dp.at[m - 1], self.d_out.at[m - 1], self.d_in.at[m - 1], (t, self.fs)
+        )
+
+    def keep(self):
+        return pltpu.make_async_copy(self.source.at[:, :, self.c], self.own, self.local)
+
+    def begin(self):
+        self.keep().start()
+        for m in range(1, self.cores):
+            self.across(m).start()
+
+    def add(self):
+        self.keep().wait()
+        for m in range(1, self.cores):
+            self.across(m).wait_recv()
+
+        def add(i, carry):
+            p, q = i // self.lanes, lax.rem(i, self.lanes)
+            total = self.own[p, q].astype(F32)
+            for m in range(1, self.cores):
+                total = total + self.from_core[m - 1, p, q].astype(F32)
+            self.own[p, q] = total.astype(BF)
+            return carry
+
+        lax.fori_loop(0, self.dps * self.lanes, add, 0)
+        for m in range(1, self.dps):
+            self.over(m).start()
+
+    def add_dp(self):
+        for m in range(1, self.dps):
+            self.over(m).wait_recv()
+        for q in range(self.lanes):
+            total = self.own[self.dp, q].astype(F32)
+            for m in range(1, self.dps):
+                total = total + self.from_dp[m - 1, q].astype(F32)
+            self.total[q] = total.astype(BF)
+        for m in range(1, self.cores):
+            self.across(m).wait_send()
+        for m in range(1, self.dps):
+            self.over(m).wait_send()
+
+
+def attend_back_kernel(
+    dps, lanes, cores, busy, block, scale,
+    da_ref, xn_ref, out_ref, q_ref, k_ref, kt_ref, v_ref, o_ref, lse_ref, cos_ref, sin_ref, w_ref, g_ref,
+    part_ref, prod_ref, line_ref, left, d_ref, acc, stage, cols, do_all, dk_acc, dv_acc,
+    load, stored, *scratch,
+):
+    dp, fs, z, c = place(cores)
+    shared = LineSum(g_ref, line_ref, scratch, dps, lanes, cores)
+    seq, width = q_ref.shape
+    tokens = part_ref.shape[2]
+    slot = jnp.minimum(head_slot(fs, lanes, cores), busy - 1)
+    fetch = pltpu.make_async_copy(
+        out_ref.at[:, pl.ds(pl.multiple_of(slot * width, HD), width)], cols, load.at[0]
+    )
+    fetch.start()
+    first, second = [pltpu.make_async_copy(ref, left, load.at[1]) for ref in (da_ref, xn_ref)]
+    first.start()
+    shard = prod_ref.shape[2]
+
+    def place_rows(lo, hi):
+        for p in range(dps):
+            for f in range(lanes * cores):
+                row = (p * lanes * cores + f) * shard
+                prod_ref[p, f, :, lo:hi] = acc[row : row + shard, : hi - lo].astype(BF)
+
+    greet(
+        [(lax.rem(dp + m, dps), fs) for m in range(1, dps)]
+        + [(dp, z * cores + lax.rem(c + m, cores)) for m in range(1, cores)]
+    )
+    shared.begin()
+    fetch.wait()
+    first.wait()
+
+    def upstream(i, carry):
+        rows = pl.ds(pl.multiple_of(i * block, block), block)
+        do_all[rows, :] = dot_nn(left[rows, :], cols[...]).astype(BF)
+        return carry
+
+    mine = head_slot(fs, lanes, cores) < busy
+
+    @pl.when(mine)
+    def _():
+        lax.fori_loop(0, seq // block, upstream, 0)
+
+    shared.add()
+
+    @pl.when(mine)
+    def _():
+        acc[:, :width] = dot_tn(left[...], o_ref[...])
+        place_rows(3 * width, 4 * width)
+
+    second.start()
+
+    def head_rows(h, carry):
+        lane = pl.ds(pl.multiple_of(h * HD, HD), HD)
+        k_lane = pl.ds(pl.multiple_of(width + h * HD, HD), HD)
+        v_lane = pl.ds(pl.multiple_of(2 * width + h * HD, HD), HD)
+        dk_acc[...] = jnp.zeros_like(dk_acc)
+        dv_acc[...] = jnp.zeros_like(dv_acc)
+        for j in range(seq // block):
+            here = slice(j * block, (j + 1) * block)
+            q = q_ref[here, lane]
+            do = do_all[here, lane]
+            row = jnp.sum((do.astype(F32) * o_ref[here, lane].astype(F32)).T, axis=0, keepdims=True)
+            lse = lse_ref[h, :, here]
+            dq = None
+            for span, edge in ([(slice(0, j * block), False)] if j else []) + [(here, True)]:
+                p = jnp.exp(dot_nt(k_ref[span, lane], q) * scale - lse)
+                if edge:
+                    p = jnp.where(causal(block), p, 0.0)
+                ds = (p * (dot_nt(v_ref[span, lane], do) - row)).astype(BF)
+                dv_acc[span, :] += dot_nn(p.astype(BF), do)
+                dk_acc[span, :] += dot_nn(ds, q)
+                term = dot_nn(kt_ref[lane, span], ds)
+                dq = term if dq is None else dq + term
+            d_ref[here, lane] = unrotate(dq.T * scale, cos_ref[here, :], sin_ref[here, :]).astype(BF)
+        d_ref[:, k_lane] = unrotate(dk_acc[...] * scale, cos_ref[...], sin_ref[...]).astype(BF)
+        d_ref[:, v_lane] = dv_acc[...].astype(BF)
+        return carry
+
+    @pl.when(mine)
+    def _():
+        lax.fori_loop(0, width // HD, head_rows, 0)
+
+    blocks = [(a, b) for a in range(lanes) for b in range(cores)]
+    saves = [
+        pltpu.make_async_copy(stage.at[n % 2], part_ref.at[a, b], stored.at[n % 2])
+        for n, (a, b) in enumerate(blocks)
+    ]
+    for n in range(len(blocks)):
+        if n >= 2:
+            saves[n - 2].wait()
+
+        @pl.when(mine)
+        def _():
+            stage[n % 2] = dot_nt(d_ref[n * tokens : (n + 1) * tokens, :], w_ref[...]).astype(BF)
+
+        @pl.when(jnp.logical_not(mine))
+        def _():
+            stage[n % 2] = jnp.zeros(stage.shape[1:], BF)
+
+        saves[n].start()
+    second.wait()
+
+    @pl.when(mine)
+    def _():
+        acc[...] = dot_tn(left[...], d_ref[...])
+        place_rows(0, 3 * width)
+
+    for save in saves[-2:]:
+        save.wait()
+    shared.add_dp()
+
+
+def attend_back(da_all, xn, out_all, saved, tables, w, g, tokens, busy, dps, lanes, cores):
+    q, k, kt, v, o, lse = saved
+    cos, sin = tables
+    seq, width = q.shape
+    model = w.shape[0]
+    block = 256
+    dma = pltpu.SemaphoreType.DMA
+    whole = pl.BlockSpec(memory_space=pltpu.VMEM)
+    return pl.pallas_call(
+        functools.partial(attend_back_kernel, dps, lanes, cores, busy, block, 1.0 / math.sqrt(HD)),
+        in_specs=[ANY] * 3 + [whole] * 9 + [ANY],
+        out_specs=[ANY, whole, whole],
+        out_shape=[
+            jax.ShapeDtypeStruct((lanes, cores, tokens, model), BF),
+            jax.ShapeDtypeStruct((dps, lanes * cores, g.shape[3], 4 * width), BF),
+            jax.ShapeDtypeStruct((lanes,) + g.shape[3:], BF),
+        ],
+        scratch_shapes=[
+            pltpu.VMEM((seq, model), BF),
+            pltpu.VMEM((seq, 3 * width), BF),
+            pltpu.VMEM((model, 3 * width), F32),
+            pltpu.VMEM((2, tokens, model), BF),
+            pltpu.VMEM((model, width), BF),
+            pltpu.VMEM((seq, width), BF),
+            pltpu.VMEM((seq, HD), F32),
+            pltpu.VMEM((seq, HD), F32),
+            dma((2,)),
+            dma((2,)),
+            pltpu.VMEM((dps, lanes) + g.shape[3:], BF),
+            pltpu.VMEM((max(cores - 1, 1), dps, lanes) + g.shape[3:], BF),
+            pltpu.VMEM((dps - 1, lanes) + g.shape[3:], BF),
+        ]
+        + pair(cores) + pair(dps) + [dma],
+        cost_estimate=lasts(50),
+        compiler_params=pltpu.CompilerParams(
+            collective_id=5, has_side_effects=True, vmem_limit_bytes=VMEM_LIMIT
+        ),
+    )(da_all, xn, out_all, q, k, kt, v, o, lse, cos, sin, w, g)
+
+
 def finish_kernel(
-    dps, lanes, cores, busy, part_ref, g_ref, s_ref, out_ref, mix_ref, sum_ref,
-    from_core, stage, inbox, from_dp, total_g, from_z, line_sum,
-    z_out, z_in, c_out, c_in, g_out, g_in, m_out, m_in, local, s_out, s_in, *scratch,
+    dps, lanes, cores, busy, part_ref, g_ref, line_sum, x_ref, gain_ref, dx_ref, wq_ref,
+    out_ref, gq_ref, go_ref, sum_ref, one_ref, mix_ref,
+    from_core, stage, inbox, from_dp, total_g, from_z,
+    z_out, z_in, c_out, c_in, g_out, g_in, m_out, m_in, local, s_out, s_in,
 ):
     dp, fs, z, c = place(cores)
     fss = lanes * cores
-    shared = SharedSum(s_ref, line_sum, scratch, dps, lanes, cores)
     greet(sequence_peers(dp, fs, fss) + [(lax.rem(dp + m, dps), fs) for m in range(1, dps)])
 
     def has_next(side):
@@ -1288,13 +1413,12 @@
                 begin(block)
 
     begin(z)
-    shared.begin()
     for m in range(1, dps):
         over(m).start()
+    for k in range(1, lanes):
+        along(k).start()
     for step in range(1, max(lanes - 1, 1)):
         advance(step)
-        if step == 1:
-            shared.add_cores()
     for m in range(1, dps):
         over(m).wait_recv()
     for f in range(fss):
@@ -1312,9 +1436,6 @@
 
     if lanes > 1:
         advance(lanes - 1)
-    shared.add_dp()
-    for k in range(1, lanes):
-        along(k).start()
     out_ref[...] = partial_sum(z)
     for side in (0, 1):
         fed = z > 0 if side == 0 else z < lanes - 1
@@ -1344,6 +1465,25 @@
         for k in range(1, fss):
             home(k, fs).wait_send()
 
+    model = out_ref.shape[1]
+    width = mix_ref.shape[2] // 4
+    one = None
+    for slot in range(busy):
+        lo = slot * width
+        wide = min(width, model - lo)
+        for p in range(3):
+            piece = mix_ref[slot, :, p * width : p * width + wide].astype(F32)
+            gq_ref[:, p * model + lo : p * model + lo + wide] = piece
+            weight = wq_ref[:, p * model + lo : p * model + lo + wide].astype(F32)
+            term = jnp.sum(weight * piece, axis=1, keepdims=True)
+            one = term if one is None else one + term
+        go_ref[:, lo : lo + wide] = mix_ref[slot, :, 3 * width : 3 * width + wide].astype(F32)
+    one_ref[...] = one
+    x = x_ref[...].astype(F32)
+    inv = lax.rsqrt(jnp.mean(x * x, axis=1, keepdims=True) + norm_eps)
+    unit = x * inv
+    scaled = out_ref[...] * gain_ref[...]
+    out_ref[...] = dx_ref[...] + inv * (scaled - unit * jnp.mean(scaled * unit, axis=1, keepdims=True))
     for step in range(1, lanes):
         for side in (0, 1):
             block, there = goal(side, step)
@@ -1359,7 +1499,7 @@
         over(m).wait_send()
 
 
-def finish(part, g, g_shared, lanes, cores, busy):
+def finish(part, g, g_line, x, gain, dx, w_qkv, lanes, cores, busy):
     dps, fss = g.shape[:2]
     tokens, model = part.shape[2:]
     dma = pltpu.SemaphoreType.DMA
@@ -1368,30 +1508,31 @@
     whole = pl.BlockSpec(memory_space=pltpu.VMEM)
     return pl.pallas_call(
         functools.partial(finish_kernel, dps, lanes, cores, busy),
-        in_specs=[whole, whole, ANY],
-        out_specs=[whole, ANY, whole],
+        in_specs=[whole] * 7,
+        out_specs=[whole] * 5,
         out_shape=[
             jax.ShapeDtypeStruct((tokens, model), F32),
-            jax.ShapeDtypeStruct((busy,) + g.shape[2:], BF),
-            jax.ShapeDtypeStruct(g_shared.shape[3:], F32),
+            jax.ShapeDtypeStruct(w_qkv.shape, F32),
+            jax.ShapeDtypeStruct((w_qkv.shape[0], model), F32),
+            jax.ShapeDtypeStruct(g_line.shape[1:], F32),
+            jax.ShapeDtypeStruct((w_qkv.shape[0], 1), F32),
         ],
         scratch_shapes=[
+            pltpu.VMEM((busy,) + g.shape[2:], BF),
             pltpu.VMEM(ways + (tokens, model), BF),
             pltpu.VMEM(hops + (tokens, model), BF),
             pltpu.VMEM(hops + (tokens, model), BF),
             pltpu.VMEM((dps - 1,) + g.shape[1:], BF),
             pltpu.VMEM(g.shape[1:], BF),
-            pltpu.VMEM((max(lanes - 1, 1),) + g_shared.shape[3:], BF),
-            pltpu.VMEM((lanes,) + g_shared.shape[3:], BF),
+            pltpu.VMEM((max(lanes - 1, 1),) + g_line.shape[1:], BF),
             dma(hops), dma(hops), dma(ways), dma(ways), dma((dps - 1,)), dma((dps - 1,)),
             dma((fss - 1,)), dma((fss - 1,)), dma, dma((max(lanes - 1, 1),)), dma((max(lanes - 1, 1),)),
-        ]
-        + shared_scratch(g_shared, dps, lanes, cores),
+        ],
         cost_estimate=lasts(66),
         compiler_params=pltpu.CompilerParams(
             collective_id=6, has_side_effects=True, vmem_limit_bytes=VMEM_LIMIT
         ),
-    )(part, g, g_shared)
+    )(part, g, g_line, x, gain, dx, w_qkv)
 
 
 def per_device(x, w_qkv, w_out, w_shared, w_experts, gains, routes, gates, d_out):
@@ -1417,60 +1558,49 @@
     cut = w_qkv.reshape(shard, 3, HEADS, HD)
     cut = jnp.pad(cut, ((0, 0), (0, 0), (0, fss * per - HEADS), (0, 0)))
     cut = cut.reshape(shard, 3, cores, lanes, width).transpose(3, 2, 0, 1, 4).reshape(fss, shard, 3 * width)
-    w_out_gains = jnp.concatenate([w_out, jnp.pad(gains, ((0, 0), (0, HD - 2)))], axis=1)
+    wide_gains = jnp.pad(gains, ((0, 0), (0, HD - 2)))
     topk = routes.shape[1]
     table = jnp.concatenate([routes.T.astype(F32), gates.T], axis=0)
     table = jnp.pad(table, ((0, -2 * topk % 8), (0, 0)))
-    x_all, slabs, tables, out_all, picks, weigh = start(
-        x, cut, table, w_out_gains, topk, busy, dps, lanes, cores
+    x_all, slabs, tables, out_all, gains_all, picks, weigh = start(
+        x, cut, table, w_out, wide_gains, topk, busy, dps, lanes, cores
     )
     x_all = x_all.reshape(seq, model)
     slabs = slabs.reshape(model, 3 * width)
-    out_all = out_all.reshape(model, model + HD)
-    gain_rows = out_all[:, model : model + 2].astype(F32).T
-    out_all = out_all[:, :model]
-    slot = c * lanes + z
-    w_heads = jnp.where(slot < busy, slabs, 0)
+    out_all = out_all.reshape(model, model)
+    gain_rows = gains_all.reshape(model, HD)[:, :2].astype(F32).T
+    w_heads = slabs
     gain_one, gain_two = gain_rows[0:1], gain_rows[1:2]
 
     half = HD // 2
-    frequency = 10000.0 ** (-jnp.arange(half, dtype=F32) / half)
-    angles = jnp.arange(seq, dtype=jnp.int32).astype(F32)[:, None] * frequency[None, :]
-    cosine, sine = jnp.cos(angles), jnp.sin(angles)
-    cos = jnp.concatenate([cosine, cosine], axis=1)
-    sin = jnp.concatenate([-sine, sine], axis=1)
-
-    xn_one, q, k, v, kt, vt = project(x_all, gain_one, w_heads, cos, sin, seq)
-
-    groups = [[e * cores + k for e in range(experts)] for k in range(cores)]
-
-    def swap(value):
-        return lax.all_to_all(
-            value, ("dp", "fsdp"), split_axis=0, concat_axis=0, tiled=True, axis_index_groups=groups
-        )
-
-    rows_here = swap(after(w_experts, x_all)).reshape(dps, lanes, shard, 3 * hidden)
-
-    o, lse = attend(q, k, vt, 256)
-
-    heads, shared_all = heads_home(o, w_shared, tokens, dps, lanes, cores, busy)
+    frequency = np.float32(10000.0) ** (-np.arange(half, dtype=np.float32) / np.float32(half))
+    angles = np.arange(seq, dtype=np.float32)[:, None] * frequency[None, :]
+    cosine, sine = np.cos(angles), np.sin(angles)
+    cos = jnp.asarray(np.concatenate([cosine, cosine], axis=1), F32)
+    sin = jnp.asarray(np.concatenate([-sine, sine], axis=1), F32)
+
+    xn_one, q, k, v, kt, vt, o, lse, heads, shared_all, rows_here, rows_low = attend(
+        x_all, gain_one, w_heads, cos, sin, w_experts, w_shared, tokens, busy, dps, lanes, cores
+    )
     heads = heads[:, :model]
     shared_all = shared_all.reshape(model, 3 * hidden)
+
     middle = x.astype(F32) + dot_nt(heads, out_all)
     inv_two = lax.rsqrt(jnp.mean(middle * middle, axis=1, keepdims=True) + norm_eps)
     unit_two = middle * inv_two
     xn_two = (unit_two * gain_two).astype(BF)
 
-    x_slots, c_slots, w_own, dx_shared, f_shared, g_shared_part = dispatch(
-        xn_two, d_out, tables, picks, rows_here, shared_all, topk, lanes, cores
+    x_slots, c_slots, w_own, w_down, dx_shared, f_shared, g_shared_part = dispatch(
+        xn_two, d_out, tables, picks, rows_here, rows_low, shared_all, topk, lanes, cores
     )
     x_slots = x_slots.reshape(-1, model)
     c_slots = c_slots.reshape(-1, model)
-    w_own = w_own.reshape(model, 3 * hidden)
-    dx_slots, gu_slots, hid_slots = expert(x_slots, c_slots, w_own, BF)
+    w_own = w_own.reshape(model, 2 * hidden)
+    w_down = w_down.reshape(model, hidden)
+    dx_slots, gu_slots, hid_slots = expert(x_slots, c_slots, w_own, w_down, BF)
 
     shape = (dps, lanes, slots, model)
-    dx_routed, f_slots = combine(dx_slots.reshape(shape), picks, hid_slots, w_own, lanes, cores)
+    dx_routed, f_slots = combine(dx_slots.reshape(shape), picks, hid_slots, w_down, lanes, cores)
     dxn_two = dx_shared + dx_routed
     scaled = dxn_two * gain_two
     dx_two = d_out.astype(F32) + inv_two * (
@@ -1483,35 +1613,24 @@
     )
     da_all = da_all.reshape(seq, model)
     layer_out = (middle + f_shared + routed).astype(BF)
-    out_cols = jnp.pad(out_all, ((0, 0), (0, fss * width - model)))
-    out_cols = lax.dynamic_slice_in_dim(out_cols, slot * width, width, 1)
-    d_o = dot_nn(da_all, out_cols).astype(BF)
-    g_out_part = dot_tn(da_all, o)
-    dq, dk, dv = attend_back(q, k, kt, v, o, d_o, lse, cos, sin, 256)
-    d_qkv = jnp.concatenate([dq, dk, dv], axis=1)
-    dxn_part = dot_nt(d_qkv, w_heads).astype(BF).reshape(lanes, cores, tokens, model)
-    g_part = jnp.concatenate([dot_tn(xn_one, d_qkv), g_out_part], axis=1).astype(BF)
-    g_part = g_part.reshape(dps, fss, shard, 4 * width)
-    dxn_one, g_mix, g_shared = finish(dxn_part, g_part, g_shared_part, lanes, cores, busy)
-    inputs = x.astype(F32)
-    inv_one = lax.rsqrt(jnp.mean(inputs * inputs, axis=1, keepdims=True) + norm_eps)
-    unit_one = inputs * inv_one
-    scaled = dxn_one * gain_one
-    d_x = dx_two + inv_one * (scaled - unit_one * jnp.mean(scaled * unit_one, axis=1, keepdims=True))
-
-    g_experts = swap(g_own).astype(F32)
-
-    g_mix = g_mix.reshape(busy, shard, 4, width).transpose(1, 2, 0, 3).reshape(shard, 4, busy * width)
-    g_mix = g_mix[:, :, :model].astype(F32)
-    g_qkv = g_mix[:, :3].reshape(shard, 3 * model)
-    g_out = g_mix[:, 3]
-
-    one = jnp.sum(w_qkv.astype(F32) * g_qkv, axis=1)
+    dxn_part, g_part, g_line = attend_back(
+        da_all, xn_one, out_all, (q, k, kt, v, o, lse), (cos, sin), w_heads, g_shared_part,
+        tokens, busy, dps, lanes, cores,
+    )
+    d_x, g_qkv, g_out, g_shared, one = finish(
+        dxn_part, g_part, g_line, x, gain_one, dx_two, w_qkv, lanes, cores, busy
+    )
+
+    groups = [[e * cores + k for e in range(experts)] for k in range(cores)]
+    g_experts = lax.all_to_all(
+        g_own, ("dp", "fsdp"), split_axis=0, concat_axis=0, tiled=True, axis_index_groups=groups
+    ).astype(F32)
+
     two = jnp.sum(w_shared[:, : 2 * hidden].astype(F32) * g_shared[:, : 2 * hidden], axis=1)
     two = two + jnp.sum(
         w_experts[:, :, : 2 * hidden].astype(F32) * g_experts[:, :, : 2 * hidden], axis=(0, 2)
     )
-    g_gains = jnp.stack([one, two], axis=1) / gains.astype(F32)
+    g_gains = jnp.concatenate([one, two[:, None]], axis=1) / gains.astype(F32)
     return (layer_out, d_x, g_qkv, g_out, g_shared, g_experts, g_gains)
 
 

time: 737 us -> 707 us (0.959)
  Pallas kernels: 620 us -> 659 us
  matrix products: 22.9 us -> 3.27 us
  starting transfers between devices: 27.1 us -> 8.64 us
  local copies, waits for them, and re-layouts: 30.8 us -> 12.7 us
  other arithmetic: 27 us -> 14.1 us
    pallas_call x4 -> x2, Pallas kernels: 161 us -> 216 us  [the longest x1 134 us: attend(): pl.pallas_call(functools.partial(attend_kernel, dps, lanes, cores, busy,...]
    all_to_all x2 -> x1, starting transfers between devices: 27.1 us -> 8.64 us  [per_device(): lax.all_to_all(g_own, ('dp', 'fsdp'), split_axis=0, concat_axis=0, tiled=...]
    pallas_call x1, Pallas kernels: 93 us -> 78.8 us  [finish(): pl.pallas_call(functools.partial(finish_kernel, dps, lanes, cores, busy),...]
    dot_general x3 -> x0, matrix products: 13.7 us -> none  [the longest x2 8.49 us: dot_tn(): lax.dot_general(a, b, (((0,), (0,)), ((), ())), preferred_element_type=F32)]
    dot_general x1 -> x0, local copies, waits for them, and re-layouts: 7.96 us -> none  [dot_tn(): lax.dot_general(a, b, (((0,), (0,)), ((), ())), preferred_element_type=F32)]
  transfers between devices with their start and end apart: 2 -> 1, of which waited for: 0 -> 0; matrix products, arithmetic and copies ran while one was open for 9% -> 1% of each run, Pallas kernels for 35% -> 23%
where the time goes in v5:
time: 707 us; the launch traced here: 699 us
  Pallas kernels  659 us (93%)
  other arithmetic  14.1 us (2%)
  local copies, waits for them, and re-layouts  12.7 us (2%)
  starting transfers between devices  8.64 us (1%)
    pallas_call x1, Pallas kernels, attend(): pl.pallas_call(functools.partial(attend_kernel, dps, lanes, cores, busy,...  134 us
    pallas_call x1, Pallas kernels, dispatch(): pl.pallas_call(functools.partial(dispatch_kernel, dps, lanes, cores, topk...  125 us
    pallas_call x1, Pallas kernels, attend_back(): pl.pallas_call(functools.partial(attend_back_kernel, dps, lanes, cores, b...  81.5 us
    pallas_call x1, Pallas kernels, finish(): pl.pallas_call(functools.partial(finish_kernel, dps, lanes, cores, busy),...  78.8 us
    pallas_call x1, Pallas kernels, turn(): pl.pallas_call(functools.partial(turn_kernel, dps, lanes, cores), in_spec...  72.4 us
    pallas_call x1, Pallas kernels, combine(): pl.pallas_call(functools.partial(combine_kernel, dps, lanes, cores), in_s...  66 us
    pallas_call x1, Pallas kernels, start(): pl.pallas_call(functools.partial(start_kernel, dps, lanes, cores, topk, b...  65.3 us
    pallas_call x1, Pallas kernels, expert(): pl.pallas_call(functools.partial(expert_kernel, hidden), grid=(rows // bl...  35.8 us
  transfers between devices with their start and end apart: 1, of which 0 were waited for; matrix products, arithmetic and copies ran while one was open for 1% of the time, Pallas kernels for 23%

profile of v5, /device:TPU:20, one launch (start us, length us, event | category | flops | bytes accessed | tf_op | source)
XLA Modules:
  0.0 699.1 jit_solution(11081707464505301620)
XLA Ops:
  0.6 0.7 convert_bitcast_fusion
  1.3 0.8 copy.30
  2.1 1.2 reshape.80
  3.2 0.6 pad.14.gn_ref
  4.5 1.3 reshape.82.wh_ref
  5.9 0.6 select_maximum_fusion.tab_ref
  6.5 65.3 %shard_map.162 = (bf16[4,2,256,1280]{3,2,1,0:T(8,128)(2,1)}, bf16[4,8,40,768]{3,2,1,0:T(8,128)(2,1)}, f32[4,16,256]{2,1,0:T(8,128)}, bf16[4,4,2,40,1280]{4,3,2,1...) custom-call(bf16[256,1280]{1,0:T(8,128)(2,1)} %x_ref.3, ...), custom_call_target="tpu_custom_call" | custom-call | bytes 252000000 | tf_op jit(solution)/shard_map/pallas_call | solution.py:476
  71.8 1.0 slice_convert_fusion
  73.0 0.6 slice_reduce_fusion
  73.7 134.0 %shard_map.163 = (bf16[2048,1280]{1,0:T(8,128)(2,1)}, bf16[2048,256]{1,0:T(8,128)(2,1)}, bf16[2048,256]{1,0:T(8,128)(2,1)}, bf16[2048,256]{1,0:T(8,128)(2,1)}, b...) custom-call(bf16[2048,1280]{1,0:T(8,128)(2,1)} %bitcast.32, ...), custom_call_target="tpu_custom_call" | custom-call | bytes 360000000 | tf_op jit(solution)/shard_map/pallas_call | solution.py:671
  207.7 3.3 multiply_reduce_fusion.1
  211.0 1.0 multiply_convert_fusion.x_ref
  212.0 125.3 %shard_map.164 = (bf16[4,4,128,1280]{3,2,1,0:T(8,128)(2,1)}, bf16[4,4,128,1280]{3,2,1,0:T(8,128)(2,1)}, bf16[4,4,2,40,1792]{4,3,2,1,0:T(8,128)(2,1)}, bf16[4,4,2...) custom-call(bf16[256,1280]{1,0:T(8,128)(2,1)} %multiply_convert_fusi, ...), custom_call_target="tpu_custom_call" | custom-call | bytes 450000000 | tf_op jit(solution)/shard_map/pallas_call | solution.py:807
  337.3 35.8 %shard_map.165 = (bf16[2048,1280]{1,0:T(8,128)(2,1)}, bf16[2048,1792]{1,0:T(8,128)(2,1)}, bf16[2048,896]{1,0:T(8,128)(2,1)}) custom-call(bf16[2048,1280]{1,0:T(8,128)(2,1)} %bitcast.22, bf16[2048,1280]{1,0:T(8,128)(2,1)} %bitcast.24, bf16[1280,1792]{1,0:T(8,128)(2,1)} %bitcast.34, bf16[1280,896]{1,0:T(8,128)(2,1)} %bitcast.26), custom_call_target="tpu_custom_call" | custom-call | bytes 132710400 | tf_op jit(solution)/shard_map/pallas_call | solution.py:73
  373.1 66.0 %shard_map.166 = (f32[256,1280]{1,0:T(8,128)}, bf16[4,4,128,1280]{3,2,1,0:T(8,128)(2,1)}) custom-call(bf16[4,4,128,1280]{3,2,1,0:T(8,128)(2,1)} %bitcast.33, bf16[4,4,128,256]{3,2,1,0:T(8,128)(2,1)} %get-tuple-element.54.pick_ref, bf16[2048,896]{1,0:T(8,128)(2,1)} %get-tuple-element.65.hid_ref, bf16[1280,896]{1,0:T(8,128)(2,1)} %bitcast.27), custom_call_target="tpu_custom_call" | custom-call | bytes 252000000 | tf_op jit(solution)/shard_map/pallas_call | solution.py:978
  439.1 1.8 multiply_reduce_fusion
  441.0 1.7 fusion.1
  442.7 72.4 %shard_map.167 = (bf16[4,2,256,1280]{3,2,1,0:T(8,128)(2,1)}, f32[256,1280]{1,0:T(8,128)}, bf16[16,40,2688]{2,1,0:T(8,128)(2,1)}) custom-call(bf16[256,1280]{1,0:T(8,128)(2,1)} %get-tuple-element.103.x_ref, bf16[4,4,128,1280]{3,2,1,0:T(8,128)(2,1)} %get-tuple-element.67.part_ref, bf16[4,4,128,256]{3,2,1,0:T(8,128)(2,1)} %get-tuple-element.68.pick_ref, ...), custom_call_target="tpu_custom_call" | custom-call | bytes 324000000 | tf_op jit(solution)/shard_map/pallas_call | solution.py:1094
  515.2 8.6 %all-to-all-start = ((bf16[16,40,2688]{2,1,0:T(8,128)(2,1)}), bf16[16,40,2688]{2,1,0:T(8,128)(2,1)}, u32[]{:S(2)}, u32[]{:S(2)}) async-start(bf16[16,40,2688]{2,1,0:T(8,128)(2,1)} %get-tuple-element.87), calls=%async_computation | async-start | bytes 6881280 | tf_op jit(solution)/shard_map/all_to_all | solution.py:1625
  523.8 81.5 %shard_map.168 = (bf16[4,2,256,1280]{3,2,1,0:T(8,128)(2,1)}, bf16[4,8,40,1024]{3,2,1,0:T(8,128)(2,1)}, bf16[4,40,2688]{2,1,0:T(8,128)(2,1)}) custom-call(bf16[2048,1280]{1,0:T(8,128)(2,1)} %bitcast.31, bf16[2048,1280]{1,0:T(8,128)(2,1)} %get-tuple-element.72.xn_ref, bf16[1280,1280]{1,0:T(8,128)(2,1)} %bitcast.36, bf16[2048,256]{1,0:T(8,128)(2,1)} %get-tuple-element.73.q_ref, ...), custom_call_target="tpu_custom_call" | custom-call | bytes 180000000 | tf_op jit(solution)/shard_map/pallas_call | solution.py:1302
  605.4 78.8 %shard_map.169 = (f32[256,1280]{1,0:T(8,128)}, f32[40,3840]{1,0:T(8,128)}, f32[40,1280]{1,0:T(8,128)}, f32[40,2688]{1,0:T(8,128)}, f32[40,1]{1,0:T(8,128)}) custom-call(bf16[4,2,256,1280]{3,2,1,0:T(8,128)(2,1)} %get-tuple-element.80.part_ref, bf16[4,8,40,1024]{3,2,1,0:T(8,128)(2,1)} %get-tuple-element.81.g_ref, ...), custom_call_target="tpu_custom_call" | custom-call | bytes 237600000 | tf_op jit(solution)/shard_map/pallas_call | solution.py:1509
  684.2 0.8 copy.32
  685.0 1.1 multiply_reduce_fusion.2
  686.1 2.3 add_convert_fusion
  688.5 2.6 convert_element_type.47
  691.5 0.6 fusion
  692.0 2.3 copy-done
  694.4 0.6 maximum_divide_fusion
  695.0 1.1 copy.39
  696.4 0.8 copy.40
  697.3 0.7 copy.41
  698.0 0.8 copy.42
  (35 shorter events, 1.8 us)
Async XLA Ops:
  4.3 1.6 copy-start.12
  73.7 134.1 %copy-start.5 = (bf16[256,1280]{1,0:T(8,128)(2,1)S(1)}, bf16[256,1280]{1,0:T(8,128)(2,1)}, u32[]{:S(2)}) copy-start(bf16[256,1280]{1,0:T(8,128)(2,1)} %x_ref.3) | copy-start | bytes 1966084
  373.1 66.0 %copy-start.2 = (f32[256,1280]{1,0:T(8,128)S(1)}, f32[256,1280]{1,0:T(8,128)}, u32[]{:S(2)}) copy-start(f32[256,1280]{1,0:T(8,128)} %get-tuple-element.59) | copy-start | bytes 3932164
  439.1 1.8 copy-start.3
  439.1 1.9 copy-start.4
  515.2 173.3 %all-to-all-start = ((bf16[16,40,2688]{2,1,0:T(8,128)(2,1)}), bf16[16,40,2688]{2,1,0:T(8,128)(2,1)}, u32[]{:S(2)}, u32[]{:S(2)}) async-start(bf16[16,40,2688]{2,1,0:T(8,128)(2,1)} %get-tuple-element.87), calls=%async_computation | async-start | bytes 6881280 | tf_op jit(solution)/shard_map/all_to_all | solution.py:1625
  605.4 79.7 %copy-start.10 = (bf16[40,2688]{1,0:T(8,128)(2,1)S(1)}, bf16[40,2688]{1,0:T(8,128)(2,1)}, u32[]{:S(2)}) copy-start(bf16[40,2688]{1,0:T(8,128)(2,1)} %sh_ref.1) | copy-start | bytes 645124
  605.4 80.8 %copy-start.7 = (f32[256,1280]{1,0:T(8,128)S(1)}, f32[256,1280]{1,0:T(8,128)}, u32[]{:S(2)}) copy-start(f32[256,1280]{1,0:T(8,128)} %get-tuple-element.58) | copy-start | bytes 3932164
  688.5 3.0 copy-start.1
  691.5 2.9 copy-start
  691.5 2.9 copy-start.13
  691.5 3.5 copy-start.6
  695.0 1.5 copy-start.9
  695.0 2.3 copy-start.11
  696.4 1.5 copy-start.8

commit v6 on v5

--- a/solution.py
+++ b/solution.py
@@ -55,39 +55,6 @@
     dgate = (down * up * sig * (1.0 + gate * (1.0 - sig))).astype(BF)
     dx = dot_nt(dgate, w_ref[:, :hidden]) + dot_nt(dup, w_ref[:, hidden : 2 * hidden])
     return dx, dgate, dup, (act * up).astype(BF)
-
-
-def expert_kernel(hidden, x_ref, c_ref, w_ref, down_ref, dx_ref, gu_ref, hid_ref):
-    dx, dgate, dup, hid = feed(x_ref[...], c_ref[...], w_ref, down_ref, hidden)
-    dx_ref[...] = dx.astype(dx_ref.dtype)
-    gu_ref[:, :hidden] = dgate
-    gu_ref[:, hidden:] = dup
-    hid_ref[...] = hid
-
-
-def expert(x, c, w, down, kind):
-    rows, model = x.shape
-    hidden = down.shape[1]
-    block = min(512, rows)
-    row = lambda cols: pl.BlockSpec((block, cols), lambda i: (i, 0))
-    return pl.pallas_call(
-        functools.partial(expert_kernel, hidden),
-        grid=(rows // block,),
-        in_specs=[
-            row(model),
-            row(model),
-            pl.BlockSpec(w.shape, lambda i: (0, 0)),
-            pl.BlockSpec(down.shape, lambda i: (0, 0)),
-        ],
-        out_specs=[row(model), row(2 * hidden), row(hidden)],
-        out_shape=[
-            jax.ShapeDtypeStruct((rows, model), kind),
-            jax.ShapeDtypeStruct((rows, 2 * hidden), BF),
-            jax.ShapeDtypeStruct((rows, hidden), BF),
-        ],
-        compiler_params=pltpu.CompilerParams(vmem_limit_bytes=VMEM_LIMIT),
-        cost_estimate=lasts(0.018 * rows),
-    )(x, c, w, down)
 
 
 MESH = pl.DeviceIdType.MESH
@@ -708,10 +675,45 @@
     pl.semaphore_wait(barrier, dps - 1 + cores - 1 + ends)
 
 
+class CoreSum:
+    def __init__(self, source, own, scratch, dps, lanes, cores):
+        self.source, self.own = source, own
+        self.from_core, self.out, self.came = scratch
+        self.dps, self.lanes, self.cores = dps, lanes, cores
+        self.dp, self.fs, self.z, self.c = place(cores)
+
+    def across(self, m):
+        t = lax.rem(self.c + m, self.cores)
+        return send(
+            self.source.at[t], self.from_core.at[m - 1], self.out.at[m - 1], self.came.at[m - 1],
+            (self.dp, self.z * self.cores + t),
+        )
+
+    def begin(self):
+        for m in range(1, self.cores):
+            self.across(m).start()
+
+    def finish(self):
+        for m in range(1, self.cores):
+            self.across(m).wait_recv()
+
+        def add(i, carry):
+            p, q = i // self.lanes, lax.rem(i, self.lanes)
+            total = self.source[self.c, p, q].astype(F32)
+            for m in range(1, self.cores):
+                total = total + self.from_core[m - 1, p, q].astype(F32)
+            self.own[p, q] = total.astype(BF)
+            return carry
+
+        lax.fori_loop(0, self.dps * self.lanes, add, 0)
+        for m in range(1, self.cores):
+            self.across(m).wait_send()
+
+
 def dispatch_kernel(
     dps, lanes, cores, topk, x_ref, up_ref, tabs_ref, pick_ref, rows_ref, low_ref, shared_ref,
-    out_ref, c_ref, w_ref, wd_ref, dx_ref, f_ref, g_ref, acts, acc, buffer, stage, up_buffer, up_stage, l_out, l_in, s_out, s_in, s_local,
-    ul_out, ul_in, us_out, us_in, us_local, w_out, w_in, w_local, wd_out, wd_in, wd_local,
+    out_ref, c_ref, w_ref, wd_ref, dx_ref, f_ref, own_ref, g_ref, acts, acc, buffer, stage, up_buffer, up_stage, l_out, l_in, s_out, s_in, s_local,
+    ul_out, ul_in, us_out, us_in, us_local, w_out, w_in, w_local, wd_out, wd_in, wd_local, *core,
 ):
     line = Line(x_ref, buffer, lanes, cores, l_out, l_in)
     spread = Spread(stage, out_ref, dps, lanes, cores, s_out, s_in, s_local)
@@ -756,6 +758,7 @@
         across(m, line.c).start()
         across_down(m, line.c).start()
     experts, shard = dps * lanes, g_ref.shape[3]
+    summed = CoreSum(g_ref, own_ref, core, dps, lanes, cores)
 
     def shared_forward():
         down_ref = shared_ref.at[:, 2 * hidden :]
@@ -772,7 +775,9 @@
             for k in range(cores):
                 row = (e * cores + k) * shard
                 piece = acc[row : row + shard, :].astype(BF)
-                g_ref[e // lanes, e % lanes, k, :, third * hidden : (third + 1) * hidden] = piece
+                g_ref[k, e // lanes, e % lanes, :, third * hidden : (third + 1) * hidden] = piece
+        if third == 2:
+            summed.begin()
 
     work = [shared_forward] + [functools.partial(shared_gradient, third) for third in range(3)]
     for step in range(1, lanes):
@@ -785,6 +790,7 @@
     line.finish()
     up_spread.finish()
     up_line.finish()
+    summed.finish()
     keep.wait()
     keep_down.wait()
     for m in range(1, cores):
@@ -815,18 +821,98 @@
             jax.ShapeDtypeStruct((dps, lanes, cores, shard, hidden), BF),
             jax.ShapeDtypeStruct((tokens, model), F32),
             jax.ShapeDtypeStruct((tokens, model), F32),
-            jax.ShapeDtypeStruct((dps, lanes, cores, shard, 3 * hidden), BF),
+            jax.ShapeDtypeStruct((dps, lanes, shard, 3 * hidden), BF),
         ],
         scratch_shapes=[
+            pltpu.VMEM((cores, dps, lanes, shard, 3 * hidden), BF),
             pltpu.VMEM((3, tokens, shared.shape[1] // 3), BF),
             pltpu.VMEM((model, shared.shape[1] // 3), F32),
         ]
-        + buffers * 2 + moves * 2 + (pair(cores) + [dma]) * 2,
+        + buffers * 2 + moves * 2 + (pair(cores) + [dma]) * 2
+        + [pltpu.VMEM((max(cores - 1, 1), dps, lanes, shard, 3 * hidden), BF)] + pair(cores),
         cost_estimate=lasts(125),
         compiler_params=pltpu.CompilerParams(
             collective_id=3, has_side_effects=True, vmem_limit_bytes=VMEM_LIMIT
         ),
     )(x, upstream, tables, picks, rows, low, shared)
+
+
+def expert_kernel(
+    steps, dps, lanes, cores, hidden, x_ref, c_ref, w_ref, down_ref, own_ref,
+    dx_ref, gu_ref, hid_ref, line_ref, mine, from_dp, out, came, local,
+):
+    dp, fs, z, c = place(cores)
+    step = pl.program_id(0)
+
+    def over(m):
+        t = lax.rem(dp + m, dps)
+        return send(own_ref.at[t], from_dp.at[m - 1], out.at[m - 1], came.at[m - 1], (t, fs))
+
+    keep = pltpu.make_async_copy(own_ref.at[dp], mine, local)
+
+    @pl.when(step == 0)
+    def _():
+        greet([(lax.rem(dp + m, dps), fs) for m in range(1, dps)])
+        for m in range(1, dps):
+            over(m).start()
+        keep.start()
+
+    dx, dgate, dup, hid = feed(x_ref[...], c_ref[...], w_ref, down_ref, hidden)
+    dx_ref[...] = dx.astype(dx_ref.dtype)
+    gu_ref[:, :hidden] = dgate
+    gu_ref[:, hidden:] = dup
+    hid_ref[...] = hid
+
+    @pl.when(step == steps - 1)
+    def _():
+        keep.wait()
+        for m in range(1, dps):
+            over(m).wait_recv()
+        for q in range(lanes):
+            total = mine[q].astype(F32)
+            for m in range(1, dps):
+                total = total + from_dp[m - 1, q].astype(F32)
+            line_ref[q] = total.astype(BF)
+        for m in range(1, dps):
+            over(m).wait_send()
+
+
+def expert(x, c, w, down, own, cores):
+    rows, model = x.shape
+    hidden = down.shape[1]
+    dps, lanes = own.shape[:2]
+    block = min(512, rows)
+    dma = pltpu.SemaphoreType.DMA
+    row = lambda cols: pl.BlockSpec((block, cols), lambda i: (i, 0))
+    return pl.pallas_call(
+        functools.partial(expert_kernel, rows // block, dps, lanes, cores, hidden),
+        grid=(rows // block,),
+        in_specs=[
+            row(model),
+            row(model),
+            pl.BlockSpec(w.shape, lambda i: (0, 0)),
+            pl.BlockSpec(down.shape, lambda i: (0, 0)),
+            ANY,
+        ],
+        out_specs=[
+            row(model), row(2 * hidden), row(hidden), pl.BlockSpec(own.shape[1:], lambda i: (0, 0, 0)),
+        ],
+        out_shape=[
+            jax.ShapeDtypeStruct((rows, model), BF),
+            jax.ShapeDtypeStruct((rows, 2 * hidden), BF),
+            jax.ShapeDtypeStruct((rows, hidden), BF),
+            jax.ShapeDtypeStruct(own.shape[1:], BF),
+        ],
+        scratch_shapes=[
+            pltpu.VMEM(own.shape[1:], BF),
+            pltpu.VMEM((dps - 1,) + own.shape[1:], BF),
+        ]
+        + pair(dps) + [dma],
+        cost_estimate=lasts(40),
+        compiler_params=pltpu.CompilerParams(
+            collective_id=7, has_side_effects=True, vmem_limit_bytes=VMEM_LIMIT
+        ),
+    )(x, c, w, down, own)
 
 
 class Combine:
@@ -939,9 +1025,11 @@
 
 
 def combine_kernel(
-    dps, lanes, cores, part_ref, pick_ref, hid_ref, w_ref, out_ref, f_ref, hid, down, load, *scratch
+    dps, lanes, cores, part_ref, pick_ref, hid_ref, w_ref, line_ref, out_ref, f_ref, sum_ref,
+    hid, down, load, from_z, s_out, s_in, *scratch,
 ):
     work = Combine(part_ref, pick_ref, out_ref, scratch, dps, lanes, cores)
+    dp, fs, z, c = place(cores)
     hidden = hid.shape[1]
     slots = f_ref.shape[2]
     loads = [
@@ -950,8 +1038,20 @@
     ]
     for copy in loads:
         copy.start()
-    greet_cross(Line(None, None, lanes, cores, None, None), dps)
+
+    def along(k):
+        t = lax.rem(z + k, lanes)
+        return send(
+            line_ref.at[t], from_z.at[k - 1], s_out.at[k - 1], s_in.at[k - 1], (dp, t * cores + c)
+        )
+
+    greet(
+        [(lax.rem(dp + m, dps), fs) for m in range(1, dps)]
+        + [(dp, lax.rem(z + k, lanes) * cores + c) for k in range(1, lanes)]
+    )
     work.begin()
+    for k in range(1, lanes):
+        along(k).start()
     for copy in loads:
         copy.wait()
 
@@ -966,10 +1066,17 @@
             forward(m)
         if step < lanes:
             work.advance(step)
+    total = line_ref[z].astype(F32)
+    for k in range(1, lanes):
+        along(k).wait_recv()
+        total = total + from_z[k - 1].astype(F32)
+    sum_ref[...] = total
     work.finish()
-
-
-def combine(parts, picks, hid, w, lanes, cores):
+    for k in range(1, lanes):
+        along(k).wait_send()
+
+
+def combine(parts, picks, hid, w, line, lanes, cores):
     dps, _, slots, model = parts.shape
     tokens = picks.shape[3]
     hidden = hid.shape[1]
@@ -977,19 +1084,26 @@
     whole = pl.BlockSpec(memory_space=pltpu.VMEM)
     return pl.pallas_call(
         functools.partial(combine_kernel, dps, lanes, cores),
-        in_specs=[ANY, whole, ANY, ANY],
-        out_specs=[whole, whole],
+        in_specs=[ANY, whole, ANY, ANY, whole],
+        out_specs=[whole] * 3,
         out_shape=[
             jax.ShapeDtypeStruct((tokens, model), F32),
             jax.ShapeDtypeStruct(parts.shape, BF),
+            jax.ShapeDtypeStruct(line.shape[1:], F32),
         ],
-        scratch_shapes=[pltpu.VMEM(hid.shape, BF), pltpu.VMEM((model, hidden), BF), dma((2,))]
+        scratch_shapes=[
+            pltpu.VMEM(hid.shape, BF),
+            pltpu.VMEM((model, hidden), BF),
+            dma((2,)),
+            pltpu.VMEM((max(lanes - 1, 1),) + line.shape[1:], BF),
+        ]
+        + pair(lanes)
         + combine_scratch(dps, lanes, slots, tokens, model),
         cost_estimate=lasts(70),
         compiler_params=pltpu.CompilerParams(
             collective_id=4, has_side_effects=True, vmem_limit_bytes=VMEM_LIMIT
         ),
-    )(parts, picks, hid, w)
+    )(parts, picks, hid, w, line)
 
 
 class Gradient:
@@ -1117,74 +1231,13 @@
     )(x, parts, picks, xs, cs, gu, hid)
 
 
-class LineSum:
-    def __init__(self, source, total, scratch, dps, lanes, cores):
-        self.source, self.total = source, total
-        self.own, self.from_core, self.from_dp = scratch[:3]
-        self.c_out, self.c_in, self.d_out, self.d_in, self.local = scratch[3:]
-        self.dps, self.lanes, self.cores = dps, lanes, cores
-        self.dp, self.fs, self.z, self.c = place(cores)
-
-    def across(self, m):
-        t = lax.rem(self.c + m, self.cores)
-        return send(
-            self.source.at[:, :, t], self.from_core.at[m - 1], self.c_out.at[m - 1], self.c_in.at[m - 1],
-            (self.dp, self.z * self.cores + t),
-        )
-
-    def over(self, m):
-        t = lax.rem(self.dp + m, self.dps)
-        return send(
-            self.own.at[t], self.from_dp.at[m - 1], self.d_out.at[m - 1], self.d_in.at[m - 1], (t, self.fs)
-        )
-
-    def keep(self):
-        return pltpu.make_async_copy(self.source.at[:, :, self.c], self.own, self.local)
-
-    def begin(self):
-        self.keep().start()
-        for m in range(1, self.cores):
-            self.across(m).start()
-
-    def add(self):
-        self.keep().wait()
-        for m in range(1, self.cores):
-            self.across(m).wait_recv()
-
-        def add(i, carry):
-            p, q = i // self.lanes, lax.rem(i, self.lanes)
-            total = self.own[p, q].astype(F32)
-            for m in range(1, self.cores):
-                total = total + self.from_core[m - 1, p, q].astype(F32)
-            self.own[p, q] = total.astype(BF)
-            return carry
-
-        lax.fori_loop(0, self.dps * self.lanes, add, 0)
-        for m in range(1, self.dps):
-            self.over(m).start()
-
-    def add_dp(self):
-        for m in range(1, self.dps):
-            self.over(m).wait_recv()
-        for q in range(self.lanes):
-            total = self.own[self.dp, q].astype(F32)
-            for m in range(1, self.dps):
-                total = total + self.from_dp[m - 1, q].astype(F32)
-            self.total[q] = total.astype(BF)
-        for m in range(1, self.cores):
-            self.across(m).wait_send()
-        for m in range(1, self.dps):
-            self.over(m).wait_send()
-
-
 def attend_back_kernel(
     dps, lanes, cores, busy, block, scale,
-    da_ref, xn_ref, out_ref, q_ref, k_ref, kt_ref, v_ref, o_ref, lse_ref, cos_ref, sin_ref, w_ref, g_ref,
-    part_ref, prod_ref, line_ref, left, d_ref, acc, stage, cols, do_all, dk_acc, dv_acc,
-    load, stored, *scratch,
+    da_ref, xn_ref, out_ref, q_ref, k_ref, kt_ref, v_ref, o_ref, lse_ref, cos_ref, sin_ref, w_ref,
+    part_ref, prod_ref, left, d_ref, acc, stage, cols, do_all, dk_acc, dv_acc,
+    load, stored,
 ):
     dp, fs, z, c = place(cores)
-    shared = LineSum(g_ref, line_ref, scratch, dps, lanes, cores)
     seq, width = q_ref.shape
     tokens = part_ref.shape[2]
     slot = jnp.minimum(head_slot(fs, lanes, cores), busy - 1)
@@ -1202,11 +1255,6 @@
                 row = (p * lanes * cores + f) * shard
                 prod_ref[p, f, :, lo:hi] = acc[row : row + shard, : hi - lo].astype(BF)
 
-    greet(
-        [(lax.rem(dp + m, dps), fs) for m in range(1, dps)]
-        + [(dp, z * cores + lax.rem(c + m, cores)) for m in range(1, cores)]
-    )
-    shared.begin()
     fetch.wait()
     first.wait()
 
@@ -1220,8 +1268,6 @@
     @pl.when(mine)
     def _():
         lax.fori_loop(0, seq // block, upstream, 0)
-
-    shared.add()
 
     @pl.when(mine)
     def _():
@@ -1288,10 +1334,9 @@
 
     for save in saves[-2:]:
         save.wait()
-    shared.add_dp()
-
-
-def attend_back(da_all, xn, out_all, saved, tables, w, g, tokens, busy, dps, lanes, cores):
+
+
+def attend_back(da_all, xn, out_all, saved, tables, w, shard, tokens, busy, dps, lanes, cores):
     q, k, kt, v, o, lse = saved
     cos, sin = tables
     seq, width = q.shape
@@ -1301,12 +1346,11 @@
     whole = pl.BlockSpec(memory_space=pltpu.VMEM)
     return pl.pallas_call(
         functools.partial(attend_back_kernel, dps, lanes, cores, busy, block, 1.0 / math.sqrt(HD)),
-        in_specs=[ANY] * 3 + [whole] * 9 + [ANY],
-        out_specs=[ANY, whole, whole],
+        in_specs=[ANY] * 3 + [whole] * 9,
+        out_specs=[ANY, whole],
         out_shape=[
             jax.ShapeDtypeStruct((lanes, cores, tokens, model), BF),
-            jax.ShapeDtypeStruct((dps, lanes * cores, g.shape[3], 4 * width), BF),
-            jax.ShapeDtypeStruct((lanes,) + g.shape[3:], BF),
+            jax.ShapeDtypeStruct((dps, lanes * cores, shard, 4 * width), BF),
         ],
         scratch_shapes=[
             pltpu.VMEM((seq, model), BF),
@@ -1319,23 +1363,17 @@
             pltpu.VMEM((seq, HD), F32),
             dma((2,)),
             dma((2,)),
-            pltpu.VMEM((dps, lanes) + g.shape[3:], BF),
-            pltpu.VMEM((max(cores - 1, 1), dps, lanes) + g.shape[3:], BF),
-            pltpu.VMEM((dps - 1, lanes) + g.shape[3:], BF),
-        ]
-        + pair(cores) + pair(dps) + [dma],
+        ],
         cost_estimate=lasts(50),
-        compiler_params=pltpu.CompilerParams(
-            collective_id=5, has_side_effects=True, vmem_limit_bytes=VMEM_LIMIT
-        ),
-    )(da_all, xn, out_all, q, k, kt, v, o, lse, cos, sin, w, g)
+        compiler_params=pltpu.CompilerParams(vmem_limit_bytes=VMEM_LIMIT),
+    )(da_all, xn, out_all, q, k, kt, v, o, lse, cos, sin, w)
 
 
 def finish_kernel(
-    dps, lanes, cores, busy, part_ref, g_ref, line_sum, x_ref, gain_ref, dx_ref, wq_ref,
-    out_ref, gq_ref, go_ref, sum_ref, one_ref, mix_ref,
-    from_core, stage, inbox, from_dp, total_g, from_z,
-    z_out, z_in, c_out, c_in, g_out, g_in, m_out, m_in, local, s_out, s_in,
+    dps, lanes, cores, busy, part_ref, g_ref, x_ref, gain_ref, dx_ref, wq_ref,
+    out_ref, gq_ref, go_ref, one_ref, mix_ref,
+    from_core, stage, inbox, from_dp, total_g,
+    z_out, z_in, c_out, c_in, g_out, g_in, m_out, m_in, local,
 ):
     dp, fs, z, c = place(cores)
     fss = lanes * cores
@@ -1364,12 +1402,6 @@
     def home(k, owner):
         t = lax.rem(fs + k, fss)
         return send(total_g.at[t], mix_ref.at[head_slot(owner, lanes, cores)], m_out.at[k - 1], m_in.at[k - 1], (dp, t))
-
-    def along(k):
-        t = lax.rem(z + k, lanes)
-        return send(
-            line_sum.at[t], from_z.at[k - 1], s_out.at[k - 1], s_in.at[k - 1], (dp, t * cores + c)
-        )
 
     def goal(side, step):
         block = z + lanes - step if side == 0 else z - lanes + step
@@ -1415,8 +1447,6 @@
     begin(z)
     for m in range(1, dps):
         over(m).start()
-    for k in range(1, lanes):
-        along(k).start()
     for step in range(1, max(lanes - 1, 1)):
         advance(step)
     for m in range(1, dps):
@@ -1445,13 +1475,6 @@
             hop(side, lanes - 1).wait_recv()
             out_ref[...] += inbox[side, lanes - 2].astype(F32)
 
-    total = line_sum[z].astype(F32)
-    for k in range(1, lanes):
-        along(k).wait_recv()
-        total = total + from_z[k - 1].astype(F32)
-    sum_ref[...] = total
-    for k in range(1, lanes):
-        along(k).wait_send()
     for k in range(1, fss):
         owner = lax.rem(fs + fss - k, fss)
 
@@ -1499,7 +1522,7 @@
         over(m).wait_send()
 
 
-def finish(part, g, g_line, x, gain, dx, w_qkv, lanes, cores, busy):
+def finish(part, g, x, gain, dx, w_qkv, lanes, cores, busy):
     dps, fss = g.shape[:2]
     tokens, model = part.shape[2:]
     dma = pltpu.SemaphoreType.DMA
@@ -1508,13 +1531,12 @@
     whole = pl.BlockSpec(memory_space=pltpu.VMEM)
     return pl.pallas_call(
         functools.partial(finish_kernel, dps, lanes, cores, busy),
-        in_specs=[whole] * 7,
-        out_specs=[whole] * 5,
+        in_specs=[whole] * 6,
+        out_specs=[whole] * 4,
         out_shape=[
             jax.ShapeDtypeStruct((tokens, model), F32),
             jax.ShapeDtypeStruct(w_qkv.shape, F32),
             jax.ShapeDtypeStruct((w_qkv.shape[0], model), F32),
-            jax.ShapeDtypeStruct(g_line.shape[1:], F32),
             jax.ShapeDtypeStruct((w_qkv.shape[0], 1), F32),
         ],
         scratch_shapes=[
@@ -1524,15 +1546,14 @@
             pltpu.VMEM(hops + (tokens, model), BF),
             pltpu.VMEM((dps - 1,) + g.shape[1:], BF),
             pltpu.VMEM(g.shape[1:], BF),
-            pltpu.VMEM((max(lanes - 1, 1),) + g_line.shape[1:], BF),
             dma(hops), dma(hops), dma(ways), dma(ways), dma((dps - 1,)), dma((dps - 1,)),
-            dma((fss - 1,)), dma((fss - 1,)), dma, dma((max(lanes - 1, 1),)), dma((max(lanes - 1, 1),)),
+            dma((fss - 1,)), dma((fss - 1,)), dma,
         ],
         cost_estimate=lasts(66),
         compiler_params=pltpu.CompilerParams(
             collective_id=6, has_side_effects=True, vmem_limit_bytes=VMEM_LIMIT
         ),
-    )(part, g, g_line, x, gain, dx, w_qkv)
+    )(part, g, x, gain, dx, w_qkv)
 
 
 def per_device(x, w_qkv, w_out, w_shared, w_experts, gains, routes, gates, d_out):
@@ -1590,17 +1611,19 @@
     unit_two = middle * inv_two
     xn_two = (unit_two * gain_two).astype(BF)
 
-    x_slots, c_slots, w_own, w_down, dx_shared, f_shared, g_shared_part = dispatch(
+    x_slots, c_slots, w_own, w_down, dx_shared, f_shared, g_core = dispatch(
         xn_two, d_out, tables, picks, rows_here, rows_low, shared_all, topk, lanes, cores
     )
     x_slots = x_slots.reshape(-1, model)
     c_slots = c_slots.reshape(-1, model)
     w_own = w_own.reshape(model, 2 * hidden)
     w_down = w_down.reshape(model, hidden)
-    dx_slots, gu_slots, hid_slots = expert(x_slots, c_slots, w_own, w_down, BF)
+    dx_slots, gu_slots, hid_slots, g_line = expert(x_slots, c_slots, w_own, w_down, g_core, cores)
 
     shape = (dps, lanes, slots, model)
-    dx_routed, f_slots = combine(dx_slots.reshape(shape), picks, hid_slots, w_down, lanes, cores)
+    dx_routed, f_slots, g_shared = combine(
+        dx_slots.reshape(shape), picks, hid_slots, w_down, g_line, lanes, cores
+    )
     dxn_two = dx_shared + dx_routed
     scaled = dxn_two * gain_two
     dx_two = d_out.astype(F32) + inv_two * (
@@ -1613,12 +1636,12 @@
     )
     da_all = da_all.reshape(seq, model)
     layer_out = (middle + f_shared + routed).astype(BF)
-    dxn_part, g_part, g_line = attend_back(
-        da_all, xn_one, out_all, (q, k, kt, v, o, lse), (cos, sin), w_heads, g_shared_part,
+    dxn_part, g_part = attend_back(
+        da_all, xn_one, out_all, (q, k, kt, v, o, lse), (cos, sin), w_heads, shard,
         tokens, busy, dps, lanes, cores,
     )
-    d_x, g_qkv, g_out, g_shared, one = finish(
-        dxn_part, g_part, g_line, x, gain_one, dx_two, w_qkv, lanes, cores, busy
+    d_x, g_qkv, g_out, one = finish(
+        dxn_part, g_part, x, gain_one, dx_two, w_qkv, lanes, cores, busy
     )
 
     groups = [[e * cores + k for e in range(experts)] for k in range(cores)]

time: 707 us -> 674 us (0.953)
  Pallas kernels: 659 us -> 627 us
    pallas_call x1, Pallas kernels: 81.5 us -> 36.9 us  [attend_back(): pl.pallas_call(functools.partial(attend_back_kernel, dps, lanes, cores, b...]
    pallas_call x1, Pallas kernels: 35.8 us -> 45.1 us  [expert(): pl.pallas_call(functools.partial(expert_kernel, rows // block, dps, lanes...]
  transfers between devices with their start and end apart: 1 -> 1, of which waited for: 0 -> 0; matrix products, arithmetic and copies ran while one was open for 1% -> 0% of each run, Pallas kernels for 23% -> 18%
where the time goes in v6:
time: 674 us; the launch traced here: 666 us
  Pallas kernels  627 us (93%)
  other arithmetic  13.1 us (2%)
  local copies, waits for them, and re-layouts  12.7 us (2%)
  starting transfers between devices  8.65 us (1%)
    pallas_call x1, Pallas kernels, attend(): pl.pallas_call(functools.partial(attend_kernel, dps, lanes, cores, busy,...  134 us
    pallas_call x1, Pallas kernels, dispatch(): pl.pallas_call(functools.partial(dispatch_kernel, dps, lanes, cores, topk...  125 us
    pallas_call x1, Pallas kernels, finish(): pl.pallas_call(functools.partial(finish_kernel, dps, lanes, cores, busy),...  80.7 us
    pallas_call x1, Pallas kernels, turn(): pl.pallas_call(functools.partial(turn_kernel, dps, lanes, cores), in_spec...  73.6 us
    pallas_call x1, Pallas kernels, combine(): pl.pallas_call(functools.partial(combine_kernel, dps, lanes, cores), in_s...  66.3 us
    pallas_call x1, Pallas kernels, start(): pl.pallas_call(functools.partial(start_kernel, dps, lanes, cores, topk, b...  65.3 us
    pallas_call x1, Pallas kernels, expert(): pl.pallas_call(functools.partial(expert_kernel, rows // block, dps, lanes...  45.1 us
    pallas_call x1, Pallas kernels, attend_back(): pl.pallas_call(functools.partial(attend_back_kernel, dps, lanes, cores, b...  36.9 us
  transfers between devices with their start and end apart: 1, of which 0 were waited for; matrix products, arithmetic and copies ran while one was open for 0% of the time, Pallas kernels for 18%

profile of v6, /device:TPU:20, one launch (start us, length us, event | category | flops | bytes accessed | tf_op | source)
XLA Modules:
  0.0 665.6 jit_solution(15235394329780411617)
XLA Ops:
  0.6 0.7 convert_bitcast_fusion
  1.3 0.8 copy.30
  2.1 1.2 reshape.80
  3.2 0.6 pad.14.gn_ref
  4.5 1.3 reshape.82.wh_ref
  5.9 0.6 select_maximum_fusion.tab_ref
  6.5 65.3 %shard_map.162 = (bf16[4,2,256,1280]{3,2,1,0:T(8,128)(2,1)}, bf16[4,8,40,768]{3,2,1,0:T(8,128)(2,1)}, f32[4,16,256]{2,1,0:T(8,128)}, bf16[4,4,2,40,1280]{4,3,2,1...) custom-call(bf16[256,1280]{1,0:T(8,128)(2,1)} %x_ref.3, ...), custom_call_target="tpu_custom_call" | custom-call | bytes 252000000 | tf_op jit(solution)/shard_map/pallas_call | solution.py:443
  71.8 1.0 slice_convert_fusion
  73.0 0.6 slice_reduce_fusion
  73.6 134.0 %shard_map.163 = (bf16[2048,1280]{1,0:T(8,128)(2,1)}, bf16[2048,256]{1,0:T(8,128)(2,1)}, bf16[2048,256]{1,0:T(8,128)(2,1)}, bf16[2048,256]{1,0:T(8,128)(2,1)}, b...) custom-call(bf16[2048,1280]{1,0:T(8,128)(2,1)} %bitcast.31, ...), custom_call_target="tpu_custom_call" | custom-call | bytes 360000000 | tf_op jit(solution)/shard_map/pallas_call | solution.py:638
  207.6 3.3 multiply_reduce_fusion.1
  210.9 1.0 multiply_convert_fusion.x_ref
  211.9 125.1 %shard_map.164 = (bf16[4,4,128,1280]{3,2,1,0:T(8,128)(2,1)}, bf16[4,4,128,1280]{3,2,1,0:T(8,128)(2,1)}, bf16[4,4,2,40,1792]{4,3,2,1,0:T(8,128)(2,1)}, bf16[4,4,2...) custom-call(bf16[256,1280]{1,0:T(8,128)(2,1)} %multiply_convert_fusion., ...), custom_call_target="tpu_custom_call" | custom-call | bytes 450000000 | tf_op jit(solution)/shard_map/pallas_call | solution.py:813
  337.0 45.1 %shard_map.165 = (bf16[2048,1280]{1,0:T(8,128)(2,1)}, bf16[2048,1792]{1,0:T(8,128)(2,1)}, bf16[2048,896]{1,0:T(8,128)(2,1)}, bf16[4,40,2688]{2,1,0:T(8,128)(2,1)}) custom-call(bf16[2048,1280]{1,0:T(8,128)(2,1)} %bitcast.22, bf16[2048,1280]{1,0:T(8,128)(2,1)} %bitcast.24, bf16[1280,1792]{1,0:T(8,128)(2,1)} %bitcast.34, bf16[1280,896]{1,0:T(8,128)(2,1)} %bitcast.26, ...), custom_call_target="tpu_custom_call" | custom-call | bytes 144000000 | tf_op jit(solution)/shard_map/pallas_call | solution.py:887
  382.1 66.3 %shard_map.166 = (f32[256,1280]{1,0:T(8,128)}, bf16[4,4,128,1280]{3,2,1,0:T(8,128)(2,1)}, f32[40,2688]{1,0:T(8,128)}) custom-call(bf16[4,4,128,1280]{3,2,1,0:T(8,128)(2,1)} %bitcast.32, bf16[4,4,128,256]{3,2,1,0:T(8,128)(2,1)} %get-tuple-element.54.pick_ref, bf16[2048,896]{1,0:T(8,128)(2,1)} %get-tuple-element.66.hid_ref, bf16[1280,896]{1,0:T(8,128)(2,1)} %bitcast.27, ...), custom_call_target="tpu_custom_call" | custom-call | bytes 252000000 | tf_op jit(solution)/shard_map/pallas_call | solution.py:1085
  448.5 1.8 multiply_reduce_fusion
  450.3 1.7 fusion.1
  452.1 73.6 %shard_map.167 = (bf16[4,2,256,1280]{3,2,1,0:T(8,128)(2,1)}, f32[256,1280]{1,0:T(8,128)}, bf16[16,40,2688]{2,1,0:T(8,128)(2,1)}) custom-call(bf16[256,1280]{1,0:T(8,128)(2,1)} %get-tuple-element.103.x_ref, bf16[4,4,128,1280]{3,2,1,0:T(8,128)(2,1)} %get-tuple-element.69.part_ref, bf16[4,4,128,256]{3,2,1,0:T(8,128)(2,1)} %get-tuple-element.70.pick_ref, ...), custom_call_target="tpu_custom_call" | custom-call | bytes 324000000 | tf_op jit(solution)/shard_map/pallas_call | solution.py:1208
  525.6 8.7 %all-to-all-start = ((bf16[16,40,2688]{2,1,0:T(8,128)(2,1)}), bf16[16,40,2688]{2,1,0:T(8,128)(2,1)}, u32[]{:S(2)}, u32[]{:S(2)}) async-start(bf16[16,40,2688]{2,1,0:T(8,128)(2,1)} %get-tuple-element.87), calls=%async_computation | async-start | bytes 6881280 | tf_op jit(solution)/shard_map/all_to_all | solution.py:1648
  534.3 36.9 %shard_map.168 = (bf16[4,2,256,1280]{3,2,1,0:T(8,128)(2,1)}, bf16[4,8,40,1024]{3,2,1,0:T(8,128)(2,1)}) custom-call(bf16[2048,1280]{1,0:T(8,128)(2,1)} %bitcast.33, bf16[2048,1280]{1,0:T(8,128)(2,1)} %get-tuple-element.74.xn_ref, bf16[1280,1280]{1,0:T(8,128)(2,1)} %bitcast.36, bf16[2048,256]{1,0:T(8,128)(2,1)} %get-tuple-element.75.q_ref, ...), custom_call_target="tpu_custom_call" | custom-call | bytes 180000000 | tf_op jit(solution)/shard_map/pallas_call | solution.py:1347
  571.2 80.7 %shard_map.169 = (f32[256,1280]{1,0:T(8,128)}, f32[40,3840]{1,0:T(8,128)}, f32[40,1280]{1,0:T(8,128)}, f32[40,1]{1,0:T(8,128)}) custom-call(bf16[4,2,256,1280]{3,2,1,0:T(8,128)(2,1)} %get-tuple-element.81.part_ref, bf16[4,8,40,1024]{3,2,1,0:T(8,128)(2,1)} %get-tuple-element.82.g_ref, bf16[256,1280]{1,0:T(8,128)(2,1)} %x_ref.3, ...), custom_call_target="tpu_custom_call" | custom-call | bytes 237600000 | tf_op jit(solution)/shard_map/pallas_call | solution.py:1532
  651.9 0.8 copy.32
  652.9 2.3 add_convert_fusion
  655.2 2.6 convert_element_type.47
  658.2 0.6 fusion
  658.8 2.3 copy-done
  661.1 0.6 maximum_divide_fusion
  661.7 1.1 copy.39
  662.7 0.4 copy-done.9
  663.2 0.8 copy.40
  664.0 0.7 copy.41
  664.7 0.8 copy.42
  (35 shorter events, 1.5 us)
Async XLA Ops:
  4.3 1.6 copy-start.12
  73.6 134.0 %copy-start.5 = (bf16[256,1280]{1,0:T(8,128)(2,1)S(1)}, bf16[256,1280]{1,0:T(8,128)(2,1)}, u32[]{:S(2)}) copy-start(bf16[256,1280]{1,0:T(8,128)(2,1)} %x_ref.3) | copy-start | bytes 1966084
  382.1 66.3 %copy-start.2 = (f32[256,1280]{1,0:T(8,128)S(1)}, f32[256,1280]{1,0:T(8,128)}, u32[]{:S(2)}) copy-start(f32[256,1280]{1,0:T(8,128)} %get-tuple-element.59) | copy-start | bytes 3932164
  448.4 1.8 copy-start.3
  448.4 1.9 copy-start.4
  525.6 129.6 %all-to-all-start = ((bf16[16,40,2688]{2,1,0:T(8,128)(2,1)}), bf16[16,40,2688]{2,1,0:T(8,128)(2,1)}, u32[]{:S(2)}, u32[]{:S(2)}) async-start(bf16[16,40,2688]{2,1,0:T(8,128)(2,1)} %get-tuple-element.87), calls=%async_computation | async-start | bytes 6881280 | tf_op jit(solution)/shard_map/all_to_all | solution.py:1648
  571.2 81.5 %copy-start.8 = (f32[40,2688]{1,0:T(8,128)S(1)}, f32[40,2688]{1,0:T(8,128)}, u32[]{:S(2)}) copy-start(f32[40,2688]{1,0:T(8,128)} %get-tuple-element.120) | copy-start | bytes 1290244
  571.2 81.5 %copy-start.10 = (bf16[40,2688]{1,0:T(8,128)(2,1)S(1)}, bf16[40,2688]{1,0:T(8,128)(2,1)}, u32[]{:S(2)}) copy-start(bf16[40,2688]{1,0:T(8,128)(2,1)} %sh_ref.1) | copy-start | bytes 645124
  571.2 81.6 %copy-start.7 = (f32[256,1280]{1,0:T(8,128)S(1)}, f32[256,1280]{1,0:T(8,128)}, u32[]{:S(2)}) copy-start(f32[256,1280]{1,0:T(8,128)} %get-tuple-element.58) | copy-start | bytes 3932164
  655.2 3.0 copy-start.1
  658.2 2.9 copy-start
  658.2 2.9 copy-start.13
  658.2 3.5 copy-start.6
  661.7 1.5 copy-start.9
  661.7 2.3 copy-start.11

commit v7 on v6

--- a/solution.py
+++ b/solution.py
@@ -839,7 +839,7 @@
 
 def expert_kernel(
     steps, dps, lanes, cores, hidden, x_ref, c_ref, w_ref, down_ref, own_ref,
-    dx_ref, gu_ref, hid_ref, line_ref, mine, from_dp, out, came, local,
+    dx_ref, gu_ref, hid_ref, f_ref, line_ref, mine, from_dp, out, came, local,
 ):
     dp, fs, z, c = place(cores)
     step = pl.program_id(0)
@@ -862,6 +862,7 @@
     gu_ref[:, :hidden] = dgate
     gu_ref[:, hidden:] = dup
     hid_ref[...] = hid
+    f_ref[...] = dot_nt(hid, down_ref[...]).astype(BF)
 
     @pl.when(step == steps - 1)
     def _():
@@ -895,12 +896,13 @@
             ANY,
         ],
         out_specs=[
-            row(model), row(2 * hidden), row(hidden), pl.BlockSpec(own.shape[1:], lambda i: (0, 0, 0)),
+            row(model), row(2 * hidden), row(hidden), row(model), pl.BlockSpec(own.shape[1:], lambda i: (0, 0, 0)),
         ],
         out_shape=[
             jax.ShapeDtypeStruct((rows, model), BF),
             jax.ShapeDtypeStruct((rows, 2 * hidden), BF),
             jax.ShapeDtypeStruct((rows, hidden), BF),
+            jax.ShapeDtypeStruct((rows, model), BF),
             jax.ShapeDtypeStruct(own.shape[1:], BF),
         ],
         scratch_shapes=[
@@ -1022,88 +1024,6 @@
         pltpu.VMEM(hops + (tokens, model), BF),
         dma(hops), dma(hops), dma(ways), dma(ways), dma((lanes,)),
     ]
-
-
-def combine_kernel(
-    dps, lanes, cores, part_ref, pick_ref, hid_ref, w_ref, line_ref, out_ref, f_ref, sum_ref,
-    hid, down, load, from_z, s_out, s_in, *scratch,
-):
-    work = Combine(part_ref, pick_ref, out_ref, scratch, dps, lanes, cores)
-    dp, fs, z, c = place(cores)
-    hidden = hid.shape[1]
-    slots = f_ref.shape[2]
-    loads = [
-        pltpu.make_async_copy(hid_ref, hid, load.at[0]),
-        pltpu.make_async_copy(w_ref, down, load.at[1]),
-    ]
-    for copy in loads:
-        copy.start()
-
-    def along(k):
-        t = lax.rem(z + k, lanes)
-        return send(
-            line_ref.at[t], from_z.at[k - 1], s_out.at[k - 1], s_in.at[k - 1], (dp, t * cores + c)
-        )
-
-    greet(
-        [(lax.rem(dp + m, dps), fs) for m in range(1, dps)]
-        + [(dp, lax.rem(z + k, lanes) * cores + c) for k in range(1, lanes)]
-    )
-    work.begin()
-    for k in range(1, lanes):
-        along(k).start()
-    for copy in loads:
-        copy.wait()
-
-    def forward(m):
-        for block in range(lanes):
-            row = (m * lanes + block) * slots
-            f_ref[m, block] = dot_nt(hid[row : row + slots, :], down[...]).astype(BF)
-
-    per = -(-dps // max(lanes - 1, 1))
-    for step in range(1, max(lanes, 2)):
-        for m in range((step - 1) * per, min(step * per, dps)):
-            forward(m)
-        if step < lanes:
-            work.advance(step)
-    total = line_ref[z].astype(F32)
-    for k in range(1, lanes):
-        along(k).wait_recv()
-        total = total + from_z[k - 1].astype(F32)
-    sum_ref[...] = total
-    work.finish()
-    for k in range(1, lanes):
-        along(k).wait_send()
-
-
-def combine(parts, picks, hid, w, line, lanes, cores):
-    dps, _, slots, model = parts.shape
-    tokens = picks.shape[3]
-    hidden = hid.shape[1]
-    dma = pltpu.SemaphoreType.DMA
-    whole = pl.BlockSpec(memory_space=pltpu.VMEM)
-    return pl.pallas_call(
-        functools.partial(combine_kernel, dps, lanes, cores),
-        in_specs=[ANY, whole, ANY, ANY, whole],
-        out_specs=[whole] * 3,
-        out_shape=[
-            jax.ShapeDtypeStruct((tokens, model), F32),
-            jax.ShapeDtypeStruct(parts.shape, BF),
-            jax.ShapeDtypeStruct(line.shape[1:], F32),
-        ],
-        scratch_shapes=[
-            pltpu.VMEM(hid.shape, BF),
-            pltpu.VMEM((model, hidden), BF),
-            dma((2,)),
-            pltpu.VMEM((max(lanes - 1, 1),) + line.shape[1:], BF),
-        ]
-        + pair(lanes)
-        + combine_scratch(dps, lanes, slots, tokens, model),
-        cost_estimate=lasts(70),
-        compiler_params=pltpu.CompilerParams(
-            collective_id=4, has_side_effects=True, vmem_limit_bytes=VMEM_LIMIT
-        ),
-    )(parts, picks, hid, w, line)
 
 
 class Gradient:
@@ -1165,56 +1085,74 @@
                 self.across(third, m).wait_send()
 
 
-def turn_kernel(
-    dps, lanes, cores, x_ref, part_ref, pick_ref, xs_ref, cs_ref, gu_ref, hid_ref,
-    full_ref, out_ref, g_ref, *scratch,
+def combine_kernel(
+    dps, lanes, cores, part_ref, pick_ref, xs_ref, cs_ref, gu_ref, hid_ref, line_ref,
+    out_ref, g_ref, sum_ref, from_z, s_out, s_in, *scratch,
 ):
     work = Combine(part_ref, pick_ref, out_ref, scratch[:8], dps, lanes, cores)
     gradient = Gradient(
-        (xs_ref, cs_ref, gu_ref, hid_ref), g_ref, scratch[8:16], g_ref.shape[0], g_ref.shape[1], cores
+        (xs_ref, cs_ref, gu_ref, hid_ref), g_ref, scratch[8:], g_ref.shape[0], g_ref.shape[1], cores
     )
-    chain = Chain(x_ref, full_ref, lanes, cores, scratch[16:])
-    dp, fs = chain.dp, chain.fs
+    dp, fs, z, c = place(cores)
+
+    def along(k):
+        t = lax.rem(z + k, lanes)
+        return send(
+            line_ref.at[t], from_z.at[k - 1], s_out.at[k - 1], s_in.at[k - 1], (dp, t * cores + c)
+        )
+
     gradient.begin()
-    greet(sequence_peers(dp, fs, lanes * cores) + [(lax.rem(dp + m, dps), fs) for m in range(1, dps)])
-    chain.begin()
+    greet(
+        [(lax.rem(dp + m, dps), fs) for m in range(1, dps)]
+        + [(dp, lax.rem(z + k, lanes) * cores + c) for k in range(1, lanes)]
+        + [(dp, z * cores + lax.rem(c + m, cores)) for m in range(1, cores)]
+    )
     work.begin()
+    for k in range(1, lanes):
+        along(k).start()
     gradient.multiply(0)
     for step in range(1, lanes):
-        chain.advance(step)
         work.advance(step)
         if step == 1:
             gradient.multiply(1)
     if lanes == 1:
         gradient.multiply(1)
     gradient.multiply(2)
-    chain.finish()
+    total = line_ref[z].astype(F32)
+    for k in range(1, lanes):
+        along(k).wait_recv()
+        total = total + from_z[k - 1].astype(F32)
+    sum_ref[...] = total
     work.finish()
     for third in range(3):
         gradient.collect(third)
     gradient.finish()
-
-
-def turn(x, parts, picks, slots_in, grads, shard, lanes, cores):
+    for k in range(1, lanes):
+        along(k).wait_send()
+
+
+def combine(parts, picks, slots_in, grads, line, lanes, cores):
     dps, _, slots, model = parts.shape
     tokens = picks.shape[3]
     xs, cs = slots_in
     gu, hid = grads
-    experts = dps * lanes
+    experts, shard = dps * lanes, line.shape[1]
     hidden = hid.shape[1]
     dma = pltpu.SemaphoreType.DMA
     others = max(cores - 1, 1)
     whole = pl.BlockSpec(memory_space=pltpu.VMEM)
     return pl.pallas_call(
-        functools.partial(turn_kernel, dps, lanes, cores),
-        in_specs=[ANY, ANY, whole] + [ANY] * 4,
-        out_specs=[ANY, whole, whole],
+        functools.partial(combine_kernel, dps, lanes, cores),
+        in_specs=[ANY, whole] + [ANY] * 4 + [whole],
+        out_specs=[whole] * 3,
         out_shape=[
-            jax.ShapeDtypeStruct((lanes, cores) + x.shape, x.dtype),
             jax.ShapeDtypeStruct((tokens, model), F32),
             jax.ShapeDtypeStruct((experts, shard, 3 * hidden), BF),
+            jax.ShapeDtypeStruct(line.shape[1:], F32),
         ],
-        scratch_shapes=combine_scratch(dps, lanes, slots, tokens, model)
+        scratch_shapes=[pltpu.VMEM((max(lanes - 1, 1),) + line.shape[1:], BF)]
+        + pair(lanes)
+        + combine_scratch(dps, lanes, slots, tokens, model)
         + [
             pltpu.VMEM(xs.shape, BF),
             pltpu.VMEM(hid.shape, BF),
@@ -1222,13 +1160,50 @@
             pltpu.VMEM((3, cores, experts, shard, hidden), BF),
             pltpu.VMEM((3, others, experts, shard, hidden), BF),
             dma((2,)), dma((3, others)), dma((3, others)),
-        ]
-        + chain_sems(lanes, cores),
+        ],
+        cost_estimate=lasts(70),
+        compiler_params=pltpu.CompilerParams(
+            collective_id=4, has_side_effects=True, vmem_limit_bytes=VMEM_LIMIT
+        ),
+    )(parts, picks, xs, cs, gu, hid, line)
+
+
+def turn_kernel(
+    dps, lanes, cores, x_ref, part_ref, pick_ref, middle_ref, shared_ref, full_ref, out_ref, routed, *scratch
+):
+    work = Combine(part_ref, pick_ref, routed, scratch[:8], dps, lanes, cores)
+    chain = Chain(x_ref, full_ref, lanes, cores, scratch[8:])
+    dp, fs = chain.dp, chain.fs
+    greet(sequence_peers(dp, fs, lanes * cores) + [(lax.rem(dp + m, dps), fs) for m in range(1, dps)])
+    chain.begin()
+    work.begin()
+    for step in range(1, lanes):
+        chain.advance(step)
+        work.advance(step)
+    chain.finish()
+    work.finish()
+    out_ref[...] = (middle_ref[...] + shared_ref[...] + routed[...]).astype(BF)
+
+
+def turn(x, parts, picks, middle, shared, lanes, cores):
+    dps, _, slots, model = parts.shape
+    tokens = picks.shape[3]
+    whole = pl.BlockSpec(memory_space=pltpu.VMEM)
+    return pl.pallas_call(
+        functools.partial(turn_kernel, dps, lanes, cores),
+        in_specs=[ANY, ANY, whole, whole, whole],
+        out_specs=[ANY, whole],
+        out_shape=[
+            jax.ShapeDtypeStruct((lanes, cores) + x.shape, x.dtype),
+            jax.ShapeDtypeStruct((tokens, model), BF),
+        ],
+        scratch_shapes=[pltpu.VMEM((tokens, model), F32)]
+        + combine_scratch(dps, lanes, slots, tokens, model) + chain_sems(lanes, cores),
         cost_estimate=lasts(90),
         compiler_params=pltpu.CompilerParams(
             collective_id=1, has_side_effects=True, vmem_limit_bytes=VMEM_LIMIT
         ),
-    )(x, parts, picks, xs, cs, gu, hid)
+    )(x, parts, picks, middle, shared)
 
 
 def attend_back_kernel(
@@ -1618,11 +1593,11 @@
     c_slots = c_slots.reshape(-1, model)
     w_own = w_own.reshape(model, 2 * hidden)
     w_down = w_down.reshape(model, hidden)
-    dx_slots, gu_slots, hid_slots, g_line = expert(x_slots, c_slots, w_own, w_down, g_core, cores)
+    dx_slots, gu_slots, hid_slots, f_slots, g_line = expert(x_slots, c_slots, w_own, w_down, g_core, cores)
 
     shape = (dps, lanes, slots, model)
-    dx_routed, f_slots, g_shared = combine(
-        dx_slots.reshape(shape), picks, hid_slots, w_down, g_line, lanes, cores
+    dx_routed, g_own, g_shared = combine(
+        dx_slots.reshape(shape), picks, (x_slots, c_slots), (gu_slots, hid_slots), g_line, lanes, cores
     )
     dxn_two = dx_shared + dx_routed
     scaled = dxn_two * gain_two
@@ -1631,11 +1606,9 @@
     )
     d_attn = dx_two.astype(BF)
 
-    da_all, routed, g_own = turn(
-        d_attn, f_slots, weigh, (x_slots, c_slots), (gu_slots, hid_slots), shard, lanes, cores
-    )
+    da_all, layer_out = turn(d_attn, f_slots.reshape(shape), weigh, middle, f_shared, lanes, cores)
+    da_all, g_own = lax.optimization_barrier((da_all, g_own))
     da_all = da_all.reshape(seq, model)
-    layer_out = (middle + f_shared + routed).astype(BF)
     dxn_part, g_part = attend_back(
         da_all, xn_one, out_all, (q, k, kt, v, o, lse), (cos, sin), w_heads, shard,
         tokens, busy, dps, lanes, cores,

time: 674 us -> 677 us (level)
  Pallas kernels: 627 us -> 637 us
    pallas_call x1, Pallas kernels: 125 us -> 137 us  [dispatch(): pl.pallas_call(functools.partial(dispatch_kernel, dps, lanes, cores, topk...]
  transfers between devices with their start and end apart: 1 -> 1, of which waited for: 0 -> 0; matrix products, arithmetic and copies ran while one was open for 0% -> 0% of each run, Pallas kernels for 18% -> 17%
where the time goes in v7:
time: 677 us; the launch traced here: 675 us
  Pallas kernels  637 us (94%)
  local copies, waits for them, and re-layouts  14.6 us (2%)
  other arithmetic  9.81 us (1%)
  starting transfers between devices  9.37 us (1%)
    pallas_call x1, Pallas kernels, dispatch(): pl.pallas_call(functools.partial(dispatch_kernel, dps, lanes, cores, topk...  137 us
    pallas_call x1, Pallas kernels, attend(): pl.pallas_call(functools.partial(attend_kernel, dps, lanes, cores, busy,...  134 us
    pallas_call x1, Pallas kernels, finish(): pl.pallas_call(functools.partial(finish_kernel, dps, lanes, cores, busy),...  81.1 us
    pallas_call x1, Pallas kernels, turn(): pl.pallas_call(functools.partial(turn_kernel, dps, lanes, cores), in_spec...  68.7 us
    pallas_call x1, Pallas kernels, combine(): pl.pallas_call(functools.partial(combine_kernel, dps, lanes, cores), in_s...  67.5 us
    pallas_call x1, Pallas kernels, start(): pl.pallas_call(functools.partial(start_kernel, dps, lanes, cores, topk, b...  65.3 us
    pallas_call x1, Pallas kernels, expert(): pl.pallas_call(functools.partial(expert_kernel, rows // block, dps, lanes...  46.9 us
    pallas_call x1, Pallas kernels, attend_back(): pl.pallas_call(functools.partial(attend_back_kernel, dps, lanes, cores, b...  36.5 us
  transfers between devices with their start and end apart: 1, of which 0 were waited for; matrix products, arithmetic and copies ran while one was open for 0% of the time, Pallas kernels for 17%

profile of v7, /device:TPU:20, one launch (start us, length us, event | category | flops | bytes accessed | tf_op | source)
XLA Modules:
  0.0 674.9 jit_solution(7429048091482047368)
XLA Ops:
  0.6 0.7 convert_bitcast_fusion
  1.3 0.8 copy.30
  2.1 1.2 reshape.83
  3.2 0.6 pad.14.gn_ref
  4.5 1.3 reshape.85.wh_ref
  5.9 0.6 select_maximum_fusion.tab_ref
  6.5 65.3 %shard_map.162 = (bf16[4,2,256,1280]{3,2,1,0:T(8,128)(2,1)}, bf16[4,8,40,768]{3,2,1,0:T(8,128)(2,1)}, f32[4,16,256]{2,1,0:T(8,128)}, bf16[4,4,2,40,1280]{4,3,2,1...) custom-call(bf16[256,1280]{1,0:T(8,128)(2,1)} %x_ref.3, ...), custom_call_target="tpu_custom_call" | custom-call | bytes 252000000 | tf_op jit(solution)/shard_map/pallas_call | solution.py:443
  71.8 1.0 slice_convert_fusion
  73.0 0.6 slice_reduce_fusion
  73.6 134.0 %shard_map.163 = (bf16[2048,1280]{1,0:T(8,128)(2,1)}, bf16[2048,256]{1,0:T(8,128)(2,1)}, bf16[2048,256]{1,0:T(8,128)(2,1)}, bf16[2048,256]{1,0:T(8,128)(2,1)}, b...) custom-call(bf16[2048,1280]{1,0:T(8,128)(2,1)} %bitcast.31, ...), custom_call_target="tpu_custom_call" | custom-call | bytes 360000000 | tf_op jit(solution)/shard_map/pallas_call | solution.py:638
  207.7 3.3 multiply_reduce_fusion.1
  211.0 1.2 multiply_convert_fusion.x_ref
  212.1 136.9 %shard_map.164 = (bf16[4,4,128,1280]{3,2,1,0:T(8,128)(2,1)}, bf16[4,4,128,1280]{3,2,1,0:T(8,128)(2,1)}, bf16[4,4,2,40,1792]{4,3,2,1,0:T(8,128)(2,1)}, bf16[4,4,2...) custom-call(bf16[256,1280]{1,0:T(8,128)(2,1)} %multiply_convert_fusion., ...), custom_call_target="tpu_custom_call" | custom-call | bytes 450000000 | tf_op jit(solution)/shard_map/pallas_call | solution.py:813
  349.1 46.9 %shard_map.165 = (bf16[2048,1280]{1,0:T(8,128)(2,1)}, bf16[2048,1792]{1,0:T(8,128)(2,1)}, bf16[2048,896]{1,0:T(8,128)(2,1)}, bf16[2048,1280]{1,0:T(8,128)(2,1)}, bf16[4,40,2688]{2,1,0:T(8,128)(2,1)}) custom-call(bf16[2048,1280]{1,0:T(8,128)(2,1)} %bitcast.23, bf16[2048,1280]{1,0:T(8,128)(2,1)} %bitcast.25, bf16[1280,1792]{1,0:T(8,128)(2,1)} %bitcast.34, ...), custom_call_target="tpu_custom_call" | custom-call | bytes 144000000 | tf_op jit(solution)/shard_map/pallas_call | solution.py:888
  396.0 67.5 %shard_map.166 = (f32[256,1280]{1,0:T(8,128)}, bf16[16,40,2688]{2,1,0:T(8,128)(2,1)}, f32[40,2688]{1,0:T(8,128)}) custom-call(bf16[4,4,128,1280]{3,2,1,0:T(8,128)(2,1)} %bitcast.33, bf16[4,4,128,256]{3,2,1,0:T(8,128)(2,1)} %get-tuple-element.56.pick_ref, bf16[2048,1280]{1,0:T(8,128)(2,1)} %bitcast.24, bf16[2048,1280]{1,0:T(8,128)(2,1)} %bitcast.26, ...), custom_call_target="tpu_custom_call" | custom-call | bytes 252000000 | tf_op jit(solution)/shard_map/pallas_call | solution.py:1144
  463.5 1.8 multiply_reduce_fusion
  465.4 1.7 fusion.1
  467.1 68.7 %shard_map.167 = (bf16[4,2,256,1280]{3,2,1,0:T(8,128)(2,1)}, bf16[256,1280]{1,0:T(8,128)(2,1)}) custom-call(bf16[256,1280]{1,0:T(8,128)(2,1)} %get-tuple-element.107.x_ref, bf16[4,4,128,1280]{3,2,1,0:T(8,128)(2,1)} %bitcast.30, bf16[4,4,128,256]{3,2,1,0:T(8,128)(2,1)} %get-tuple-element.72.pick_ref, f32[256,1280]{1,0:T(8,128)} %copy-done, ...), custom_call_target="tpu_custom_call" | custom-call | bytes 324000000 | tf_op jit(solution)/shard_map/pallas_call | solution.py:1192
  535.8 9.4 %all-to-all-start = ((bf16[16,40,2688]{2,1,0:T(8,128)(2,1)}), bf16[16,40,2688]{2,1,0:T(8,128)(2,1)S(1)}, u32[]{:S(2)}, u32[]{:S(2)}) async-start(bf16[16,40,2688]{2,1,0:T(8,128)(2,1)} %get-tuple-element.91), calls=%async_computation | async-start | bytes 6881280 | tf_op jit(solution)/shard_map/all_to_all | solution.py:1621
  545.2 36.5 %shard_map.168 = (bf16[4,2,256,1280]{3,2,1,0:T(8,128)(2,1)}, bf16[4,8,40,1024]{3,2,1,0:T(8,128)(2,1)}) custom-call(bf16[2048,1280]{1,0:T(8,128)(2,1)} %bitcast.32, bf16[2048,1280]{1,0:T(8,128)(2,1)} %get-tuple-element.78.xn_ref, bf16[1280,1280]{1,0:T(8,128)(2,1)} %bitcast.36, bf16[2048,256]{1,0:T(8,128)(2,1)} %get-tuple-element.79.q_ref, ...), custom_call_target="tpu_custom_call" | custom-call | bytes 180000000 | tf_op jit(solution)/shard_map/pallas_call | solution.py:1322
  581.6 81.1 %shard_map.169 = (f32[256,1280]{1,0:T(8,128)}, f32[40,3840]{1,0:T(8,128)}, f32[40,1280]{1,0:T(8,128)}, f32[40,1]{1,0:T(8,128)}) custom-call(bf16[4,2,256,1280]{3,2,1,0:T(8,128)(2,1)} %get-tuple-element.85.part_ref, bf16[4,8,40,1024]{3,2,1,0:T(8,128)(2,1)} %get-tuple-element.86.g_ref, bf16[256,1280]{1,0:T(8,128)(2,1)} %x_ref.3, ...), custom_call_target="tpu_custom_call" | custom-call | bytes 237600000 | tf_op jit(solution)/shard_map/pallas_call | solution.py:1507
  662.7 0.8 copy.32
  663.5 1.1 multiply_reduce_fusion.2
  665.2 1.5 copy-done.2
  666.7 0.6 fusion
  667.2 2.3 copy-done.1
  669.6 0.6 maximum_divide_fusion
  670.1 0.8 copy.40
  671.0 1.1 copy.41
  672.5 0.8 copy.42
  673.3 0.7 copy.43
  674.0 0.8 copy.44
  (35 shorter events, 1.9 us)
Async XLA Ops:
  4.3 1.6 copy-start.12
  73.6 134.0 %copy-start.6 = (bf16[256,1280]{1,0:T(8,128)(2,1)S(1)}, bf16[256,1280]{1,0:T(8,128)(2,1)}, u32[]{:S(2)}) copy-start(bf16[256,1280]{1,0:T(8,128)(2,1)} %x_ref.3) | copy-start | bytes 1966084
  210.9 254.4 %copy-start = (f32[256,1280]{1,0:T(8,128)}, f32[256,1280]{1,0:T(8,128)S(1)}, u32[]{:S(2)}) copy-start(f32[256,1280]{1,0:T(8,128)S(1)} %get-tuple-element.112.middle_ref) | copy-start | bytes 3932164
  395.9 67.5 %copy-start.3 = (f32[256,1280]{1,0:T(8,128)S(1)}, f32[256,1280]{1,0:T(8,128)}, u32[]{:S(2)}) copy-start(f32[256,1280]{1,0:T(8,128)} %get-tuple-element.60) | copy-start | bytes 3932164
  463.5 1.8 copy-start.4
  463.5 1.9 copy-start.5
  535.8 128.9 %all-to-all-start = ((bf16[16,40,2688]{2,1,0:T(8,128)(2,1)}), bf16[16,40,2688]{2,1,0:T(8,128)(2,1)S(1)}, u32[]{:S(2)}, u32[]{:S(2)}) async-start(bf16[16,40,2688]{2,1,0:T(8,128)(2,1)} %get-tuple-element.91), calls=%async_computation | async-start | bytes 6881280 | tf_op jit(solution)/shard_map/all_to_all | solution.py:1621
  664.7 2.0 copy-start.2
  666.7 2.9 copy-start.1
  666.7 2.9 copy-start.13
  666.7 3.5 copy-start.9
  669.5 1.4 copy-start.7
  671.0 1.5 copy-start.10
  671.0 2.3 copy-start.11
  672.4 1.5 copy-start.8
